TPU v7x, 512 devices: a whole 4x4x16 slice. The times are simulated.
512 devices in a mesh: brick: 32 (over y, x, z_hi), chan: 16 (over z_lo, core).
Axes of the slice: x: 4, y: 4, z: 16 (z_hi: 2, z_lo: 8; z = z_hi * 8 + z_lo), core: 2. Of those that a mesh axis runs over, the one named last changes fastest.
Arguments:
- node_x: bfloat16 [49, 128, 4096], P(None, 'chan', 'brick'), may hold values from -6 to 6
- cotangent: bfloat16 [49, 128, 4096], P(None, 'chan', 'brick'), may hold values from -6 to 6
- wigner: bfloat16 [235, 32768], P(None, 'brick'), may hold values from -4 to 4
- src_index: int32 [32768], P('brick'), may hold values from 0 to 191
- dst_index: int32 [32768], P('brick'), may hold values from 0 to 127
- edge_scale: float32 [32768], P('brick'), may hold values from 0.1 to 1
- edge_count: int32 [32], P('brick'), may hold values from 341 to 1024, as said below
- w_zero: bfloat16 [7, 128, 7, 128], P(None, 'chan'), may hold values from -0.1875 to 0.1875
- w_one: bfloat16 [2, 6, 128, 6, 128], P(None, None, 'chan'), may hold values from -0.15625 to 0.15625
- w_two: bfloat16 [2, 5, 128, 5, 128], P(None, None, 'chan'), may hold values from -0.15625 to 0.15625
Outputs:
- grad_x: float32 [49, 128, 4096], P(None, 'chan', 'brick')
- grad_w_zero: float32 [7, 128, 7, 128], P(None, 'chan', None, 'brick')
- grad_w_one: float32 [2, 6, 128, 6, 128], P(None, None, 'chan', None, 'brick')
- grad_w_two: float32 [2, 5, 128, 5, 128], P(None, None, 'chan', None, 'brick')
Inputs may be any that keep to these rules, and one draw needn't show every extreme that they name: Slots 0 to edge_count[b] - 1 of brick b hold edges, the rest are padding; one brick's list is full.
All inputs are finite; a program needn't handle non-finite values.
Results may differ from a plain program's by a relative error of at most 0.0065.
Values may be sent and summed in bfloat16 or wider, within the bound.
No kernel may reach another device: no remote copies, remote signals or barrier semaphores. Data moves between devices by JAX's collectives and lax.ppermute only.
A program may use at most 64 MiB of HBM per device.

v0:
```python
import jax
import jax.numpy as jnp
from jax import lax
from jax.sharding import PartitionSpec as P


def padded(x, sides, width):
    for axis, dim in sides:
        devices, length = (lax.axis_size(axis), x.shape[dim])
        up = [(i, (i + 1) % devices) for i in range(devices)]
        down = [(j, i) for i, j in up]
        last = lax.slice_in_dim(x, length - width, length, axis=dim)
        initial = lax.slice_in_dim(x, 0, width, axis=dim)
        before = lax.ppermute(last, axis, up)
        after = lax.ppermute(initial, axis, down)
        x = jnp.concatenate([before, x, after], axis=dim)
    return x


def passed_along(block, axis, distance):
    devices = range(lax.axis_size(axis))
    route = [((i - distance) % len(devices), i) for i in devices]
    return lax.ppermute(block, axis, route)


def kept_row(degree, azimuth):
    if azimuth == 0:
        return degree
    if azimuth == 1:
        return 6 + degree
    if azimuth == -1:
        return 12 + degree
    if azimuth == 2:
        return 17 + degree
    return 22 + degree


def to_edge_frame(values, wigner):
    kept_rows = [None] * 29
    offset = 0
    for degree in range(7):
        max_order = min(degree, 2)
        span_cols = 2 * degree + 1
        for azimuth in range(-max_order, max_order + 1):
            running = jnp.zeros(values.shape[1:], jnp.float32)
            for column in range(span_cols):
                factor = wigner[offset + (azimuth + max_order) * span_cols + column].astype(
                    jnp.float32
                )
                running = running + factor[None, :] * values[degree * degree + column].astype(
                    jnp.float32
                )
            kept_rows[kept_row(degree, azimuth)] = running
        offset += (2 * max_order + 1) * span_cols
    return jnp.stack(kept_rows)


def from_edge_frame(kept_rows, wigner):
    full_rows = []
    offset = 0
    for degree in range(7):
        max_order = min(degree, 2)
        span_cols = 2 * degree + 1
        for column in range(span_cols):
            running = jnp.zeros(kept_rows.shape[1:], jnp.float32)
            for azimuth in range(-max_order, max_order + 1):
                factor = wigner[offset + (azimuth + max_order) * span_cols + column].astype(
                    jnp.float32
                )
                running = running + factor[None, :] * kept_rows[kept_row(degree, azimuth)]
            full_rows.append(running)
        offset += (2 * max_order + 1) * span_cols
    return jnp.stack(full_rows)


def contract(weights, grads):
    return lax.dot_general(
        weights, grads, (((2, 3), (0, 1)), ((), ())), preferred_element_type=jnp.float32
    )


def outer(inputs, grads):
    return lax.dot_general(
        inputs, grads, (((2,), (2,)), ((), ())), preferred_element_type=jnp.float32
    )


def so2_back(w_zero, w_one, w_two, edge_grad, edge_in):
    back_rows = [contract(w_zero, edge_grad[0:7])]
    term_zero = outer(edge_in[0:7], edge_grad[0:7])
    weight_terms = []
    for weights, bottom, middle, ceiling in ((w_one, 7, 13, 19), (w_two, 19, 24, 29)):
        grad_plus = edge_grad[bottom:middle]
        grad_minus = edge_grad[middle:ceiling]
        in_plus = edge_in[bottom:middle]
        in_minus = edge_in[middle:ceiling]
        back_rows.append(contract(weights[0], grad_plus) + contract(weights[1], grad_minus))
        back_rows.append(contract(weights[0], grad_minus) - contract(weights[1], grad_plus))
        weight_terms.append(
            jnp.stack(
                [
                    outer(in_plus, grad_plus) + outer(in_minus, grad_minus),
                    outer(in_plus, grad_minus) - outer(in_minus, grad_plus),
                ]
            )
        )
    return (jnp.concatenate(back_rows, axis=0), term_zero, weight_terms[0], weight_terms[1])


def add_columns(summed, term, first_col, axis_dim):
    current = lax.dynamic_slice_in_dim(summed, first_col, term.shape[axis_dim], axis_dim)
    return lax.dynamic_update_slice_in_dim(summed, current + term, first_col, axis_dim)


def body(
    node_x, cotangent, wigner, src_index, dst_index, edge_scale, edge_count, w_zero, w_one, w_two
):
    atom_count = node_x.shape[2]
    own_chan = node_x.shape[1]
    coef_count = node_x.shape[0]
    chan_total = w_zero.shape[3]
    rim_len = atom_count // 4
    slot_count = src_index.shape[0]
    block_len = min(512, slot_count)
    live_count = edge_count[0]
    padded_len = atom_count + 2 * rim_len
    extended = padded(node_x, (("brick", 2),), rim_len)
    at_source = jnp.take(extended, src_index, axis=2)
    edge_in = to_edge_frame(at_source, wigner).astype(jnp.bfloat16)
    block_total = slot_count // block_len
    initial = (
        jnp.zeros((29, own_chan, slot_count), jnp.float32),
        jnp.zeros(w_zero.shape[:3] + (chan_total,), jnp.float32),
        jnp.zeros(w_one.shape[:4] + (chan_total,), jnp.float32),
        jnp.zeros(w_two.shape[:4] + (chan_total,), jnp.float32),
    )
    full_grad = lax.all_gather(cotangent, "chan", axis=1, tiled=True)

    def block_step(block_index, running):
        edge_back, sum_zero, sum_one, sum_two = running
        begin_at = block_index * block_len
        dst_block = lax.dynamic_slice_in_dim(dst_index, begin_at, block_len)
        wig_block = lax.dynamic_slice_in_dim(wigner, begin_at, block_len, 1)
        scale_block = lax.dynamic_slice_in_dim(edge_scale, begin_at, block_len)
        position = begin_at + lax.iota(jnp.int32, block_len)
        factor = jnp.where(position < live_count, 0.25 * scale_block, 0.0)
        at_dest = jnp.take(full_grad, dst_block, axis=2)
        edge_grad = (to_edge_frame(at_dest, wig_block) * factor).astype(jnp.bfloat16)
        edge_block = lax.dynamic_slice_in_dim(edge_in, begin_at, block_len, 2)
        back_rows, term_zero, term_one, term_two = so2_back(
            w_zero, w_one, w_two, edge_grad, edge_block
        )
        edge_back = add_columns(edge_back, back_rows, begin_at, 2)
        sum_zero = add_columns(sum_zero, term_zero, 0, 3)
        sum_one = add_columns(sum_one, term_one, 0, 4)
        sum_two = add_columns(sum_two, term_two, 0, 4)
        return (edge_back, sum_zero, sum_one, sum_two)

    folded = lax.fori_loop(0, block_total, block_step, initial)
    edge_back, sum_zero, sum_one, sum_two = folded

    def back_step(block_index, summed):
        begin_at = block_index * block_len
        kept_rows = lax.dynamic_slice_in_dim(edge_back, begin_at, block_len, 2)
        wig_block = lax.dynamic_slice_in_dim(wigner, begin_at, block_len, 1)
        src_block = lax.dynamic_slice_in_dim(src_index, begin_at, block_len)
        full_rows = from_edge_frame(kept_rows, wig_block)
        onehot = (src_block[:, None] == lax.iota(jnp.int32, padded_len)[None, :]).astype(
            jnp.bfloat16
        )
        high_part = full_rows.astype(jnp.bfloat16)
        rest = full_rows - high_part.astype(jnp.float32)
        low_part = rest.astype(jnp.bfloat16)
        dims = (((2,), (0,)), ((), ()))
        summed = summed + lax.dot_general(
            high_part, onehot, dims, preferred_element_type=jnp.float32
        )
        return summed + lax.dot_general(low_part, onehot, dims, preferred_element_type=jnp.float32)

    grad_ext = lax.fori_loop(
        0, block_total, back_step, jnp.zeros((coef_count, own_chan, padded_len), jnp.float32)
    )
    own_part = grad_ext[:, :, rim_len : rim_len + atom_count]
    from_above = passed_along(grad_ext[:, :, :rim_len], "brick", -1)
    from_below = passed_along(grad_ext[:, :, rim_len + atom_count :], "brick", 1)
    own_part = own_part.at[:, :, :rim_len].add(from_below)
    grad_x = own_part.at[:, :, atom_count - rim_len :].add(from_above)
    return (
        grad_x,
        lax.psum_scatter(sum_zero, "brick", scatter_dimension=3, tiled=True),
        lax.psum_scatter(
            sum_one.reshape((-1,) + sum_one.shape[2:]), "brick", scatter_dimension=3, tiled=True
        ).reshape(sum_one.shape[:4] + (-1,)),
        lax.psum_scatter(
            sum_two.reshape((-1,) + sum_two.shape[2:]), "brick", scatter_dimension=3, tiled=True
        ).reshape(sum_two.shape[:4] + (-1,)),
    )


def solution(mesh):
    in_specs = (
        P(None, "chan", "brick"),
        P(None, "chan", "brick"),
        P(None, "brick"),
        P("brick"),
        P("brick"),
        P("brick"),
        P("brick"),
        P(None, "chan", None, None),
        P(None, None, "chan", None, None),
        P(None, None, "chan", None, None),
    )
    out_specs = (
        P(None, "chan", "brick"),
        P(None, "chan", None, "brick"),
        P(None, None, "chan", None, "brick"),
        P(None, None, "chan", None, "brick"),
    )
    return jax.shard_map(body, mesh=mesh, in_specs=in_specs, out_specs=out_specs, check_vma=False)
```

profile of v0, /device:TPU:1, one launch (start us, length us, event | category | flops | bytes accessed | tf_op | source)
XLA Modules:
  0.0 1859.1 jit_solution(16352673800812166662)
XLA Ops:
  8.3 16.3 collective-permute-start
  24.6 6.6 collective-permute-start.1
  55.1 3.3 gather_fusion.1
  90.6 19.4 %all-gather.2.cloned.1.call-done = bf16[49,128,128]{2,1,0:T(8,128)(2,1)} async-done(((bf16[49,8,128]{2,1,0:T(8,128)(2,1)}), bf16[49,128,128]{2,1,0:T(8,128)(2,1)}) %all-gather.2.cloned.1.call-update) | async-done | bytes 1605648 | tf_op jit(solution)/shard_map/all_gather | solution.py:137
  113.0 225.6 %while.36 = (s32[]{:T(128)}, f32[29,8,1024]{2,1,0:T(8,128)S(1)}, f32[7,8,7,128]{3,1,2,0:T(8,128)}, f32[2,6,8,6,128]{4,2,3,1,0:T(8,128)}, f32[2,5,8,5,128]{4,2,3,...) while((s32[]{:T(128)}, f32[29,8,1024]{2,1,0:T(8,128)S(1)}, ...), condition=%wide.region_1.2_spmd.clone, body=%wide.region_0.1_spmd.clone.sunk | while | flops 666715776 | bytes 142993584 | solution.py:159
  113.3 4.6 gather_fusion
  117.9 12.2 copy.642
  130.1 6.1 select_bitcast_fusion.3
  202.7 4.3 multiply_convert_fusion.3
  225.2 4.6 gather_fusion
  229.8 12.2 copy.642
  242.0 6.1 select_bitcast_fusion.3
  314.6 4.3 multiply_convert_fusion.3
  341.8 3.3 copy.623
  345.2 9.8 while.37
  355.1 5.7 collective-permute-start.2
  360.8 3.2 copy.621
  364.1 30.9 %collective-permute-done.2 = f32[49,8,32]{2,1,0:T(8,128)S(1)} collective-permute-done((f32[49,8,32]{2,1,0:T(8,128)S(1)}, f32[49,8,32]{2,1,0:T(8,128)S(1)}, u32[]{:S(2)}, u32[]{:S(2)}) %collective-permute-start.2) | collective-permute-done | bytes 50208 | tf_op jit(solution)/shard_map/ppermute | solution.py:23
  395.1 4.1 collective-permute-start.3
  401.9 33.7 %collective-permute-done.3 = f32[49,8,32]{2,1,0:T(8,128)S(1)} collective-permute-done((f32[49,8,32]{2,1,0:T(8,128)S(1)}, f32[49,8,32]{2,1,0:T(8,128)S(1)}, u32[]{:S(2)}, u32[]{:S(2)}) %collective-permute-start.3) | collective-permute-done | bytes 50208 | tf_op jit(solution)/shard_map/ppermute | solution.py:23
  435.7 7.2 scatter-add.9
  442.9 666.8 %all-reduce.3.cloned.1.call-done = f32[7,8,7,128]{1,3,2,0:T(8,128)} async-done(((f32[7,8,7,128]{1,3,2,0:T(8,128)}), f32[7,8,7,128]{1,3,2,0:T(8,128)}) %all-reduce.3.cloned.1.call-update) | async-done | bytes 200720
  1111.4 387.4 %reduce-scatter.6.cloned.1.call-done = f32[10,8,5,4]{0,1,2,3:T(8,128)} async-done(((f32[10,8,5,128]{0,1,2,3:T(8,128)}), f32[10,8,5,4]{0,1,2,3:T(8,128)}) %reduce-scatter.6.cloned.1.call-update) | async-done | bytes 6416 | tf_op jit(solution)/shard_map/reduce_scatter | solution.py:194
  1500.5 350.3 %reduce-scatter.4.cloned.1.call-done = f32[12,8,6,4]{0,1,2,3:T(8,128)} async-done(((f32[12,8,6,128]{0,1,2,3:T(8,128)}), f32[12,8,6,4]{0,1,2,3:T(8,128)}) %reduce-scatter.4.cloned.1.call-update) | async-done | bytes 9232 | tf_op jit(solution)/shard_map/reduce_scatter | solution.py:191
  (425 shorter events, 249.5 us)
Async XLA Ops:
  7.2 102.9 %all-gather.2.cloned.1.call-start = ((), (), s32[]{:S(2)}) async-start(), calls=%async_computation.2 | async-start | bytes 1705984 | tf_op jit(solution)/shard_map/all_gather | solution.py:137
  8.3 46.6 %collective-permute-start = (bf16[49,8,32]{0,1,2:T(8,128)(2,1)S(1)}, bf16[49,8,32]{0,1,2:T(8,128)(2,1)S(1)}, u32[]{:S(2)}, u32[]{:S(2)}) collective-permute-start(bf16[49,8,32]{0,1,2:T(8,128)(2,1)S(1)} %get-tuple-element.1240), channel_id=1, source_target_pairs={{0,16},{16,32},{32,48},{48,64},{64,80},{80,96},{96,112},{112,128},... | collective-permute-start | bytes 75272 | tf_op jit(solution)/shard_map/ppermute | solution.py:14
  24.6 30.4 %collective-permute-start.1 = (bf16[49,8,32]{0,1,2:T(8,128)(2,1)S(1)}, bf16[49,8,32]{0,1,2:T(8,128)(2,1)S(1)}, u32[]{:S(2)}, u32[]{:S(2)}) collective-permute-start(bf16[49,8,32]{0,1,2:T(8,128)(2,1)S(1)} %get-tuple-element.1241), channel_id=1, source_target_pairs={{16,0},{32,16},{48,32},{64,48},{80,64},{96,80},{112,96},{128,112},... | collective-permute-start | bytes 75272 | tf_op jit(solution)/shard_map/ppermute | solution.py:15
  31.2 1078.6 %all-reduce.3.cloned.1.call-start = ((), (), s32[]{:S(2)}) async-start(), calls=%async_computation.5 | async-start | bytes 6422528
  58.5 26.9 %copy-start.9 = (f32[1,1024]{1,0:T(1,128)S(1)}, f32[1,1024]{1,0:T(1,128)}, u32[]{:S(2)}) copy-start(f32[1,1024]{1,0:T(1,128)} %get-tuple-element.1080) | copy-start | bytes 12292
  58.5 26.9 %copy-start.10 = (f32[1,1024]{1,0:T(1,128)S(1)}, f32[1,1024]{1,0:T(1,128)}, u32[]{:S(2)}) copy-start(f32[1,1024]{1,0:T(1,128)} %get-tuple-element.1072) | copy-start | bytes 12292
  58.5 26.9 %copy-start.11 = (f32[1,1024]{1,0:T(1,128)S(1)}, f32[1,1024]{1,0:T(1,128)}, u32[]{:S(2)}) copy-start(f32[1,1024]{1,0:T(1,128)} %get-tuple-element.1073) | copy-start | bytes 12292
  58.6 26.8 %copy-start.12 = (f32[1,1024]{1,0:T(1,128)S(1)}, f32[1,1024]{1,0:T(1,128)}, u32[]{:S(2)}) copy-start(f32[1,1024]{1,0:T(1,128)} %get-tuple-element.1074) | copy-start | bytes 12292
  58.6 26.8 %copy-start.13 = (f32[1,1024]{1,0:T(1,128)S(1)}, f32[1,1024]{1,0:T(1,128)}, u32[]{:S(2)}) copy-start(f32[1,1024]{1,0:T(1,128)} %get-tuple-element.1075) | copy-start | bytes 12292
  58.6 26.8 %copy-start.14 = (f32[1,1024]{1,0:T(1,128)S(1)}, f32[1,1024]{1,0:T(1,128)}, u32[]{:S(2)}) copy-start(f32[1,1024]{1,0:T(1,128)} %get-tuple-element.1076) | copy-start | bytes 12292
  58.6 26.8 %copy-start.15 = (f32[1,1024]{1,0:T(1,128)S(1)}, f32[1,1024]{1,0:T(1,128)}, u32[]{:S(2)}) copy-start(f32[1,1024]{1,0:T(1,128)} %get-tuple-element.1077) | copy-start | bytes 12292
  58.6 28.8 %copy-start.24 = (f32[1,1024]{1,0:T(1,128)S(1)}, f32[1,1024]{1,0:T(1,128)}, u32[]{:S(2)}) copy-start(f32[1,1024]{1,0:T(1,128)} %get-tuple-element.1043) | copy-start | bytes 12292
  58.6 28.8 %copy-start.25 = (f32[1,1024]{1,0:T(1,128)S(1)}, f32[1,1024]{1,0:T(1,128)}, u32[]{:S(2)}) copy-start(f32[1,1024]{1,0:T(1,128)} %get-tuple-element.1044) | copy-start | bytes 12292
  58.6 28.8 %copy-start.26 = (f32[1,1024]{1,0:T(1,128)S(1)}, f32[1,1024]{1,0:T(1,128)}, u32[]{:S(2)}) copy-start(f32[1,1024]{1,0:T(1,128)} %get-tuple-element.1045) | copy-start | bytes 12292
  58.6 28.8 %copy-start.27 = (f32[1,1024]{1,0:T(1,128)S(1)}, f32[1,1024]{1,0:T(1,128)}, u32[]{:S(2)}) copy-start(f32[1,1024]{1,0:T(1,128)} %get-tuple-element.1046) | copy-start | bytes 12292
  58.6 28.8 %copy-start.28 = (f32[1,1024]{1,0:T(1,128)S(1)}, f32[1,1024]{1,0:T(1,128)}, u32[]{:S(2)}) copy-start(f32[1,1024]{1,0:T(1,128)} %get-tuple-element.1047) | copy-start | bytes 12292
  58.7 54.3 %copy-start.2 = (bf16[235,1024]{1,0:T(8,128)(2,1)S(1)}, bf16[235,1024]{1,0:T(8,128)(2,1)}, u32[]{:S(2)}) copy-start(bf16[235,1024]{1,0:T(8,128)(2,1)} %param.20) | copy-start | bytes 1443844
  58.7 54.3 %copy-start.7 = (s32[1024]{0:T(1024)S(1)}, s32[1024]{0:T(1024)}, u32[]{:S(2)}) copy-start(s32[1024]{0:T(1024)} %param.22) | copy-start | bytes 12292
  58.7 54.3 %copy-start.8 = (f32[1024]{0:T(1024)S(1)}, f32[1024]{0:T(1024)}, u32[]{:S(2)}) copy-start(f32[1024]{0:T(1024)} %param.23) | copy-start | bytes 12292
  341.8 1157.0 %reduce-scatter.6.cloned.1.call-start = ((), (), s32[]{:S(2)}) async-start(), calls=%async_computation.4 | async-start | bytes 2703360 | tf_op jit(solution)/shard_map/reduce_scatter | solution.py:194
  345.1 1505.7 %reduce-scatter.4.cloned.1.call-start = ((), (), s32[]{:S(2)}) async-start(), calls=%async_computation.3 | async-start | bytes 3244032 | tf_op jit(solution)/shard_map/reduce_scatter | solution.py:191
  355.1 39.9 %collective-permute-start.2 = (f32[49,8,32]{2,1,0:T(8,128)S(1)}, f32[49,8,32]{2,1,0:T(8,128)S(1)}, u32[]{:S(2)}, u32[]{:S(2)}) collective-permute-start(f32[49,8,32]{2,1,0:T(8,128)S(1)} %slice.5721), channel_id=1, source_target_pairs={{496,0},{0,16},{16,32},{32,48},{48,64},{64,80},{80,96},{96,112},{1... | collective-permute-start | bytes 150536 | tf_op jit(solution)/shard_map/ppermute | solution.py:23
  395.1 40.5 %collective-permute-start.3 = (f32[49,8,32]{2,1,0:T(8,128)S(1)}, f32[49,8,32]{2,1,0:T(8,128)S(1)}, u32[]{:S(2)}, u32[]{:S(2)}) collective-permute-start(f32[49,8,32]{2,1,0:T(8,128)S(1)} %get-tuple-element.1238), channel_id=1, source_target_pairs={{16,0},{32,16},{48,32},{64,48},{80,64},{96,80},{112,96},{128,112},... | collective-permute-start | bytes 150536 | tf_op jit(solution)/shard_map/ppermute | solution.py:23
  442.9 1409.6 %copy-start.5 = (f32[49,8,128]{2,1,0:T(8,128)}, f32[49,8,128]{2,1,0:T(8,128)S(1)}, u32[]{:S(2)}) copy-start(f32[49,8,128]{2,1,0:T(8,128)S(1)} %scatter-add.9) | copy-start | bytes 602116
  (26 other events, 411.9 us)
Sparse Core Ops, SparseCore 0:
  31.3 78.6 all-gather.1
  341.9 767.8 all-reduce.2
  1112.9 385.8 reduce-scatter.5
  1506.0 344.7 reduce-scatter.3
where the time goes:
time: 1870 us; the launch traced here: 1860 us
  waiting for transfers between devices  1490 us (80%)
  other arithmetic  219 us (12%)
  local copies, waits for them, and re-layouts  69.7 us (4%)
  starting transfers between devices  32.8 us (2%)
  matrix products  31.9 us (2%)
    unnamed x5, waiting for transfers between devices  667 us
    reduce_scatter x1, waiting for transfers between devices, body(): lax.psum_scatter(sum_two.reshape((-1,) + sum_two.shape[2:]), 'brick', sca...  387 us
    reduce_scatter x1, waiting for transfers between devices, body(): lax.psum_scatter(sum_one.reshape((-1,) + sum_one.shape[2:]), 'brick', sca...  350 us
    while x152, other arithmetic  125 us
    ppermute x2, waiting for transfers between devices, passed_along(): return lax.ppermute(block, axis, route)  64.6 us
  transfers between devices with their start and end apart: 8, of which 6 were waited for; matrix products, arithmetic and copies ran while one was open for 5% of the time, Pallas kernels for 0%

commit v1 on v0

v1 whole, which is shorter than its diff:
```python
import functools

import jax
import jax.numpy as jnp
from jax import lax
from jax.experimental import pallas as pl
from jax.experimental.pallas import tpu as pltpu
from jax.sharding import PartitionSpec as P

BF = jnp.bfloat16
F32 = jnp.float32
EB = 256
LANES = 128
VMEM_LIMIT = 48 * 1024 * 1024
ZORD = (0, 2, 4, 6, 1, 3, 5)

NN = (((1,), (0,)), ((), ()))
NT = (((1,), (1,)), ((), ()))


def mm(a, b, dims=NN):
    return lax.dot_general(a, b, dims, preferred_element_type=F32)


def kept_row(degree, azimuth):
    if azimuth == 0:
        return degree
    if azimuth == 1:
        return 6 + degree
    if azimuth == -1:
        return 12 + degree
    if azimuth == 2:
        return 17 + degree
    return 22 + degree


def wig_row(degree, azimuth, column):
    start = sum((2 * min(k, 2) + 1) * (2 * k + 1) for k in range(degree))
    return start + (azimuth + min(degree, 2)) * (2 * degree + 1) + column


def orders(degree):
    reach = min(degree, 2)
    return range(-reach, reach + 1)


def eg_place(row):
    return ZORD.index(row) if row < 7 else row


def x_place(row):
    if row < 7:
        return row * 8
    if row < 13:
        return 64 + (row - 7) * 8
    if row < 19:
        return 112 + (row - 13) * 8
    if row < 24:
        return 160 + (row - 19) * 8
    return 208 + (row - 24) * 8


def iota(shape, axis):
    return lax.broadcasted_iota(jnp.int32, shape, axis)


def hot(match):
    return jnp.where(match, 1.0, 0.0).astype(BF)


def source_hots(src):
    width = src.shape[1]
    atom = iota((LANES, width), 0)
    own = hot(atom == src - 32)
    before = [hot(atom == jnp.where(src < 32, src + 32 * q, -1)) for q in range(4)]
    after = [hot(atom == jnp.where(src >= 160, src - 160 + 32 * q, -1)) for q in range(4)]
    return own, before, after


def pack_kernel(h_ref, node_ref, a_ref, b_ref):
    h = h_ref[0]
    base_a = jnp.where(h == 0, 96, 0)
    base_b = 96 - base_a
    node = node_ref[...]
    atom, lane = iota((LANES, LANES), 0), iota((LANES, LANES), 1)
    parts = []
    for q in range(4):
        inside = (lane >= 32 * q) & (lane < 32 * q + 32)
        pick_a = hot(inside & (atom == lane - 32 * q + base_a))
        pick_b = hot(inside & (atom == lane - 32 * q + base_b))
        parts.append(mm(node, jnp.concatenate([pick_a, pick_b], axis=1)))
    rows = []
    for g in range(14):
        total = jnp.zeros((8, 2 * LANES), F32)
        for q in range(4):
            coef = 4 * g + q
            if coef < 49:
                total = total + parts[q][coef * 8 : coef * 8 + 8]
        rows.append(total)
    packed = jnp.concatenate(rows, axis=0).astype(BF)
    a_ref[...] = packed[:, :LANES]
    b_ref[...] = packed[:, LANES:]


def edge_in_kernel(h_ref, node_ref, ra_ref, rb_ref, src_ref, wig_ref, x_ref, rot, gathered):
    h = h_ref[0]
    src = src_ref[...]
    own, before, after = source_hots(src)
    gathered[...] = mm(node_ref[...], own)
    rot[...] = wig_ref[...].astype(F32)
    first, second = ra_ref[...], rb_ref[...]
    from_before = jnp.where(h == 0, second, first)
    from_after = jnp.where(h == 0, first, second)
    for q in range(4):
        part = mm(from_before, before[q]) + mm(from_after, after[q])
        for g in range(13):
            coef = 4 * g + q
            if coef < 49:
                gathered[coef * 8 : coef * 8 + 8, :] += part[g * 8 : g * 8 + 8]
    rows = {}
    for degree in range(7):
        span = 2 * degree + 1
        vals = [gathered[(degree * degree + j) * 8 : (degree * degree + j + 1) * 8, :] for j in range(span)]
        for m in orders(degree):
            total = None
            for j in range(span):
                at = wig_row(degree, m, j)
                term = rot[at : at + 1, :] * vals[j]
                total = term if total is None else total + term
            rows[kept_row(degree, m)] = total
    blank = jnp.zeros((8, EB), F32)
    groups = [
        (0, [rows[r] for r in range(7)] + [blank]),
        (64, [rows[r] for r in range(7, 13)]),
        (112, [rows[r] for r in range(13, 19)]),
        (160, [rows[r] for r in range(19, 24)] + [blank]),
        (208, [rows[r] for r in range(24, 29)] + [blank]),
    ]
    for start, members in groups:
        x_ref[start : start + 8 * len(members), :] = jnp.concatenate(members, axis=0).astype(BF)


def weight_kernel(k_ref, own_ref, sib_ref, zero_ref, one_ref, two_ref):
    k = k_ref[0]
    chan, lane = iota((LANES, LANES), 0), iota((LANES, LANES), 1)

    def pick(offset):
        spot = lane - offset
        wanted = (spot // 8) * 16 + k * 8 + spot % 8
        return hot((spot >= 0) & (spot < 64) & (chan == wanted))

    low, high = pick(0), pick(64)
    own, sib = own_ref[...], sib_ref[...]
    sides = [(mm(own, low), mm(own, high)), (mm(sib, low), mm(sib, high))]

    def tile(entries, place):
        halves = []
        for side in sides:
            total = None
            for half, entry in enumerate(entries):
                if entry is None:
                    continue
                sign, at = entry
                piece = side[half][at * 8 : at * 8 + 8]
                piece = piece if sign > 0 else -piece
                total = piece if total is None else total + piece
            halves.append(total)
        return jnp.concatenate(halves, axis=0).astype(BF)

    for lp in range(7):
        for p in range(4):
            entries = [
                (1, lp * 7 + ZORD[n]) if n < 7 else None for n in (2 * p, 2 * p + 1)
            ]
            zero_ref[lp * 16 : lp * 16 + 16, p * 128 : p * 128 + 128] = tile(entries, p)
    for ref, count, base in ((one_ref, 6, 49), (two_ref, 5, 121)):
        for out in range(2):
            for lp in range(count):
                for p in range(count):
                    entries = []
                    for n in (2 * p, 2 * p + 1):
                        inp, l = n // count, n % count
                        which = 0 if inp == out else 1
                        sign = -1 if (out == 1 and inp == 0) else 1
                        entries.append((sign, base + which * count * count + lp * count + l))
                    row = (out * count + lp) * 16
                    ref[row : row + 16, p * 128 : p * 128 + 128] = tile(entries, p)


def grad_kernel(
    z_ref, count_ref, blk0, blk1, blk2, blk3, blk4, blk5, blk6, blk7,
    dst_ref, scale_ref, wig_ref, xo_ref, xs_ref,
    eg_ref, so_ref, ss_ref,
    vals, gathered, rot, acc, sem,
):
    step = pl.program_id(0)
    blocks = (blk0, blk1, blk2, blk3, blk4, blk5, blk6, blk7)

    @pl.when(step == 0)
    def _():
        z = z_ref[0]
        copies = [
            pltpu.make_async_copy(blk, vals.at[z ^ j], sem.at[j]) for j, blk in enumerate(blocks)
        ]
        for copy in copies:
            copy.start()
        acc[...] = jnp.zeros_like(acc)
        for copy in copies:
            copy.wait()

    slot = step * EB + iota((1, EB), 1)
    factor = jnp.where(slot < count_ref[0], 0.25 * scale_ref[...], 0.0)
    rot[...] = wig_ref[...].astype(F32) * factor
    dest = hot(iota((LANES, EB), 0) == dst_ref[...])

    def pair(zp, carry):
        for side in range(2):
            gathered[side] = mm(vals[2 * zp + side], dest)
        for half in range(EB // LANES):
            lanes = slice(half * LANES, half * LANES + LANES)
            for degree in range(7):
                span = 2 * degree + 1
                at0 = degree * degree
                cols = [
                    [gathered[side, (at0 + j) * 8 : (at0 + j + 1) * 8, lanes] for j in range(span)]
                    for side in range(2)
                ]
                for m in orders(degree):
                    totals = [None, None]
                    for j in range(span):
                        at = wig_row(degree, m, j)
                        coeff = jnp.broadcast_to(rot[at : at + 1, lanes], (8, LANES))
                        for side in range(2):
                            term = coeff * cols[side][j]
                            totals[side] = term if totals[side] is None else totals[side] + term
                    place = eg_place(kept_row(degree, m)) * 64
                    rows = pl.ds(pl.multiple_of(place + zp * 16, 16), 16)
                    eg_ref[rows, lanes] = jnp.concatenate(totals, axis=0).astype(BF)
        return carry

    lax.fori_loop(0, 4, pair, 0)

    def stacked(*pieces):
        return jnp.concatenate(pieces, axis=0)

    def blank(rows):
        return jnp.zeros((rows, EB), BF)

    xo, xs = xo_ref[...], xs_ref[...]
    even = stacked(xo[:64], blank(64), xs[:64], blank(64))
    odd = stacked(blank(64), xo[:64], blank(64), xs[:64])
    acc[0:256] += mm(eg_ref[0:256], even, NT)
    acc[256:448] += mm(eg_ref[256:448], odd, NT)
    for start, count, plus, minus in ((448, 6, 64, 112), (1216, 5, 160, 208)):
        ahead = stacked(
            xo[plus : plus + 48], -xo[minus : minus + 48], blank(32),
            xs[plus : plus + 48], -xs[minus : minus + 48], blank(32),
        )
        cross = stacked(
            xo[minus : minus + 48], xo[plus : plus + 48], blank(32),
            xs[minus : minus + 48], xs[plus : plus + 48], blank(32),
        )
        size = count * 64
        at = 448 if count == 6 else 832
        acc[at : at + size] += mm(eg_ref[start : start + size], ahead, NT) + mm(
            eg_ref[start + size : start + 2 * size], cross, NT
        )

    @pl.when(step == pl.num_programs(0) - 1)
    def _():
        for zb in range(8):
            tiles = []
            for t in range(4):
                tile = acc[t * 64 + zb * 8 : t * 64 + zb * 8 + 8]
                if t < 3:
                    tile = tile + acc[256 + t * 64 + zb * 8 : 256 + t * 64 + zb * 8 + 8]
                tiles.append(tile)
            for n in range(11):
                tiles.append(acc[448 + n * 64 + zb * 8 : 448 + n * 64 + zb * 8 + 8])
            tiles.append(jnp.zeros((8, 2 * LANES), F32))
            whole = jnp.concatenate(tiles, axis=0).astype(BF)
            so_ref[zb] = whole[:, :LANES]
            ss_ref[zb] = whole[:, LANES:]


def back_kernel(
    eg_ref, zero_ref, one_ref, two_ref, src_ref, wig_ref, own_ref, sib_ref, rot, back, full, acc, rims
):
    step = pl.program_id(0)

    @pl.when(step == 0)
    def _():
        acc[...] = jnp.zeros_like(acc)
        rims[...] = jnp.zeros_like(rims)

    rot[...] = wig_ref[...].astype(F32)
    back[0:112] = mm(zero_ref[:, 0:448], eg_ref[0:448])
    back[112:304] = mm(one_ref[...], eg_ref[448:1216])
    back[304:464] = mm(two_ref[...], eg_ref[1216:1856])
    quarter_start = (0, 13, 25, 37)
    for half in range(EB // LANES):
        lanes = slice(half * LANES, half * LANES + LANES)
        for degree in range(7):
            vals = {m: back[kept_row(degree, m) * 16 : kept_row(degree, m) * 16 + 16, lanes] for m in orders(degree)}
            for j in range(2 * degree + 1):
                total = None
                for m in orders(degree):
                    at = wig_row(degree, m, j)
                    term = rot[at : at + 1, lanes] * vals[m]
                    total = term if total is None else total + term
                coef = degree * degree + j
                row = (quarter_start[coef % 4] + coef // 4) * 16
                full[row : row + 16, lanes] = total.astype(BF)
    own, before, after = source_hots(src_ref[...])
    for q in range(4):
        start, size = quarter_start[q] * 16, (13 if q == 0 else 12) * 16
        rows = full[start : start + size]
        acc[start : start + size] += mm(rows, own, NT)
        rims[0:size] += mm(rows, jnp.concatenate([before[q], after[q]], axis=0), NT)

    @pl.when(step == pl.num_programs(0) - 1)
    def _():
        for side, ref, kind in ((0, own_ref, F32), (1, sib_ref, BF)):
            tiles = []
            for coef in range(49):
                row = (quarter_start[coef % 4] + coef // 4) * 16 + side * 8
                tiles.append(acc[row : row + 8])
            tiles.append(jnp.zeros((8, LANES), F32))
            for rim in range(2):
                for g in range(13):
                    tiles.append(rims[g * 16 + side * 8 : g * 16 + side * 8 + 8, rim * LANES : rim * LANES + LANES])
                tiles.append(jnp.zeros((8, LANES), F32))
            ref[...] = jnp.concatenate(tiles, axis=0).astype(kind)


def join_kernel(h_ref, own_ref, ra_ref, rb_ref, out_ref):
    h = h_ref[0]
    base_a = jnp.where(h == 0, 96, 0)
    base_b = 96 - base_a
    lane, atom = iota((LANES, LANES), 0), iota((LANES, LANES), 1)
    ra, rb = ra_ref[...], rb_ref[...]
    for q in range(4):
        inside = (lane >= 32 * q) & (lane < 32 * q + 32)
        put_a = hot(inside & (atom == lane - 32 * q + base_a))
        put_b = hot(inside & (atom == lane - 32 * q + base_b))
        part = mm(ra, put_a) + mm(rb, put_b)
        for g in range(13):
            coef = 4 * g + q
            if coef < 49:
                out_ref[coef] = own_ref[coef * 8 : coef * 8 + 8] + part[g * 8 : g * 8 + 8]


def smem():
    return pl.BlockSpec(memory_space=pltpu.SMEM)


def params():
    return pltpu.CompilerParams(vmem_limit_bytes=VMEM_LIMIT)


def whole(shape):
    return pl.BlockSpec(shape, lambda *_: (0,) * len(shape))


def sds(shape, dtype):
    return jax.ShapeDtypeStruct(shape, dtype)


def body(
    node_x, cotangent, wigner, src_index, dst_index, edge_scale, edge_count, w_zero, w_one, w_two
):
    chan = lax.axis_index("chan")
    brick = lax.axis_index("brick")
    z, core = chan // 2, chan % 2
    high = brick % 2
    z_s = z.astype(jnp.int32).reshape(1)
    k_s = core.astype(jnp.int32).reshape(1)
    h_s = high.astype(jnp.int32).reshape(1)
    slots = src_index.shape[0]
    steps = slots // EB
    src = src_index.reshape(1, slots)
    dst = dst_index.reshape(1, slots)
    scale = edge_scale.reshape(1, slots)

    def across(x, mask):
        return lax.ppermute(x, "chan", [(i, i ^ mask) for i in range(16)])

    def swap_a(x):
        return lax.ppermute(x, "brick", [(i, i ^ 1) for i in range(32)])

    def swap_b(x):
        route = [(i, (i - 1) % 32 if i % 2 == 0 else (i + 1) % 32) for i in range(32)]
        return lax.ppermute(x, "brick", route)

    def padded(x):
        return jnp.pad(x.reshape(392, 128), ((0, 8), (0, 0)))

    b0 = padded(cotangent)
    b4 = across(b0, 8)
    b2 = across(b0, 4)
    b1 = across(b0, 2)
    b6 = across(b4, 4)
    b5 = across(b4, 2)
    b3 = across(b2, 2)
    b7 = across(b6, 2)

    node = padded(node_x)
    send_a, send_b = pl.pallas_call(
        pack_kernel,
        out_shape=(sds((112, 128), BF), sds((112, 128), BF)),
        in_specs=[smem(), whole((400, 128))],
        out_specs=(whole((112, 128)), whole((112, 128))),
        grid=(1,),
        compiler_params=params(),
        name="pack_rims",
    )(h_s, node)
    got_a, got_b = swap_a(send_a), swap_b(send_b)
    row_spec = pl.BlockSpec((1, EB), lambda i: (0, i))
    wig_spec = pl.BlockSpec((235, EB), lambda i: (0, i))
    x_spec = pl.BlockSpec((256, EB), lambda i: (0, i))
    x_own = pl.pallas_call(
        edge_in_kernel,
        out_shape=sds((256, slots), BF),
        grid=(steps,),
        in_specs=[smem(), whole((400, 128)), whole((112, 128)), whole((112, 128)), row_spec, wig_spec],
        out_specs=x_spec,
        scratch_shapes=[pltpu.VMEM((235, EB), F32), pltpu.VMEM((400, EB), F32)],
        compiler_params=params(),
        name="edge_in",
    )(h_s, node, got_a, got_b, src, wigner)
    x_sib = across(x_own, 1)

    w_own = jnp.concatenate(
        [
            w_zero.transpose(0, 2, 1, 3).reshape(392, 128),
            w_one.transpose(0, 1, 3, 2, 4).reshape(576, 128),
            w_two.transpose(0, 1, 3, 2, 4).reshape(400, 128),
            jnp.zeros((8, 128), BF),
        ],
        axis=0,
    )
    w_sib = across(w_own, 1)
    wz, wo, wt = pl.pallas_call(
        weight_kernel,
        out_shape=(sds((112, 512), BF), sds((192, 768), BF), sds((160, 640), BF)),
        grid=(1,),
        in_specs=[smem(), whole((1376, 128)), whole((1376, 128))],
        out_specs=(whole((112, 512)), whole((192, 768)), whole((160, 640))),
        compiler_params=params(),
        name="weights",
    )(k_s, w_own, w_sib)

    any_spec = pl.BlockSpec(memory_space=pl.ANY)
    eg_spec = pl.BlockSpec((1856, EB), lambda i: (0, i))
    eg, s_own, s_sib = pl.pallas_call(
        grad_kernel,
        out_shape=(sds((1856, slots), BF), sds((8, 128, 128), BF), sds((8, 128, 128), BF)),
        grid=(steps,),
        in_specs=[smem(), smem()] + [any_spec] * 8 + [row_spec, row_spec, wig_spec, x_spec, x_spec],
        out_specs=(eg_spec, whole((8, 128, 128)), whole((8, 128, 128))),
        scratch_shapes=[
            pltpu.VMEM((8, 400, 128), BF),
            pltpu.VMEM((2, 400, EB), F32),
            pltpu.VMEM((235, EB), F32),
            pltpu.VMEM((1152, 256), F32),
            pltpu.SemaphoreType.DMA((8,)),
        ],
        compiler_params=params(),
        name="edge_grad",
    )(z_s, edge_count, b0, b1, b2, b3, b4, b5, b6, b7, dst, scale, wigner, x_own, x_sib)

    s_got = across(s_sib, 1)
    is_even = core == 0
    send = jnp.stack(
        [jnp.where(is_even, s_own, s_got), jnp.where(is_even, s_got, s_own)], axis=1
    ).reshape(16, 128, 128)
    groups = [[2 * j + h for j in range(16)] for h in range(2)]
    pieces = lax.all_to_all(send, "brick", 0, 0, axis_index_groups=groups)
    summed = pieces.astype(F32).sum(axis=0).reshape(16, 2, 4, 128)
    mine = jnp.where(high == 0, summed[:, 0], summed[:, 1])
    other = jnp.where(high == 0, summed[:, 1], summed[:, 0])
    final = mine + swap_a(other.astype(BF).reshape(64, 128)).astype(F32).reshape(16, 4, 128)

    zero_rows = [None] * 7
    for n, degree in enumerate(ZORD):
        zero_rows[degree] = final[n, :, 0:56] if n < 4 else final[n - 4, :, 64:120]
    grad_zero = jnp.stack(zero_rows).reshape(7, 4, 7, 8).transpose(2, 3, 0, 1)
    grad_one = final[4:10, :, 0:96].reshape(6, 4, 2, 6, 8).transpose(2, 3, 4, 0, 1)
    two = jnp.stack([final[10:15, :, 0:40], final[10:15, :, 48:88]], axis=2)
    grad_two = two.reshape(5, 4, 2, 5, 8).transpose(2, 3, 4, 0, 1)

    g_own, g_sib = pl.pallas_call(
        back_kernel,
        out_shape=(sds((624, 128), F32), sds((624, 128), BF)),
        grid=(steps,),
        in_specs=[eg_spec, whole((112, 512)), whole((192, 768)), whole((160, 640)), row_spec, wig_spec],
        out_specs=(whole((624, 128)), whole((624, 128))),
        scratch_shapes=[
            pltpu.VMEM((235, EB), F32),
            pltpu.VMEM((464, EB), F32),
            pltpu.VMEM((784, EB), BF),
            pltpu.VMEM((784, LANES), F32),
            pltpu.VMEM((208, 2 * LANES), F32),
        ],
        compiler_params=params(),
        name="back",
    )(eg, wz, wo, wt, src, wigner)
    g_all = g_own + across(g_sib, 1).astype(F32)
    left, right = g_all[400:512].astype(BF), g_all[512:624].astype(BF)
    rim_a = swap_a(jnp.where(high == 0, right, left))
    rim_b = swap_b(jnp.where(high == 0, left, right))
    grad_x = pl.pallas_call(
        join_kernel,
        out_shape=sds((49, 8, 128), F32),
        grid=(1,),
        in_specs=[smem(), whole((400, 128)), whole((112, 128)), whole((112, 128))],
        out_specs=whole((49, 8, 128)),
        compiler_params=params(),
        name="join",
    )(h_s, g_all[:400], rim_a, rim_b)
    return grad_x, grad_zero, grad_one, grad_two


def solution(mesh):
    in_specs = (
        P(None, "chan", "brick"),
        P(None, "chan", "brick"),
        P(None, "brick"),
        P("brick"),
        P("brick"),
        P("brick"),
        P("brick"),
        P(None, "chan", None, None),
        P(None, None, "chan", None, None),
        P(None, None, "chan", None, None),
    )
    out_specs = (
        P(None, "chan", "brick"),
        P(None, "chan", None, "brick"),
        P(None, None, "chan", None, "brick"),
        P(None, None, "chan", None, "brick"),
    )
    return jax.shard_map(body, mesh=mesh, in_specs=in_specs, out_specs=out_specs, check_vma=False)
```

time: 1870 us -> 142 us (0.08)
  the two profiles are of different devices: /device:TPU:1 before, /device:TPU:64 now
where the time goes in v1:
time: 142 us; the launch traced here: 141 us
  starting transfers between devices  77.5 us (55%)
  waiting for transfers between devices  29 us (20%)
  Pallas kernels  19.6 us (14%)
  local copies, waits for them, and re-layouts  11.8 us (8%)
  between operations  1.72 us (1%)
  other arithmetic  1.55 us (1%)
    ppermute x11, starting transfers between devices, across(): return lax.ppermute(x, 'chan', [(i, i ^ mask) for i in range(16)])  31.4 us
    ppermute x3, starting transfers between devices, swap_a(): return lax.ppermute(x, 'brick', [(i, i ^ 1) for i in range(32)])  21.2 us
    ppermute x2, starting transfers between devices, swap_b(): return lax.ppermute(x, 'brick', route)  21.2 us
    ppermute x2, waiting for transfers between devices, swap_b(): return lax.ppermute(x, 'brick', route)  12.8 us
    pallas_call x1, Pallas kernels, body(): pl.pallas_call(grad_kernel, out_shape=(sds((1856, slots), BF), sds((8, 12...  11.5 us
    ppermute x3, waiting for transfers between devices, swap_a(): return lax.ppermute(x, 'brick', [(i, i ^ 1) for i in range(32)])  9.29 us
    unnamed x25, local copies, waits for them, and re-layouts  8.51 us
    ppermute x11, waiting for transfers between devices, across(): return lax.ppermute(x, 'chan', [(i, i ^ mask) for i in range(16)])  6.98 us
  transfers between devices with their start and end apart: 17, of which 5 were waited for; matrix products, arithmetic and copies ran while one was open for 2% of the time, Pallas kernels for 14%

profile of v1, /device:TPU:64, one launch (start us, length us, event | category | flops | bytes accessed | tf_op | source)
XLA Modules:
  0.0 141.2 jit_solution(11052034247327568346)
XLA Ops:
  1.6 9.1 %collective-permute-start.3 = (bf16[400,128]{1,0:T(8,128)(2,1)S(1)}, bf16[400,128]{1,0:T(8,128)(2,1)S(1)}, u32[]{:S(2)}, u32[]{:S(2)}) collective-permute-start(bf16[400,128]{1,0:T(8,128)(2,1)S(1)} %pad.7.blk0), channel_id=1, source_target_pairs={{0,8},{1,9},{2,10},{3,11},{4,12},{5,13},{6,14},{7,15},{8,0},{9,1},... | collective-permute-start | bytes 307208 | tf_op jit(solution)/shard_map/ppermute | solution.py:386
  10.7 1.9 %collective-permute-start.1 = (bf16[400,128]{1,0:T(8,128)(2,1)S(1)}, bf16[400,128]{1,0:T(8,128)(2,1)S(1)}, u32[]{:S(2)}, u32[]{:S(2)}) collective-permute-start(bf16[400,128]{1,0:T(8,128)(2,1)S(1)} %pad.7.blk0), channel_id=1, source_target_pairs={{0,4},{1,5},{2,6},{3,7},{4,0},{5,1},{6,2},{7,3},{8,12},{9,13},{10,... | collective-permute-start | bytes 307208 | tf_op jit(solution)/shard_map/ppermute | solution.py:386
  12.6 6.2 %collective-permute-done.3.blk4 = bf16[400,128]{1,0:T(8,128)(2,1)S(1)} collective-permute-done((bf16[400,128]{1,0:T(8,128)(2,1)S(1)}, bf16[400,128]{1,0:T(8,128)(2,1)S(1)}, u32[]{:S(2)}, u32[]{:S(2)}) %collective-permute-start.3) | collective-permute-done | bytes 102432 | tf_op jit(solution)/shard_map/ppermute | solution.py:386
  18.8 2.6 %collective-permute-start.5 = (bf16[400,128]{1,0:T(8,128)(2,1)S(1)}, bf16[400,128]{1,0:T(8,128)(2,1)S(1)}, u32[]{:S(2)}, u32[]{:S(2)}) collective-permute-start(bf16[400,128]{1,0:T(8,128)(2,1)S(1)} %collective-permute-done.3.blk4), channel_id=1, source_target_pairs={{0,4},{1,5},{2,6},{3,7},{4,0},{5,1},{6,2},{7,3},{8,12},{9,13},{10,... | collective-permute-start | bytes 307208 | tf_op jit(solution)/shard_map/ppermute | solution.py:386
  22.7 14.6 %collective-permute-start.7 = (bf16[112,128]{1,0:T(8,128)(2,1)S(1)}, bf16[112,128]{1,0:T(8,128)(2,1)S(1)}, u32[]{:S(2)}, u32[]{:S(2)}) collective-permute-start(bf16[112,128]{1,0:T(8,128)(2,1)S(1)} %get-tuple-element.14), channel_id=1, source_target_pairs={{0,16},{16,0},{32,48},{48,32},{64,80},{80,64},{96,112},{112,96},{1... | collective-permute-start | bytes 86024 | tf_op jit(solution)/shard_map/ppermute | solution.py:389
  37.3 6.6 %collective-permute-start.8 = (bf16[112,128]{1,0:T(8,128)(2,1)S(1)}, bf16[112,128]{1,0:T(8,128)(2,1)S(1)}, u32[]{:S(2)}, u32[]{:S(2)}) collective-permute-start(bf16[112,128]{1,0:T(8,128)(2,1)S(1)} %get-tuple-element.15), channel_id=1, source_target_pairs={{0,496},{16,32},{32,16},{48,64},{64,48},{80,96},{96,80},{112,128},... | collective-permute-start | bytes 86024 | tf_op jit(solution)/shard_map/ppermute | solution.py:393
  43.9 1.9 %collective-permute-start = (bf16[400,128]{1,0:T(8,128)(2,1)S(1)}, bf16[400,128]{1,0:T(8,128)(2,1)S(1)}, u32[]{:S(2)}, u32[]{:S(2)}) collective-permute-start(bf16[400,128]{1,0:T(8,128)(2,1)S(1)} %pad.7.blk0), channel_id=1, source_target_pairs={{0,2},{1,3},{2,0},{3,1},{4,6},{5,7},{6,4},{7,5},{8,10},{9,11},{10,... | collective-permute-start | bytes 307208 | tf_op jit(solution)/shard_map/ppermute | solution.py:386
  45.9 10.4 %collective-permute-done.8.rb_ref = bf16[112,128]{1,0:T(8,128)(2,1)S(1)} collective-permute-done((bf16[112,128]{1,0:T(8,128)(2,1)S(1)}, bf16[112,128]{1,0:T(8,128)(2,1)S(1)}, u32[]{:S(2)}, u32[]{:S(2)}) %collective-permute-start.8) | collective-permute-done | bytes 28704 | tf_op jit(solution)/shard_map/ppermute | solution.py:393
  60.0 1.9 %collective-permute-start.9 = (bf16[256,1024]{1,0:T(8,128)(2,1)S(1)}, bf16[256,1024]{1,0:T(8,128)(2,1)S(1)}, u32[]{:S(2)}, u32[]{:S(2)}) collective-permute-start(bf16[256,1024]{1,0:T(8,128)(2,1)S(1)} %edge_in.1.xo_ref), channel_id=1, source_target_pairs={{0,1},{1,0},{2,3},{3,2},{4,5},{5,4},{6,7},{7,6},{8,9},{9,8},{10,11... | collective-permute-start | bytes 1572872 | tf_op jit(solution)/shard_map/ppermute | solution.py:386
  61.9 1.9 %collective-permute-start.4 = (bf16[400,128]{1,0:T(8,128)(2,1)S(1)}, bf16[400,128]{1,0:T(8,128)(2,1)S(1)}, u32[]{:S(2)}, u32[]{:S(2)}) collective-permute-start(bf16[400,128]{1,0:T(8,128)(2,1)S(1)} %collective-permute-done.3.blk4), channel_id=1, source_target_pairs={{0,2},{1,3},{2,0},{3,1},{4,6},{5,7},{6,4},{7,5},{8,10},{9,11},{10,... | collective-permute-start | bytes 307208 | tf_op jit(solution)/shard_map/ppermute | solution.py:386
  63.8 3.9 %collective-permute-start.2 = (bf16[400,128]{1,0:T(8,128)(2,1)S(1)}, bf16[400,128]{1,0:T(8,128)(2,1)S(1)}, u32[]{:S(2)}, u32[]{:S(2)}) collective-permute-start(bf16[400,128]{1,0:T(8,128)(2,1)S(1)} %collective-permute-done.1.blk2), channel_id=1, source_target_pairs={{0,2},{1,3},{2,0},{3,1},{4,6},{5,7},{6,4},{7,5},{8,10},{9,11},{10,... | collective-permute-start | bytes 307208 | tf_op jit(solution)/shard_map/ppermute | solution.py:386
  67.8 1.9 %collective-permute-start.6 = (bf16[400,128]{1,0:T(8,128)(2,1)S(1)}, bf16[400,128]{1,0:T(8,128)(2,1)S(1)}, u32[]{:S(2)}, u32[]{:S(2)}) collective-permute-start(bf16[400,128]{1,0:T(8,128)(2,1)S(1)} %collective-permute-done.5.blk6), channel_id=1, source_target_pairs={{0,2},{1,3},{2,0},{3,1},{4,6},{5,7},{6,4},{7,5},{8,10},{9,11},{10,... | collective-permute-start | bytes 307208 | tf_op jit(solution)/shard_map/ppermute | solution.py:386
  71.0 1.9 %collective-permute-start.10 = (bf16[1376,128]{1,0:T(8,128)(2,1)S(1)}, bf16[1376,128]{1,0:T(8,128)(2,1)S(1)}, u32[]{:S(2)}, u32[]{:S(2)}) collective-permute-start(bf16[1376,128]{1,0:T(8,128)(2,1)S(1)} %maximum_maximum_fusion.own_ref), channel_id=1, source_target_pairs={{0,1},{1,0},{2,3},{3,2},{4,5},{5,4},{6,7},{7,6},{8,9},{9,8},{10,11... | collective-permute-start | bytes 1056776 | tf_op jit(solution)/shard_map/ppermute | solution.py:386
  76.8 11.5 %edge_grad.1 = (bf16[1856,1024]{1,0:T(8,128)(2,1)}, bf16[8,128,128]{2,1,0:T(8,128)(2,1)S(1)}, bf16[8,128,128]{2,1,0:T(8,128)(2,1)}) custom-call(s32[1]{0:T(128)} %bitcast.1.z_ref, s32[1]{0:T(128)S(6)} %copy.28.count_ref, bf16[400,128]{1,0:T(8,128)(2,1)S(1)} %pad.7.blk0, bf16[400,128]{1,0:T(8,128)(2,1)S(1)} %collective-permute-done.blk1, ...), custom_call_target="tpu_custom_call" | custom-call | tf_op jit(solution)/shard_map/edge_grad/pallas_call | solution.py:455
  88.3 1.9 %collective-permute-start.14 = (bf16[8,128,128]{2,1,0:T(8,128)(2,1)}, bf16[8,128,128]{2,1,0:T(8,128)(2,1)S(1)}, u32[]{:S(2)}, u32[]{:S(2)}) collective-permute-start(bf16[8,128,128]{2,1,0:T(8,128)(2,1)} %get-tuple-element.23), channel_id=1, source_target_pairs={{0,1},{1,0},{2,3},{3,2},{4,5},{5,4},{6,7},{7,6},{8,9},{9,8},{10,11... | collective-permute-start | bytes 786440 | tf_op jit(solution)/shard_map/ppermute | solution.py:386
  90.8 2.1 %copy-done.3 = bf16[1856,1024]{1,0:T(8,128)(2,1)S(1)} copy-done((bf16[1856,1024]{1,0:T(8,128)(2,1)S(1)}, bf16[1856,1024]{1,0:T(8,128)(2,1)}, u32[]{:S(2)}) %copy-start.3) | copy-done | bytes 3801112
  92.9 4.4 %back.1 = (f32[624,128]{1,0:T(8,128)S(1)}, bf16[624,128]{1,0:T(8,128)(2,1)S(1)}) custom-call(bf16[1856,1024]{1,0:T(8,128)(2,1)S(1)} %copy-done.3, bf16[112,512]{1,0:T(8,128)(2,1)S(1)} %get-tuple-element.17.zero_ref, bf16[192,768]{1,0:T(8,128)(2,1)S(1)} %get-tuple-element.18.one_ref, bf16[160,640]{1,0:T(8,128)(2,1)S(1)} %get-tuple-element.19.two_ref, ...), custom_call_target="tpu_custom_call" | custom-call | tf_op jit(solution)/shard_map/back/pallas_call | solution.py:492
  97.3 2.4 %collective-permute-start.11 = (bf16[624,128]{1,0:T(8,128)(2,1)S(1)}, bf16[624,128]{1,0:T(8,128)(2,1)S(1)}, u32[]{:S(2)}, u32[]{:S(2)}) collective-permute-start(bf16[624,128]{1,0:T(8,128)(2,1)S(1)} %get-tuple-element.21), channel_id=1, source_target_pairs={{0,1},{1,0},{2,3},{3,2},{4,5},{5,4},{6,7},{7,6},{8,9},{9,8},{10,11... | collective-permute-start | bytes 479240 | tf_op jit(solution)/shard_map/ppermute | solution.py:386
  100.7 3.7 %all-to-all-start = ((bf16[16,128,128]{2,1,0:T(8,128)(2,1)}), bf16[16,128,128]{2,1,0:T(8,128)(2,1)S(1)}, u32[]{:S(2)}, u32[]{:S(2)}) async-start(bf16[16,128,128]{2,1,0:T(8,128)(2,1)} %bitcast.16), calls=%async_computation | async-start | bytes 1048576 | tf_op jit(solution)/shard_map/all_to_all | solution.py:478
  104.5 4.6 %collective-permute-start.12 = (bf16[112,128]{1,0:T(8,128)(2,1)S(1)}, bf16[112,128]{1,0:T(8,128)(2,1)S(1)}, u32[]{:S(2)}, u32[]{:S(2)}) collective-permute-start(bf16[112,128]{1,0:T(8,128)(2,1)S(1)} %get-tuple-element.37), channel_id=1, source_target_pairs={{0,16},{16,0},{32,48},{48,32},{64,80},{80,64},{96,112},{112,96},{1... | collective-permute-start | bytes 86024 | tf_op jit(solution)/shard_map/ppermute | solution.py:389
  109.1 14.6 %collective-permute-start.13 = (bf16[112,128]{1,0:T(8,128)(2,1)S(1)}, bf16[112,128]{1,0:T(8,128)(2,1)S(1)}, u32[]{:S(2)}, u32[]{:S(2)}) collective-permute-start(bf16[112,128]{1,0:T(8,128)(2,1)S(1)} %get-tuple-element.36), channel_id=1, source_target_pairs={{0,496},{16,32},{32,16},{48,64},{64,48},{80,96},{96,80},{112,128},... | collective-permute-start | bytes 86024 | tf_op jit(solution)/shard_map/ppermute | solution.py:393
  123.8 1.9 %collective-permute-start.15 = (bf16[64,128]{1,0:T(8,128)(2,1)S(1)}, bf16[64,128]{1,0:T(8,128)(2,1)S(1)}, u32[]{:S(2)}, u32[]{:S(2)}) collective-permute-start(bf16[64,128]{1,0:T(8,128)(2,1)S(1)} %bitcast.46), channel_id=1, source_target_pairs={{0,16},{16,0},{32,48},{48,32},{64,80},{80,64},{96,112},{112,96},{1... | collective-permute-start | bytes 49160 | tf_op jit(solution)/shard_map/ppermute | solution.py:389
  125.8 2.3 %collective-permute-done.13.rb_ref = bf16[112,128]{1,0:T(8,128)(2,1)S(1)} collective-permute-done((bf16[112,128]{1,0:T(8,128)(2,1)S(1)}, bf16[112,128]{1,0:T(8,128)(2,1)S(1)}, u32[]{:S(2)}, u32[]{:S(2)}) %collective-permute-start.13) | collective-permute-done | bytes 28704 | tf_op jit(solution)/shard_map/ppermute | solution.py:393
  129.1 9.3 %collective-permute-done.15 = bf16[64,128]{1,0:T(8,128)(2,1)S(1)} collective-permute-done((bf16[64,128]{1,0:T(8,128)(2,1)S(1)}, bf16[64,128]{1,0:T(8,128)(2,1)S(1)}, u32[]{:S(2)}, u32[]{:S(2)}) %collective-permute-start.15) | collective-permute-done | bytes 16416 | tf_op jit(solution)/shard_map/ppermute | solution.py:389
  (63 shorter events, 15.8 us)
Async XLA Ops:
  0.6 90.1 %copy-start.5 = (s32[1024]{0:T(1024)S(1)}, s32[1024]{0:T(1024)}, u32[]{:S(2)}) copy-start(s32[1024]{0:T(1024)} %param.13) | copy-start | bytes 12292
  0.6 90.1 %copy-start.2 = (bf16[235,1024]{1,0:T(8,128)(2,1)S(1)}, bf16[235,1024]{1,0:T(8,128)(2,1)}, u32[]{:S(2)}) copy-start(bf16[235,1024]{1,0:T(8,128)(2,1)} %wig_ref.5) | copy-start | bytes 1443844
  1.6 17.2 %collective-permute-start.3 = (bf16[400,128]{1,0:T(8,128)(2,1)S(1)}, bf16[400,128]{1,0:T(8,128)(2,1)S(1)}, u32[]{:S(2)}, u32[]{:S(2)}) collective-permute-start(bf16[400,128]{1,0:T(8,128)(2,1)S(1)} %pad.7.blk0), channel_id=1, source_target_pairs={{0,8},{1,9},{2,10},{3,11},{4,12},{5,13},{6,14},{7,15},{8,0},{9,1},... | collective-permute-start | bytes 307208 | tf_op jit(solution)/shard_map/ppermute | solution.py:386
  10.7 53.1 %collective-permute-start.1 = (bf16[400,128]{1,0:T(8,128)(2,1)S(1)}, bf16[400,128]{1,0:T(8,128)(2,1)S(1)}, u32[]{:S(2)}, u32[]{:S(2)}) collective-permute-start(bf16[400,128]{1,0:T(8,128)(2,1)S(1)} %pad.7.blk0), channel_id=1, source_target_pairs={{0,4},{1,5},{2,6},{3,7},{4,0},{5,1},{6,2},{7,3},{8,12},{9,13},{10,... | collective-permute-start | bytes 307208 | tf_op jit(solution)/shard_map/ppermute | solution.py:386
  18.8 49.0 %collective-permute-start.5 = (bf16[400,128]{1,0:T(8,128)(2,1)S(1)}, bf16[400,128]{1,0:T(8,128)(2,1)S(1)}, u32[]{:S(2)}, u32[]{:S(2)}) collective-permute-start(bf16[400,128]{1,0:T(8,128)(2,1)S(1)} %collective-permute-done.3.blk4), channel_id=1, source_target_pairs={{0,4},{1,5},{2,6},{3,7},{4,0},{5,1},{6,2},{7,3},{8,12},{9,13},{10,... | collective-permute-start | bytes 307208 | tf_op jit(solution)/shard_map/ppermute | solution.py:386
  22.7 23.2 %collective-permute-start.7 = (bf16[112,128]{1,0:T(8,128)(2,1)S(1)}, bf16[112,128]{1,0:T(8,128)(2,1)S(1)}, u32[]{:S(2)}, u32[]{:S(2)}) collective-permute-start(bf16[112,128]{1,0:T(8,128)(2,1)S(1)} %get-tuple-element.14), channel_id=1, source_target_pairs={{0,16},{16,0},{32,48},{48,32},{64,80},{80,64},{96,112},{112,96},{1... | collective-permute-start | bytes 86024 | tf_op jit(solution)/shard_map/ppermute | solution.py:389
  37.3 19.0 %collective-permute-start.8 = (bf16[112,128]{1,0:T(8,128)(2,1)S(1)}, bf16[112,128]{1,0:T(8,128)(2,1)S(1)}, u32[]{:S(2)}, u32[]{:S(2)}) collective-permute-start(bf16[112,128]{1,0:T(8,128)(2,1)S(1)} %get-tuple-element.15), channel_id=1, source_target_pairs={{0,496},{16,32},{32,16},{48,64},{64,48},{80,96},{96,80},{112,128},... | collective-permute-start | bytes 86024 | tf_op jit(solution)/shard_map/ppermute | solution.py:393
  43.9 27.1 %collective-permute-start = (bf16[400,128]{1,0:T(8,128)(2,1)S(1)}, bf16[400,128]{1,0:T(8,128)(2,1)S(1)}, u32[]{:S(2)}, u32[]{:S(2)}) collective-permute-start(bf16[400,128]{1,0:T(8,128)(2,1)S(1)} %pad.7.blk0), channel_id=1, source_target_pairs={{0,2},{1,3},{2,0},{3,1},{4,6},{5,7},{6,4},{7,5},{8,10},{9,11},{10,... | collective-permute-start | bytes 307208 | tf_op jit(solution)/shard_map/ppermute | solution.py:386
  56.3 1.0 copy-start
  57.4 0.7 copy-start.4
  60.0 14.4 %collective-permute-start.9 = (bf16[256,1024]{1,0:T(8,128)(2,1)S(1)}, bf16[256,1024]{1,0:T(8,128)(2,1)S(1)}, u32[]{:S(2)}, u32[]{:S(2)}) collective-permute-start(bf16[256,1024]{1,0:T(8,128)(2,1)S(1)} %edge_in.1.xo_ref), channel_id=1, source_target_pairs={{0,1},{1,0},{2,3},{3,2},{4,5},{5,4},{6,7},{7,6},{8,9},{9,8},{10,11... | collective-permute-start | bytes 1572872 | tf_op jit(solution)/shard_map/ppermute | solution.py:386
  61.9 11.7 %collective-permute-start.4 = (bf16[400,128]{1,0:T(8,128)(2,1)S(1)}, bf16[400,128]{1,0:T(8,128)(2,1)S(1)}, u32[]{:S(2)}, u32[]{:S(2)}) collective-permute-start(bf16[400,128]{1,0:T(8,128)(2,1)S(1)} %collective-permute-done.3.blk4), channel_id=1, source_target_pairs={{0,2},{1,3},{2,0},{3,1},{4,6},{5,7},{6,4},{7,5},{8,10},{9,11},{10,... | collective-permute-start | bytes 307208 | tf_op jit(solution)/shard_map/ppermute | solution.py:386
  63.8 9.8 %collective-permute-start.2 = (bf16[400,128]{1,0:T(8,128)(2,1)S(1)}, bf16[400,128]{1,0:T(8,128)(2,1)S(1)}, u32[]{:S(2)}, u32[]{:S(2)}) collective-permute-start(bf16[400,128]{1,0:T(8,128)(2,1)S(1)} %collective-permute-done.1.blk2), channel_id=1, source_target_pairs={{0,2},{1,3},{2,0},{3,1},{4,6},{5,7},{6,4},{7,5},{8,10},{9,11},{10,... | collective-permute-start | bytes 307208 | tf_op jit(solution)/shard_map/ppermute | solution.py:386
  67.8 6.6 %collective-permute-start.6 = (bf16[400,128]{1,0:T(8,128)(2,1)S(1)}, bf16[400,128]{1,0:T(8,128)(2,1)S(1)}, u32[]{:S(2)}, u32[]{:S(2)}) collective-permute-start(bf16[400,128]{1,0:T(8,128)(2,1)S(1)} %collective-permute-done.5.blk6), channel_id=1, source_target_pairs={{0,2},{1,3},{2,0},{3,1},{4,6},{5,7},{6,4},{7,5},{8,10},{9,11},{10,... | collective-permute-start | bytes 307208 | tf_op jit(solution)/shard_map/ppermute | solution.py:386
  71.0 19.3 %collective-permute-start.10 = (bf16[1376,128]{1,0:T(8,128)(2,1)S(1)}, bf16[1376,128]{1,0:T(8,128)(2,1)S(1)}, u32[]{:S(2)}, u32[]{:S(2)}) collective-permute-start(bf16[1376,128]{1,0:T(8,128)(2,1)S(1)} %maximum_maximum_fusion.own_ref), channel_id=1, source_target_pairs={{0,1},{1,0},{2,3},{3,2},{4,5},{5,4},{6,7},{7,6},{8,9},{9,8},{10,11... | collective-permute-start | bytes 1056776 | tf_op jit(solution)/shard_map/ppermute | solution.py:386
  74.4 1.0 copy-start.1
  75.4 0.7 copy-start.6
  88.3 11.4 %collective-permute-start.14 = (bf16[8,128,128]{2,1,0:T(8,128)(2,1)}, bf16[8,128,128]{2,1,0:T(8,128)(2,1)S(1)}, u32[]{:S(2)}, u32[]{:S(2)}) collective-permute-start(bf16[8,128,128]{2,1,0:T(8,128)(2,1)} %get-tuple-element.23), channel_id=1, source_target_pairs={{0,1},{1,0},{2,3},{3,2},{4,5},{5,4},{6,7},{7,6},{8,9},{9,8},{10,11... | collective-permute-start | bytes 786440 | tf_op jit(solution)/shard_map/ppermute | solution.py:386
  90.8 2.1 %copy-start.3 = (bf16[1856,1024]{1,0:T(8,128)(2,1)S(1)}, bf16[1856,1024]{1,0:T(8,128)(2,1)}, u32[]{:S(2)}) copy-start(bf16[1856,1024]{1,0:T(8,128)(2,1)} %get-tuple-element.16.eg_ref) | copy-start | bytes 11403268
  97.3 7.1 %collective-permute-start.11 = (bf16[624,128]{1,0:T(8,128)(2,1)S(1)}, bf16[624,128]{1,0:T(8,128)(2,1)S(1)}, u32[]{:S(2)}, u32[]{:S(2)}) collective-permute-start(bf16[624,128]{1,0:T(8,128)(2,1)S(1)} %get-tuple-element.21), channel_id=1, source_target_pairs={{0,1},{1,0},{2,3},{3,2},{4,5},{5,4},{6,7},{7,6},{8,9},{9,8},{10,11... | collective-permute-start | bytes 479240 | tf_op jit(solution)/shard_map/ppermute | solution.py:386
  100.7 23.1 %all-to-all-start = ((bf16[16,128,128]{2,1,0:T(8,128)(2,1)}), bf16[16,128,128]{2,1,0:T(8,128)(2,1)S(1)}, u32[]{:S(2)}, u32[]{:S(2)}) async-start(bf16[16,128,128]{2,1,0:T(8,128)(2,1)} %bitcast.16), calls=%async_computation | async-start | bytes 1048576 | tf_op jit(solution)/shard_map/all_to_all | solution.py:478
  104.5 21.3 %collective-permute-start.12 = (bf16[112,128]{1,0:T(8,128)(2,1)S(1)}, bf16[112,128]{1,0:T(8,128)(2,1)S(1)}, u32[]{:S(2)}, u32[]{:S(2)}) collective-permute-start(bf16[112,128]{1,0:T(8,128)(2,1)S(1)} %get-tuple-element.37), channel_id=1, source_target_pairs={{0,16},{16,0},{32,48},{48,32},{64,80},{80,64},{96,112},{112,96},{1... | collective-permute-start | bytes 86024 | tf_op jit(solution)/shard_map/ppermute | solution.py:389
  109.1 19.0 %collective-permute-start.13 = (bf16[112,128]{1,0:T(8,128)(2,1)S(1)}, bf16[112,128]{1,0:T(8,128)(2,1)S(1)}, u32[]{:S(2)}, u32[]{:S(2)}) collective-permute-start(bf16[112,128]{1,0:T(8,128)(2,1)S(1)} %get-tuple-element.36), channel_id=1, source_target_pairs={{0,496},{16,32},{32,16},{48,64},{64,48},{80,96},{96,80},{112,128},... | collective-permute-start | bytes 86024 | tf_op jit(solution)/shard_map/ppermute | solution.py:393
  123.8 14.5 %collective-permute-start.15 = (bf16[64,128]{1,0:T(8,128)(2,1)S(1)}, bf16[64,128]{1,0:T(8,128)(2,1)S(1)}, u32[]{:S(2)}, u32[]{:S(2)}) collective-permute-start(bf16[64,128]{1,0:T(8,128)(2,1)S(1)} %bitcast.46), channel_id=1, source_target_pairs={{0,16},{16,0},{32,48},{48,32},{64,80},{80,64},{96,112},{112,96},{1... | collective-permute-start | bytes 49160 | tf_op jit(solution)/shard_map/ppermute | solution.py:389
  (1 other events, 0.7 us)

commit v2 on v1

--- a/solution.py
+++ b/solution.py
@@ -11,7 +11,7 @@
 F32 = jnp.float32
 EB = 256
 LANES = 128
-VMEM_LIMIT = 48 * 1024 * 1024
+VMEM_LIMIT = 60 * 1024 * 1024
 ZORD = (0, 2, 4, 6, 1, 3, 5)
 
 NN = (((1,), (0,)), ((), ()))
@@ -77,40 +77,41 @@
     return own, before, after
 
 
-def pack_kernel(h_ref, node_ref, a_ref, b_ref):
-    h = h_ref[0]
-    base_a = jnp.where(h == 0, 96, 0)
-    base_b = 96 - base_a
-    node = node_ref[...]
+def pack_kernel(node_ref, cot_ref, node_out, cot_out, rim_out):
+    blank = jnp.zeros((8, LANES), F32)
+
+    def rows(ref):
+        return jnp.concatenate([ref[...].astype(F32).reshape(392, LANES), blank], axis=0).astype(BF)
+
+    cot_out[...] = rows(cot_ref)
+    node = rows(node_ref)
+    node_out[...] = node
     atom, lane = iota((LANES, LANES), 0), iota((LANES, LANES), 1)
     parts = []
     for q in range(4):
         inside = (lane >= 32 * q) & (lane < 32 * q + 32)
-        pick_a = hot(inside & (atom == lane - 32 * q + base_a))
-        pick_b = hot(inside & (atom == lane - 32 * q + base_b))
-        parts.append(mm(node, jnp.concatenate([pick_a, pick_b], axis=1)))
-    rows = []
-    for g in range(14):
-        total = jnp.zeros((8, 2 * LANES), F32)
-        for q in range(4):
-            coef = 4 * g + q
-            if coef < 49:
-                total = total + parts[q][coef * 8 : coef * 8 + 8]
-        rows.append(total)
-    packed = jnp.concatenate(rows, axis=0).astype(BF)
-    a_ref[...] = packed[:, :LANES]
-    b_ref[...] = packed[:, LANES:]
-
-
-def edge_in_kernel(h_ref, node_ref, ra_ref, rb_ref, src_ref, wig_ref, x_ref, rot, gathered):
+        last = hot(inside & (atom == lane - 32 * q + 96))
+        first = hot(inside & (atom == lane - 32 * q))
+        parts.append(mm(node, jnp.concatenate([last, first], axis=1)))
+    total = []
+    for g in range(13):
+        members = [parts[q][(4 * g + q) * 8 : (4 * g + q) * 8 + 8] for q in range(4) if 4 * g + q < 49]
+        total.append(sum(members[1:], members[0]))
+    total.append(jnp.zeros((8, 2 * LANES), F32))
+    packed = jnp.concatenate(total, axis=0).astype(BF)
+    rim_out[:112] = packed[:, :LANES]
+    rim_out[112:] = packed[:, LANES:]
+
+
+def edge_in_kernel(h_ref, node_ref, near_ref, far_ref, src_ref, wig_ref, x_ref, rot, gathered):
     h = h_ref[0]
     src = src_ref[...]
     own, before, after = source_hots(src)
     gathered[...] = mm(node_ref[...], own)
     rot[...] = wig_ref[...].astype(F32)
-    first, second = ra_ref[...], rb_ref[...]
-    from_before = jnp.where(h == 0, second, first)
-    from_after = jnp.where(h == 0, first, second)
+    far = far_ref[...]
+    from_before = jnp.where(h == 0, far, near_ref[:112])
+    from_after = jnp.where(h == 0, near_ref[112:], far)
     for q in range(4):
         part = mm(from_before, before[q]) + mm(from_after, after[q])
         for g in range(13):
@@ -333,12 +334,12 @@
             ref[...] = jnp.concatenate(tiles, axis=0).astype(kind)
 
 
-def join_kernel(h_ref, own_ref, ra_ref, rb_ref, out_ref):
+def join_kernel(h_ref, own_ref, rim_ref, out_ref):
     h = h_ref[0]
     base_a = jnp.where(h == 0, 96, 0)
     base_b = 96 - base_a
     lane, atom = iota((LANES, LANES), 0), iota((LANES, LANES), 1)
-    ra, rb = ra_ref[...], rb_ref[...]
+    ra, rb = rim_ref[0:112], rim_ref[112:224]
     for q in range(4):
         inside = (lane >= 32 * q) & (lane < 32 * q + 32)
         put_a = hot(inside & (atom == lane - 32 * q + base_a))
@@ -356,6 +357,10 @@
 
 def params():
     return pltpu.CompilerParams(vmem_limit_bytes=VMEM_LIMIT)
+
+
+def light():
+    return pl.CostEstimate(flops=1, bytes_accessed=1, transcendentals=0)
 
 
 def whole(shape):
@@ -385,36 +390,36 @@
     def across(x, mask):
         return lax.ppermute(x, "chan", [(i, i ^ mask) for i in range(16)])
 
-    def swap_a(x):
+    def cross(x):
         return lax.ppermute(x, "brick", [(i, i ^ 1) for i in range(32)])
 
-    def swap_b(x):
-        route = [(i, (i - 1) % 32 if i % 2 == 0 else (i + 1) % 32) for i in range(32)]
+    def shift(x, away):
+        route = [(i, (i + (2 if (i % 2 == 0) == away else -2)) % 32) for i in range(32)]
         return lax.ppermute(x, "brick", route)
 
-    def padded(x):
-        return jnp.pad(x.reshape(392, 128), ((0, 8), (0, 0)))
-
-    b0 = padded(cotangent)
+    node, b0, rims = pl.pallas_call(
+        pack_kernel,
+        out_shape=(sds((400, 128), BF), sds((400, 128), BF), sds((224, 128), BF)),
+        in_specs=[whole((49, 8, 128)), whole((49, 8, 128))],
+        out_specs=(whole((400, 128)), whole((400, 128)), whole((224, 128))),
+        grid=(1,),
+        compiler_params=params(),
+        cost_estimate=light(),
+        name="pack",
+    )(node_x, cotangent)
+    near = cross(rims)
+
     b4 = across(b0, 8)
     b2 = across(b0, 4)
     b1 = across(b0, 2)
     b6 = across(b4, 4)
     b5 = across(b4, 2)
+    near, b2, b4 = lax.optimization_barrier((near, b2, b4))
     b3 = across(b2, 2)
+    far = shift(lax.dynamic_slice_in_dim(near, 112 * high, 112, 0), True)
+    far, b1, b3, b5, b6 = lax.optimization_barrier((far, b1, b3, b5, b6))
     b7 = across(b6, 2)
 
-    node = padded(node_x)
-    send_a, send_b = pl.pallas_call(
-        pack_kernel,
-        out_shape=(sds((112, 128), BF), sds((112, 128), BF)),
-        in_specs=[smem(), whole((400, 128))],
-        out_specs=(whole((112, 128)), whole((112, 128))),
-        grid=(1,),
-        compiler_params=params(),
-        name="pack_rims",
-    )(h_s, node)
-    got_a, got_b = swap_a(send_a), swap_b(send_b)
     row_spec = pl.BlockSpec((1, EB), lambda i: (0, i))
     wig_spec = pl.BlockSpec((235, EB), lambda i: (0, i))
     x_spec = pl.BlockSpec((256, EB), lambda i: (0, i))
@@ -422,12 +427,13 @@
         edge_in_kernel,
         out_shape=sds((256, slots), BF),
         grid=(steps,),
-        in_specs=[smem(), whole((400, 128)), whole((112, 128)), whole((112, 128)), row_spec, wig_spec],
+        in_specs=[smem(), whole((400, 128)), whole((224, 128)), whole((112, 128)), row_spec, wig_spec],
         out_specs=x_spec,
         scratch_shapes=[pltpu.VMEM((235, EB), F32), pltpu.VMEM((400, EB), F32)],
         compiler_params=params(),
+        cost_estimate=light(),
         name="edge_in",
-    )(h_s, node, got_a, got_b, src, wigner)
+    )(h_s, node, near, far, src, wigner)
     x_sib = across(x_own, 1)
 
     w_own = jnp.concatenate(
@@ -447,6 +453,7 @@
         in_specs=[smem(), whole((1376, 128)), whole((1376, 128))],
         out_specs=(whole((112, 512)), whole((192, 768)), whole((160, 640))),
         compiler_params=params(),
+        cost_estimate=light(),
         name="weights",
     )(k_s, w_own, w_sib)
 
@@ -466,29 +473,20 @@
             pltpu.SemaphoreType.DMA((8,)),
         ],
         compiler_params=params(),
+        cost_estimate=light(),
         name="edge_grad",
     )(z_s, edge_count, b0, b1, b2, b3, b4, b5, b6, b7, dst, scale, wigner, x_own, x_sib)
 
     s_got = across(s_sib, 1)
     is_even = core == 0
-    send = jnp.stack(
-        [jnp.where(is_even, s_own, s_got), jnp.where(is_even, s_got, s_own)], axis=1
-    ).reshape(16, 128, 128)
-    groups = [[2 * j + h for j in range(16)] for h in range(2)]
+    send = jnp.concatenate([jnp.where(is_even, s_own, s_got), jnp.where(is_even, s_got, s_own)], axis=0)
+    groups = [[2 * (2 * zb + p) + h for p in range(2) for zb in range(8)] for h in range(2)]
     pieces = lax.all_to_all(send, "brick", 0, 0, axis_index_groups=groups)
     summed = pieces.astype(F32).sum(axis=0).reshape(16, 2, 4, 128)
     mine = jnp.where(high == 0, summed[:, 0], summed[:, 1])
     other = jnp.where(high == 0, summed[:, 1], summed[:, 0])
-    final = mine + swap_a(other.astype(BF).reshape(64, 128)).astype(F32).reshape(16, 4, 128)
-
-    zero_rows = [None] * 7
-    for n, degree in enumerate(ZORD):
-        zero_rows[degree] = final[n, :, 0:56] if n < 4 else final[n - 4, :, 64:120]
-    grad_zero = jnp.stack(zero_rows).reshape(7, 4, 7, 8).transpose(2, 3, 0, 1)
-    grad_one = final[4:10, :, 0:96].reshape(6, 4, 2, 6, 8).transpose(2, 3, 4, 0, 1)
-    two = jnp.stack([final[10:15, :, 0:40], final[10:15, :, 48:88]], axis=2)
-    grad_two = two.reshape(5, 4, 2, 5, 8).transpose(2, 3, 4, 0, 1)
-
+
+    eg, send = lax.optimization_barrier((eg, send))
     g_own, g_sib = pl.pallas_call(
         back_kernel,
         out_shape=(sds((624, 128), F32), sds((624, 128), BF)),
@@ -503,21 +501,35 @@
             pltpu.VMEM((208, 2 * LANES), F32),
         ],
         compiler_params=params(),
+        cost_estimate=light(),
         name="back",
     )(eg, wz, wo, wt, src, wigner)
     g_all = g_own + across(g_sib, 1).astype(F32)
     left, right = g_all[400:512].astype(BF), g_all[512:624].astype(BF)
-    rim_a = swap_a(jnp.where(high == 0, right, left))
-    rim_b = swap_b(jnp.where(high == 0, left, right))
+    near_rim = jnp.where(high == 0, right, left)
+    far_rim = shift(jnp.where(high == 0, left, right), False)
+
+    crossed = cross(jnp.concatenate([near_rim, far_rim, other.astype(BF).reshape(64, 128)], axis=0))
+    final = mine + crossed[224:].astype(F32).reshape(16, 4, 128)
     grad_x = pl.pallas_call(
         join_kernel,
         out_shape=sds((49, 8, 128), F32),
         grid=(1,),
-        in_specs=[smem(), whole((400, 128)), whole((112, 128)), whole((112, 128))],
+        in_specs=[smem(), whole((400, 128)), whole((288, 128))],
         out_specs=whole((49, 8, 128)),
         compiler_params=params(),
+        cost_estimate=light(),
         name="join",
-    )(h_s, g_all[:400], rim_a, rim_b)
+    )(h_s, g_all[:400], crossed)
+
+    zero_rows = [None] * 7
+    for n, degree in enumerate(ZORD):
+        zero_rows[degree] = final[n, :, 0:56] if n < 4 else final[n - 4, :, 64:120]
+    grad_zero = jnp.stack(zero_rows).reshape(7, 4, 7, 8).transpose(2, 3, 0, 1)
+    grad_one = final[4:10, :, 0:96].reshape(6, 4, 2, 6, 8).transpose(2, 3, 4, 0, 1)
+    two = jnp.stack([final[10:15, :, 0:40], final[10:15, :, 48:88]], axis=2)
+    grad_two = two.reshape(5, 4, 2, 5, 8).transpose(2, 3, 4, 0, 1)
+
     return grad_x, grad_zero, grad_one, grad_two
 
 

time: 142 us -> 134 us (0.944)
  the two profiles are of different devices: /device:TPU:64 before, /device:TPU:96 now
where the time goes in v2:
time: 134 us; the launch traced here: 133 us
  starting transfers between devices  66 us (49%)
  Pallas kernels  29 us (22%)
  waiting for transfers between devices  26.5 us (20%)
  local copies, waits for them, and re-layouts  5.63 us (4%)
  other arithmetic  4.27 us (3%)
  between operations  1.7 us (1%)
    ppermute x11, starting transfers between devices, across(): return lax.ppermute(x, 'chan', [(i, i ^ mask) for i in range(16)])  34.9 us
    ppermute x2, waiting for transfers between devices, cross(): return lax.ppermute(x, 'brick', [(i, i ^ 1) for i in range(32)])  16.9 us
    ppermute x2, starting transfers between devices, cross(): return lax.ppermute(x, 'brick', [(i, i ^ 1) for i in range(32)])  16.9 us
    pallas_call x1, Pallas kernels, body(): pl.pallas_call(grad_kernel, out_shape=(sds((1856, slots), BF), sds((8, 12...  12.2 us
    ppermute x2, starting transfers between devices, shift(): return lax.ppermute(x, 'brick', route)  10.5 us
    pallas_call x1, Pallas kernels, body(): pl.pallas_call(back_kernel, out_shape=(sds((624, 128), F32), sds((624, 12...  6.37 us
    ppermute x2, waiting for transfers between devices, shift(): return lax.ppermute(x, 'brick', route)  5.59 us
    unnamed x35, local copies, waits for them, and re-layouts  4.39 us
  transfers between devices with their start and end apart: 16, of which 5 were waited for; matrix products, arithmetic and copies ran while one was open for 2% of the time, Pallas kernels for 11%

profile of v2, /device:TPU:96, one launch (start us, length us, event | category | flops | bytes accessed | tf_op | source)
XLA Modules:
  0.0 133.1 jit_solution(13406725323321263954)
XLA Ops:
  0.6 1.9 %pack.1 = (bf16[400,128]{1,0:T(8,128)(2,1)}, bf16[400,128]{1,0:T(8,128)(2,1)}, bf16[224,128]{1,0:T(8,128)(2,1)}) custom-call(bf16[49,8,128]{2,1,0:T(8,128)(2,1)} %node_ref.1, bf16[49,8,128]{2,1,0:T(8,128)(2,1)} %cot_ref.1), custom_call_target="tpu_custom_call" | custom-call | flops 1 | bytes 1 | tf_op jit(solution)/shard_map/pack/pallas_call | solution.py:400
  2.6 9.1 %collective-permute-start.2 = (bf16[400,128]{1,0:T(8,128)(2,1)}, bf16[400,128]{1,0:T(8,128)(2,1)S(1)}, u32[]{:S(2)}, u32[]{:S(2)}) collective-permute-start(bf16[400,128]{1,0:T(8,128)(2,1)} %get-tuple-element.24.blk0), channel_id=1, source_target_pairs={{0,8},{1,9},{2,10},{3,11},{4,12},{5,13},{6,14},{7,15},{8,0},{9,1},... | collective-permute-start | bytes 307208 | tf_op jit(solution)/shard_map/ppermute | solution.py:391
  11.7 1.9 %collective-permute-start.1 = (bf16[400,128]{1,0:T(8,128)(2,1)}, bf16[400,128]{1,0:T(8,128)(2,1)S(1)}, u32[]{:S(2)}, u32[]{:S(2)}) collective-permute-start(bf16[400,128]{1,0:T(8,128)(2,1)} %get-tuple-element.24.blk0), channel_id=1, source_target_pairs={{0,4},{1,5},{2,6},{3,7},{4,0},{5,1},{6,2},{7,3},{8,12},{9,13},{10,... | collective-permute-start | bytes 307208 | tf_op jit(solution)/shard_map/ppermute | solution.py:391
  13.6 9.7 %collective-permute-start = (bf16[224,128]{1,0:T(8,128)(2,1)}, bf16[224,128]{1,0:T(8,128)(2,1)S(1)}, u32[]{:S(2)}, u32[]{:S(2)}) collective-permute-start(bf16[224,128]{1,0:T(8,128)(2,1)} %get-tuple-element.25), channel_id=1, source_target_pairs={{0,16},{16,0},{32,48},{48,32},{64,80},{80,64},{96,112},{112,96},{1... | collective-permute-start | bytes 172040 | tf_op jit(solution)/shard_map/ppermute | solution.py:394
  23.2 2.9 %collective-permute-start.4 = (bf16[400,128]{1,0:T(8,128)(2,1)}, bf16[400,128]{1,0:T(8,128)(2,1)S(1)}, u32[]{:S(2)}, u32[]{:S(2)}) collective-permute-start(bf16[400,128]{1,0:T(8,128)(2,1)} %get-tuple-element.24.blk0), channel_id=1, source_target_pairs={{0,2},{1,3},{2,0},{3,1},{4,6},{5,7},{6,4},{7,5},{8,10},{9,11},{10,... | collective-permute-start | bytes 307208 | tf_op jit(solution)/shard_map/ppermute | solution.py:391
  26.2 7.4 %collective-permute-done.near_ref = bf16[224,128]{1,0:T(8,128)(2,1)S(1)} collective-permute-done((bf16[224,128]{1,0:T(8,128)(2,1)}, bf16[224,128]{1,0:T(8,128)(2,1)S(1)}, u32[]{:S(2)}, u32[]{:S(2)}) %collective-permute-start) | collective-permute-done | bytes 57376 | tf_op jit(solution)/shard_map/ppermute | solution.py:394
  33.6 1.9 %collective-permute-start.5 = (bf16[400,128]{1,0:T(8,128)(2,1)S(1)}, bf16[400,128]{1,0:T(8,128)(2,1)S(1)}, u32[]{:S(2)}, u32[]{:S(2)}) collective-permute-start(bf16[400,128]{1,0:T(8,128)(2,1)S(1)} %collective-permute-done.1.blk2), channel_id=1, source_target_pairs={{0,2},{1,3},{2,0},{3,1},{4,6},{5,7},{6,4},{7,5},{8,10},{9,11},{10,... | collective-permute-start | bytes 307208 | tf_op jit(solution)/shard_map/ppermute | solution.py:391
  35.5 3.9 %collective-permute-start.6 = (bf16[400,128]{1,0:T(8,128)(2,1)S(1)}, bf16[400,128]{1,0:T(8,128)(2,1)S(1)}, u32[]{:S(2)}, u32[]{:S(2)}) collective-permute-start(bf16[400,128]{1,0:T(8,128)(2,1)S(1)} %collective-permute-done.2.blk4), channel_id=1, source_target_pairs={{0,2},{1,3},{2,0},{3,1},{4,6},{5,7},{6,4},{7,5},{8,10},{9,11},{10,... | collective-permute-start | bytes 307208 | tf_op jit(solution)/shard_map/ppermute | solution.py:391
  39.4 4.6 %collective-permute-start.7 = (bf16[400,128]{1,0:T(8,128)(2,1)S(1)}, bf16[400,128]{1,0:T(8,128)(2,1)S(1)}, u32[]{:S(2)}, u32[]{:S(2)}) collective-permute-start(bf16[400,128]{1,0:T(8,128)(2,1)S(1)} %collective-permute-done.2.blk4), channel_id=1, source_target_pairs={{0,4},{1,5},{2,6},{3,7},{4,0},{5,1},{6,2},{7,3},{8,12},{9,13},{10,... | collective-permute-start | bytes 307208 | tf_op jit(solution)/shard_map/ppermute | solution.py:391
  44.1 3.4 %collective-permute-start.3 = (bf16[112,128]{1,0:T(8,128)(2,1)S(1)}, bf16[112,128]{1,0:T(8,128)(2,1)S(1)}, u32[]{:S(2)}, u32[]{:S(2)}) collective-permute-start(bf16[112,128]{1,0:T(8,128)(2,1)S(1)} %constant_dynamic-slice_fusion), channel_id=1, source_target_pairs={{0,32},{16,496},{32,64},{48,16},{64,96},{80,48},{96,128},{112,80},... | collective-permute-start | bytes 86024 | tf_op jit(solution)/shard_map/ppermute | solution.py:398
  47.6 5.6 %collective-permute-done.3.far_ref = bf16[112,128]{1,0:T(8,128)(2,1)S(1)} collective-permute-done((bf16[112,128]{1,0:T(8,128)(2,1)S(1)}, bf16[112,128]{1,0:T(8,128)(2,1)S(1)}, u32[]{:S(2)}, u32[]{:S(2)}) %collective-permute-start.3) | collective-permute-done | bytes 28704 | tf_op jit(solution)/shard_map/ppermute | solution.py:398
  53.8 4.2 %edge_in.1.xo_ref = bf16[256,1024]{1,0:T(8,128)(2,1)} custom-call(s32[1]{0:T(128)} %bitcast.h_ref, bf16[400,128]{1,0:T(8,128)(2,1)} %get-tuple-element.33.node_ref, bf16[224,128]{1,0:T(8,128)(2,1)} %copy-done.3, bf16[112,128]{1,0:T(8,128)(2,1)} %copy-done.12, s32[1,1024]{1,0:T(1,128)} %bitcast.34, bf16[235,1024]{1,0:T(8,128)(2,1)} %wig_ref.5), custom_call_target="tpu_custom_call" | custom-call | flops 1 | bytes 1 | tf_op jit(solution)/shard_map/edge_in/pallas_call | solution.py:426
  59.8 1.9 %collective-permute-start.8 = (bf16[400,128]{1,0:T(8,128)(2,1)S(1)}, bf16[400,128]{1,0:T(8,128)(2,1)S(1)}, u32[]{:S(2)}, u32[]{:S(2)}) collective-permute-start(bf16[400,128]{1,0:T(8,128)(2,1)S(1)} %collective-permute-done.7.blk6), channel_id=1, source_target_pairs={{0,2},{1,3},{2,0},{3,1},{4,6},{5,7},{6,4},{7,5},{8,10},{9,11},{10,... | collective-permute-start | bytes 307208 | tf_op jit(solution)/shard_map/ppermute | solution.py:391
  63.0 2.4 %collective-permute-start.11 = (bf16[1376,128]{1,0:T(8,128)(2,1)S(1)}, bf16[1376,128]{1,0:T(8,128)(2,1)S(1)}, u32[]{:S(2)}, u32[]{:S(2)}) collective-permute-start(bf16[1376,128]{1,0:T(8,128)(2,1)S(1)} %maximum_maximum_fusion.own_ref), channel_id=1, source_target_pairs={{0,1},{1,0},{2,3},{3,2},{4,5},{5,4},{6,7},{7,6},{8,9},{9,8},{10,11... | collective-permute-start | bytes 1056776 | tf_op jit(solution)/shard_map/ppermute | solution.py:391
  67.9 12.2 %edge_grad.1 = (bf16[1856,1024]{1,0:T(8,128)(2,1)}, bf16[8,128,128]{2,1,0:T(8,128)(2,1)}, bf16[8,128,128]{2,1,0:T(8,128)(2,1)}) custom-call(s32[1]{0:T(128)} %bitcast.1.z_ref, s32[1]{0:T(128)S(6)} %copy.23.count_ref, bf16[400,128]{1,0:T(8,128)(2,1)} %get-tuple-element.24.blk0, bf16[400,128]{1,0:T(8,128)(2,1)} %copy-done.7, bf16[400,128]{1,0:T(8,128)(2,1)} %copy-done.6, ...), custom_call_target="tpu_custom_call" | custom-call | flops 1 | bytes 1 | tf_op jit(solution)/shard_map/edge_grad/pallas_call | solution.py:462
  82.8 2.3 %weights.1 = (bf16[112,512]{1,0:T(8,128)(2,1)}, bf16[192,768]{1,0:T(8,128)(2,1)}, bf16[160,640]{1,0:T(8,128)(2,1)}) custom-call(s32[1]{0:T(128)} %bitcast.5.k_ref, bf16[1376,128]{1,0:T(8,128)(2,1)} %copy-done, bf16[1376,128]{1,0:T(8,128)(2,1)} %copy-done.2), custom_call_target="tpu_custom_call" | custom-call | flops 1 | bytes 1 | tf_op jit(solution)/shard_map/weights/pallas_call | solution.py:449
  87.0 6.4 %back.1 = (f32[624,128]{1,0:T(8,128)}, bf16[624,128]{1,0:T(8,128)(2,1)}) custom-call(bf16[1856,1024]{1,0:T(8,128)(2,1)} %get-tuple-element.38.eg_ref, bf16[112,512]{1,0:T(8,128)(2,1)} %get-tuple-element.39.zero_ref, bf16[192,768]{1,0:T(8,128)(2,1)} %get-tuple-element.40.one_ref, bf16[160,640]{1,0:T(8,128)(2,1)} %get-tuple-element.41.two_ref, ...), custom_call_target="tpu_custom_call" | custom-call | flops 1 | bytes 1 | tf_op jit(solution)/shard_map/back/pallas_call | solution.py:490
  93.3 2.4 %collective-permute-start.12 = (bf16[624,128]{1,0:T(8,128)(2,1)}, bf16[624,128]{1,0:T(8,128)(2,1)S(1)}, u32[]{:S(2)}, u32[]{:S(2)}) collective-permute-start(bf16[624,128]{1,0:T(8,128)(2,1)} %get-tuple-element.43), channel_id=1, source_target_pairs={{0,1},{1,0},{2,3},{3,2},{4,5},{5,4},{6,7},{7,6},{8,9},{9,8},{10,11... | collective-permute-start | bytes 479240 | tf_op jit(solution)/shard_map/ppermute | solution.py:391
  95.7 3.7 %all-to-all-start = ((bf16[16,128,128]{2,1,0:T(8,128)(2,1)}), bf16[16,128,128]{2,1,0:T(8,128)(2,1)S(1)}, u32[]{:S(2)}, u32[]{:S(2)}) async-start(bf16[16,128,128]{2,1,0:T(8,128)(2,1)} %pad_maximum_fusion), calls=%async_computation | async-start | bytes 1048576 | tf_op jit(solution)/shard_map/all_to_all | solution.py:484
  100.5 7.2 %collective-permute-start.13 = (bf16[112,128]{1,0:T(8,128)(2,1)S(1)}, bf16[112,128]{1,0:T(8,128)(2,1)S(1)}, u32[]{:S(2)}, u32[]{:S(2)}) collective-permute-start(bf16[112,128]{1,0:T(8,128)(2,1)S(1)} %get-tuple-element.53), channel_id=1, source_target_pairs={{0,480},{16,48},{32,0},{48,80},{64,32},{80,112},{96,64},{112,144},... | collective-permute-start | bytes 86024 | tf_op jit(solution)/shard_map/ppermute | solution.py:398
  107.7 3.1 %all-to-all-done = bf16[16,128,128]{2,1,0:T(8,128)(2,1)S(1)} async-done(((bf16[16,128,128]{2,1,0:T(8,128)(2,1)}), bf16[16,128,128]{2,1,0:T(8,128)(2,1)S(1)}, u32[]{:S(2)}, u32[]{:S(2)}) %all-to-all-start) | async-done | bytes 524320 | tf_op jit(solution)/shard_map/all_to_all | solution.py:484
  110.9 7.2 %collective-permute-start.14 = (bf16[288,128]{1,0:T(8,128)(2,1)S(1)}, bf16[288,128]{1,0:T(8,128)(2,1)S(1)}, u32[]{:S(2)}, u32[]{:S(2)}) collective-permute-start(bf16[288,128]{1,0:T(8,128)(2,1)S(1)} %pad_maximum_fusion.1), channel_id=1, source_target_pairs={{0,16},{16,0},{32,48},{48,32},{64,80},{80,64},{96,112},{112,96},{1... | collective-permute-start | bytes 221192 | tf_op jit(solution)/shard_map/ppermute | solution.py:394
  118.8 9.5 %collective-permute-done.14.rim_ref = bf16[288,128]{1,0:T(8,128)(2,1)S(1)} collective-permute-done((bf16[288,128]{1,0:T(8,128)(2,1)S(1)}, bf16[288,128]{1,0:T(8,128)(2,1)S(1)}, u32[]{:S(2)}, u32[]{:S(2)}) %collective-permute-start.14) | collective-permute-done | bytes 73760 | tf_op jit(solution)/shard_map/ppermute | solution.py:394
  131.2 1.9 %join.1 = f32[49,8,128]{2,1,0:T(8,128)} custom-call(s32[1]{0:T(128)} %bitcast.h_ref, f32[400,128]{1,0:T(8,128)} %slice.68.own_ref, bf16[288,128]{1,0:T(8,128)(2,1)} %copy-done.4), custom_call_target="tpu_custom_call" | custom-call | flops 1 | bytes 1 | tf_op jit(solution)/shard_map/join/pallas_call | solution.py:514
  (71 shorter events, 14.7 us)
Async XLA Ops:
  2.6 31.0 %collective-permute-start.2 = (bf16[400,128]{1,0:T(8,128)(2,1)}, bf16[400,128]{1,0:T(8,128)(2,1)S(1)}, u32[]{:S(2)}, u32[]{:S(2)}) collective-permute-start(bf16[400,128]{1,0:T(8,128)(2,1)} %get-tuple-element.24.blk0), channel_id=1, source_target_pairs={{0,8},{1,9},{2,10},{3,11},{4,12},{5,13},{6,14},{7,15},{8,0},{9,1},... | collective-permute-start | bytes 307208 | tf_op jit(solution)/shard_map/ppermute | solution.py:391
  11.7 21.9 %collective-permute-start.1 = (bf16[400,128]{1,0:T(8,128)(2,1)}, bf16[400,128]{1,0:T(8,128)(2,1)S(1)}, u32[]{:S(2)}, u32[]{:S(2)}) collective-permute-start(bf16[400,128]{1,0:T(8,128)(2,1)} %get-tuple-element.24.blk0), channel_id=1, source_target_pairs={{0,4},{1,5},{2,6},{3,7},{4,0},{5,1},{6,2},{7,3},{8,12},{9,13},{10,... | collective-permute-start | bytes 307208 | tf_op jit(solution)/shard_map/ppermute | solution.py:391
  13.6 20.0 %collective-permute-start = (bf16[224,128]{1,0:T(8,128)(2,1)}, bf16[224,128]{1,0:T(8,128)(2,1)S(1)}, u32[]{:S(2)}, u32[]{:S(2)}) collective-permute-start(bf16[224,128]{1,0:T(8,128)(2,1)} %get-tuple-element.25), channel_id=1, source_target_pairs={{0,16},{16,0},{32,48},{48,32},{64,80},{80,64},{96,112},{112,96},{1... | collective-permute-start | bytes 172040 | tf_op jit(solution)/shard_map/ppermute | solution.py:394
  23.2 24.3 %collective-permute-start.4 = (bf16[400,128]{1,0:T(8,128)(2,1)}, bf16[400,128]{1,0:T(8,128)(2,1)S(1)}, u32[]{:S(2)}, u32[]{:S(2)}) collective-permute-start(bf16[400,128]{1,0:T(8,128)(2,1)} %get-tuple-element.24.blk0), channel_id=1, source_target_pairs={{0,2},{1,3},{2,0},{3,1},{4,6},{5,7},{6,4},{7,5},{8,10},{9,11},{10,... | collective-permute-start | bytes 307208 | tf_op jit(solution)/shard_map/ppermute | solution.py:391
  33.6 19.6 %copy-start.3 = (bf16[224,128]{1,0:T(8,128)(2,1)}, bf16[224,128]{1,0:T(8,128)(2,1)S(1)}, u32[]{:S(2)}) copy-start(bf16[224,128]{1,0:T(8,128)(2,1)S(1)} %collective-permute-done.near_ref) | copy-start | bytes 172036
  33.6 33.4 %copy-start.5 = (bf16[400,128]{1,0:T(8,128)(2,1)}, bf16[400,128]{1,0:T(8,128)(2,1)S(1)}, u32[]{:S(2)}) copy-start(bf16[400,128]{1,0:T(8,128)(2,1)S(1)} %collective-permute-done.2.blk4) | copy-start | bytes 307204
  33.6 33.4 %copy-start.6 = (bf16[400,128]{1,0:T(8,128)(2,1)}, bf16[400,128]{1,0:T(8,128)(2,1)S(1)}, u32[]{:S(2)}) copy-start(bf16[400,128]{1,0:T(8,128)(2,1)S(1)} %collective-permute-done.1.blk2) | copy-start | bytes 307204
  33.6 19.6 %collective-permute-start.5 = (bf16[400,128]{1,0:T(8,128)(2,1)S(1)}, bf16[400,128]{1,0:T(8,128)(2,1)S(1)}, u32[]{:S(2)}, u32[]{:S(2)}) collective-permute-start(bf16[400,128]{1,0:T(8,128)(2,1)S(1)} %collective-permute-done.1.blk2), channel_id=1, source_target_pairs={{0,2},{1,3},{2,0},{3,1},{4,6},{5,7},{6,4},{7,5},{8,10},{9,11},{10,... | collective-permute-start | bytes 307208 | tf_op jit(solution)/shard_map/ppermute | solution.py:391
  35.5 17.6 %collective-permute-start.6 = (bf16[400,128]{1,0:T(8,128)(2,1)S(1)}, bf16[400,128]{1,0:T(8,128)(2,1)S(1)}, u32[]{:S(2)}, u32[]{:S(2)}) collective-permute-start(bf16[400,128]{1,0:T(8,128)(2,1)S(1)} %collective-permute-done.2.blk4), channel_id=1, source_target_pairs={{0,2},{1,3},{2,0},{3,1},{4,6},{5,7},{6,4},{7,5},{8,10},{9,11},{10,... | collective-permute-start | bytes 307208 | tf_op jit(solution)/shard_map/ppermute | solution.py:391
  39.4 13.7 %collective-permute-start.7 = (bf16[400,128]{1,0:T(8,128)(2,1)S(1)}, bf16[400,128]{1,0:T(8,128)(2,1)S(1)}, u32[]{:S(2)}, u32[]{:S(2)}) collective-permute-start(bf16[400,128]{1,0:T(8,128)(2,1)S(1)} %collective-permute-done.2.blk4), channel_id=1, source_target_pairs={{0,4},{1,5},{2,6},{3,7},{4,0},{5,1},{6,2},{7,3},{8,12},{9,13},{10,... | collective-permute-start | bytes 307208 | tf_op jit(solution)/shard_map/ppermute | solution.py:391
  44.1 9.1 %collective-permute-start.3 = (bf16[112,128]{1,0:T(8,128)(2,1)S(1)}, bf16[112,128]{1,0:T(8,128)(2,1)S(1)}, u32[]{:S(2)}, u32[]{:S(2)}) collective-permute-start(bf16[112,128]{1,0:T(8,128)(2,1)S(1)} %constant_dynamic-slice_fusion), channel_id=1, source_target_pairs={{0,32},{16,496},{32,64},{48,16},{64,96},{80,48},{96,128},{112,80},... | collective-permute-start | bytes 86024 | tf_op jit(solution)/shard_map/ppermute | solution.py:398
  47.6 19.5 %copy-start.7 = (bf16[400,128]{1,0:T(8,128)(2,1)}, bf16[400,128]{1,0:T(8,128)(2,1)S(1)}, u32[]{:S(2)}) copy-start(bf16[400,128]{1,0:T(8,128)(2,1)S(1)} %collective-permute-done.4.blk1) | copy-start | bytes 307204
  53.2 13.9 %copy-start.8 = (bf16[400,128]{1,0:T(8,128)(2,1)}, bf16[400,128]{1,0:T(8,128)(2,1)S(1)}, u32[]{:S(2)}) copy-start(bf16[400,128]{1,0:T(8,128)(2,1)S(1)} %collective-permute-done.5.blk3) | copy-start | bytes 307204
  53.2 13.9 %copy-start.9 = (bf16[400,128]{1,0:T(8,128)(2,1)}, bf16[400,128]{1,0:T(8,128)(2,1)S(1)}, u32[]{:S(2)}) copy-start(bf16[400,128]{1,0:T(8,128)(2,1)S(1)} %collective-permute-done.6.blk5) | copy-start | bytes 307204
  53.2 13.9 %copy-start.10 = (bf16[400,128]{1,0:T(8,128)(2,1)}, bf16[400,128]{1,0:T(8,128)(2,1)S(1)}, u32[]{:S(2)}) copy-start(bf16[400,128]{1,0:T(8,128)(2,1)S(1)} %collective-permute-done.7.blk6) | copy-start | bytes 307204
  57.9 9.1 %collective-permute-start.9 = (bf16[256,1024]{1,0:T(8,128)(2,1)}, bf16[256,1024]{1,0:T(8,128)(2,1)S(1)}, u32[]{:S(2)}, u32[]{:S(2)}) collective-permute-start(bf16[256,1024]{1,0:T(8,128)(2,1)} %edge_in.1.xo_ref), channel_id=1, source_target_pairs={{0,1},{1,0},{2,3},{3,2},{4,5},{5,4},{6,7},{7,6},{8,9},{9,8},{10,11... | collective-permute-start | bytes 1572872 | tf_op jit(solution)/shard_map/ppermute | solution.py:391
  59.8 7.2 %collective-permute-start.8 = (bf16[400,128]{1,0:T(8,128)(2,1)S(1)}, bf16[400,128]{1,0:T(8,128)(2,1)S(1)}, u32[]{:S(2)}, u32[]{:S(2)}) collective-permute-start(bf16[400,128]{1,0:T(8,128)(2,1)S(1)} %collective-permute-done.7.blk6), channel_id=1, source_target_pairs={{0,2},{1,3},{2,0},{3,1},{4,6},{5,7},{6,4},{7,5},{8,10},{9,11},{10,... | collective-permute-start | bytes 307208 | tf_op jit(solution)/shard_map/ppermute | solution.py:391
  63.0 19.0 %copy-start = (bf16[1376,128]{1,0:T(8,128)(2,1)}, bf16[1376,128]{1,0:T(8,128)(2,1)S(1)}, u32[]{:S(2)}) copy-start(bf16[1376,128]{1,0:T(8,128)(2,1)S(1)} %maximum_maximum_fusion.own_ref) | copy-start | bytes 1056772
  63.0 19.0 %collective-permute-start.11 = (bf16[1376,128]{1,0:T(8,128)(2,1)S(1)}, bf16[1376,128]{1,0:T(8,128)(2,1)S(1)}, u32[]{:S(2)}, u32[]{:S(2)}) collective-permute-start(bf16[1376,128]{1,0:T(8,128)(2,1)S(1)} %maximum_maximum_fusion.own_ref), channel_id=1, source_target_pairs={{0,1},{1,0},{2,3},{3,2},{4,5},{5,4},{6,7},{7,6},{8,9},{9,8},{10,11... | collective-permute-start | bytes 1056776 | tf_op jit(solution)/shard_map/ppermute | solution.py:391
  80.1 5.0 %collective-permute-start.10 = (bf16[8,128,128]{2,1,0:T(8,128)(2,1)}, bf16[8,128,128]{2,1,0:T(8,128)(2,1)S(1)}, u32[]{:S(2)}, u32[]{:S(2)}) collective-permute-start(bf16[8,128,128]{2,1,0:T(8,128)(2,1)} %get-tuple-element.37), channel_id=1, source_target_pairs={{0,1},{1,0},{2,3},{3,2},{4,5},{5,4},{6,7},{7,6},{8,9},{9,8},{10,11... | collective-permute-start | bytes 786440 | tf_op jit(solution)/shard_map/ppermute | solution.py:391
  93.3 6.1 %collective-permute-start.12 = (bf16[624,128]{1,0:T(8,128)(2,1)}, bf16[624,128]{1,0:T(8,128)(2,1)S(1)}, u32[]{:S(2)}, u32[]{:S(2)}) collective-permute-start(bf16[624,128]{1,0:T(8,128)(2,1)} %get-tuple-element.43), channel_id=1, source_target_pairs={{0,1},{1,0},{2,3},{3,2},{4,5},{5,4},{6,7},{7,6},{8,9},{9,8},{10,11... | collective-permute-start | bytes 479240 | tf_op jit(solution)/shard_map/ppermute | solution.py:391
  95.7 15.0 %all-to-all-start = ((bf16[16,128,128]{2,1,0:T(8,128)(2,1)}), bf16[16,128,128]{2,1,0:T(8,128)(2,1)S(1)}, u32[]{:S(2)}, u32[]{:S(2)}) async-start(bf16[16,128,128]{2,1,0:T(8,128)(2,1)} %pad_maximum_fusion), calls=%async_computation | async-start | bytes 1048576 | tf_op jit(solution)/shard_map/all_to_all | solution.py:484
  100.5 10.4 %collective-permute-start.13 = (bf16[112,128]{1,0:T(8,128)(2,1)S(1)}, bf16[112,128]{1,0:T(8,128)(2,1)S(1)}, u32[]{:S(2)}, u32[]{:S(2)}) collective-permute-start(bf16[112,128]{1,0:T(8,128)(2,1)S(1)} %get-tuple-element.53), channel_id=1, source_target_pairs={{0,480},{16,48},{32,0},{48,80},{64,32},{80,112},{96,64},{112,144},... | collective-permute-start | bytes 86024 | tf_op jit(solution)/shard_map/ppermute | solution.py:398
  110.9 17.4 %collective-permute-start.14 = (bf16[288,128]{1,0:T(8,128)(2,1)S(1)}, bf16[288,128]{1,0:T(8,128)(2,1)S(1)}, u32[]{:S(2)}, u32[]{:S(2)}) collective-permute-start(bf16[288,128]{1,0:T(8,128)(2,1)S(1)} %pad_maximum_fusion.1), channel_id=1, source_target_pairs={{0,16},{16,0},{32,48},{48,32},{64,80},{80,64},{96,112},{112,96},{1... | collective-permute-start | bytes 221192 | tf_op jit(solution)/shard_map/ppermute | solution.py:394
  (5 other events, 5.7 us)

commit v3 on v2

--- a/solution.py
+++ b/solution.py
@@ -11,7 +11,8 @@
 F32 = jnp.float32
 EB = 256
 LANES = 128
-VMEM_LIMIT = 60 * 1024 * 1024
+VMEM_LIMIT = 28 * 1024 * 1024
+EDGE_VMEM = 60 * 1024 * 1024
 ZORD = (0, 2, 4, 6, 1, 3, 5)
 
 NN = (((1,), (0,)), ((), ()))
@@ -77,7 +78,7 @@
     return own, before, after
 
 
-def pack_kernel(node_ref, cot_ref, node_out, cot_out, rim_out):
+def pack_kernel(node_ref, cot_ref, zero_ref, one_ref, two_ref, node_out, cot_out, rim_out, weight_out):
     blank = jnp.zeros((8, LANES), F32)
 
     def rows(ref):
@@ -101,6 +102,8 @@
     packed = jnp.concatenate(total, axis=0).astype(BF)
     rim_out[:112] = packed[:, :LANES]
     rim_out[112:] = packed[:, LANES:]
+    parts = [ref[...].astype(F32).reshape(-1, LANES) for ref in (zero_ref, one_ref, two_ref)]
+    weight_out[...] = jnp.concatenate(parts + [blank], axis=0).astype(BF)
 
 
 def edge_in_kernel(h_ref, node_ref, near_ref, far_ref, src_ref, wig_ref, x_ref, rot, gathered):
@@ -188,42 +191,47 @@
                     ref[row : row + 16, p * 128 : p * 128 + 128] = tile(entries, p)
 
 
-def grad_kernel(
-    z_ref, count_ref, blk0, blk1, blk2, blk3, blk4, blk5, blk6, blk7,
-    dst_ref, scale_ref, wig_ref, xo_ref, xs_ref,
-    eg_ref, so_ref, ss_ref,
-    vals, gathered, rot, acc, sem,
+def edge_kernel(
+    z_ref, count_ref, blk0, blk4, blk26, blk15, blk37,
+    dst_ref, src_ref, scale_ref, wig_ref, xo_ref, xs_ref, zero_ref, one_ref, two_ref,
+    so_ref, go_ref, sib_ref,
+    vals, gathered, rot, plain, eg, acc, back, full, atoms, rims, sem,
 ):
     step = pl.program_id(0)
-    blocks = (blk0, blk1, blk2, blk3, blk4, blk5, blk6, blk7)
+    blocks = [(0, blk0), (4, blk4)]
+    for n, pair_ref in ((2, blk26), (1, blk15), (3, blk37)):
+        blocks += [(n, pair_ref.at[pl.ds(0, 400)]), (n + 4, pair_ref.at[pl.ds(400, 400)])]
 
     @pl.when(step == 0)
     def _():
         z = z_ref[0]
         copies = [
-            pltpu.make_async_copy(blk, vals.at[z ^ j], sem.at[j]) for j, blk in enumerate(blocks)
+            pltpu.make_async_copy(blk, vals.at[z ^ j], sem.at[j]) for j, blk in blocks
         ]
         for copy in copies:
             copy.start()
         acc[...] = jnp.zeros_like(acc)
+        atoms[...] = jnp.zeros_like(atoms)
+        rims[...] = jnp.zeros_like(rims)
         for copy in copies:
             copy.wait()
 
     slot = step * EB + iota((1, EB), 1)
     factor = jnp.where(slot < count_ref[0], 0.25 * scale_ref[...], 0.0)
-    rot[...] = wig_ref[...].astype(F32) * factor
+    entries = wig_ref[...].astype(F32)
+    plain[...] = entries
+    rot[...] = entries * factor
     dest = hot(iota((LANES, EB), 0) == dst_ref[...])
-
-    def pair(zp, carry):
+    for zp in range(4):
         for side in range(2):
-            gathered[side] = mm(vals[2 * zp + side], dest)
+            gathered[zp % 2, side] = mm(vals[2 * zp + side], dest)
         for half in range(EB // LANES):
             lanes = slice(half * LANES, half * LANES + LANES)
             for degree in range(7):
                 span = 2 * degree + 1
                 at0 = degree * degree
                 cols = [
-                    [gathered[side, (at0 + j) * 8 : (at0 + j + 1) * 8, lanes] for j in range(span)]
+                    [gathered[zp % 2, side, (at0 + j) * 8 : (at0 + j + 1) * 8, lanes] for j in range(span)]
                     for side in range(2)
                 ]
                 for m in orders(degree):
@@ -234,12 +242,8 @@
                         for side in range(2):
                             term = coeff * cols[side][j]
                             totals[side] = term if totals[side] is None else totals[side] + term
-                    place = eg_place(kept_row(degree, m)) * 64
-                    rows = pl.ds(pl.multiple_of(place + zp * 16, 16), 16)
-                    eg_ref[rows, lanes] = jnp.concatenate(totals, axis=0).astype(BF)
-        return carry
-
-    lax.fori_loop(0, 4, pair, 0)
+                    row = eg_place(kept_row(degree, m)) * 64 + zp * 16
+                    eg[row : row + 16, lanes] = jnp.concatenate(totals, axis=0).astype(BF)
 
     def stacked(*pieces):
         return jnp.concatenate(pieces, axis=0)
@@ -248,10 +252,7 @@
         return jnp.zeros((rows, EB), BF)
 
     xo, xs = xo_ref[...], xs_ref[...]
-    even = stacked(xo[:64], blank(64), xs[:64], blank(64))
-    odd = stacked(blank(64), xo[:64], blank(64), xs[:64])
-    acc[0:256] += mm(eg_ref[0:256], even, NT)
-    acc[256:448] += mm(eg_ref[256:448], odd, NT)
+    acc[0:448] += mm(eg[0:448], stacked(xo[:64], blank(64), xs[:64], blank(64)), NT)
     for start, count, plus, minus in ((448, 6, 64, 112), (1216, 5, 160, 208)):
         ahead = stacked(
             xo[plus : plus + 48], -xo[minus : minus + 48], blank(32),
@@ -263,51 +264,26 @@
         )
         size = count * 64
         at = 448 if count == 6 else 832
-        acc[at : at + size] += mm(eg_ref[start : start + size], ahead, NT) + mm(
-            eg_ref[start + size : start + 2 * size], cross, NT
+        acc[at : at + size] += mm(eg[start : start + size], ahead, NT) + mm(
+            eg[start + size : start + 2 * size], cross, NT
         )
 
-    @pl.when(step == pl.num_programs(0) - 1)
-    def _():
-        for zb in range(8):
-            tiles = []
-            for t in range(4):
-                tile = acc[t * 64 + zb * 8 : t * 64 + zb * 8 + 8]
-                if t < 3:
-                    tile = tile + acc[256 + t * 64 + zb * 8 : 256 + t * 64 + zb * 8 + 8]
-                tiles.append(tile)
-            for n in range(11):
-                tiles.append(acc[448 + n * 64 + zb * 8 : 448 + n * 64 + zb * 8 + 8])
-            tiles.append(jnp.zeros((8, 2 * LANES), F32))
-            whole = jnp.concatenate(tiles, axis=0).astype(BF)
-            so_ref[zb] = whole[:, :LANES]
-            ss_ref[zb] = whole[:, LANES:]
-
-
-def back_kernel(
-    eg_ref, zero_ref, one_ref, two_ref, src_ref, wig_ref, own_ref, sib_ref, rot, back, full, acc, rims
-):
-    step = pl.program_id(0)
-
-    @pl.when(step == 0)
-    def _():
-        acc[...] = jnp.zeros_like(acc)
-        rims[...] = jnp.zeros_like(rims)
-
-    rot[...] = wig_ref[...].astype(F32)
-    back[0:112] = mm(zero_ref[:, 0:448], eg_ref[0:448])
-    back[112:304] = mm(one_ref[...], eg_ref[448:1216])
-    back[304:464] = mm(two_ref[...], eg_ref[1216:1856])
+    back[0:112] = mm(zero_ref[:, 0:448], eg[0:448])
+    back[112:304] = mm(one_ref[...], eg[448:1216])
+    back[304:464] = mm(two_ref[...], eg[1216:1856])
     quarter_start = (0, 13, 25, 37)
     for half in range(EB // LANES):
         lanes = slice(half * LANES, half * LANES + LANES)
         for degree in range(7):
-            vals = {m: back[kept_row(degree, m) * 16 : kept_row(degree, m) * 16 + 16, lanes] for m in orders(degree)}
+            vals_m = {
+                m: back[kept_row(degree, m) * 16 : kept_row(degree, m) * 16 + 16, lanes]
+                for m in orders(degree)
+            }
             for j in range(2 * degree + 1):
                 total = None
                 for m in orders(degree):
                     at = wig_row(degree, m, j)
-                    term = rot[at : at + 1, lanes] * vals[m]
+                    term = plain[at : at + 1, lanes] * vals_m[m]
                     total = term if total is None else total + term
                 coef = degree * degree + j
                 row = (quarter_start[coef % 4] + coef // 4) * 16
@@ -316,22 +292,74 @@
     for q in range(4):
         start, size = quarter_start[q] * 16, (13 if q == 0 else 12) * 16
         rows = full[start : start + size]
-        acc[start : start + size] += mm(rows, own, NT)
+        atoms[start : start + size] += mm(rows, own, NT)
         rims[0:size] += mm(rows, jnp.concatenate([before[q], after[q]], axis=0), NT)
 
     @pl.when(step == pl.num_programs(0) - 1)
     def _():
-        for side, ref, kind in ((0, own_ref, F32), (1, sib_ref, BF)):
+        for zb in range(8):
+            tiles = []
+            for t in range(4):
+                tile = acc[t * 64 + zb * 8 : t * 64 + zb * 8 + 8]
+                if t < 3:
+                    odd = acc[256 + t * 64 + zb * 8 : 256 + t * 64 + zb * 8 + 8]
+                    halves = [pltpu.roll(odd[:, n : n + LANES], 64, 1) for n in (0, LANES)]
+                    tile = tile + jnp.concatenate(halves, axis=1)
+                tiles.append(tile)
+            for n in range(11):
+                tiles.append(acc[448 + n * 64 + zb * 8 : 448 + n * 64 + zb * 8 + 8])
+            tiles.append(jnp.zeros((8, 2 * LANES), F32))
+            whole_tile = jnp.concatenate(tiles, axis=0).astype(BF)
+            so_ref[zb * 128 : zb * 128 + 128] = whole_tile[:, :LANES]
+            sib_ref[zb * 128 : zb * 128 + 128] = whole_tile[:, LANES:]
+        for side in range(2):
             tiles = []
             for coef in range(49):
                 row = (quarter_start[coef % 4] + coef // 4) * 16 + side * 8
-                tiles.append(acc[row : row + 8])
+                tiles.append(atoms[row : row + 8])
             tiles.append(jnp.zeros((8, LANES), F32))
             for rim in range(2):
                 for g in range(13):
-                    tiles.append(rims[g * 16 + side * 8 : g * 16 + side * 8 + 8, rim * LANES : rim * LANES + LANES])
+                    row = g * 16 + side * 8
+                    tiles.append(rims[row : row + 8, rim * LANES : rim * LANES + LANES])
                 tiles.append(jnp.zeros((8, LANES), F32))
-            ref[...] = jnp.concatenate(tiles, axis=0).astype(kind)
+            if side == 0:
+                go_ref[...] = jnp.concatenate(tiles, axis=0)
+            else:
+                sib_ref[1024:1648] = jnp.concatenate(tiles, axis=0).astype(BF)
+
+
+def edge_call(z_s, edge_count, blocks, dst, src, scale, wigner, x_own, x_sib, weights):
+    slots = dst.shape[1]
+    any_spec = pl.BlockSpec(memory_space=pl.ANY)
+    row_spec = pl.BlockSpec((1, EB), lambda i: (0, i))
+    wig_spec = pl.BlockSpec((235, EB), lambda i: (0, i))
+    x_spec = pl.BlockSpec((256, EB), lambda i: (0, i))
+    return pl.pallas_call(
+        edge_kernel,
+        out_shape=(sds((1024, 128), BF), sds((624, 128), F32), sds((1648, 128), BF)),
+        grid=(slots // EB,),
+        in_specs=[smem(), smem()]
+        + [any_spec] * 5
+        + [row_spec, row_spec, row_spec, wig_spec, x_spec, x_spec]
+        + [whole((112, 512)), whole((192, 768)), whole((160, 640))],
+        out_specs=(whole((1024, 128)), whole((624, 128)), whole((1648, 128))),
+        scratch_shapes=[
+            pltpu.VMEM((8, 400, 128), BF),
+            pltpu.VMEM((2, 2, 400, EB), F32),
+            pltpu.VMEM((235, EB), F32),
+            pltpu.VMEM((235, EB), F32),
+            pltpu.VMEM((1856, EB), BF),
+            pltpu.VMEM((1152, 256), F32),
+            pltpu.VMEM((464, EB), F32),
+            pltpu.VMEM((784, EB), BF),
+            pltpu.VMEM((784, LANES), F32),
+            pltpu.VMEM((208, 2 * LANES), F32),
+            pltpu.SemaphoreType.DMA((8,)),
+        ],
+        compiler_params=pltpu.CompilerParams(vmem_limit_bytes=EDGE_VMEM),
+        name="edge",
+    )(z_s, edge_count, *blocks, dst, src, scale, wigner, x_own, x_sib, *weights)
 
 
 def join_kernel(h_ref, own_ref, rim_ref, out_ref):
@@ -397,28 +425,42 @@
         route = [(i, (i + (2 if (i % 2 == 0) == away else -2)) % 32) for i in range(32)]
         return lax.ppermute(x, "brick", route)
 
-    node, b0, rims = pl.pallas_call(
+    w_tiles = (
+        w_zero.transpose(0, 2, 1, 3).reshape(49, 8, 128),
+        w_one.transpose(0, 1, 3, 2, 4).reshape(72, 8, 128),
+        w_two.transpose(0, 1, 3, 2, 4).reshape(50, 8, 128),
+    )
+    node, b0, rims, w_own = pl.pallas_call(
         pack_kernel,
-        out_shape=(sds((400, 128), BF), sds((400, 128), BF), sds((224, 128), BF)),
-        in_specs=[whole((49, 8, 128)), whole((49, 8, 128))],
-        out_specs=(whole((400, 128)), whole((400, 128)), whole((224, 128))),
+        out_shape=(sds((400, 128), BF), sds((400, 128), BF), sds((224, 128), BF), sds((1376, 128), BF)),
+        in_specs=[whole((n, 8, 128)) for n in (49, 49, 49, 72, 50)],
+        out_specs=(whole((400, 128)), whole((400, 128)), whole((224, 128)), whole((1376, 128))),
         grid=(1,),
+        compiler_params=pltpu.CompilerParams(vmem_limit_bytes=EDGE_VMEM),
+        cost_estimate=light(),
+        name="pack",
+    )(node_x, cotangent, *w_tiles)
+    near = cross(rims)
+
+    w_sib = across(w_own, 1)
+    wz, wo, wt = pl.pallas_call(
+        weight_kernel,
+        out_shape=(sds((112, 512), BF), sds((192, 768), BF), sds((160, 640), BF)),
+        grid=(1,),
+        in_specs=[smem(), whole((1376, 128)), whole((1376, 128))],
+        out_specs=(whole((112, 512)), whole((192, 768)), whole((160, 640))),
         compiler_params=params(),
         cost_estimate=light(),
-        name="pack",
-    )(node_x, cotangent)
-    near = cross(rims)
+        name="weights",
+    )(k_s, w_own, w_sib)
 
     b4 = across(b0, 8)
-    b2 = across(b0, 4)
-    b1 = across(b0, 2)
-    b6 = across(b4, 4)
-    b5 = across(b4, 2)
-    near, b2, b4 = lax.optimization_barrier((near, b2, b4))
-    b3 = across(b2, 2)
+    two = jnp.concatenate([b0, b4], axis=0)
+    two, near = lax.optimization_barrier((two, near))
+    b26 = across(two, 4)
     far = shift(lax.dynamic_slice_in_dim(near, 112 * high, 112, 0), True)
-    far, b1, b3, b5, b6 = lax.optimization_barrier((far, b1, b3, b5, b6))
-    b7 = across(b6, 2)
+    b15 = across(two, 2)
+    far, b15 = lax.optimization_barrier((far, b15))
 
     row_spec = pl.BlockSpec((1, EB), lambda i: (0, i))
     wig_spec = pl.BlockSpec((235, EB), lambda i: (0, i))
@@ -434,50 +476,17 @@
         cost_estimate=light(),
         name="edge_in",
     )(h_s, node, near, far, src, wigner)
+    x_own, b26 = lax.optimization_barrier((x_own, b26))
+    b37 = across(b26, 2)
     x_sib = across(x_own, 1)
 
-    w_own = jnp.concatenate(
-        [
-            w_zero.transpose(0, 2, 1, 3).reshape(392, 128),
-            w_one.transpose(0, 1, 3, 2, 4).reshape(576, 128),
-            w_two.transpose(0, 1, 3, 2, 4).reshape(400, 128),
-            jnp.zeros((8, 128), BF),
-        ],
-        axis=0,
+    s_own, g_own, to_sib = edge_call(
+        z_s, edge_count, (b0, b4, b26, b15, b37), dst, src, scale, wigner, x_own, x_sib, (wz, wo, wt)
     )
-    w_sib = across(w_own, 1)
-    wz, wo, wt = pl.pallas_call(
-        weight_kernel,
-        out_shape=(sds((112, 512), BF), sds((192, 768), BF), sds((160, 640), BF)),
-        grid=(1,),
-        in_specs=[smem(), whole((1376, 128)), whole((1376, 128))],
-        out_specs=(whole((112, 512)), whole((192, 768)), whole((160, 640))),
-        compiler_params=params(),
-        cost_estimate=light(),
-        name="weights",
-    )(k_s, w_own, w_sib)
-
-    any_spec = pl.BlockSpec(memory_space=pl.ANY)
-    eg_spec = pl.BlockSpec((1856, EB), lambda i: (0, i))
-    eg, s_own, s_sib = pl.pallas_call(
-        grad_kernel,
-        out_shape=(sds((1856, slots), BF), sds((8, 128, 128), BF), sds((8, 128, 128), BF)),
-        grid=(steps,),
-        in_specs=[smem(), smem()] + [any_spec] * 8 + [row_spec, row_spec, wig_spec, x_spec, x_spec],
-        out_specs=(eg_spec, whole((8, 128, 128)), whole((8, 128, 128))),
-        scratch_shapes=[
-            pltpu.VMEM((8, 400, 128), BF),
-            pltpu.VMEM((2, 400, EB), F32),
-            pltpu.VMEM((235, EB), F32),
-            pltpu.VMEM((1152, 256), F32),
-            pltpu.SemaphoreType.DMA((8,)),
-        ],
-        compiler_params=params(),
-        cost_estimate=light(),
-        name="edge_grad",
-    )(z_s, edge_count, b0, b1, b2, b3, b4, b5, b6, b7, dst, scale, wigner, x_own, x_sib)
-
-    s_got = across(s_sib, 1)
+
+    got = across(to_sib, 1)
+    s_got = got[:1024].reshape(8, 128, 128)
+    s_own = s_own.reshape(8, 128, 128)
     is_even = core == 0
     send = jnp.concatenate([jnp.where(is_even, s_own, s_got), jnp.where(is_even, s_got, s_own)], axis=0)
     groups = [[2 * (2 * zb + p) + h for p in range(2) for zb in range(8)] for h in range(2)]
@@ -486,25 +495,7 @@
     mine = jnp.where(high == 0, summed[:, 0], summed[:, 1])
     other = jnp.where(high == 0, summed[:, 1], summed[:, 0])
 
-    eg, send = lax.optimization_barrier((eg, send))
-    g_own, g_sib = pl.pallas_call(
-        back_kernel,
-        out_shape=(sds((624, 128), F32), sds((624, 128), BF)),
-        grid=(steps,),
-        in_specs=[eg_spec, whole((112, 512)), whole((192, 768)), whole((160, 640)), row_spec, wig_spec],
-        out_specs=(whole((624, 128)), whole((624, 128))),
-        scratch_shapes=[
-            pltpu.VMEM((235, EB), F32),
-            pltpu.VMEM((464, EB), F32),
-            pltpu.VMEM((784, EB), BF),
-            pltpu.VMEM((784, LANES), F32),
-            pltpu.VMEM((208, 2 * LANES), F32),
-        ],
-        compiler_params=params(),
-        cost_estimate=light(),
-        name="back",
-    )(eg, wz, wo, wt, src, wigner)
-    g_all = g_own + across(g_sib, 1).astype(F32)
+    g_all = g_own + got[1024:].astype(F32)
     left, right = g_all[400:512].astype(BF), g_all[512:624].astype(BF)
     near_rim = jnp.where(high == 0, right, left)
     far_rim = shift(jnp.where(high == 0, left, right), False)

time: 134 us -> 125 us (0.933)
  the two profiles are of different devices: /device:TPU:96 before, /device:TPU:4 now
where the time goes in v3:
time: 125 us; the launch traced here: 124 us
  starting transfers between devices  63.1 us (50%)
  waiting for transfers between devices  31.5 us (25%)
  Pallas kernels  18.9 us (15%)
  local copies, waits for them, and re-layouts  5.74 us (5%)
  other arithmetic  3.02 us (2%)
  between operations  1.67 us (1%)
    ppermute x7, starting transfers between devices, across(): return lax.ppermute(x, 'chan', [(i, i ^ mask) for i in range(16)])  33.5 us
    ppermute x2, starting transfers between devices, cross(): return lax.ppermute(x, 'brick', [(i, i ^ 1) for i in range(32)])  16.5 us
    ppermute x2, waiting for transfers between devices, cross(): return lax.ppermute(x, 'brick', [(i, i ^ 1) for i in range(32)])  14.5 us
    pallas_call x1, Pallas kernels, edge_call(): pl.pallas_call(edge_kernel, out_shape=(sds((1024, 128), BF), sds((624, 12...  13.2 us
    all_to_all x1, starting transfers between devices, body(): pieces = lax.all_to_all(send, 'brick', 0, 0, axis_index_groups=groups)  7.57 us
    all_to_all x1, waiting for transfers between devices, body(): pieces = lax.all_to_all(send, 'brick', 0, 0, axis_index_groups=groups)  7.28 us
    ppermute x7, waiting for transfers between devices, across(): return lax.ppermute(x, 'chan', [(i, i ^ mask) for i in range(16)])  7.1 us
    ppermute x2, starting transfers between devices, shift(): return lax.ppermute(x, 'brick', route)  5.58 us
  transfers between devices with their start and end apart: 12, of which 7 were waited for; matrix products, arithmetic and copies ran while one was open for 1% of the time, Pallas kernels for 2%

profile of v3, /device:TPU:4, one launch (start us, length us, event | category | flops | bytes accessed | tf_op | source)
XLA Modules:
  0.0 124.0 jit_solution(8729732305848223636)
XLA Ops:
  0.6 2.3 %pack.1 = (bf16[400,128]{1,0:T(8,128)(2,1)}, bf16[400,128]{1,0:T(8,128)(2,1)}, bf16[224,128]{1,0:T(8,128)(2,1)}, bf16[1376,128]{1,0:T(8,128)(2,1)}) custom-call(bf16[49,8,128]{2,1,0:T(8,128)(2,1)} %node_ref.1, bf16[49,8,128]{2,1,0:T(8,128)(2,1)} %cot_ref.1, bf16[49,8,128]{2,1,0:T(8,128)(2,1)} %bitcast.37, bf16[72,8,128]{2,1,0:T(8,128)(2,1)} %bitcast.35, ...), custom_call_target="tpu_custom_call" | custom-call | flops 1 | bytes 1 | tf_op jit(solution)/shard_map/pack/pallas_call | solution.py:433
  2.9 9.1 %collective-permute-start = (bf16[400,128]{1,0:T(8,128)(2,1)}, bf16[400,128]{1,0:T(8,128)(2,1)S(1)}, u32[]{:S(2)}, u32[]{:S(2)}) collective-permute-start(bf16[400,128]{1,0:T(8,128)(2,1)} %get-tuple-element.20.blk0), channel_id=1, source_target_pairs={{0,8},{1,9},{2,10},{3,11},{4,12},{5,13},{6,14},{7,15},{8,0},{9,1},... | collective-permute-start | bytes 307208 | tf_op jit(solution)/shard_map/ppermute | solution.py:419
  12.0 10.9 %collective-permute-start.1 = (bf16[224,128]{1,0:T(8,128)(2,1)}, bf16[224,128]{1,0:T(8,128)(2,1)S(1)}, u32[]{:S(2)}, u32[]{:S(2)}) collective-permute-start(bf16[224,128]{1,0:T(8,128)(2,1)} %get-tuple-element.22), channel_id=1, source_target_pairs={{0,16},{16,0},{32,48},{48,32},{64,80},{80,64},{96,112},{112,96},{1... | collective-permute-start | bytes 172040 | tf_op jit(solution)/shard_map/ppermute | solution.py:422
  23.0 1.0 pad_maximum_fusion.1
  24.0 3.1 %collective-permute-done.1.near_ref = bf16[224,128]{1,0:T(8,128)(2,1)S(1)} collective-permute-done((bf16[224,128]{1,0:T(8,128)(2,1)}, bf16[224,128]{1,0:T(8,128)(2,1)S(1)}, u32[]{:S(2)}, u32[]{:S(2)}) %collective-permute-start.1) | collective-permute-done | bytes 57376 | tf_op jit(solution)/shard_map/ppermute | solution.py:422
  27.1 3.9 %collective-permute-start.3 = (bf16[800,128]{1,0:T(8,128)(2,1)S(1)}, bf16[800,128]{1,0:T(8,128)(2,1)S(1)}, u32[]{:S(2)}, u32[]{:S(2)}) collective-permute-start(bf16[800,128]{1,0:T(8,128)(2,1)S(1)} %pad_maximum_fusion.1), channel_id=1, source_target_pairs={{0,2},{1,3},{2,0},{3,1},{4,6},{5,7},{6,4},{7,5},{8,10},{9,11},{10,... | collective-permute-start | bytes 614408 | tf_op jit(solution)/shard_map/ppermute | solution.py:419
  31.0 12.4 %collective-permute-start.4 = (bf16[800,128]{1,0:T(8,128)(2,1)S(1)}, bf16[800,128]{1,0:T(8,128)(2,1)S(1)}, u32[]{:S(2)}, u32[]{:S(2)}) collective-permute-start(bf16[800,128]{1,0:T(8,128)(2,1)S(1)} %pad_maximum_fusion.1), channel_id=1, source_target_pairs={{0,4},{1,5},{2,6},{3,7},{4,0},{5,1},{6,2},{7,3},{8,12},{9,13},{10,... | collective-permute-start | bytes 614408 | tf_op jit(solution)/shard_map/ppermute | solution.py:419
  43.4 3.1 %collective-permute-start.2 = (bf16[112,128]{1,0:T(8,128)(2,1)S(1)}, bf16[112,128]{1,0:T(8,128)(2,1)S(1)}, u32[]{:S(2)}, u32[]{:S(2)}) collective-permute-start(bf16[112,128]{1,0:T(8,128)(2,1)S(1)} %constant_dynamic-slice_fusion), channel_id=1, source_target_pairs={{0,32},{16,496},{32,64},{48,16},{64,96},{80,48},{96,128},{112,80},... | collective-permute-start | bytes 86024 | tf_op jit(solution)/shard_map/ppermute | solution.py:426
  46.5 2.7 %collective-permute-done.2.far_ref = bf16[112,128]{1,0:T(8,128)(2,1)S(1)} collective-permute-done((bf16[112,128]{1,0:T(8,128)(2,1)S(1)}, bf16[112,128]{1,0:T(8,128)(2,1)S(1)}, u32[]{:S(2)}, u32[]{:S(2)}) %collective-permute-start.2) | collective-permute-done | bytes 28704 | tf_op jit(solution)/shard_map/ppermute | solution.py:426
  49.2 1.9 %edge_in.1.xo_ref = bf16[256,1024]{1,0:T(8,128)(2,1)S(1)} custom-call(s32[1]{0:T(128)} %bitcast.h_ref, bf16[400,128]{1,0:T(8,128)(2,1)S(1)} %copy-done.6, bf16[224,128]{1,0:T(8,128)(2,1)S(1)} %collective-permute-done.1.near_ref, bf16[112,128]{1,0:T(8,128)(2,1)S(1)} %collective-permute-done.2.far_ref, s32[1,1024]{1,0:T(1,128)S(1)} %bitcast.28, ...), custom_call_target="tpu_custom_call" | custom-call | flops 1 | bytes 1 | tf_op jit(solution)/shard_map/edge_in/pallas_call | solution.py:468
  51.1 1.5 %collective-permute-done.4.blk26 = bf16[800,128]{1,0:T(8,128)(2,1)S(1)} collective-permute-done((bf16[800,128]{1,0:T(8,128)(2,1)S(1)}, bf16[800,128]{1,0:T(8,128)(2,1)S(1)}, u32[]{:S(2)}, u32[]{:S(2)}) %collective-permute-start.4) | collective-permute-done | bytes 204832 | tf_op jit(solution)/shard_map/ppermute | solution.py:419
  52.6 1.9 %collective-permute-start.6 = (bf16[256,1024]{1,0:T(8,128)(2,1)S(1)}, bf16[256,1024]{1,0:T(8,128)(2,1)S(1)}, u32[]{:S(2)}, u32[]{:S(2)}) collective-permute-start(bf16[256,1024]{1,0:T(8,128)(2,1)S(1)} %edge_in.1.xo_ref), channel_id=1, source_target_pairs={{0,1},{1,0},{2,3},{3,2},{4,5},{5,4},{6,7},{7,6},{8,9},{9,8},{10,11... | collective-permute-start | bytes 1572872 | tf_op jit(solution)/shard_map/ppermute | solution.py:419
  54.5 2.4 %collective-permute-start.7 = (bf16[1376,128]{1,0:T(8,128)(2,1)S(1)}, bf16[1376,128]{1,0:T(8,128)(2,1)S(1)}, u32[]{:S(2)}, u32[]{:S(2)}) collective-permute-start(bf16[1376,128]{1,0:T(8,128)(2,1)S(1)} %copy-done.2), channel_id=1, source_target_pairs={{0,1},{1,0},{2,3},{3,2},{4,5},{5,4},{6,7},{7,6},{8,9},{9,8},{10,11... | collective-permute-start | bytes 1056776 | tf_op jit(solution)/shard_map/ppermute | solution.py:419
  56.9 1.9 %collective-permute-start.5 = (bf16[800,128]{1,0:T(8,128)(2,1)S(1)}, bf16[800,128]{1,0:T(8,128)(2,1)S(1)}, u32[]{:S(2)}, u32[]{:S(2)}) collective-permute-start(bf16[800,128]{1,0:T(8,128)(2,1)S(1)} %collective-permute-done.4.blk26), channel_id=1, source_target_pairs={{0,2},{1,3},{2,0},{3,1},{4,6},{5,7},{6,4},{7,5},{8,10},{9,11},{10,... | collective-permute-start | bytes 614408 | tf_op jit(solution)/shard_map/ppermute | solution.py:419
  62.1 3.7 %collective-permute-done.5.blk37 = bf16[800,128]{1,0:T(8,128)(2,1)S(1)} collective-permute-done((bf16[800,128]{1,0:T(8,128)(2,1)S(1)}, bf16[800,128]{1,0:T(8,128)(2,1)S(1)}, u32[]{:S(2)}, u32[]{:S(2)}) %collective-permute-start.5) | collective-permute-done | bytes 204832 | tf_op jit(solution)/shard_map/ppermute | solution.py:419
  66.7 13.2 %edge.1 = (bf16[1024,128]{1,0:T(8,128)(2,1)}, f32[624,128]{1,0:T(8,128)}, bf16[1648,128]{1,0:T(8,128)(2,1)}) custom-call(s32[1]{0:T(128)} %bitcast.1.z_ref, s32[1]{0:T(128)S(6)} %copy.23.count_ref, bf16[400,128]{1,0:T(8,128)(2,1)} %get-tuple-element.20.blk0, bf16[400,128]{1,0:T(8,128)(2,1)} %copy-done.9, bf16[800,128]{1,0:T(8,128)(2,1)} %copy-done.12, ...), custom_call_target="tpu_custom_call" | custom-call | tf_op jit(solution)/shard_map/edge/pallas_call | solution.py:338
  79.9 1.9 %collective-permute-start.8 = (bf16[1648,128]{1,0:T(8,128)(2,1)}, bf16[1648,128]{1,0:T(8,128)(2,1)S(1)}, u32[]{:S(2)}, u32[]{:S(2)}) collective-permute-start(bf16[1648,128]{1,0:T(8,128)(2,1)} %get-tuple-element.34), channel_id=1, source_target_pairs={{0,1},{1,0},{2,3},{3,2},{4,5},{5,4},{6,7},{7,6},{8,9},{9,8},{10,11... | collective-permute-start | bytes 1265672 | tf_op jit(solution)/shard_map/ppermute | solution.py:419
  81.9 1.9 %collective-permute-done.8 = bf16[1648,128]{1,0:T(8,128)(2,1)S(1)} collective-permute-done((bf16[1648,128]{1,0:T(8,128)(2,1)}, bf16[1648,128]{1,0:T(8,128)(2,1)S(1)}, u32[]{:S(2)}, u32[]{:S(2)}) %collective-permute-start.8) | collective-permute-done | bytes 421920 | tf_op jit(solution)/shard_map/ppermute | solution.py:419
  83.8 1.0 broadcast_select_fusion.1
  85.7 7.6 %all-to-all-start = ((bf16[16,128,128]{2,1,0:T(8,128)(2,1)}), bf16[16,128,128]{2,1,0:T(8,128)(2,1)S(1)}, u32[]{:S(2)}, u32[]{:S(2)}) async-start(bf16[16,128,128]{2,1,0:T(8,128)(2,1)} %pad_maximum_fusion), calls=%async_computation | async-start | bytes 1048576 | tf_op jit(solution)/shard_map/all_to_all | solution.py:493
  93.3 2.5 %collective-permute-start.9 = (bf16[112,128]{1,0:T(8,128)(2,1)S(1)}, bf16[112,128]{1,0:T(8,128)(2,1)S(1)}, u32[]{:S(2)}, u32[]{:S(2)}) collective-permute-start(bf16[112,128]{1,0:T(8,128)(2,1)S(1)} %get-tuple-element.45), channel_id=1, source_target_pairs={{0,480},{16,48},{32,0},{48,80},{64,32},{80,112},{96,64},{112,144},... | collective-permute-start | bytes 86024 | tf_op jit(solution)/shard_map/ppermute | solution.py:426
  95.8 7.3 %all-to-all-done = bf16[16,128,128]{2,1,0:T(8,128)(2,1)S(1)} async-done(((bf16[16,128,128]{2,1,0:T(8,128)(2,1)}), bf16[16,128,128]{2,1,0:T(8,128)(2,1)S(1)}, u32[]{:S(2)}, u32[]{:S(2)}) %all-to-all-start) | async-done | bytes 524320 | tf_op jit(solution)/shard_map/all_to_all | solution.py:493
  103.2 5.6 %collective-permute-start.10 = (bf16[288,128]{1,0:T(8,128)(2,1)S(1)}, bf16[288,128]{1,0:T(8,128)(2,1)S(1)}, u32[]{:S(2)}, u32[]{:S(2)}) collective-permute-start(bf16[288,128]{1,0:T(8,128)(2,1)S(1)} %pad_maximum_fusion.2), channel_id=1, source_target_pairs={{0,16},{16,0},{32,48},{48,32},{64,80},{80,64},{96,112},{112,96},{1... | collective-permute-start | bytes 221192 | tf_op jit(solution)/shard_map/ppermute | solution.py:422
  108.8 11.4 %collective-permute-done.10.rim_ref = bf16[288,128]{1,0:T(8,128)(2,1)S(1)} collective-permute-done((bf16[288,128]{1,0:T(8,128)(2,1)S(1)}, bf16[288,128]{1,0:T(8,128)(2,1)S(1)}, u32[]{:S(2)}, u32[]{:S(2)}) %collective-permute-start.10) | collective-permute-done | bytes 73760 | tf_op jit(solution)/shard_map/ppermute | solution.py:422
  (62 shorter events, 8.3 us)
Async XLA Ops:
  0.6 48.5 %copy-start.1 = (bf16[235,1024]{1,0:T(8,128)(2,1)S(1)}, bf16[235,1024]{1,0:T(8,128)(2,1)}, u32[]{:S(2)}) copy-start(bf16[235,1024]{1,0:T(8,128)(2,1)} %wig_ref.3) | copy-start | bytes 1443844
  2.9 20.0 %collective-permute-start = (bf16[400,128]{1,0:T(8,128)(2,1)}, bf16[400,128]{1,0:T(8,128)(2,1)S(1)}, u32[]{:S(2)}, u32[]{:S(2)}) collective-permute-start(bf16[400,128]{1,0:T(8,128)(2,1)} %get-tuple-element.20.blk0), channel_id=1, source_target_pairs={{0,8},{1,9},{2,10},{3,11},{4,12},{5,13},{6,14},{7,15},{8,0},{9,1},... | collective-permute-start | bytes 307208 | tf_op jit(solution)/shard_map/ppermute | solution.py:419
  12.0 15.1 %collective-permute-start.1 = (bf16[224,128]{1,0:T(8,128)(2,1)}, bf16[224,128]{1,0:T(8,128)(2,1)S(1)}, u32[]{:S(2)}, u32[]{:S(2)}) collective-permute-start(bf16[224,128]{1,0:T(8,128)(2,1)} %get-tuple-element.22), channel_id=1, source_target_pairs={{0,16},{16,0},{32,48},{48,32},{64,80},{80,64},{96,112},{112,96},{1... | collective-permute-start | bytes 172040 | tf_op jit(solution)/shard_map/ppermute | solution.py:422
  22.9 1.0 copy-start.9
  23.0 26.2 %copy-start.6 = (bf16[400,128]{1,0:T(8,128)(2,1)S(1)}, bf16[400,128]{1,0:T(8,128)(2,1)}, u32[]{:S(2)}) copy-start(bf16[400,128]{1,0:T(8,128)(2,1)} %get-tuple-element.21.node_ref) | copy-start | bytes 307204
  27.1 22.1 %collective-permute-start.3 = (bf16[800,128]{1,0:T(8,128)(2,1)S(1)}, bf16[800,128]{1,0:T(8,128)(2,1)S(1)}, u32[]{:S(2)}, u32[]{:S(2)}) collective-permute-start(bf16[800,128]{1,0:T(8,128)(2,1)S(1)} %pad_maximum_fusion.1), channel_id=1, source_target_pairs={{0,2},{1,3},{2,0},{3,1},{4,6},{5,7},{6,4},{7,5},{8,10},{9,11},{10,... | collective-permute-start | bytes 614408 | tf_op jit(solution)/shard_map/ppermute | solution.py:419
  31.0 21.6 %collective-permute-start.4 = (bf16[800,128]{1,0:T(8,128)(2,1)S(1)}, bf16[800,128]{1,0:T(8,128)(2,1)S(1)}, u32[]{:S(2)}, u32[]{:S(2)}) collective-permute-start(bf16[800,128]{1,0:T(8,128)(2,1)S(1)} %pad_maximum_fusion.1), channel_id=1, source_target_pairs={{0,4},{1,5},{2,6},{3,7},{4,0},{5,1},{6,2},{7,3},{8,12},{9,13},{10,... | collective-permute-start | bytes 614408 | tf_op jit(solution)/shard_map/ppermute | solution.py:419
  43.4 5.8 %copy-start.7 = (s32[1024]{0:T(1024)S(1)}, s32[1024]{0:T(1024)}, u32[]{:S(2)}) copy-start(s32[1024]{0:T(1024)} %param.13) | copy-start | bytes 12292
  43.4 5.8 %collective-permute-start.2 = (bf16[112,128]{1,0:T(8,128)(2,1)S(1)}, bf16[112,128]{1,0:T(8,128)(2,1)S(1)}, u32[]{:S(2)}, u32[]{:S(2)}) collective-permute-start(bf16[112,128]{1,0:T(8,128)(2,1)S(1)} %constant_dynamic-slice_fusion), channel_id=1, source_target_pairs={{0,32},{16,496},{32,64},{48,16},{64,96},{80,48},{96,128},{112,80},... | collective-permute-start | bytes 86024 | tf_op jit(solution)/shard_map/ppermute | solution.py:426
  49.2 2.0 %copy-start.11 = (bf16[800,128]{1,0:T(8,128)(2,1)}, bf16[800,128]{1,0:T(8,128)(2,1)S(1)}, u32[]{:S(2)}) copy-start(bf16[800,128]{1,0:T(8,128)(2,1)S(1)} %collective-permute-done.3.blk15) | copy-start | bytes 614404
  49.2 5.3 %copy-start.2 = (bf16[1376,128]{1,0:T(8,128)(2,1)S(1)}, bf16[1376,128]{1,0:T(8,128)(2,1)}, u32[]{:S(2)}) copy-start(bf16[1376,128]{1,0:T(8,128)(2,1)} %get-tuple-element.29.own_ref) | copy-start | bytes 1056772
  51.1 14.7 %copy-start = (bf16[256,1024]{1,0:T(8,128)(2,1)}, bf16[256,1024]{1,0:T(8,128)(2,1)S(1)}, u32[]{:S(2)}) copy-start(bf16[256,1024]{1,0:T(8,128)(2,1)S(1)} %edge_in.1.xo_ref) | copy-start | bytes 1572868
  52.6 7.5 %copy-start.12 = (bf16[800,128]{1,0:T(8,128)(2,1)}, bf16[800,128]{1,0:T(8,128)(2,1)S(1)}, u32[]{:S(2)}) copy-start(bf16[800,128]{1,0:T(8,128)(2,1)S(1)} %collective-permute-done.4.blk26) | copy-start | bytes 614404
  52.6 13.2 %collective-permute-start.6 = (bf16[256,1024]{1,0:T(8,128)(2,1)S(1)}, bf16[256,1024]{1,0:T(8,128)(2,1)S(1)}, u32[]{:S(2)}, u32[]{:S(2)}) collective-permute-start(bf16[256,1024]{1,0:T(8,128)(2,1)S(1)} %edge_in.1.xo_ref), channel_id=1, source_target_pairs={{0,1},{1,0},{2,3},{3,2},{4,5},{5,4},{6,7},{7,6},{8,9},{9,8},{10,11... | collective-permute-start | bytes 1572872 | tf_op jit(solution)/shard_map/ppermute | solution.py:419
  54.5 5.0 %collective-permute-start.7 = (bf16[1376,128]{1,0:T(8,128)(2,1)S(1)}, bf16[1376,128]{1,0:T(8,128)(2,1)S(1)}, u32[]{:S(2)}, u32[]{:S(2)}) collective-permute-start(bf16[1376,128]{1,0:T(8,128)(2,1)S(1)} %copy-done.2), channel_id=1, source_target_pairs={{0,1},{1,0},{2,3},{3,2},{4,5},{5,4},{6,7},{7,6},{8,9},{9,8},{10,11... | collective-permute-start | bytes 1056776 | tf_op jit(solution)/shard_map/ppermute | solution.py:419
  56.9 8.9 %collective-permute-start.5 = (bf16[800,128]{1,0:T(8,128)(2,1)S(1)}, bf16[800,128]{1,0:T(8,128)(2,1)S(1)}, u32[]{:S(2)}, u32[]{:S(2)}) collective-permute-start(bf16[800,128]{1,0:T(8,128)(2,1)S(1)} %collective-permute-done.4.blk26), channel_id=1, source_target_pairs={{0,2},{1,3},{2,0},{3,1},{4,6},{5,7},{6,4},{7,5},{8,10},{9,11},{10,... | collective-permute-start | bytes 614408 | tf_op jit(solution)/shard_map/ppermute | solution.py:419
  60.1 0.7 copy-start.3
  60.8 0.7 copy-start.4
  65.8 0.9 copy-start.8
  79.9 3.9 %collective-permute-start.8 = (bf16[1648,128]{1,0:T(8,128)(2,1)}, bf16[1648,128]{1,0:T(8,128)(2,1)S(1)}, u32[]{:S(2)}, u32[]{:S(2)}) collective-permute-start(bf16[1648,128]{1,0:T(8,128)(2,1)} %get-tuple-element.34), channel_id=1, source_target_pairs={{0,1},{1,0},{2,3},{3,2},{4,5},{5,4},{6,7},{7,6},{8,9},{9,8},{10,11... | collective-permute-start | bytes 1265672 | tf_op jit(solution)/shard_map/ppermute | solution.py:419
  85.7 7.6 %copy-start.10 = (f32[624,128]{1,0:T(8,128)S(1)}, f32[624,128]{1,0:T(8,128)}, u32[]{:S(2)}) copy-start(f32[624,128]{1,0:T(8,128)} %get-tuple-element.33) | copy-start | bytes 958468
  85.7 17.4 %all-to-all-start = ((bf16[16,128,128]{2,1,0:T(8,128)(2,1)}), bf16[16,128,128]{2,1,0:T(8,128)(2,1)S(1)}, u32[]{:S(2)}, u32[]{:S(2)}) async-start(bf16[16,128,128]{2,1,0:T(8,128)(2,1)} %pad_maximum_fusion), calls=%async_computation | async-start | bytes 1048576 | tf_op jit(solution)/shard_map/all_to_all | solution.py:493
  93.3 9.9 %collective-permute-start.9 = (bf16[112,128]{1,0:T(8,128)(2,1)S(1)}, bf16[112,128]{1,0:T(8,128)(2,1)S(1)}, u32[]{:S(2)}, u32[]{:S(2)}) collective-permute-start(bf16[112,128]{1,0:T(8,128)(2,1)S(1)} %get-tuple-element.45), channel_id=1, source_target_pairs={{0,480},{16,48},{32,0},{48,80},{64,32},{80,112},{96,64},{112,144},... | collective-permute-start | bytes 86024 | tf_op jit(solution)/shard_map/ppermute | solution.py:426
  103.2 17.0 %collective-permute-start.10 = (bf16[288,128]{1,0:T(8,128)(2,1)S(1)}, bf16[288,128]{1,0:T(8,128)(2,1)S(1)}, u32[]{:S(2)}, u32[]{:S(2)}) collective-permute-start(bf16[288,128]{1,0:T(8,128)(2,1)S(1)} %pad_maximum_fusion.2), channel_id=1, source_target_pairs={{0,16},{16,0},{32,48},{48,32},{64,80},{80,64},{96,112},{112,96},{1... | collective-permute-start | bytes 221192 | tf_op jit(solution)/shard_map/ppermute | solution.py:422
  (2 other events, 1.3 us)

commit v4 on v3

--- a/solution.py
+++ b/solution.py
@@ -12,7 +12,7 @@
 EB = 256
 LANES = 128
 VMEM_LIMIT = 28 * 1024 * 1024
-EDGE_VMEM = 60 * 1024 * 1024
+PACK_VMEM = 60 * 1024 * 1024
 ZORD = (0, 2, 4, 6, 1, 3, 5)
 
 NN = (((1,), (0,)), ((), ()))
@@ -150,7 +150,8 @@
 
     def pick(offset):
         spot = lane - offset
-        wanted = (spot // 8) * 16 + k * 8 + spot % 8
+        block = (spot // 8 % 2) * 4 + spot // 16
+        wanted = block * 16 + k * 8 + spot % 8
         return hot((spot >= 0) & (spot < 64) & (chan == wanted))
 
     low, high = pick(0), pick(64)
@@ -191,59 +192,76 @@
                     ref[row : row + 16, p * 128 : p * 128 + 128] = tile(entries, p)
 
 
+def rotate_pair(z, pair_ref, dest, rot, gathered, store):
+    for side in range(2):
+        start = pl.multiple_of(400 * (side ^ (z // 4)), 16)
+        gathered[side] = mm(pair_ref[pl.ds(start, 400), :], dest)
+    for half in range(EB // LANES):
+        lanes = slice(half * LANES, half * LANES + LANES)
+        for degree in range(7):
+            span = 2 * degree + 1
+            at0 = degree * degree
+            cols = [
+                [gathered[side, (at0 + j) * 8 : (at0 + j + 1) * 8, lanes] for j in range(span)]
+                for side in range(2)
+            ]
+            for m in orders(degree):
+                totals = [None, None]
+                for j in range(span):
+                    at = wig_row(degree, m, j)
+                    coeff = jnp.broadcast_to(rot[at : at + 1, lanes], (8, LANES))
+                    for side in range(2):
+                        term = coeff * cols[side][j]
+                        totals[side] = term if totals[side] is None else totals[side] + term
+                place = eg_place(kept_row(degree, m))
+                store(place, lanes, jnp.concatenate(totals, axis=0).astype(BF))
+
+
+def edge_factor(step, count_ref, scale_ref):
+    slot = step * EB + iota((1, EB), 1)
+    return jnp.where(slot < count_ref[0], 0.25 * scale_ref[...], 0.0)
+
+
+def rotate_kernel(z_ref, count_ref, pair_ref, dst_ref, scale_ref, wig_ref, eg_ref, gathered, rot):
+    rot[...] = wig_ref[...].astype(F32) * edge_factor(pl.program_id(0), count_ref, scale_ref)
+    dest = hot(iota((LANES, EB), 0) == dst_ref[...])
+
+    def store(place, lanes, tile):
+        eg_ref[place * 16 : place * 16 + 16, lanes] = tile
+
+    rotate_pair(z_ref[0], pair_ref, dest, rot, gathered, store)
+
+
 def edge_kernel(
-    z_ref, count_ref, blk0, blk4, blk26, blk15, blk37,
+    z_ref, count_ref, eg0, eg2, eg1, pair_ref,
     dst_ref, src_ref, scale_ref, wig_ref, xo_ref, xs_ref, zero_ref, one_ref, two_ref,
     so_ref, go_ref, sib_ref,
-    vals, gathered, rot, plain, eg, acc, back, full, atoms, rims, sem,
+    gathered, rot, plain, eg, acc, back, full, atoms, rims,
 ):
     step = pl.program_id(0)
-    blocks = [(0, blk0), (4, blk4)]
-    for n, pair_ref in ((2, blk26), (1, blk15), (3, blk37)):
-        blocks += [(n, pair_ref.at[pl.ds(0, 400)]), (n + 4, pair_ref.at[pl.ds(400, 400)])]
 
     @pl.when(step == 0)
     def _():
-        z = z_ref[0]
-        copies = [
-            pltpu.make_async_copy(blk, vals.at[z ^ j], sem.at[j]) for j, blk in blocks
-        ]
-        for copy in copies:
-            copy.start()
         acc[...] = jnp.zeros_like(acc)
         atoms[...] = jnp.zeros_like(atoms)
         rims[...] = jnp.zeros_like(rims)
-        for copy in copies:
-            copy.wait()
-
-    slot = step * EB + iota((1, EB), 1)
-    factor = jnp.where(slot < count_ref[0], 0.25 * scale_ref[...], 0.0)
+
+    z = z_ref[0]
     entries = wig_ref[...].astype(F32)
     plain[...] = entries
-    rot[...] = entries * factor
+    rot[...] = entries * edge_factor(step, count_ref, scale_ref)
     dest = hot(iota((LANES, EB), 0) == dst_ref[...])
-    for zp in range(4):
-        for side in range(2):
-            gathered[zp % 2, side] = mm(vals[2 * zp + side], dest)
-        for half in range(EB // LANES):
-            lanes = slice(half * LANES, half * LANES + LANES)
-            for degree in range(7):
-                span = 2 * degree + 1
-                at0 = degree * degree
-                cols = [
-                    [gathered[zp % 2, side, (at0 + j) * 8 : (at0 + j + 1) * 8, lanes] for j in range(span)]
-                    for side in range(2)
-                ]
-                for m in orders(degree):
-                    totals = [None, None]
-                    for j in range(span):
-                        at = wig_row(degree, m, j)
-                        coeff = jnp.broadcast_to(rot[at : at + 1, lanes], (8, LANES))
-                        for side in range(2):
-                            term = coeff * cols[side][j]
-                            totals[side] = term if totals[side] is None else totals[side] + term
-                    row = eg_place(kept_row(degree, m)) * 64 + zp * 16
-                    eg[row : row + 16, lanes] = jnp.concatenate(totals, axis=0).astype(BF)
+
+    def rows_of(place, n):
+        return pl.ds(pl.multiple_of(place * 64 + ((z % 4) ^ n) * 16, 16), 16)
+
+    def store(place, lanes, tile):
+        eg[rows_of(place, 3), lanes] = tile
+
+    rotate_pair(z, pair_ref, dest, rot, gathered, store)
+    for n, ref in ((0, eg0), (2, eg2), (1, eg1)):
+        for place in range(29):
+            eg[rows_of(place, n), :] = ref[place * 16 : place * 16 + 16]
 
     def stacked(*pieces):
         return jnp.concatenate(pieces, axis=0)
@@ -299,15 +317,16 @@
     def _():
         for zb in range(8):
             tiles = []
+            spot = zb % 4 * 16 + zb // 4 * 8
             for t in range(4):
-                tile = acc[t * 64 + zb * 8 : t * 64 + zb * 8 + 8]
+                tile = acc[t * 64 + spot : t * 64 + spot + 8]
                 if t < 3:
-                    odd = acc[256 + t * 64 + zb * 8 : 256 + t * 64 + zb * 8 + 8]
+                    odd = acc[256 + t * 64 + spot : 256 + t * 64 + spot + 8]
                     halves = [pltpu.roll(odd[:, n : n + LANES], 64, 1) for n in (0, LANES)]
                     tile = tile + jnp.concatenate(halves, axis=1)
                 tiles.append(tile)
             for n in range(11):
-                tiles.append(acc[448 + n * 64 + zb * 8 : 448 + n * 64 + zb * 8 + 8])
+                tiles.append(acc[448 + n * 64 + spot : 448 + n * 64 + spot + 8])
             tiles.append(jnp.zeros((8, 2 * LANES), F32))
             whole_tile = jnp.concatenate(tiles, axis=0).astype(BF)
             so_ref[zb * 128 : zb * 128 + 128] = whole_tile[:, :LANES]
@@ -329,24 +348,42 @@
                 sib_ref[1024:1648] = jnp.concatenate(tiles, axis=0).astype(BF)
 
 
-def edge_call(z_s, edge_count, blocks, dst, src, scale, wigner, x_own, x_sib, weights):
+def row_spec():
+    return pl.BlockSpec((1, EB), lambda i: (0, i))
+
+
+def wig_spec():
+    return pl.BlockSpec((235, EB), lambda i: (0, i))
+
+
+def rotate_call(z_s, edge_count, pair, dst, scale, wigner):
     slots = dst.shape[1]
-    any_spec = pl.BlockSpec(memory_space=pl.ANY)
-    row_spec = pl.BlockSpec((1, EB), lambda i: (0, i))
-    wig_spec = pl.BlockSpec((235, EB), lambda i: (0, i))
+    return pl.pallas_call(
+        rotate_kernel,
+        out_shape=sds((464, slots), BF),
+        grid=(slots // EB,),
+        in_specs=[smem(), smem(), whole((800, 128)), row_spec(), row_spec(), wig_spec()],
+        out_specs=pl.BlockSpec((464, EB), lambda i: (0, i)),
+        scratch_shapes=[pltpu.VMEM((2, 400, EB), F32), pltpu.VMEM((235, EB), F32)],
+        compiler_params=params(),
+        name="rotate",
+    )(z_s, edge_count, pair, dst, scale, wigner)
+
+
+def edge_call(z_s, edge_count, egs, pair, dst, src, scale, wigner, x_own, x_sib, weights):
+    slots = dst.shape[1]
     x_spec = pl.BlockSpec((256, EB), lambda i: (0, i))
     return pl.pallas_call(
         edge_kernel,
         out_shape=(sds((1024, 128), BF), sds((624, 128), F32), sds((1648, 128), BF)),
         grid=(slots // EB,),
         in_specs=[smem(), smem()]
-        + [any_spec] * 5
-        + [row_spec, row_spec, row_spec, wig_spec, x_spec, x_spec]
+        + [pl.BlockSpec((464, EB), lambda i: (0, i))] * 3
+        + [whole((800, 128)), row_spec(), row_spec(), row_spec(), wig_spec(), x_spec, x_spec]
         + [whole((112, 512)), whole((192, 768)), whole((160, 640))],
         out_specs=(whole((1024, 128)), whole((624, 128)), whole((1648, 128))),
         scratch_shapes=[
-            pltpu.VMEM((8, 400, 128), BF),
-            pltpu.VMEM((2, 2, 400, EB), F32),
+            pltpu.VMEM((2, 400, EB), F32),
             pltpu.VMEM((235, EB), F32),
             pltpu.VMEM((235, EB), F32),
             pltpu.VMEM((1856, EB), BF),
@@ -355,11 +392,30 @@
             pltpu.VMEM((784, EB), BF),
             pltpu.VMEM((784, LANES), F32),
             pltpu.VMEM((208, 2 * LANES), F32),
-            pltpu.SemaphoreType.DMA((8,)),
         ],
-        compiler_params=pltpu.CompilerParams(vmem_limit_bytes=EDGE_VMEM),
+        compiler_params=params(),
         name="edge",
-    )(z_s, edge_count, *blocks, dst, src, scale, wigner, x_own, x_sib, *weights)
+    )(z_s, edge_count, *egs, pair, dst, src, scale, wigner, x_own, x_sib, *weights)
+
+
+def finish_kernel(mine_ref, got_ref, zero_ref, one_ref, two_ref):
+    total = mine_ref[...] + got_ref[...].astype(F32)
+
+    def moved(lane):
+        return total if lane == 0 else pltpu.roll(total, LANES - lane, 1)
+
+    for lp in range(7):
+        even, odd = moved(lp * 8), moved(64 + lp * 8)
+        for n, l in enumerate(ZORD):
+            source, row = (even, n * 4) if n < 4 else (odd, (n - 4) * 4)
+            zero_ref[lp, l] = source[row : row + 4, 0:8]
+    for ref, count, first, stride in ((one_ref, 6, 4, 48), (two_ref, 5, 10, 48)):
+        for w in range(2):
+            for lp in range(count):
+                source = moved(w * stride + lp * 8)
+                for l in range(count):
+                    row = (first + l) * 4
+                    ref[w, lp, l] = source[row : row + 4, 0:8]
 
 
 def join_kernel(h_ref, own_ref, rim_ref, out_ref):
@@ -436,7 +492,7 @@
         in_specs=[whole((n, 8, 128)) for n in (49, 49, 49, 72, 50)],
         out_specs=(whole((400, 128)), whole((400, 128)), whole((224, 128)), whole((1376, 128))),
         grid=(1,),
-        compiler_params=pltpu.CompilerParams(vmem_limit_bytes=EDGE_VMEM),
+        compiler_params=pltpu.CompilerParams(vmem_limit_bytes=PACK_VMEM),
         cost_estimate=light(),
         name="pack",
     )(node_x, cotangent, *w_tiles)
@@ -459,29 +515,33 @@
     two, near = lax.optimization_barrier((two, near))
     b26 = across(two, 4)
     far = shift(lax.dynamic_slice_in_dim(near, 112 * high, 112, 0), True)
-    b15 = across(two, 2)
-    far, b15 = lax.optimization_barrier((far, b15))
-
-    row_spec = pl.BlockSpec((1, EB), lambda i: (0, i))
-    wig_spec = pl.BlockSpec((235, EB), lambda i: (0, i))
+
+    def rotated(pair):
+        return rotate_call(z_s, edge_count, pair, dst, scale, wigner)
+
+    eg0 = rotated(two)
+
     x_spec = pl.BlockSpec((256, EB), lambda i: (0, i))
     x_own = pl.pallas_call(
         edge_in_kernel,
         out_shape=sds((256, slots), BF),
         grid=(steps,),
-        in_specs=[smem(), whole((400, 128)), whole((224, 128)), whole((112, 128)), row_spec, wig_spec],
+        in_specs=[smem(), whole((400, 128)), whole((224, 128)), whole((112, 128)), row_spec(), wig_spec()],
         out_specs=x_spec,
         scratch_shapes=[pltpu.VMEM((235, EB), F32), pltpu.VMEM((400, EB), F32)],
         compiler_params=params(),
         cost_estimate=light(),
         name="edge_in",
     )(h_s, node, near, far, src, wigner)
-    x_own, b26 = lax.optimization_barrier((x_own, b26))
+    again, b26, x_own, eg0, wz, wo, wt = lax.optimization_barrier((two, b26, x_own, eg0, wz, wo, wt))
+    b15 = across(again, 2)
     b37 = across(b26, 2)
+    eg2 = rotated(b26)
+    eg1 = rotated(b15)
     x_sib = across(x_own, 1)
 
     s_own, g_own, to_sib = edge_call(
-        z_s, edge_count, (b0, b4, b26, b15, b37), dst, src, scale, wigner, x_own, x_sib, (wz, wo, wt)
+        z_s, edge_count, (eg0, eg2, eg1), b37, dst, src, scale, wigner, x_own, x_sib, (wz, wo, wt)
     )
 
     got = across(to_sib, 1)
@@ -500,27 +560,33 @@
     near_rim = jnp.where(high == 0, right, left)
     far_rim = shift(jnp.where(high == 0, left, right), False)
 
-    crossed = cross(jnp.concatenate([near_rim, far_rim, other.astype(BF).reshape(64, 128)], axis=0))
-    final = mine + crossed[224:].astype(F32).reshape(16, 4, 128)
+    crossed = cross(jnp.concatenate([near_rim, far_rim], axis=0))
+    crossed, mine = lax.optimization_barrier((crossed, mine))
+    got_half = cross(other.astype(BF).reshape(64, 128))
     grad_x = pl.pallas_call(
         join_kernel,
         out_shape=sds((49, 8, 128), F32),
         grid=(1,),
-        in_specs=[smem(), whole((400, 128)), whole((288, 128))],
+        in_specs=[smem(), whole((400, 128)), whole((224, 128))],
         out_specs=whole((49, 8, 128)),
         compiler_params=params(),
         cost_estimate=light(),
         name="join",
     )(h_s, g_all[:400], crossed)
 
-    zero_rows = [None] * 7
-    for n, degree in enumerate(ZORD):
-        zero_rows[degree] = final[n, :, 0:56] if n < 4 else final[n - 4, :, 64:120]
-    grad_zero = jnp.stack(zero_rows).reshape(7, 4, 7, 8).transpose(2, 3, 0, 1)
-    grad_one = final[4:10, :, 0:96].reshape(6, 4, 2, 6, 8).transpose(2, 3, 4, 0, 1)
-    two = jnp.stack([final[10:15, :, 0:40], final[10:15, :, 48:88]], axis=2)
-    grad_two = two.reshape(5, 4, 2, 5, 8).transpose(2, 3, 4, 0, 1)
-
+    zero, one, second = pl.pallas_call(
+        finish_kernel,
+        out_shape=(sds((7, 7, 4, 8), F32), sds((2, 6, 6, 4, 8), F32), sds((2, 5, 5, 4, 8), F32)),
+        grid=(1,),
+        in_specs=[whole((64, 128)), whole((64, 128))],
+        out_specs=(whole((7, 7, 4, 8)), whole((2, 6, 6, 4, 8)), whole((2, 5, 5, 4, 8))),
+        compiler_params=params(),
+        cost_estimate=light(),
+        name="finish",
+    )(mine.reshape(64, 128), got_half)
+    grad_zero = zero.transpose(0, 3, 1, 2)
+    grad_one = one.transpose(0, 1, 4, 2, 3)
+    grad_two = second.transpose(0, 1, 4, 2, 3)
     return grad_x, grad_zero, grad_one, grad_two
 
 

time: 125 us -> 118 us (0.944)
  the two profiles are of different devices: /device:TPU:4 before, /device:TPU:128 now
where the time goes in v4:
time: 118 us; the launch traced here: 117 us
  starting transfers between devices  62.8 us (53%)
  waiting for transfers between devices  29.8 us (25%)
  Pallas kernels  20.1 us (17%)
  other arithmetic  1.97 us (2%)
  between operations  1.62 us (1%)
    ppermute x3, starting transfers between devices, cross(): return lax.ppermute(x, 'brick', [(i, i ^ 1) for i in range(32)])  27.7 us
    ppermute x3, waiting for transfers between devices, cross(): return lax.ppermute(x, 'brick', [(i, i ^ 1) for i in range(32)])  20.2 us
    ppermute x7, starting transfers between devices, across(): return lax.ppermute(x, 'chan', [(i, i ^ mask) for i in range(16)])  19.5 us
    ppermute x2, starting transfers between devices, shift(): return lax.ppermute(x, 'brick', route)  10.6 us
    pallas_call x1, Pallas kernels, edge_call(): pl.pallas_call(edge_kernel, out_shape=(sds((1024, 128), BF), sds((624, 12...  7.66 us
    pallas_call x3, Pallas kernels, rotate_call(): pl.pallas_call(rotate_kernel, out_shape=sds((464, slots), BF), grid=(slot...  5.88 us
    ppermute x7, waiting for transfers between devices, across(): return lax.ppermute(x, 'chan', [(i, i ^ mask) for i in range(16)])  5.69 us
    all_to_all x1, starting transfers between devices, body(): pieces = lax.all_to_all(send, 'brick', 0, 0, axis_index_groups=groups)  5.09 us
  transfers between devices with their start and end apart: 13, of which 8 were waited for; matrix products, arithmetic and copies ran while one was open for 1% of the time, Pallas kernels for 8%

profile of v4, /device:TPU:128, one launch (start us, length us, event | category | flops | bytes accessed | tf_op | source)
XLA Modules:
  0.0 117.0 jit_solution(12502851390149486576)
XLA Ops:
  0.6 2.3 %pack.1 = (bf16[400,128]{1,0:T(8,128)(2,1)}, bf16[400,128]{1,0:T(8,128)(2,1)}, bf16[224,128]{1,0:T(8,128)(2,1)}, bf16[1376,128]{1,0:T(8,128)(2,1)}) custom-call(bf16[49,8,128]{2,1,0:T(8,128)(2,1)} %node_ref.1, bf16[49,8,128]{2,1,0:T(8,128)(2,1)} %cot_ref.1, bf16[49,8,128]{2,1,0:T(8,128)(2,1)} %bitcast.42, bf16[72,8,128]{2,1,0:T(8,128)(2,1)} %bitcast.40, ...), custom_call_target="tpu_custom_call" | custom-call | flops 1 | bytes 1 | tf_op jit(solution)/shard_map/pack/pallas_call | solution.py:489
  2.9 6.0 %collective-permute-start = (bf16[400,128]{1,0:T(8,128)(2,1)}, bf16[400,128]{1,0:T(8,128)(2,1)S(1)}, u32[]{:S(2)}, u32[]{:S(2)}) collective-permute-start(bf16[400,128]{1,0:T(8,128)(2,1)} %get-tuple-element.28), channel_id=1, source_target_pairs={{0,8},{1,9},{2,10},{3,11},{4,12},{5,13},{6,14},{7,15},{8,0},{9,1},... | collective-permute-start | bytes 307208 | tf_op jit(solution)/shard_map/ppermute | solution.py:475
  8.9 1.9 %collective-permute-start.4 = (bf16[1376,128]{1,0:T(8,128)(2,1)}, bf16[1376,128]{1,0:T(8,128)(2,1)S(1)}, u32[]{:S(2)}, u32[]{:S(2)}) collective-permute-start(bf16[1376,128]{1,0:T(8,128)(2,1)} %get-tuple-element.33.own_ref), channel_id=1, source_target_pairs={{0,1},{1,0},{2,3},{3,2},{4,5},{5,4},{6,7},{7,6},{8,9},{9,8},{10,11... | collective-permute-start | bytes 1056776 | tf_op jit(solution)/shard_map/ppermute | solution.py:475
  10.9 10.3 %collective-permute-start.1 = (bf16[224,128]{1,0:T(8,128)(2,1)}, bf16[224,128]{1,0:T(8,128)(2,1)S(1)}, u32[]{:S(2)}, u32[]{:S(2)}) collective-permute-start(bf16[224,128]{1,0:T(8,128)(2,1)} %get-tuple-element.29), channel_id=1, source_target_pairs={{0,16},{16,0},{32,48},{48,32},{64,80},{80,64},{96,112},{112,96},{1... | collective-permute-start | bytes 172040 | tf_op jit(solution)/shard_map/ppermute | solution.py:478
  22.1 8.8 %collective-permute-done.1.near_ref = bf16[224,128]{1,0:T(8,128)(2,1)S(1)} collective-permute-done((bf16[224,128]{1,0:T(8,128)(2,1)}, bf16[224,128]{1,0:T(8,128)(2,1)S(1)}, u32[]{:S(2)}, u32[]{:S(2)}) %collective-permute-start.1) | collective-permute-done | bytes 57376 | tf_op jit(solution)/shard_map/ppermute | solution.py:478
  30.9 1.9 %collective-permute-start.2 = (bf16[800,128]{1,0:T(8,128)(2,1)S(1)}, bf16[800,128]{1,0:T(8,128)(2,1)S(1)}, u32[]{:S(2)}, u32[]{:S(2)}) collective-permute-start(bf16[800,128]{1,0:T(8,128)(2,1)S(1)} %pad_maximum_fusion.1.pair_ref), channel_id=1, source_target_pairs={{0,4},{1,5},{2,6},{3,7},{4,0},{5,1},{6,2},{7,3},{8,12},{9,13},{10,... | collective-permute-start | bytes 614408 | tf_op jit(solution)/shard_map/ppermute | solution.py:475
  32.9 3.4 %collective-permute-start.3 = (bf16[112,128]{1,0:T(8,128)(2,1)S(1)}, bf16[112,128]{1,0:T(8,128)(2,1)S(1)}, u32[]{:S(2)}, u32[]{:S(2)}) collective-permute-start(bf16[112,128]{1,0:T(8,128)(2,1)S(1)} %constant_dynamic-slice_fusion), channel_id=1, source_target_pairs={{0,32},{16,496},{32,64},{48,16},{64,96},{80,48},{96,128},{112,80},... | collective-permute-start | bytes 86024 | tf_op jit(solution)/shard_map/ppermute | solution.py:482
  37.7 1.9 %rotate.3.eg0 = bf16[464,1024]{1,0:T(8,128)(2,1)S(1)} custom-call(s32[1]{0:T(128)} %bitcast.1.z_ref, s32[1]{0:T(128)S(6)} %copy.14.count_ref, bf16[800,128]{1,0:T(8,128)(2,1)S(1)} %pad_maximum_fusion.1.pair_ref, s32[1,1024]{1,0:T(1,128)S(1)} %bitcast.26, f32[1,1024]{1,0:T(1,128)S(1)} %bitcast.30, bf16[235,1024]{1,0:T(8,128)(2,1)S(1)} %copy-done), custom_call_target="tpu_custom_call" | custom-call | tf_op jit(solution)/shard_map/rotate/pallas_call | solution.py:361
  39.6 2.3 %collective-permute-done.3.far_ref = bf16[112,128]{1,0:T(8,128)(2,1)S(1)} collective-permute-done((bf16[112,128]{1,0:T(8,128)(2,1)S(1)}, bf16[112,128]{1,0:T(8,128)(2,1)S(1)}, u32[]{:S(2)}, u32[]{:S(2)}) %collective-permute-start.3) | collective-permute-done | bytes 28704 | tf_op jit(solution)/shard_map/ppermute | solution.py:482
  42.0 1.9 %edge_in.1.xo_ref = bf16[256,1024]{1,0:T(8,128)(2,1)S(1)} custom-call(s32[1]{0:T(128)} %bitcast.h_ref, bf16[400,128]{1,0:T(8,128)(2,1)S(1)} %copy-done.2, bf16[224,128]{1,0:T(8,128)(2,1)S(1)} %collective-permute-done.1.near_ref, bf16[112,128]{1,0:T(8,128)(2,1)S(1)} %collective-permute-done.3.far_ref, s32[1,1024]{1,0:T(1,128)S(1)} %bitcast.34, ...), custom_call_target="tpu_custom_call" | custom-call | flops 1 | bytes 1 | tf_op jit(solution)/shard_map/edge_in/pallas_call | solution.py:525
  44.5 1.9 %collective-permute-start.7 = (bf16[256,1024]{1,0:T(8,128)(2,1)S(1)}, bf16[256,1024]{1,0:T(8,128)(2,1)S(1)}, u32[]{:S(2)}, u32[]{:S(2)}) collective-permute-start(bf16[256,1024]{1,0:T(8,128)(2,1)S(1)} %edge_in.1.xo_ref), channel_id=1, source_target_pairs={{0,1},{1,0},{2,3},{3,2},{4,5},{5,4},{6,7},{7,6},{8,9},{9,8},{10,11... | collective-permute-start | bytes 1572872 | tf_op jit(solution)/shard_map/ppermute | solution.py:475
  46.4 1.9 %collective-permute-start.5 = (bf16[800,128]{1,0:T(8,128)(2,1)S(1)}, bf16[800,128]{1,0:T(8,128)(2,1)S(1)}, u32[]{:S(2)}, u32[]{:S(2)}) collective-permute-start(bf16[800,128]{1,0:T(8,128)(2,1)S(1)} %pad_maximum_fusion.1.pair_ref), channel_id=1, source_target_pairs={{0,2},{1,3},{2,0},{3,1},{4,6},{5,7},{6,4},{7,5},{8,10},{9,11},{10,... | collective-permute-start | bytes 614408 | tf_op jit(solution)/shard_map/ppermute | solution.py:475
  48.3 3.9 %collective-permute-start.6 = (bf16[800,128]{1,0:T(8,128)(2,1)S(1)}, bf16[800,128]{1,0:T(8,128)(2,1)S(1)}, u32[]{:S(2)}, u32[]{:S(2)}) collective-permute-start(bf16[800,128]{1,0:T(8,128)(2,1)S(1)} %collective-permute-done.2.pair_ref), channel_id=1, source_target_pairs={{0,2},{1,3},{2,0},{3,1},{4,6},{5,7},{6,4},{7,5},{8,10},{9,11},{10,... | collective-permute-start | bytes 614408 | tf_op jit(solution)/shard_map/ppermute | solution.py:475
  52.2 2.0 %rotate.4.eg2 = bf16[464,1024]{1,0:T(8,128)(2,1)S(1)} custom-call(s32[1]{0:T(128)} %bitcast.1.z_ref, s32[1]{0:T(128)S(6)} %copy.14.count_ref, bf16[800,128]{1,0:T(8,128)(2,1)S(1)} %collective-permute-done.2.pair_ref, s32[1,1024]{1,0:T(1,128)S(1)} %bitcast.27, f32[1,1024]{1,0:T(1,128)S(1)} %bitcast.31, bf16[235,1024]{1,0:T(8,128)(2,1)S(1)} %copy-done), custom_call_target="tpu_custom_call" | custom-call | tf_op jit(solution)/shard_map/rotate/pallas_call | solution.py:361
  54.2 1.9 %collective-permute-done.5.pair_ref = bf16[800,128]{1,0:T(8,128)(2,1)S(1)} collective-permute-done((bf16[800,128]{1,0:T(8,128)(2,1)S(1)}, bf16[800,128]{1,0:T(8,128)(2,1)S(1)}, u32[]{:S(2)}, u32[]{:S(2)}) %collective-permute-start.5) | collective-permute-done | bytes 204832 | tf_op jit(solution)/shard_map/ppermute | solution.py:475
  56.2 1.9 %rotate.5.eg1 = bf16[464,1024]{1,0:T(8,128)(2,1)S(1)} custom-call(s32[1]{0:T(128)} %bitcast.1.z_ref, s32[1]{0:T(128)S(6)} %copy.14.count_ref, bf16[800,128]{1,0:T(8,128)(2,1)S(1)} %collective-permute-done.5.pair_ref, s32[1,1024]{1,0:T(1,128)S(1)} %bitcast.28, f32[1,1024]{1,0:T(1,128)S(1)} %bitcast.32, bf16[235,1024]{1,0:T(8,128)(2,1)S(1)} %copy-done), custom_call_target="tpu_custom_call" | custom-call | tf_op jit(solution)/shard_map/rotate/pallas_call | solution.py:361
  58.1 2.0 %collective-permute-done.6.pair_ref = bf16[800,128]{1,0:T(8,128)(2,1)S(1)} collective-permute-done((bf16[800,128]{1,0:T(8,128)(2,1)S(1)}, bf16[800,128]{1,0:T(8,128)(2,1)S(1)}, u32[]{:S(2)}, u32[]{:S(2)}) %collective-permute-start.6) | collective-permute-done | bytes 204832 | tf_op jit(solution)/shard_map/ppermute | solution.py:475
  60.1 7.7 %edge.1 = (bf16[1024,128]{1,0:T(8,128)(2,1)S(1)}, f32[624,128]{1,0:T(8,128)S(1)}, bf16[1648,128]{1,0:T(8,128)(2,1)S(1)}) custom-call(s32[1]{0:T(128)} %bitcast.1.z_ref, s32[1]{0:T(128)S(6)} %copy.14.count_ref, bf16[464,1024]{1,0:T(8,128)(2,1)S(1)} %rotate.3.eg0, bf16[464,1024]{1,0:T(8,128)(2,1)S(1)} %rotate.4.eg2, bf16[464,1024]{1,0:T(8,128)(2,1)S(1)} %rotate.5.eg1, ...), custom_call_target="tpu_custom_call" | custom-call | tf_op jit(solution)/shard_map/edge/pallas_call | solution.py:376
  67.8 1.9 %collective-permute-start.8 = (bf16[1648,128]{1,0:T(8,128)(2,1)S(1)}, bf16[1648,128]{1,0:T(8,128)(2,1)S(1)}, u32[]{:S(2)}, u32[]{:S(2)}) collective-permute-start(bf16[1648,128]{1,0:T(8,128)(2,1)S(1)} %get-tuple-element.45), channel_id=1, source_target_pairs={{0,1},{1,0},{2,3},{3,2},{4,5},{5,4},{6,7},{7,6},{8,9},{9,8},{10,11... | collective-permute-start | bytes 1265672 | tf_op jit(solution)/shard_map/ppermute | solution.py:475
  72.4 5.1 %all-to-all-start = ((bf16[16,128,128]{2,1,0:T(8,128)(2,1)}), bf16[16,128,128]{2,1,0:T(8,128)(2,1)S(1)}, u32[]{:S(2)}, u32[]{:S(2)}) async-start(bf16[16,128,128]{2,1,0:T(8,128)(2,1)} %pad_maximum_fusion), calls=%async_computation | async-start | bytes 1048576 | tf_op jit(solution)/shard_map/all_to_all | solution.py:553
  77.5 7.2 %collective-permute-start.9 = (bf16[112,128]{1,0:T(8,128)(2,1)S(1)}, bf16[112,128]{1,0:T(8,128)(2,1)S(1)}, u32[]{:S(2)}, u32[]{:S(2)}) collective-permute-start(bf16[112,128]{1,0:T(8,128)(2,1)S(1)} %get-tuple-element.57), channel_id=1, source_target_pairs={{0,480},{16,48},{32,0},{48,80},{64,32},{80,112},{96,64},{112,144},... | collective-permute-start | bytes 86024 | tf_op jit(solution)/shard_map/ppermute | solution.py:482
  86.3 15.4 %collective-permute-start.10 = (bf16[224,128]{1,0:T(8,128)(2,1)S(1)}, bf16[224,128]{1,0:T(8,128)(2,1)S(1)}, u32[]{:S(2)}, u32[]{:S(2)}) collective-permute-start(bf16[224,128]{1,0:T(8,128)(2,1)S(1)} %pad_maximum_fusion.2), channel_id=1, source_target_pairs={{0,16},{16,0},{32,48},{48,32},{64,80},{80,64},{96,112},{112,96},{1... | collective-permute-start | bytes 172040 | tf_op jit(solution)/shard_map/ppermute | solution.py:478
  101.8 1.9 %collective-permute-start.11 = (bf16[64,128]{1,0:T(8,128)(2,1)S(1)}, bf16[64,128]{1,0:T(8,128)(2,1)S(1)}, u32[]{:S(2)}, u32[]{:S(2)}) collective-permute-start(bf16[64,128]{1,0:T(8,128)(2,1)S(1)} %bitcast.43), channel_id=1, source_target_pairs={{0,16},{16,0},{32,48},{48,32},{64,80},{80,64},{96,112},{112,96},{1... | collective-permute-start | bytes 49160 | tf_op jit(solution)/shard_map/ppermute | solution.py:478
  105.6 10.6 %collective-permute-done.11.got_ref = bf16[64,128]{1,0:T(8,128)(2,1)S(1)} collective-permute-done((bf16[64,128]{1,0:T(8,128)(2,1)S(1)}, bf16[64,128]{1,0:T(8,128)(2,1)S(1)}, u32[]{:S(2)}, u32[]{:S(2)}) %collective-permute-start.11) | collective-permute-done | bytes 16416 | tf_op jit(solution)/shard_map/ppermute | solution.py:478
  (34 shorter events, 9.2 us)
Async XLA Ops:
  0.6 36.3 %copy-start = (bf16[235,1024]{1,0:T(8,128)(2,1)S(1)}, bf16[235,1024]{1,0:T(8,128)(2,1)}, u32[]{:S(2)}) copy-start(bf16[235,1024]{1,0:T(8,128)(2,1)} %wig_ref.9) | copy-start | bytes 1443844
  2.9 18.3 %collective-permute-start = (bf16[400,128]{1,0:T(8,128)(2,1)}, bf16[400,128]{1,0:T(8,128)(2,1)S(1)}, u32[]{:S(2)}, u32[]{:S(2)}) collective-permute-start(bf16[400,128]{1,0:T(8,128)(2,1)} %get-tuple-element.28), channel_id=1, source_target_pairs={{0,8},{1,9},{2,10},{3,11},{4,12},{5,13},{6,14},{7,15},{8,0},{9,1},... | collective-permute-start | bytes 307208 | tf_op jit(solution)/shard_map/ppermute | solution.py:475
  8.9 34.9 %collective-permute-start.4 = (bf16[1376,128]{1,0:T(8,128)(2,1)}, bf16[1376,128]{1,0:T(8,128)(2,1)S(1)}, u32[]{:S(2)}, u32[]{:S(2)}) collective-permute-start(bf16[1376,128]{1,0:T(8,128)(2,1)} %get-tuple-element.33.own_ref), channel_id=1, source_target_pairs={{0,1},{1,0},{2,3},{3,2},{4,5},{5,4},{6,7},{7,6},{8,9},{9,8},{10,11... | collective-permute-start | bytes 1056776 | tf_op jit(solution)/shard_map/ppermute | solution.py:475
  10.9 20.1 %collective-permute-start.1 = (bf16[224,128]{1,0:T(8,128)(2,1)}, bf16[224,128]{1,0:T(8,128)(2,1)S(1)}, u32[]{:S(2)}, u32[]{:S(2)}) collective-permute-start(bf16[224,128]{1,0:T(8,128)(2,1)} %get-tuple-element.29), channel_id=1, source_target_pairs={{0,16},{16,0},{32,48},{48,32},{64,80},{80,64},{96,112},{112,96},{1... | collective-permute-start | bytes 172040 | tf_op jit(solution)/shard_map/ppermute | solution.py:478
  30.9 13.5 %collective-permute-start.2 = (bf16[800,128]{1,0:T(8,128)(2,1)S(1)}, bf16[800,128]{1,0:T(8,128)(2,1)S(1)}, u32[]{:S(2)}, u32[]{:S(2)}) collective-permute-start(bf16[800,128]{1,0:T(8,128)(2,1)S(1)} %pad_maximum_fusion.1.pair_ref), channel_id=1, source_target_pairs={{0,4},{1,5},{2,6},{3,7},{4,0},{5,1},{6,2},{7,3},{8,12},{9,13},{10,... | collective-permute-start | bytes 614408 | tf_op jit(solution)/shard_map/ppermute | solution.py:475
  32.9 9.1 %collective-permute-start.3 = (bf16[112,128]{1,0:T(8,128)(2,1)S(1)}, bf16[112,128]{1,0:T(8,128)(2,1)S(1)}, u32[]{:S(2)}, u32[]{:S(2)}) collective-permute-start(bf16[112,128]{1,0:T(8,128)(2,1)S(1)} %constant_dynamic-slice_fusion), channel_id=1, source_target_pairs={{0,32},{16,496},{32,64},{48,16},{64,96},{80,48},{96,128},{112,80},... | collective-permute-start | bytes 86024 | tf_op jit(solution)/shard_map/ppermute | solution.py:482
  36.9 0.7 copy-start.4
  37.0 0.7 copy-start.3
  37.7 4.3 %copy-start.2 = (bf16[400,128]{1,0:T(8,128)(2,1)S(1)}, bf16[400,128]{1,0:T(8,128)(2,1)}, u32[]{:S(2)}) copy-start(bf16[400,128]{1,0:T(8,128)(2,1)} %get-tuple-element.31.node_ref) | copy-start | bytes 307204
  39.6 2.4 %copy-start.5 = (s32[1024]{0:T(1024)S(1)}, s32[1024]{0:T(1024)}, u32[]{:S(2)}) copy-start(s32[1024]{0:T(1024)} %param.13) | copy-start | bytes 12292
  42.0 1.9 %copy-start.1 = (bf16[1376,128]{1,0:T(8,128)(2,1)S(1)}, bf16[1376,128]{1,0:T(8,128)(2,1)}, u32[]{:S(2)}) copy-start(bf16[1376,128]{1,0:T(8,128)(2,1)} %get-tuple-element.33.own_ref) | copy-start | bytes 1056772
  44.5 15.7 %collective-permute-start.7 = (bf16[256,1024]{1,0:T(8,128)(2,1)S(1)}, bf16[256,1024]{1,0:T(8,128)(2,1)S(1)}, u32[]{:S(2)}, u32[]{:S(2)}) collective-permute-start(bf16[256,1024]{1,0:T(8,128)(2,1)S(1)} %edge_in.1.xo_ref), channel_id=1, source_target_pairs={{0,1},{1,0},{2,3},{3,2},{4,5},{5,4},{6,7},{7,6},{8,9},{9,8},{10,11... | collective-permute-start | bytes 1572872 | tf_op jit(solution)/shard_map/ppermute | solution.py:475
  46.4 9.8 %collective-permute-start.5 = (bf16[800,128]{1,0:T(8,128)(2,1)S(1)}, bf16[800,128]{1,0:T(8,128)(2,1)S(1)}, u32[]{:S(2)}, u32[]{:S(2)}) collective-permute-start(bf16[800,128]{1,0:T(8,128)(2,1)S(1)} %pad_maximum_fusion.1.pair_ref), channel_id=1, source_target_pairs={{0,2},{1,3},{2,0},{3,1},{4,6},{5,7},{6,4},{7,5},{8,10},{9,11},{10,... | collective-permute-start | bytes 614408 | tf_op jit(solution)/shard_map/ppermute | solution.py:475
  48.3 11.8 %collective-permute-start.6 = (bf16[800,128]{1,0:T(8,128)(2,1)S(1)}, bf16[800,128]{1,0:T(8,128)(2,1)S(1)}, u32[]{:S(2)}, u32[]{:S(2)}) collective-permute-start(bf16[800,128]{1,0:T(8,128)(2,1)S(1)} %collective-permute-done.2.pair_ref), channel_id=1, source_target_pairs={{0,2},{1,3},{2,0},{3,1},{4,6},{5,7},{6,4},{7,5},{8,10},{9,11},{10,... | collective-permute-start | bytes 614408 | tf_op jit(solution)/shard_map/ppermute | solution.py:475
  67.8 3.7 %collective-permute-start.8 = (bf16[1648,128]{1,0:T(8,128)(2,1)S(1)}, bf16[1648,128]{1,0:T(8,128)(2,1)S(1)}, u32[]{:S(2)}, u32[]{:S(2)}) collective-permute-start(bf16[1648,128]{1,0:T(8,128)(2,1)S(1)} %get-tuple-element.45), channel_id=1, source_target_pairs={{0,1},{1,0},{2,3},{3,2},{4,5},{5,4},{6,7},{7,6},{8,9},{9,8},{10,11... | collective-permute-start | bytes 1265672 | tf_op jit(solution)/shard_map/ppermute | solution.py:475
  72.4 29.3 %all-to-all-start = ((bf16[16,128,128]{2,1,0:T(8,128)(2,1)}), bf16[16,128,128]{2,1,0:T(8,128)(2,1)S(1)}, u32[]{:S(2)}, u32[]{:S(2)}) async-start(bf16[16,128,128]{2,1,0:T(8,128)(2,1)} %pad_maximum_fusion), calls=%async_computation | async-start | bytes 1048576 | tf_op jit(solution)/shard_map/all_to_all | solution.py:553
  77.5 8.7 %collective-permute-start.9 = (bf16[112,128]{1,0:T(8,128)(2,1)S(1)}, bf16[112,128]{1,0:T(8,128)(2,1)S(1)}, u32[]{:S(2)}, u32[]{:S(2)}) collective-permute-start(bf16[112,128]{1,0:T(8,128)(2,1)S(1)} %get-tuple-element.57), channel_id=1, source_target_pairs={{0,480},{16,48},{32,0},{48,80},{64,32},{80,112},{96,64},{112,144},... | collective-permute-start | bytes 86024 | tf_op jit(solution)/shard_map/ppermute | solution.py:482
  86.3 18.4 %collective-permute-start.10 = (bf16[224,128]{1,0:T(8,128)(2,1)S(1)}, bf16[224,128]{1,0:T(8,128)(2,1)S(1)}, u32[]{:S(2)}, u32[]{:S(2)}) collective-permute-start(bf16[224,128]{1,0:T(8,128)(2,1)S(1)} %pad_maximum_fusion.2), channel_id=1, source_target_pairs={{0,16},{16,0},{32,48},{48,32},{64,80},{80,64},{96,112},{112,96},{1... | collective-permute-start | bytes 172040 | tf_op jit(solution)/shard_map/ppermute | solution.py:478
  101.8 14.3 %collective-permute-start.11 = (bf16[64,128]{1,0:T(8,128)(2,1)S(1)}, bf16[64,128]{1,0:T(8,128)(2,1)S(1)}, u32[]{:S(2)}, u32[]{:S(2)}) collective-permute-start(bf16[64,128]{1,0:T(8,128)(2,1)S(1)} %bitcast.43), channel_id=1, source_target_pairs={{0,16},{16,0},{32,48},{48,32},{64,80},{80,64},{96,112},{112,96},{1... | collective-permute-start | bytes 49160 | tf_op jit(solution)/shard_map/ppermute | solution.py:478

commit v5 on v4

--- a/solution.py
+++ b/solution.py
@@ -399,7 +399,7 @@
 
 
 def finish_kernel(mine_ref, got_ref, zero_ref, one_ref, two_ref):
-    total = mine_ref[...] + got_ref[...].astype(F32)
+    total = mine_ref[...] + got_ref[224:288].astype(F32)
 
     def moved(lane):
         return total if lane == 0 else pltpu.roll(total, LANES - lane, 1)
@@ -512,14 +512,18 @@
 
     b4 = across(b0, 8)
     two = jnp.concatenate([b0, b4], axis=0)
-    two, near = lax.optimization_barrier((two, near))
     b26 = across(two, 4)
-    far = shift(lax.dynamic_slice_in_dim(near, 112 * high, 112, 0), True)
 
     def rotated(pair):
         return rotate_call(z_s, edge_count, pair, dst, scale, wigner)
 
     eg0 = rotated(two)
+    again, b26, near, eg0 = lax.optimization_barrier((two, b26, near, eg0))
+    b15 = across(again, 2)
+    b37 = across(b26, 2)
+    eg2 = rotated(b26)
+    eg1 = rotated(b15)
+    far = shift(lax.dynamic_slice_in_dim(near, 112 * high, 112, 0), True)
 
     x_spec = pl.BlockSpec((256, EB), lambda i: (0, i))
     x_own = pl.pallas_call(
@@ -533,11 +537,7 @@
         cost_estimate=light(),
         name="edge_in",
     )(h_s, node, near, far, src, wigner)
-    again, b26, x_own, eg0, wz, wo, wt = lax.optimization_barrier((two, b26, x_own, eg0, wz, wo, wt))
-    b15 = across(again, 2)
-    b37 = across(b26, 2)
-    eg2 = rotated(b26)
-    eg1 = rotated(b15)
+    x_own, b37, eg1, eg2, wz, wo, wt = lax.optimization_barrier((x_own, b37, eg1, eg2, wz, wo, wt))
     x_sib = across(x_own, 1)
 
     s_own, g_own, to_sib = edge_call(
@@ -560,30 +560,28 @@
     near_rim = jnp.where(high == 0, right, left)
     far_rim = shift(jnp.where(high == 0, left, right), False)
 
-    crossed = cross(jnp.concatenate([near_rim, far_rim], axis=0))
-    crossed, mine = lax.optimization_barrier((crossed, mine))
-    got_half = cross(other.astype(BF).reshape(64, 128))
+    crossed = cross(jnp.concatenate([near_rim, far_rim, other.astype(BF).reshape(64, 128)], axis=0))
     grad_x = pl.pallas_call(
         join_kernel,
         out_shape=sds((49, 8, 128), F32),
         grid=(1,),
-        in_specs=[smem(), whole((400, 128)), whole((224, 128))],
+        in_specs=[smem(), whole((624, 128)), whole((288, 128))],
         out_specs=whole((49, 8, 128)),
         compiler_params=params(),
         cost_estimate=light(),
         name="join",
-    )(h_s, g_all[:400], crossed)
+    )(h_s, g_all, crossed)
 
     zero, one, second = pl.pallas_call(
         finish_kernel,
         out_shape=(sds((7, 7, 4, 8), F32), sds((2, 6, 6, 4, 8), F32), sds((2, 5, 5, 4, 8), F32)),
         grid=(1,),
-        in_specs=[whole((64, 128)), whole((64, 128))],
+        in_specs=[whole((64, 128)), whole((288, 128))],
         out_specs=(whole((7, 7, 4, 8)), whole((2, 6, 6, 4, 8)), whole((2, 5, 5, 4, 8))),
         compiler_params=params(),
         cost_estimate=light(),
         name="finish",
-    )(mine.reshape(64, 128), got_half)
+    )(mine.reshape(64, 128), crossed)
     grad_zero = zero.transpose(0, 3, 1, 2)
     grad_one = one.transpose(0, 1, 4, 2, 3)
     grad_two = second.transpose(0, 1, 4, 2, 3)

time: 118 us -> 118 us (level)
  the two profiles are of different devices: /device:TPU:128 before, /device:TPU:32 now
where the time goes in v5:
time: 118 us
  starting transfers between devices  57.8 us (49%)
  waiting for transfers between devices  35.2 us (30%)
  Pallas kernels  20.2 us (17%)
  local copies, waits for them, and re-layouts  1.64 us (1%)
  between operations  1.63 us (1%)
    ppermute x7, starting transfers between devices, across(): return lax.ppermute(x, 'chan', [(i, i ^ mask) for i in range(16)])  26.2 us
    ppermute x2, waiting for transfers between devices, cross(): return lax.ppermute(x, 'brick', [(i, i ^ 1) for i in range(32)])  17.3 us
    ppermute x2, starting transfers between devices, cross(): return lax.ppermute(x, 'brick', [(i, i ^ 1) for i in range(32)])  17.3 us
    ppermute x2, starting transfers between devices, shift(): return lax.ppermute(x, 'brick', route)  10.6 us
    ppermute x7, waiting for transfers between devices, across(): return lax.ppermute(x, 'chan', [(i, i ^ mask) for i in range(16)])  10.1 us
    pallas_call x1, Pallas kernels, edge_call(): pl.pallas_call(edge_kernel, out_shape=(sds((1024, 128), BF), sds((624, 12...  7.68 us
    pallas_call x3, Pallas kernels, rotate_call(): pl.pallas_call(rotate_kernel, out_shape=sds((464, slots), BF), grid=(slot...  5.98 us
    all_to_all x1, waiting for transfers between devices, body(): pieces = lax.all_to_all(send, 'brick', 0, 0, axis_index_groups=groups)  4.14 us
  transfers between devices with their start and end apart: 12, of which 7 were waited for; matrix products, arithmetic and copies ran while one was open for 1% of the time, Pallas kernels for 7%

profile of v5, /device:TPU:32, one launch (start us, length us, event | category | flops | bytes accessed | tf_op | source)
XLA Modules:
  0.0 117.6 jit_solution(256397961650419645)
XLA Ops:
  0.6 2.3 %pack.1 = (bf16[400,128]{1,0:T(8,128)(2,1)}, bf16[400,128]{1,0:T(8,128)(2,1)}, bf16[224,128]{1,0:T(8,128)(2,1)}, bf16[1376,128]{1,0:T(8,128)(2,1)}) custom-call(bf16[49,8,128]{2,1,0:T(8,128)(2,1)} %node_ref.1, bf16[49,8,128]{2,1,0:T(8,128)(2,1)} %cot_ref.1, bf16[49,8,128]{2,1,0:T(8,128)(2,1)} %bitcast.40, bf16[72,8,128]{2,1,0:T(8,128)(2,1)} %bitcast.38, ...), custom_call_target="tpu_custom_call" | custom-call | flops 1 | bytes 1 | tf_op jit(solution)/shard_map/pack/pallas_call | solution.py:489
  2.9 9.2 %collective-permute-start = (bf16[400,128]{1,0:T(8,128)(2,1)}, bf16[400,128]{1,0:T(8,128)(2,1)S(1)}, u32[]{:S(2)}, u32[]{:S(2)}) collective-permute-start(bf16[400,128]{1,0:T(8,128)(2,1)} %get-tuple-element.28), channel_id=1, source_target_pairs={{0,8},{1,9},{2,10},{3,11},{4,12},{5,13},{6,14},{7,15},{8,0},{9,1},... | collective-permute-start | bytes 307208 | tf_op jit(solution)/shard_map/ppermute | solution.py:475
  13.1 6.6 %collective-permute-done = bf16[400,128]{1,0:T(8,128)(2,1)S(1)} collective-permute-done((bf16[400,128]{1,0:T(8,128)(2,1)}, bf16[400,128]{1,0:T(8,128)(2,1)S(1)}, u32[]{:S(2)}, u32[]{:S(2)}) %collective-permute-start) | collective-permute-done | bytes 102432 | tf_op jit(solution)/shard_map/ppermute | solution.py:475
  19.7 5.3 %collective-permute-start.1 = (bf16[800,128]{1,0:T(8,128)(2,1)S(1)}, bf16[800,128]{1,0:T(8,128)(2,1)S(1)}, u32[]{:S(2)}, u32[]{:S(2)}) collective-permute-start(bf16[800,128]{1,0:T(8,128)(2,1)S(1)} %constant_dynamic-update-slice_fusion.pair_ref), channel_id=1, source_target_pairs={{0,4},{1,5},{2,6},{3,7},{4,0},{5,1},{6,2},{7,3},{8,12},{9,13},{10,... | collective-permute-start | bytes 614408 | tf_op jit(solution)/shard_map/ppermute | solution.py:475
  25.0 1.9 %collective-permute-start.6 = (bf16[1376,128]{1,0:T(8,128)(2,1)S(1)}, bf16[1376,128]{1,0:T(8,128)(2,1)S(1)}, u32[]{:S(2)}, u32[]{:S(2)}) collective-permute-start(bf16[1376,128]{1,0:T(8,128)(2,1)S(1)} %copy-done.1), channel_id=1, source_target_pairs={{0,1},{1,0},{2,3},{3,2},{4,5},{5,4},{6,7},{7,6},{8,9},{9,8},{10,11... | collective-permute-start | bytes 1056776 | tf_op jit(solution)/shard_map/ppermute | solution.py:475
  27.0 9.9 %collective-permute-start.2 = (bf16[224,128]{1,0:T(8,128)(2,1)S(1)}, bf16[224,128]{1,0:T(8,128)(2,1)S(1)}, u32[]{:S(2)}, u32[]{:S(2)}) collective-permute-start(bf16[224,128]{1,0:T(8,128)(2,1)S(1)} %copy-done.6), channel_id=1, source_target_pairs={{0,16},{16,0},{32,48},{48,32},{64,80},{80,64},{96,112},{112,96},{1... | collective-permute-start | bytes 172040 | tf_op jit(solution)/shard_map/ppermute | solution.py:478
  38.3 2.0 %rotate.3.eg0 = bf16[464,1024]{1,0:T(8,128)(2,1)S(1)} custom-call(s32[1]{0:T(128)} %bitcast.1.z_ref, s32[1]{0:T(128)S(6)} %copy.15.count_ref, bf16[800,128]{1,0:T(8,128)(2,1)S(1)} %constant_dynamic-update-slice_fusion.pair_ref, s32[1,1024]{1,0:T(1,128)S(1)} %bitcast.24, f32[1,1024]{1,0:T(1,128)S(1)} %bitcast.28, bf16[235,1024]{1,0:T(8,128)(2,1)S(1)} %copy-done), custom_call_target="tpu_custom_call" | custom-call | tf_op jit(solution)/shard_map/rotate/pallas_call | solution.py:361
  40.2 8.8 %collective-permute-done.2.near_ref = bf16[224,128]{1,0:T(8,128)(2,1)S(1)} collective-permute-done((bf16[224,128]{1,0:T(8,128)(2,1)S(1)}, bf16[224,128]{1,0:T(8,128)(2,1)S(1)}, u32[]{:S(2)}, u32[]{:S(2)}) %collective-permute-start.2) | collective-permute-done | bytes 57376 | tf_op jit(solution)/shard_map/ppermute | solution.py:478
  49.0 1.9 %collective-permute-start.5 = (bf16[800,128]{1,0:T(8,128)(2,1)S(1)}, bf16[800,128]{1,0:T(8,128)(2,1)S(1)}, u32[]{:S(2)}, u32[]{:S(2)}) collective-permute-start(bf16[800,128]{1,0:T(8,128)(2,1)S(1)} %constant_dynamic-update-slice_fusion.pair_ref), channel_id=1, source_target_pairs={{0,2},{1,3},{2,0},{3,1},{4,6},{5,7},{6,4},{7,5},{8,10},{9,11},{10,... | collective-permute-start | bytes 614408 | tf_op jit(solution)/shard_map/ppermute | solution.py:475
  51.0 3.9 %collective-permute-start.4 = (bf16[800,128]{1,0:T(8,128)(2,1)S(1)}, bf16[800,128]{1,0:T(8,128)(2,1)S(1)}, u32[]{:S(2)}, u32[]{:S(2)}) collective-permute-start(bf16[800,128]{1,0:T(8,128)(2,1)S(1)} %collective-permute-done.1.pair_ref), channel_id=1, source_target_pairs={{0,2},{1,3},{2,0},{3,1},{4,6},{5,7},{6,4},{7,5},{8,10},{9,11},{10,... | collective-permute-start | bytes 614408 | tf_op jit(solution)/shard_map/ppermute | solution.py:475
  54.9 3.4 %collective-permute-start.3 = (bf16[112,128]{1,0:T(8,128)(2,1)S(1)}, bf16[112,128]{1,0:T(8,128)(2,1)S(1)}, u32[]{:S(2)}, u32[]{:S(2)}) collective-permute-start(bf16[112,128]{1,0:T(8,128)(2,1)S(1)} %constant_dynamic-slice_fusion), channel_id=1, source_target_pairs={{0,32},{16,496},{32,64},{48,16},{64,96},{80,48},{96,128},{112,80},... | collective-permute-start | bytes 86024 | tf_op jit(solution)/shard_map/ppermute | solution.py:482
  58.3 2.0 %rotate.5.eg2 = bf16[464,1024]{1,0:T(8,128)(2,1)S(1)} custom-call(s32[1]{0:T(128)} %bitcast.1.z_ref, s32[1]{0:T(128)S(6)} %copy.15.count_ref, bf16[800,128]{1,0:T(8,128)(2,1)S(1)} %collective-permute-done.1.pair_ref, s32[1,1024]{1,0:T(1,128)S(1)} %bitcast.25, f32[1,1024]{1,0:T(1,128)S(1)} %bitcast.29, bf16[235,1024]{1,0:T(8,128)(2,1)S(1)} %copy-done), custom_call_target="tpu_custom_call" | custom-call | tf_op jit(solution)/shard_map/rotate/pallas_call | solution.py:361
  60.4 3.6 %collective-permute-done.3.far_ref = bf16[112,128]{1,0:T(8,128)(2,1)S(1)} collective-permute-done((bf16[112,128]{1,0:T(8,128)(2,1)S(1)}, bf16[112,128]{1,0:T(8,128)(2,1)S(1)}, u32[]{:S(2)}, u32[]{:S(2)}) %collective-permute-start.3) | collective-permute-done | bytes 28704 | tf_op jit(solution)/shard_map/ppermute | solution.py:482
  64.0 1.9 %edge_in.1.xo_ref = bf16[256,1024]{1,0:T(8,128)(2,1)S(1)} custom-call(s32[1]{0:T(128)} %bitcast.h_ref, bf16[400,128]{1,0:T(8,128)(2,1)S(1)} %copy-done.2, bf16[224,128]{1,0:T(8,128)(2,1)S(1)} %collective-permute-done.2.near_ref, bf16[112,128]{1,0:T(8,128)(2,1)S(1)} %collective-permute-done.3.far_ref, s32[1,1024]{1,0:T(1,128)S(1)} %bitcast.32, ...), custom_call_target="tpu_custom_call" | custom-call | flops 1 | bytes 1 | tf_op jit(solution)/shard_map/edge_in/pallas_call | solution.py:529
  66.5 2.0 %rotate.4.eg1 = bf16[464,1024]{1,0:T(8,128)(2,1)S(1)} custom-call(s32[1]{0:T(128)} %bitcast.1.z_ref, s32[1]{0:T(128)S(6)} %copy.15.count_ref, bf16[800,128]{1,0:T(8,128)(2,1)S(1)} %collective-permute-done.5.pair_ref, s32[1,1024]{1,0:T(1,128)S(1)} %bitcast.26, f32[1,1024]{1,0:T(1,128)S(1)} %bitcast.30, bf16[235,1024]{1,0:T(8,128)(2,1)S(1)} %copy-done), custom_call_target="tpu_custom_call" | custom-call | tf_op jit(solution)/shard_map/rotate/pallas_call | solution.py:361
  68.5 1.9 %collective-permute-start.7 = (bf16[256,1024]{1,0:T(8,128)(2,1)S(1)}, bf16[256,1024]{1,0:T(8,128)(2,1)S(1)}, u32[]{:S(2)}, u32[]{:S(2)}) collective-permute-start(bf16[256,1024]{1,0:T(8,128)(2,1)S(1)} %edge_in.1.xo_ref), channel_id=1, source_target_pairs={{0,1},{1,0},{2,3},{3,2},{4,5},{5,4},{6,7},{7,6},{8,9},{9,8},{10,11... | collective-permute-start | bytes 1572872 | tf_op jit(solution)/shard_map/ppermute | solution.py:475
  70.4 1.9 %collective-permute-done.7.xs_ref = bf16[256,1024]{1,0:T(8,128)(2,1)S(1)} collective-permute-done((bf16[256,1024]{1,0:T(8,128)(2,1)S(1)}, bf16[256,1024]{1,0:T(8,128)(2,1)S(1)}, u32[]{:S(2)}, u32[]{:S(2)}) %collective-permute-start.7) | collective-permute-done | bytes 524320 | tf_op jit(solution)/shard_map/ppermute | solution.py:475
  72.3 7.7 %edge.1 = (bf16[1024,128]{1,0:T(8,128)(2,1)S(1)}, f32[624,128]{1,0:T(8,128)S(1)}, bf16[1648,128]{1,0:T(8,128)(2,1)S(1)}) custom-call(s32[1]{0:T(128)} %bitcast.1.z_ref, s32[1]{0:T(128)S(6)} %copy.15.count_ref, bf16[464,1024]{1,0:T(8,128)(2,1)S(1)} %rotate.3.eg0, bf16[464,1024]{1,0:T(8,128)(2,1)S(1)} %rotate.5.eg2, bf16[464,1024]{1,0:T(8,128)(2,1)S(1)} %rotate.4.eg1, ...), custom_call_target="tpu_custom_call" | custom-call | tf_op jit(solution)/shard_map/edge/pallas_call | solution.py:376
  80.0 2.0 %collective-permute-start.8 = (bf16[1648,128]{1,0:T(8,128)(2,1)S(1)}, bf16[1648,128]{1,0:T(8,128)(2,1)S(1)}, u32[]{:S(2)}, u32[]{:S(2)}) collective-permute-start(bf16[1648,128]{1,0:T(8,128)(2,1)S(1)} %get-tuple-element.47), channel_id=1, source_target_pairs={{0,1},{1,0},{2,3},{3,2},{4,5},{5,4},{6,7},{7,6},{8,9},{9,8},{10,11... | collective-permute-start | bytes 1265672 | tf_op jit(solution)/shard_map/ppermute | solution.py:475
  84.5 3.8 %all-to-all-start = ((bf16[16,128,128]{2,1,0:T(8,128)(2,1)}), bf16[16,128,128]{2,1,0:T(8,128)(2,1)S(1)}, u32[]{:S(2)}, u32[]{:S(2)}) async-start(bf16[16,128,128]{2,1,0:T(8,128)(2,1)} %pad_maximum_fusion), calls=%async_computation | async-start | bytes 1048576 | tf_op jit(solution)/shard_map/all_to_all | solution.py:553
  88.4 7.2 %collective-permute-start.9 = (bf16[112,128]{1,0:T(8,128)(2,1)S(1)}, bf16[112,128]{1,0:T(8,128)(2,1)S(1)}, u32[]{:S(2)}, u32[]{:S(2)}) collective-permute-start(bf16[112,128]{1,0:T(8,128)(2,1)S(1)} %get-tuple-element.57), channel_id=1, source_target_pairs={{0,480},{16,48},{32,0},{48,80},{64,32},{80,112},{96,64},{112,144},... | collective-permute-start | bytes 86024 | tf_op jit(solution)/shard_map/ppermute | solution.py:482
  95.6 4.1 %all-to-all-done = bf16[16,128,128]{2,1,0:T(8,128)(2,1)S(1)} async-done(((bf16[16,128,128]{2,1,0:T(8,128)(2,1)}), bf16[16,128,128]{2,1,0:T(8,128)(2,1)S(1)}, u32[]{:S(2)}, u32[]{:S(2)}) %all-to-all-start) | async-done | bytes 524320 | tf_op jit(solution)/shard_map/all_to_all | solution.py:553
  99.8 7.4 %collective-permute-start.10 = (bf16[288,128]{1,0:T(8,128)(2,1)S(1)}, bf16[288,128]{1,0:T(8,128)(2,1)S(1)}, u32[]{:S(2)}, u32[]{:S(2)}) collective-permute-start(bf16[288,128]{1,0:T(8,128)(2,1)S(1)} %pad_maximum_fusion.1), channel_id=1, source_target_pairs={{0,16},{16,0},{32,48},{48,32},{64,80},{80,64},{96,112},{112,96},{1... | collective-permute-start | bytes 221192 | tf_op jit(solution)/shard_map/ppermute | solution.py:478
  107.2 8.5 %collective-permute-done.10.rim_ref.got_ref = bf16[288,128]{1,0:T(8,128)(2,1)S(1)} collective-permute-done((bf16[288,128]{1,0:T(8,128)(2,1)S(1)}, bf16[288,128]{1,0:T(8,128)(2,1)S(1)}, u32[]{:S(2)}, u32[]{:S(2)}) %collective-permute-start.10) | collective-permute-done | bytes 73760 | tf_op jit(solution)/shard_map/ppermute | solution.py:478
  (34 shorter events, 6.7 us)
Async XLA Ops:
  0.6 36.9 %copy-start = (bf16[235,1024]{1,0:T(8,128)(2,1)S(1)}, bf16[235,1024]{1,0:T(8,128)(2,1)}, u32[]{:S(2)}) copy-start(bf16[235,1024]{1,0:T(8,128)(2,1)} %wig_ref.9) | copy-start | bytes 1443844
  2.9 22.1 %copy-start.1 = (bf16[1376,128]{1,0:T(8,128)(2,1)S(1)}, bf16[1376,128]{1,0:T(8,128)(2,1)}, u32[]{:S(2)}) copy-start(bf16[1376,128]{1,0:T(8,128)(2,1)} %get-tuple-element.35.own_ref) | copy-start | bytes 1056772
  2.9 16.8 %collective-permute-start = (bf16[400,128]{1,0:T(8,128)(2,1)}, bf16[400,128]{1,0:T(8,128)(2,1)S(1)}, u32[]{:S(2)}, u32[]{:S(2)}) collective-permute-start(bf16[400,128]{1,0:T(8,128)(2,1)} %get-tuple-element.28), channel_id=1, source_target_pairs={{0,8},{1,9},{2,10},{3,11},{4,12},{5,13},{6,14},{7,15},{8,0},{9,1},... | collective-permute-start | bytes 307208 | tf_op jit(solution)/shard_map/ppermute | solution.py:475
  13.1 13.9 %copy-start.6 = (bf16[224,128]{1,0:T(8,128)(2,1)S(1)}, bf16[224,128]{1,0:T(8,128)(2,1)}, u32[]{:S(2)}) copy-start(bf16[224,128]{1,0:T(8,128)(2,1)} %get-tuple-element.29) | copy-start | bytes 172036
  19.7 29.3 %collective-permute-start.1 = (bf16[800,128]{1,0:T(8,128)(2,1)S(1)}, bf16[800,128]{1,0:T(8,128)(2,1)S(1)}, u32[]{:S(2)}, u32[]{:S(2)}) collective-permute-start(bf16[800,128]{1,0:T(8,128)(2,1)S(1)} %constant_dynamic-update-slice_fusion.pair_ref), channel_id=1, source_target_pairs={{0,4},{1,5},{2,6},{3,7},{4,0},{5,1},{6,2},{7,3},{8,12},{9,13},{10,... | collective-permute-start | bytes 614408 | tf_op jit(solution)/shard_map/ppermute | solution.py:475
  25.0 40.9 %collective-permute-start.6 = (bf16[1376,128]{1,0:T(8,128)(2,1)S(1)}, bf16[1376,128]{1,0:T(8,128)(2,1)S(1)}, u32[]{:S(2)}, u32[]{:S(2)}) collective-permute-start(bf16[1376,128]{1,0:T(8,128)(2,1)S(1)} %copy-done.1), channel_id=1, source_target_pairs={{0,1},{1,0},{2,3},{3,2},{4,5},{5,4},{6,7},{7,6},{8,9},{9,8},{10,11... | collective-permute-start | bytes 1056776 | tf_op jit(solution)/shard_map/ppermute | solution.py:475
  27.0 22.1 %collective-permute-start.2 = (bf16[224,128]{1,0:T(8,128)(2,1)S(1)}, bf16[224,128]{1,0:T(8,128)(2,1)S(1)}, u32[]{:S(2)}, u32[]{:S(2)}) collective-permute-start(bf16[224,128]{1,0:T(8,128)(2,1)S(1)} %copy-done.6), channel_id=1, source_target_pairs={{0,16},{16,0},{32,48},{48,32},{64,80},{80,64},{96,112},{112,96},{1... | collective-permute-start | bytes 172040 | tf_op jit(solution)/shard_map/ppermute | solution.py:478
  37.5 0.7 copy-start.4
  37.6 0.7 copy-start.3
  49.0 17.4 %collective-permute-start.5 = (bf16[800,128]{1,0:T(8,128)(2,1)S(1)}, bf16[800,128]{1,0:T(8,128)(2,1)S(1)}, u32[]{:S(2)}, u32[]{:S(2)}) collective-permute-start(bf16[800,128]{1,0:T(8,128)(2,1)S(1)} %constant_dynamic-update-slice_fusion.pair_ref), channel_id=1, source_target_pairs={{0,2},{1,3},{2,0},{3,1},{4,6},{5,7},{6,4},{7,5},{8,10},{9,11},{10,... | collective-permute-start | bytes 614408 | tf_op jit(solution)/shard_map/ppermute | solution.py:475
  51.0 17.5 %collective-permute-start.4 = (bf16[800,128]{1,0:T(8,128)(2,1)S(1)}, bf16[800,128]{1,0:T(8,128)(2,1)S(1)}, u32[]{:S(2)}, u32[]{:S(2)}) collective-permute-start(bf16[800,128]{1,0:T(8,128)(2,1)S(1)} %collective-permute-done.1.pair_ref), channel_id=1, source_target_pairs={{0,2},{1,3},{2,0},{3,1},{4,6},{5,7},{6,4},{7,5},{8,10},{9,11},{10,... | collective-permute-start | bytes 614408 | tf_op jit(solution)/shard_map/ppermute | solution.py:475
  54.9 9.1 %collective-permute-start.3 = (bf16[112,128]{1,0:T(8,128)(2,1)S(1)}, bf16[112,128]{1,0:T(8,128)(2,1)S(1)}, u32[]{:S(2)}, u32[]{:S(2)}) collective-permute-start(bf16[112,128]{1,0:T(8,128)(2,1)S(1)} %constant_dynamic-slice_fusion), channel_id=1, source_target_pairs={{0,32},{16,496},{32,64},{48,16},{64,96},{80,48},{96,128},{112,80},... | collective-permute-start | bytes 86024 | tf_op jit(solution)/shard_map/ppermute | solution.py:482
  58.3 5.7 %copy-start.2 = (bf16[400,128]{1,0:T(8,128)(2,1)S(1)}, bf16[400,128]{1,0:T(8,128)(2,1)}, u32[]{:S(2)}) copy-start(bf16[400,128]{1,0:T(8,128)(2,1)} %get-tuple-element.31.node_ref) | copy-start | bytes 307204
  60.4 3.6 %copy-start.5 = (s32[1024]{0:T(1024)S(1)}, s32[1024]{0:T(1024)}, u32[]{:S(2)}) copy-start(s32[1024]{0:T(1024)} %param.13) | copy-start | bytes 12292
  68.5 3.8 %collective-permute-start.7 = (bf16[256,1024]{1,0:T(8,128)(2,1)S(1)}, bf16[256,1024]{1,0:T(8,128)(2,1)S(1)}, u32[]{:S(2)}, u32[]{:S(2)}) collective-permute-start(bf16[256,1024]{1,0:T(8,128)(2,1)S(1)} %edge_in.1.xo_ref), channel_id=1, source_target_pairs={{0,1},{1,0},{2,3},{3,2},{4,5},{5,4},{6,7},{7,6},{8,9},{9,8},{10,11... | collective-permute-start | bytes 1572872 | tf_op jit(solution)/shard_map/ppermute | solution.py:475
  80.0 3.7 %collective-permute-start.8 = (bf16[1648,128]{1,0:T(8,128)(2,1)S(1)}, bf16[1648,128]{1,0:T(8,128)(2,1)S(1)}, u32[]{:S(2)}, u32[]{:S(2)}) collective-permute-start(bf16[1648,128]{1,0:T(8,128)(2,1)S(1)} %get-tuple-element.47), channel_id=1, source_target_pairs={{0,1},{1,0},{2,3},{3,2},{4,5},{5,4},{6,7},{7,6},{8,9},{9,8},{10,11... | collective-permute-start | bytes 1265672 | tf_op jit(solution)/shard_map/ppermute | solution.py:475
  84.5 15.2 %all-to-all-start = ((bf16[16,128,128]{2,1,0:T(8,128)(2,1)}), bf16[16,128,128]{2,1,0:T(8,128)(2,1)S(1)}, u32[]{:S(2)}, u32[]{:S(2)}) async-start(bf16[16,128,128]{2,1,0:T(8,128)(2,1)} %pad_maximum_fusion), calls=%async_computation | async-start | bytes 1048576 | tf_op jit(solution)/shard_map/all_to_all | solution.py:553
  88.4 11.4 %collective-permute-start.9 = (bf16[112,128]{1,0:T(8,128)(2,1)S(1)}, bf16[112,128]{1,0:T(8,128)(2,1)S(1)}, u32[]{:S(2)}, u32[]{:S(2)}) collective-permute-start(bf16[112,128]{1,0:T(8,128)(2,1)S(1)} %get-tuple-element.57), channel_id=1, source_target_pairs={{0,480},{16,48},{32,0},{48,80},{64,32},{80,112},{96,64},{112,144},... | collective-permute-start | bytes 86024 | tf_op jit(solution)/shard_map/ppermute | solution.py:482
  99.8 16.0 %collective-permute-start.10 = (bf16[288,128]{1,0:T(8,128)(2,1)S(1)}, bf16[288,128]{1,0:T(8,128)(2,1)S(1)}, u32[]{:S(2)}, u32[]{:S(2)}) collective-permute-start(bf16[288,128]{1,0:T(8,128)(2,1)S(1)} %pad_maximum_fusion.1), channel_id=1, source_target_pairs={{0,16},{16,0},{32,48},{48,32},{64,80},{80,64},{96,112},{112,96},{1... | collective-permute-start | bytes 221192 | tf_op jit(solution)/shard_map/ppermute | solution.py:478

commit v6 on v5

--- a/solution.py
+++ b/solution.py
@@ -498,6 +498,19 @@
     )(node_x, cotangent, *w_tiles)
     near = cross(rims)
 
+    far = shift(lax.dynamic_slice_in_dim(near, 112 * high, 112, 0), True)
+    b4 = across(b0, 8)
+    b4, far = lax.optimization_barrier((b4, far))
+    two = jnp.concatenate([b0, b4], axis=0)
+    two, far, w_own = lax.optimization_barrier((two, far, w_own))
+    b26 = across(two, 4)
+
+    def rotated(pair):
+        return rotate_call(z_s, edge_count, pair, dst, scale, wigner)
+
+    eg0 = rotated(two)
+    far, eg0 = lax.optimization_barrier((far, eg0))
+
     w_sib = across(w_own, 1)
     wz, wo, wt = pl.pallas_call(
         weight_kernel,
@@ -509,21 +522,6 @@
         cost_estimate=light(),
         name="weights",
     )(k_s, w_own, w_sib)
-
-    b4 = across(b0, 8)
-    two = jnp.concatenate([b0, b4], axis=0)
-    b26 = across(two, 4)
-
-    def rotated(pair):
-        return rotate_call(z_s, edge_count, pair, dst, scale, wigner)
-
-    eg0 = rotated(two)
-    again, b26, near, eg0 = lax.optimization_barrier((two, b26, near, eg0))
-    b15 = across(again, 2)
-    b37 = across(b26, 2)
-    eg2 = rotated(b26)
-    eg1 = rotated(b15)
-    far = shift(lax.dynamic_slice_in_dim(near, 112 * high, 112, 0), True)
 
     x_spec = pl.BlockSpec((256, EB), lambda i: (0, i))
     x_own = pl.pallas_call(
@@ -537,7 +535,13 @@
         cost_estimate=light(),
         name="edge_in",
     )(h_s, node, near, far, src, wigner)
-    x_own, b37, eg1, eg2, wz, wo, wt = lax.optimization_barrier((x_own, b37, eg1, eg2, wz, wo, wt))
+    two, b26, x_own, eg0, wz, wo, wt = lax.optimization_barrier(
+        (two, b26, x_own, eg0, wz, wo, wt)
+    )
+    b15 = across(two, 2)
+    b37 = across(b26, 2)
+    eg2 = rotated(b26)
+    eg1 = rotated(b15)
     x_sib = across(x_own, 1)
 
     s_own, g_own, to_sib = edge_call(

time: 118 us -> 117 us (level)
  the two profiles are of different devices: /device:TPU:32 before, /device:TPU:4 now
where the time goes in v6:
time: 117 us; the launch traced here: 116 us
  starting transfers between devices  56.7 us (48%)
  waiting for transfers between devices  34.6 us (30%)
  Pallas kernels  20.1 us (17%)
  other arithmetic  1.97 us (2%)
  between operations  1.59 us (1%)
  local copies, waits for them, and re-layouts  1.37 us (1%)
    ppermute x2, starting transfers between devices, cross(): return lax.ppermute(x, 'brick', [(i, i ^ 1) for i in range(32)])  25.8 us
    ppermute x7, starting transfers between devices, across(): return lax.ppermute(x, 'chan', [(i, i ^ mask) for i in range(16)])  17.9 us
    ppermute x7, waiting for transfers between devices, across(): return lax.ppermute(x, 'chan', [(i, i ^ mask) for i in range(16)])  17 us
    pallas_call x1, Pallas kernels, edge_call(): pl.pallas_call(edge_kernel, out_shape=(sds((1024, 128), BF), sds((624, 12...  7.66 us
    ppermute x2, waiting for transfers between devices, cross(): return lax.ppermute(x, 'brick', [(i, i ^ 1) for i in range(32)])  7.63 us
    all_to_all x1, starting transfers between devices, body(): pieces = lax.all_to_all(send, 'brick', 0, 0, axis_index_groups=groups)  7.44 us
    all_to_all x1, waiting for transfers between devices, body(): pieces = lax.all_to_all(send, 'brick', 0, 0, axis_index_groups=groups)  7.28 us
    pallas_call x3, Pallas kernels, rotate_call(): pl.pallas_call(rotate_kernel, out_shape=sds((464, slots), BF), grid=(slot...  5.96 us
  transfers between devices with their start and end apart: 12, of which 8 were waited for; matrix products, arithmetic and copies ran while one was open for 0% of the time, Pallas kernels for 7%

profile of v6, /device:TPU:4, one launch (start us, length us, event | category | flops | bytes accessed | tf_op | source)
XLA Modules:
  0.0 116.4 jit_solution(6561250945782139149)
XLA Ops:
  0.6 2.3 %pack.1 = (bf16[400,128]{1,0:T(8,128)(2,1)}, bf16[400,128]{1,0:T(8,128)(2,1)}, bf16[224,128]{1,0:T(8,128)(2,1)}, bf16[1376,128]{1,0:T(8,128)(2,1)}) custom-call(bf16[49,8,128]{2,1,0:T(8,128)(2,1)} %node_ref.1, bf16[49,8,128]{2,1,0:T(8,128)(2,1)} %cot_ref.1, bf16[49,8,128]{2,1,0:T(8,128)(2,1)} %bitcast.40, bf16[72,8,128]{2,1,0:T(8,128)(2,1)} %bitcast.38, ...), custom_call_target="tpu_custom_call" | custom-call | flops 1 | bytes 1 | tf_op jit(solution)/shard_map/pack/pallas_call | solution.py:489
  2.9 15.8 %collective-permute-start.1 = (bf16[224,128]{1,0:T(8,128)(2,1)}, bf16[224,128]{1,0:T(8,128)(2,1)S(1)}, u32[]{:S(2)}, u32[]{:S(2)}) collective-permute-start(bf16[224,128]{1,0:T(8,128)(2,1)} %get-tuple-element.32), channel_id=1, source_target_pairs={{0,16},{16,0},{32,48},{48,32},{64,80},{80,64},{96,112},{112,96},{1... | collective-permute-start | bytes 172040 | tf_op jit(solution)/shard_map/ppermute | solution.py:478
  18.8 4.3 %collective-permute-start = (bf16[400,128]{1,0:T(8,128)(2,1)}, bf16[400,128]{1,0:T(8,128)(2,1)S(1)}, u32[]{:S(2)}, u32[]{:S(2)}) collective-permute-start(bf16[400,128]{1,0:T(8,128)(2,1)} %get-tuple-element.31), channel_id=1, source_target_pairs={{0,8},{1,9},{2,10},{3,11},{4,12},{5,13},{6,14},{7,15},{8,0},{9,1},... | collective-permute-start | bytes 307208 | tf_op jit(solution)/shard_map/ppermute | solution.py:475
  23.1 3.1 %collective-permute-start.2 = (bf16[112,128]{1,0:T(8,128)(2,1)S(1)}, bf16[112,128]{1,0:T(8,128)(2,1)S(1)}, u32[]{:S(2)}, u32[]{:S(2)}) collective-permute-start(bf16[112,128]{1,0:T(8,128)(2,1)S(1)} %constant_dynamic-slice_fusion), channel_id=1, source_target_pairs={{0,32},{16,496},{32,64},{48,16},{64,96},{80,48},{96,128},{112,80},... | collective-permute-start | bytes 86024 | tf_op jit(solution)/shard_map/ppermute | solution.py:482
  26.2 2.7 %collective-permute-done.2.far_ref = bf16[112,128]{1,0:T(8,128)(2,1)S(1)} collective-permute-done((bf16[112,128]{1,0:T(8,128)(2,1)S(1)}, bf16[112,128]{1,0:T(8,128)(2,1)S(1)}, u32[]{:S(2)}, u32[]{:S(2)}) %collective-permute-start.2) | collective-permute-done | bytes 28704 | tf_op jit(solution)/shard_map/ppermute | solution.py:482
  28.9 6.8 %collective-permute-done = bf16[400,128]{1,0:T(8,128)(2,1)S(1)} collective-permute-done((bf16[400,128]{1,0:T(8,128)(2,1)}, bf16[400,128]{1,0:T(8,128)(2,1)S(1)}, u32[]{:S(2)}, u32[]{:S(2)}) %collective-permute-start) | collective-permute-done | bytes 102432 | tf_op jit(solution)/shard_map/ppermute | solution.py:475
  36.6 1.9 %collective-permute-start.4 = (bf16[1376,128]{1,0:T(8,128)(2,1)S(1)}, bf16[1376,128]{1,0:T(8,128)(2,1)S(1)}, u32[]{:S(2)}, u32[]{:S(2)}) collective-permute-start(bf16[1376,128]{1,0:T(8,128)(2,1)S(1)} %copy-done.1), channel_id=1, source_target_pairs={{0,1},{1,0},{2,3},{3,2},{4,5},{5,4},{6,7},{7,6},{8,9},{9,8},{10,11... | collective-permute-start | bytes 1056776 | tf_op jit(solution)/shard_map/ppermute | solution.py:475
  38.6 1.9 %collective-permute-start.3 = (bf16[800,128]{1,0:T(8,128)(2,1)S(1)}, bf16[800,128]{1,0:T(8,128)(2,1)S(1)}, u32[]{:S(2)}, u32[]{:S(2)}) collective-permute-start(bf16[800,128]{1,0:T(8,128)(2,1)S(1)} %pad_maximum_fusion.1.pair_ref), channel_id=1, source_target_pairs={{0,4},{1,5},{2,6},{3,7},{4,0},{5,1},{6,2},{7,3},{8,12},{9,13},{10,... | collective-permute-start | bytes 614408 | tf_op jit(solution)/shard_map/ppermute | solution.py:475
  41.9 2.0 %rotate.3.eg0 = bf16[464,1024]{1,0:T(8,128)(2,1)S(1)} custom-call(s32[1]{0:T(128)} %bitcast.1.z_ref, s32[1]{0:T(128)S(6)} %copy.14.count_ref, bf16[800,128]{1,0:T(8,128)(2,1)S(1)} %pad_maximum_fusion.1.pair_ref, s32[1,1024]{1,0:T(1,128)S(1)} %bitcast.24, f32[1,1024]{1,0:T(1,128)S(1)} %bitcast.28, bf16[235,1024]{1,0:T(8,128)(2,1)S(1)} %copy-done), custom_call_target="tpu_custom_call" | custom-call | tf_op jit(solution)/shard_map/rotate/pallas_call | solution.py:361
  47.0 4.6 %collective-permute-done.3.pair_ref = bf16[800,128]{1,0:T(8,128)(2,1)S(1)} collective-permute-done((bf16[800,128]{1,0:T(8,128)(2,1)S(1)}, bf16[800,128]{1,0:T(8,128)(2,1)S(1)}, u32[]{:S(2)}, u32[]{:S(2)}) %collective-permute-start.3) | collective-permute-done | bytes 204832 | tf_op jit(solution)/shard_map/ppermute | solution.py:475
  51.6 2.0 %collective-permute-start.7 = (bf16[256,1024]{1,0:T(8,128)(2,1)S(1)}, bf16[256,1024]{1,0:T(8,128)(2,1)S(1)}, u32[]{:S(2)}, u32[]{:S(2)}) collective-permute-start(bf16[256,1024]{1,0:T(8,128)(2,1)S(1)} %edge_in.1.xo_ref), channel_id=1, source_target_pairs={{0,1},{1,0},{2,3},{3,2},{4,5},{5,4},{6,7},{7,6},{8,9},{9,8},{10,11... | collective-permute-start | bytes 1572872 | tf_op jit(solution)/shard_map/ppermute | solution.py:475
  53.6 1.9 %collective-permute-start.5 = (bf16[800,128]{1,0:T(8,128)(2,1)S(1)}, bf16[800,128]{1,0:T(8,128)(2,1)S(1)}, u32[]{:S(2)}, u32[]{:S(2)}) collective-permute-start(bf16[800,128]{1,0:T(8,128)(2,1)S(1)} %pad_maximum_fusion.1.pair_ref), channel_id=1, source_target_pairs={{0,2},{1,3},{2,0},{3,1},{4,6},{5,7},{6,4},{7,5},{8,10},{9,11},{10,... | collective-permute-start | bytes 614408 | tf_op jit(solution)/shard_map/ppermute | solution.py:475
  55.5 3.9 %collective-permute-start.6 = (bf16[800,128]{1,0:T(8,128)(2,1)S(1)}, bf16[800,128]{1,0:T(8,128)(2,1)S(1)}, u32[]{:S(2)}, u32[]{:S(2)}) collective-permute-start(bf16[800,128]{1,0:T(8,128)(2,1)S(1)} %collective-permute-done.3.pair_ref), channel_id=1, source_target_pairs={{0,2},{1,3},{2,0},{3,1},{4,6},{5,7},{6,4},{7,5},{8,10},{9,11},{10,... | collective-permute-start | bytes 614408 | tf_op jit(solution)/shard_map/ppermute | solution.py:475
  59.4 2.0 %rotate.4.eg2 = bf16[464,1024]{1,0:T(8,128)(2,1)S(1)} custom-call(s32[1]{0:T(128)} %bitcast.1.z_ref, s32[1]{0:T(128)S(6)} %copy.14.count_ref, bf16[800,128]{1,0:T(8,128)(2,1)S(1)} %collective-permute-done.3.pair_ref, s32[1,1024]{1,0:T(1,128)S(1)} %bitcast.25, f32[1,1024]{1,0:T(1,128)S(1)} %bitcast.29, bf16[235,1024]{1,0:T(8,128)(2,1)S(1)} %copy-done), custom_call_target="tpu_custom_call" | custom-call | tf_op jit(solution)/shard_map/rotate/pallas_call | solution.py:361
  61.4 1.9 %collective-permute-done.5.pair_ref = bf16[800,128]{1,0:T(8,128)(2,1)S(1)} collective-permute-done((bf16[800,128]{1,0:T(8,128)(2,1)S(1)}, bf16[800,128]{1,0:T(8,128)(2,1)S(1)}, u32[]{:S(2)}, u32[]{:S(2)}) %collective-permute-start.5) | collective-permute-done | bytes 204832 | tf_op jit(solution)/shard_map/ppermute | solution.py:475
  63.3 2.0 %rotate.5.eg1 = bf16[464,1024]{1,0:T(8,128)(2,1)S(1)} custom-call(s32[1]{0:T(128)} %bitcast.1.z_ref, s32[1]{0:T(128)S(6)} %copy.14.count_ref, bf16[800,128]{1,0:T(8,128)(2,1)S(1)} %collective-permute-done.5.pair_ref, s32[1,1024]{1,0:T(1,128)S(1)} %bitcast.26, f32[1,1024]{1,0:T(1,128)S(1)} %bitcast.30, bf16[235,1024]{1,0:T(8,128)(2,1)S(1)} %copy-done), custom_call_target="tpu_custom_call" | custom-call | tf_op jit(solution)/shard_map/rotate/pallas_call | solution.py:361
  65.3 1.9 %collective-permute-done.6.pair_ref = bf16[800,128]{1,0:T(8,128)(2,1)S(1)} collective-permute-done((bf16[800,128]{1,0:T(8,128)(2,1)S(1)}, bf16[800,128]{1,0:T(8,128)(2,1)S(1)}, u32[]{:S(2)}, u32[]{:S(2)}) %collective-permute-start.6) | collective-permute-done | bytes 204832 | tf_op jit(solution)/shard_map/ppermute | solution.py:475
  67.3 7.7 %edge.1 = (bf16[1024,128]{1,0:T(8,128)(2,1)S(1)}, f32[624,128]{1,0:T(8,128)S(1)}, bf16[1648,128]{1,0:T(8,128)(2,1)S(1)}) custom-call(s32[1]{0:T(128)} %bitcast.1.z_ref, s32[1]{0:T(128)S(6)} %copy.14.count_ref, bf16[464,1024]{1,0:T(8,128)(2,1)S(1)} %rotate.3.eg0, bf16[464,1024]{1,0:T(8,128)(2,1)S(1)} %rotate.4.eg2, bf16[464,1024]{1,0:T(8,128)(2,1)S(1)} %rotate.5.eg1, ...), custom_call_target="tpu_custom_call" | custom-call | tf_op jit(solution)/shard_map/edge/pallas_call | solution.py:376
  74.9 1.9 %collective-permute-start.8 = (bf16[1648,128]{1,0:T(8,128)(2,1)S(1)}, bf16[1648,128]{1,0:T(8,128)(2,1)S(1)}, u32[]{:S(2)}, u32[]{:S(2)}) collective-permute-start(bf16[1648,128]{1,0:T(8,128)(2,1)S(1)} %get-tuple-element.53), channel_id=1, source_target_pairs={{0,1},{1,0},{2,3},{3,2},{4,5},{5,4},{6,7},{7,6},{8,9},{9,8},{10,11... | collective-permute-start | bytes 1265672 | tf_op jit(solution)/shard_map/ppermute | solution.py:475
  79.5 7.4 %all-to-all-start = ((bf16[16,128,128]{2,1,0:T(8,128)(2,1)}), bf16[16,128,128]{2,1,0:T(8,128)(2,1)S(1)}, u32[]{:S(2)}, u32[]{:S(2)}) async-start(bf16[16,128,128]{2,1,0:T(8,128)(2,1)} %pad_maximum_fusion), calls=%async_computation | async-start | bytes 1048576 | tf_op jit(solution)/shard_map/all_to_all | solution.py:557
  87.0 2.5 %collective-permute-start.9 = (bf16[112,128]{1,0:T(8,128)(2,1)S(1)}, bf16[112,128]{1,0:T(8,128)(2,1)S(1)}, u32[]{:S(2)}, u32[]{:S(2)}) collective-permute-start(bf16[112,128]{1,0:T(8,128)(2,1)S(1)} %get-tuple-element.63), channel_id=1, source_target_pairs={{0,480},{16,48},{32,0},{48,80},{64,32},{80,112},{96,64},{112,144},... | collective-permute-start | bytes 86024 | tf_op jit(solution)/shard_map/ppermute | solution.py:482
  89.5 7.3 %all-to-all-done = bf16[16,128,128]{2,1,0:T(8,128)(2,1)S(1)} async-done(((bf16[16,128,128]{2,1,0:T(8,128)(2,1)}), bf16[16,128,128]{2,1,0:T(8,128)(2,1)S(1)}, u32[]{:S(2)}, u32[]{:S(2)}) %all-to-all-start) | async-done | bytes 524320 | tf_op jit(solution)/shard_map/all_to_all | solution.py:557
  96.9 10.0 %collective-permute-start.10 = (bf16[288,128]{1,0:T(8,128)(2,1)S(1)}, bf16[288,128]{1,0:T(8,128)(2,1)S(1)}, u32[]{:S(2)}, u32[]{:S(2)}) collective-permute-start(bf16[288,128]{1,0:T(8,128)(2,1)S(1)} %pad_maximum_fusion.2), channel_id=1, source_target_pairs={{0,16},{16,0},{32,48},{48,32},{64,80},{80,64},{96,112},{112,96},{1... | collective-permute-start | bytes 221192 | tf_op jit(solution)/shard_map/ppermute | solution.py:478
  106.9 7.6 %collective-permute-done.10.rim_ref.got_ref = bf16[288,128]{1,0:T(8,128)(2,1)S(1)} collective-permute-done((bf16[288,128]{1,0:T(8,128)(2,1)S(1)}, bf16[288,128]{1,0:T(8,128)(2,1)S(1)}, u32[]{:S(2)}, u32[]{:S(2)}) %collective-permute-start.10) | collective-permute-done | bytes 73760 | tf_op jit(solution)/shard_map/ppermute | solution.py:478
  (31 shorter events, 9.3 us)
Async XLA Ops:
  0.6 40.5 %copy-start = (bf16[235,1024]{1,0:T(8,128)(2,1)S(1)}, bf16[235,1024]{1,0:T(8,128)(2,1)}, u32[]{:S(2)}) copy-start(bf16[235,1024]{1,0:T(8,128)(2,1)} %wig_ref.9) | copy-start | bytes 1443844
  2.9 33.7 %copy-start.1 = (bf16[1376,128]{1,0:T(8,128)(2,1)S(1)}, bf16[1376,128]{1,0:T(8,128)(2,1)}, u32[]{:S(2)}) copy-start(bf16[1376,128]{1,0:T(8,128)(2,1)} %get-tuple-element.41.own_ref) | copy-start | bytes 1056772
  2.9 20.2 %collective-permute-start.1 = (bf16[224,128]{1,0:T(8,128)(2,1)}, bf16[224,128]{1,0:T(8,128)(2,1)S(1)}, u32[]{:S(2)}, u32[]{:S(2)}) collective-permute-start(bf16[224,128]{1,0:T(8,128)(2,1)} %get-tuple-element.32), channel_id=1, source_target_pairs={{0,16},{16,0},{32,48},{48,32},{64,80},{80,64},{96,112},{112,96},{1... | collective-permute-start | bytes 172040 | tf_op jit(solution)/shard_map/ppermute | solution.py:478
  18.8 16.9 %collective-permute-start = (bf16[400,128]{1,0:T(8,128)(2,1)}, bf16[400,128]{1,0:T(8,128)(2,1)S(1)}, u32[]{:S(2)}, u32[]{:S(2)}) collective-permute-start(bf16[400,128]{1,0:T(8,128)(2,1)} %get-tuple-element.31), channel_id=1, source_target_pairs={{0,8},{1,9},{2,10},{3,11},{4,12},{5,13},{6,14},{7,15},{8,0},{9,1},... | collective-permute-start | bytes 307208 | tf_op jit(solution)/shard_map/ppermute | solution.py:475
  23.1 5.8 %collective-permute-start.2 = (bf16[112,128]{1,0:T(8,128)(2,1)S(1)}, bf16[112,128]{1,0:T(8,128)(2,1)S(1)}, u32[]{:S(2)}, u32[]{:S(2)}) collective-permute-start(bf16[112,128]{1,0:T(8,128)(2,1)S(1)} %constant_dynamic-slice_fusion), channel_id=1, source_target_pairs={{0,32},{16,496},{32,64},{48,16},{64,96},{80,48},{96,128},{112,80},... | collective-permute-start | bytes 86024 | tf_op jit(solution)/shard_map/ppermute | solution.py:482
  36.6 9.8 %collective-permute-start.4 = (bf16[1376,128]{1,0:T(8,128)(2,1)S(1)}, bf16[1376,128]{1,0:T(8,128)(2,1)S(1)}, u32[]{:S(2)}, u32[]{:S(2)}) collective-permute-start(bf16[1376,128]{1,0:T(8,128)(2,1)S(1)} %copy-done.1), channel_id=1, source_target_pairs={{0,1},{1,0},{2,3},{3,2},{4,5},{5,4},{6,7},{7,6},{8,9},{9,8},{10,11... | collective-permute-start | bytes 1056776 | tf_op jit(solution)/shard_map/ppermute | solution.py:475
  38.6 13.0 %collective-permute-start.3 = (bf16[800,128]{1,0:T(8,128)(2,1)S(1)}, bf16[800,128]{1,0:T(8,128)(2,1)S(1)}, u32[]{:S(2)}, u32[]{:S(2)}) collective-permute-start(bf16[800,128]{1,0:T(8,128)(2,1)S(1)} %pad_maximum_fusion.1.pair_ref), channel_id=1, source_target_pairs={{0,4},{1,5},{2,6},{3,7},{4,0},{5,1},{6,2},{7,3},{8,12},{9,13},{10,... | collective-permute-start | bytes 614408 | tf_op jit(solution)/shard_map/ppermute | solution.py:475
  41.1 0.7 copy-start.4
  41.2 0.7 copy-start.3
  41.9 2.0 %copy-start.2 = (bf16[400,128]{1,0:T(8,128)(2,1)S(1)}, bf16[400,128]{1,0:T(8,128)(2,1)}, u32[]{:S(2)}) copy-start(bf16[400,128]{1,0:T(8,128)(2,1)} %get-tuple-element.37.node_ref) | copy-start | bytes 307204
  43.8 0.7 copy-start.5
  51.6 15.7 %collective-permute-start.7 = (bf16[256,1024]{1,0:T(8,128)(2,1)S(1)}, bf16[256,1024]{1,0:T(8,128)(2,1)S(1)}, u32[]{:S(2)}, u32[]{:S(2)}) collective-permute-start(bf16[256,1024]{1,0:T(8,128)(2,1)S(1)} %edge_in.1.xo_ref), channel_id=1, source_target_pairs={{0,1},{1,0},{2,3},{3,2},{4,5},{5,4},{6,7},{7,6},{8,9},{9,8},{10,11... | collective-permute-start | bytes 1572872 | tf_op jit(solution)/shard_map/ppermute | solution.py:475
  53.6 9.8 %collective-permute-start.5 = (bf16[800,128]{1,0:T(8,128)(2,1)S(1)}, bf16[800,128]{1,0:T(8,128)(2,1)S(1)}, u32[]{:S(2)}, u32[]{:S(2)}) collective-permute-start(bf16[800,128]{1,0:T(8,128)(2,1)S(1)} %pad_maximum_fusion.1.pair_ref), channel_id=1, source_target_pairs={{0,2},{1,3},{2,0},{3,1},{4,6},{5,7},{6,4},{7,5},{8,10},{9,11},{10,... | collective-permute-start | bytes 614408 | tf_op jit(solution)/shard_map/ppermute | solution.py:475
  55.5 11.8 %collective-permute-start.6 = (bf16[800,128]{1,0:T(8,128)(2,1)S(1)}, bf16[800,128]{1,0:T(8,128)(2,1)S(1)}, u32[]{:S(2)}, u32[]{:S(2)}) collective-permute-start(bf16[800,128]{1,0:T(8,128)(2,1)S(1)} %collective-permute-done.3.pair_ref), channel_id=1, source_target_pairs={{0,2},{1,3},{2,0},{3,1},{4,6},{5,7},{6,4},{7,5},{8,10},{9,11},{10,... | collective-permute-start | bytes 614408 | tf_op jit(solution)/shard_map/ppermute | solution.py:475
  74.9 3.7 %collective-permute-start.8 = (bf16[1648,128]{1,0:T(8,128)(2,1)S(1)}, bf16[1648,128]{1,0:T(8,128)(2,1)S(1)}, u32[]{:S(2)}, u32[]{:S(2)}) collective-permute-start(bf16[1648,128]{1,0:T(8,128)(2,1)S(1)} %get-tuple-element.53), channel_id=1, source_target_pairs={{0,1},{1,0},{2,3},{3,2},{4,5},{5,4},{6,7},{7,6},{8,9},{9,8},{10,11... | collective-permute-start | bytes 1265672 | tf_op jit(solution)/shard_map/ppermute | solution.py:475
  79.5 17.3 %all-to-all-start = ((bf16[16,128,128]{2,1,0:T(8,128)(2,1)}), bf16[16,128,128]{2,1,0:T(8,128)(2,1)S(1)}, u32[]{:S(2)}, u32[]{:S(2)}) async-start(bf16[16,128,128]{2,1,0:T(8,128)(2,1)} %pad_maximum_fusion), calls=%async_computation | async-start | bytes 1048576 | tf_op jit(solution)/shard_map/all_to_all | solution.py:557
  87.0 9.9 %collective-permute-start.9 = (bf16[112,128]{1,0:T(8,128)(2,1)S(1)}, bf16[112,128]{1,0:T(8,128)(2,1)S(1)}, u32[]{:S(2)}, u32[]{:S(2)}) collective-permute-start(bf16[112,128]{1,0:T(8,128)(2,1)S(1)} %get-tuple-element.63), channel_id=1, source_target_pairs={{0,480},{16,48},{32,0},{48,80},{64,32},{80,112},{96,64},{112,144},... | collective-permute-start | bytes 86024 | tf_op jit(solution)/shard_map/ppermute | solution.py:482
  96.9 17.7 %collective-permute-start.10 = (bf16[288,128]{1,0:T(8,128)(2,1)S(1)}, bf16[288,128]{1,0:T(8,128)(2,1)S(1)}, u32[]{:S(2)}, u32[]{:S(2)}) collective-permute-start(bf16[288,128]{1,0:T(8,128)(2,1)S(1)} %pad_maximum_fusion.2), channel_id=1, source_target_pairs={{0,16},{16,0},{32,48},{48,32},{64,80},{80,64},{96,112},{112,96},{1... | collective-permute-start | bytes 221192 | tf_op jit(solution)/shard_map/ppermute | solution.py:478

commit v7 on v6

--- a/solution.py
+++ b/solution.py
@@ -192,10 +192,9 @@
                     ref[row : row + 16, p * 128 : p * 128 + 128] = tile(entries, p)
 
 
-def rotate_pair(z, pair_ref, dest, rot, gathered, store):
-    for side in range(2):
-        start = pl.multiple_of(400 * (side ^ (z // 4)), 16)
-        gathered[side] = mm(pair_ref[pl.ds(start, 400), :], dest)
+def rotate_pair(z, near_ref, far_ref, dest, rot, gathered, store):
+    gathered[z // 4] = mm(near_ref[...], dest)
+    gathered[1 - z // 4] = mm(far_ref[...], dest)
     for half in range(EB // LANES):
         lanes = slice(half * LANES, half * LANES + LANES)
         for degree in range(7):
@@ -222,18 +221,18 @@
     return jnp.where(slot < count_ref[0], 0.25 * scale_ref[...], 0.0)
 
 
-def rotate_kernel(z_ref, count_ref, pair_ref, dst_ref, scale_ref, wig_ref, eg_ref, gathered, rot):
+def rotate_kernel(z_ref, count_ref, near_ref, far_ref, dst_ref, scale_ref, wig_ref, eg_ref, gathered, rot):
     rot[...] = wig_ref[...].astype(F32) * edge_factor(pl.program_id(0), count_ref, scale_ref)
     dest = hot(iota((LANES, EB), 0) == dst_ref[...])
 
     def store(place, lanes, tile):
         eg_ref[place * 16 : place * 16 + 16, lanes] = tile
 
-    rotate_pair(z_ref[0], pair_ref, dest, rot, gathered, store)
+    rotate_pair(z_ref[0], near_ref, far_ref, dest, rot, gathered, store)
 
 
 def edge_kernel(
-    z_ref, count_ref, eg0, eg2, eg1, pair_ref,
+    z_ref, count_ref, eg0, eg2, eg1, near_ref, far_ref,
     dst_ref, src_ref, scale_ref, wig_ref, xo_ref, xs_ref, zero_ref, one_ref, two_ref,
     so_ref, go_ref, sib_ref,
     gathered, rot, plain, eg, acc, back, full, atoms, rims,
@@ -258,7 +257,7 @@
     def store(place, lanes, tile):
         eg[rows_of(place, 3), lanes] = tile
 
-    rotate_pair(z, pair_ref, dest, rot, gathered, store)
+    rotate_pair(z, near_ref, far_ref, dest, rot, gathered, store)
     for n, ref in ((0, eg0), (2, eg2), (1, eg1)):
         for place in range(29):
             eg[rows_of(place, n), :] = ref[place * 16 : place * 16 + 16]
@@ -362,12 +361,12 @@
         rotate_kernel,
         out_shape=sds((464, slots), BF),
         grid=(slots // EB,),
-        in_specs=[smem(), smem(), whole((800, 128)), row_spec(), row_spec(), wig_spec()],
+        in_specs=[smem(), smem(), whole((400, 128)), whole((400, 128)), row_spec(), row_spec(), wig_spec()],
         out_specs=pl.BlockSpec((464, EB), lambda i: (0, i)),
         scratch_shapes=[pltpu.VMEM((2, 400, EB), F32), pltpu.VMEM((235, EB), F32)],
         compiler_params=params(),
         name="rotate",
-    )(z_s, edge_count, pair, dst, scale, wigner)
+    )(z_s, edge_count, *pair, dst, scale, wigner)
 
 
 def edge_call(z_s, edge_count, egs, pair, dst, src, scale, wigner, x_own, x_sib, weights):
@@ -379,7 +378,7 @@
         grid=(slots // EB,),
         in_specs=[smem(), smem()]
         + [pl.BlockSpec((464, EB), lambda i: (0, i))] * 3
-        + [whole((800, 128)), row_spec(), row_spec(), row_spec(), wig_spec(), x_spec, x_spec]
+        + [whole((400, 128)), whole((400, 128)), row_spec(), row_spec(), row_spec(), wig_spec(), x_spec, x_spec]
         + [whole((112, 512)), whole((192, 768)), whole((160, 640))],
         out_specs=(whole((1024, 128)), whole((624, 128)), whole((1648, 128))),
         scratch_shapes=[
@@ -395,7 +394,7 @@
         ],
         compiler_params=params(),
         name="edge",
-    )(z_s, edge_count, *egs, pair, dst, src, scale, wigner, x_own, x_sib, *weights)
+    )(z_s, edge_count, *egs, *pair, dst, src, scale, wigner, x_own, x_sib, *weights)
 
 
 def finish_kernel(mine_ref, got_ref, zero_ref, one_ref, two_ref):
@@ -498,17 +497,18 @@
     )(node_x, cotangent, *w_tiles)
     near = cross(rims)
 
+    def rotated(*pair):
+        return rotate_call(z_s, edge_count, pair, dst, scale, wigner)
+
+    b4 = across(b0, 8)
+    b2 = across(b0, 4)
+    b1 = across(b0, 2)
+    b4, b2, b1, near, w_own = lax.optimization_barrier((b4, b2, b1, near, w_own))
+    b6 = across(b4, 4)
+    b5 = across(b4, 2)
+    b3 = across(b2, 2)
     far = shift(lax.dynamic_slice_in_dim(near, 112 * high, 112, 0), True)
-    b4 = across(b0, 8)
-    b4, far = lax.optimization_barrier((b4, far))
-    two = jnp.concatenate([b0, b4], axis=0)
-    two, far, w_own = lax.optimization_barrier((two, far, w_own))
-    b26 = across(two, 4)
-
-    def rotated(pair):
-        return rotate_call(z_s, edge_count, pair, dst, scale, wigner)
-
-    eg0 = rotated(two)
+    eg0 = rotated(b0, b4)
     far, eg0 = lax.optimization_barrier((far, eg0))
 
     w_sib = across(w_own, 1)
@@ -535,17 +535,16 @@
         cost_estimate=light(),
         name="edge_in",
     )(h_s, node, near, far, src, wigner)
-    two, b26, x_own, eg0, wz, wo, wt = lax.optimization_barrier(
-        (two, b26, x_own, eg0, wz, wo, wt)
+    b6, b5, b3, x_own, eg0, wz, wo, wt = lax.optimization_barrier(
+        (b6, b5, b3, x_own, eg0, wz, wo, wt)
     )
-    b15 = across(two, 2)
-    b37 = across(b26, 2)
-    eg2 = rotated(b26)
-    eg1 = rotated(b15)
+    b7 = across(b6, 2)
+    eg2 = rotated(b2, b6)
+    eg1 = rotated(b1, b5)
     x_sib = across(x_own, 1)
 
     s_own, g_own, to_sib = edge_call(
-        z_s, edge_count, (eg0, eg2, eg1), b37, dst, src, scale, wigner, x_own, x_sib, (wz, wo, wt)
+        z_s, edge_count, (eg0, eg2, eg1), (b3, b7), dst, src, scale, wigner, x_own, x_sib, (wz, wo, wt)
     )
 
     got = across(to_sib, 1)

time: 117 us -> 119 us (1.017)
  the two profiles are of different devices: /device:TPU:4 before, /device:TPU:2 now
where the time goes in v7:
time: 119 us; the launch traced here: 118 us
  starting transfers between devices  69.8 us (59%)
  waiting for transfers between devices  22.7 us (19%)
  Pallas kernels  21.7 us (18%)
  between operations  1.66 us (1%)
  local copies, waits for them, and re-layouts  1.35 us (1%)
    ppermute x10, starting transfers between devices, across(): return lax.ppermute(x, 'chan', [(i, i ^ mask) for i in range(16)])  38.5 us
    ppermute x2, starting transfers between devices, cross(): return lax.ppermute(x, 'brick', [(i, i ^ 1) for i in range(32)])  18.7 us
    ppermute x2, waiting for transfers between devices, cross(): return lax.ppermute(x, 'brick', [(i, i ^ 1) for i in range(32)])  12.8 us
    all_to_all x1, waiting for transfers between devices, body(): pieces = lax.all_to_all(send, 'brick', 0, 0, axis_index_groups=groups)  8.31 us
    pallas_call x1, Pallas kernels, edge_call(): pl.pallas_call(edge_kernel, out_shape=(sds((1024, 128), BF), sds((624, 12...  7.94 us
    all_to_all x1, starting transfers between devices, body(): pieces = lax.all_to_all(send, 'brick', 0, 0, axis_index_groups=groups)  7.23 us
    pallas_call x3, Pallas kernels, rotate_call(): pl.pallas_call(rotate_kernel, out_shape=sds((464, slots), BF), grid=(slot...  7.22 us
    ppermute x2, starting transfers between devices, shift(): return lax.ppermute(x, 'brick', route)  5.41 us
  transfers between devices with their start and end apart: 15, of which 4 were waited for; matrix products, arithmetic and copies ran while one was open for 0% of the time, Pallas kernels for 8%

profile of v7, /device:TPU:2, one launch (start us, length us, event | category | flops | bytes accessed | tf_op | source)
XLA Modules:
  0.0 118.2 jit_solution(16944014799485997885)
XLA Ops:
  0.6 2.3 %pack.1 = (bf16[400,128]{1,0:T(8,128)(2,1)}, bf16[400,128]{1,0:T(8,128)(2,1)}, bf16[224,128]{1,0:T(8,128)(2,1)}, bf16[1376,128]{1,0:T(8,128)(2,1)}) custom-call(bf16[49,8,128]{2,1,0:T(8,128)(2,1)} %node_ref.1, bf16[49,8,128]{2,1,0:T(8,128)(2,1)} %cot_ref.1, bf16[49,8,128]{2,1,0:T(8,128)(2,1)} %bitcast.40, bf16[72,8,128]{2,1,0:T(8,128)(2,1)} %bitcast.38, ...), custom_call_target="tpu_custom_call" | custom-call | flops 1 | bytes 1 | tf_op jit(solution)/shard_map/pack/pallas_call | solution.py:488
  2.9 9.2 %collective-permute-start = (bf16[400,128]{1,0:T(8,128)(2,1)}, bf16[400,128]{1,0:T(8,128)(2,1)S(1)}, u32[]{:S(2)}, u32[]{:S(2)}) collective-permute-start(bf16[400,128]{1,0:T(8,128)(2,1)} %get-tuple-element.32.near_ref), channel_id=1, source_target_pairs={{0,8},{1,9},{2,10},{3,11},{4,12},{5,13},{6,14},{7,15},{8,0},{9,1},... | collective-permute-start | bytes 307208 | tf_op jit(solution)/shard_map/ppermute | solution.py:474
  12.1 5.2 %collective-permute-start.1 = (bf16[400,128]{1,0:T(8,128)(2,1)}, bf16[400,128]{1,0:T(8,128)(2,1)S(1)}, u32[]{:S(2)}, u32[]{:S(2)}) collective-permute-start(bf16[400,128]{1,0:T(8,128)(2,1)} %get-tuple-element.32.near_ref), channel_id=1, source_target_pairs={{0,4},{1,5},{2,6},{3,7},{4,0},{5,1},{6,2},{7,3},{8,12},{9,13},{10,... | collective-permute-start | bytes 307208 | tf_op jit(solution)/shard_map/ppermute | solution.py:474
  17.3 3.8 %collective-permute-start.2 = (bf16[400,128]{1,0:T(8,128)(2,1)}, bf16[400,128]{1,0:T(8,128)(2,1)S(1)}, u32[]{:S(2)}, u32[]{:S(2)}) collective-permute-start(bf16[400,128]{1,0:T(8,128)(2,1)} %get-tuple-element.32.near_ref), channel_id=1, source_target_pairs={{0,2},{1,3},{2,0},{3,1},{4,6},{5,7},{6,4},{7,5},{8,10},{9,11},{10,... | collective-permute-start | bytes 307208 | tf_op jit(solution)/shard_map/ppermute | solution.py:474
  21.2 8.2 %collective-permute-start.3 = (bf16[224,128]{1,0:T(8,128)(2,1)}, bf16[224,128]{1,0:T(8,128)(2,1)S(1)}, u32[]{:S(2)}, u32[]{:S(2)}) collective-permute-start(bf16[224,128]{1,0:T(8,128)(2,1)} %get-tuple-element.33), channel_id=1, source_target_pairs={{0,16},{16,0},{32,48},{48,32},{64,80},{80,64},{96,112},{112,96},{1... | collective-permute-start | bytes 172040 | tf_op jit(solution)/shard_map/ppermute | solution.py:477
  29.4 6.8 %collective-permute-done.3.near_ref = bf16[224,128]{1,0:T(8,128)(2,1)S(1)} collective-permute-done((bf16[224,128]{1,0:T(8,128)(2,1)}, bf16[224,128]{1,0:T(8,128)(2,1)S(1)}, u32[]{:S(2)}, u32[]{:S(2)}) %collective-permute-start.3) | collective-permute-done | bytes 57376 | tf_op jit(solution)/shard_map/ppermute | solution.py:477
  36.2 1.9 %collective-permute-start.8 = (bf16[1376,128]{1,0:T(8,128)(2,1)}, bf16[1376,128]{1,0:T(8,128)(2,1)S(1)}, u32[]{:S(2)}, u32[]{:S(2)}) collective-permute-start(bf16[1376,128]{1,0:T(8,128)(2,1)} %get-tuple-element.41.own_ref), channel_id=1, source_target_pairs={{0,1},{1,0},{2,3},{3,2},{4,5},{5,4},{6,7},{7,6},{8,9},{9,8},{10,11... | collective-permute-start | bytes 1056776 | tf_op jit(solution)/shard_map/ppermute | solution.py:474
  38.1 2.6 %collective-permute-start.4 = (bf16[400,128]{1,0:T(8,128)(2,1)S(1)}, bf16[400,128]{1,0:T(8,128)(2,1)S(1)}, u32[]{:S(2)}, u32[]{:S(2)}) collective-permute-start(bf16[400,128]{1,0:T(8,128)(2,1)S(1)} %collective-permute-done.far_ref), channel_id=1, source_target_pairs={{0,4},{1,5},{2,6},{3,7},{4,0},{5,1},{6,2},{7,3},{8,12},{9,13},{10,... | collective-permute-start | bytes 307208 | tf_op jit(solution)/shard_map/ppermute | solution.py:474
  40.8 5.8 %collective-permute-start.5 = (bf16[400,128]{1,0:T(8,128)(2,1)S(1)}, bf16[400,128]{1,0:T(8,128)(2,1)S(1)}, u32[]{:S(2)}, u32[]{:S(2)}) collective-permute-start(bf16[400,128]{1,0:T(8,128)(2,1)S(1)} %collective-permute-done.far_ref), channel_id=1, source_target_pairs={{0,2},{1,3},{2,0},{3,1},{4,6},{5,7},{6,4},{7,5},{8,10},{9,11},{10,... | collective-permute-start | bytes 307208 | tf_op jit(solution)/shard_map/ppermute | solution.py:474
  46.6 1.9 %collective-permute-start.6 = (bf16[400,128]{1,0:T(8,128)(2,1)S(1)}, bf16[400,128]{1,0:T(8,128)(2,1)S(1)}, u32[]{:S(2)}, u32[]{:S(2)}) collective-permute-start(bf16[400,128]{1,0:T(8,128)(2,1)S(1)} %collective-permute-done.1.near_ref), channel_id=1, source_target_pairs={{0,2},{1,3},{2,0},{3,1},{4,6},{5,7},{6,4},{7,5},{8,10},{9,11},{10,... | collective-permute-start | bytes 307208 | tf_op jit(solution)/shard_map/ppermute | solution.py:474
  48.5 3.4 %collective-permute-start.7 = (bf16[112,128]{1,0:T(8,128)(2,1)S(1)}, bf16[112,128]{1,0:T(8,128)(2,1)S(1)}, u32[]{:S(2)}, u32[]{:S(2)}) collective-permute-start(bf16[112,128]{1,0:T(8,128)(2,1)S(1)} %constant_dynamic-slice_fusion), channel_id=1, source_target_pairs={{0,32},{16,496},{32,64},{48,16},{64,96},{80,48},{96,128},{112,80},... | collective-permute-start | bytes 86024 | tf_op jit(solution)/shard_map/ppermute | solution.py:481
  53.3 2.4 %rotate.3.eg0 = bf16[464,1024]{1,0:T(8,128)(2,1)S(1)} custom-call(s32[1]{0:T(128)} %bitcast.1.z_ref, s32[1]{0:T(128)S(6)} %copy.14.count_ref, bf16[400,128]{1,0:T(8,128)(2,1)S(1)} %copy-done.3, bf16[400,128]{1,0:T(8,128)(2,1)S(1)} %collective-permute-done.far_ref, s32[1,1024]{1,0:T(1,128)S(1)} %bitcast.24, f32[1,1024]{1,0:T(1,128)S(1)} %bitcast.28, ...), custom_call_target="tpu_custom_call" | custom-call | tf_op jit(solution)/shard_map/rotate/pallas_call | solution.py:360
  56.4 1.9 %edge_in.1.xo_ref = bf16[256,1024]{1,0:T(8,128)(2,1)S(1)} custom-call(s32[1]{0:T(128)} %bitcast.h_ref, bf16[400,128]{1,0:T(8,128)(2,1)S(1)} %copy-done.2, bf16[224,128]{1,0:T(8,128)(2,1)S(1)} %collective-permute-done.3.near_ref, bf16[112,128]{1,0:T(8,128)(2,1)S(1)} %collective-permute-done.7.far_ref, s32[1,1024]{1,0:T(1,128)S(1)} %bitcast.32, ...), custom_call_target="tpu_custom_call" | custom-call | flops 1 | bytes 1 | tf_op jit(solution)/shard_map/edge_in/pallas_call | solution.py:527
  58.9 1.9 %collective-permute-start.10 = (bf16[256,1024]{1,0:T(8,128)(2,1)S(1)}, bf16[256,1024]{1,0:T(8,128)(2,1)S(1)}, u32[]{:S(2)}, u32[]{:S(2)}) collective-permute-start(bf16[256,1024]{1,0:T(8,128)(2,1)S(1)} %edge_in.1.xo_ref), channel_id=1, source_target_pairs={{0,1},{1,0},{2,3},{3,2},{4,5},{5,4},{6,7},{7,6},{8,9},{9,8},{10,11... | collective-permute-start | bytes 1572872 | tf_op jit(solution)/shard_map/ppermute | solution.py:474
  60.8 3.9 %collective-permute-start.9 = (bf16[400,128]{1,0:T(8,128)(2,1)S(1)}, bf16[400,128]{1,0:T(8,128)(2,1)S(1)}, u32[]{:S(2)}, u32[]{:S(2)}) collective-permute-start(bf16[400,128]{1,0:T(8,128)(2,1)S(1)} %collective-permute-done.4.far_ref), channel_id=1, source_target_pairs={{0,2},{1,3},{2,0},{3,1},{4,6},{5,7},{6,4},{7,5},{8,10},{9,11},{10,... | collective-permute-start | bytes 307208 | tf_op jit(solution)/shard_map/ppermute | solution.py:474
  64.8 2.4 %rotate.4.eg2 = bf16[464,1024]{1,0:T(8,128)(2,1)S(1)} custom-call(s32[1]{0:T(128)} %bitcast.1.z_ref, s32[1]{0:T(128)S(6)} %copy.14.count_ref, bf16[400,128]{1,0:T(8,128)(2,1)S(1)} %collective-permute-done.1.near_ref, bf16[400,128]{1,0:T(8,128)(2,1)S(1)} %collective-permute-done.4.far_ref, s32[1,1024]{1,0:T(1,128)S(1)} %bitcast.25, f32[1,1024]{1,0:T(1,128)S(1)} %bitcast.29, ...), custom_call_target="tpu_custom_call" | custom-call | tf_op jit(solution)/shard_map/rotate/pallas_call | solution.py:360
  67.2 2.4 %rotate.5.eg1 = bf16[464,1024]{1,0:T(8,128)(2,1)S(1)} custom-call(s32[1]{0:T(128)} %bitcast.1.z_ref, s32[1]{0:T(128)S(6)} %copy.14.count_ref, bf16[400,128]{1,0:T(8,128)(2,1)S(1)} %collective-permute-done.2.near_ref, bf16[400,128]{1,0:T(8,128)(2,1)S(1)} %collective-permute-done.5.far_ref, s32[1,1024]{1,0:T(1,128)S(1)} %bitcast.26, f32[1,1024]{1,0:T(1,128)S(1)} %bitcast.30, ...), custom_call_target="tpu_custom_call" | custom-call | tf_op jit(solution)/shard_map/rotate/pallas_call | solution.py:360
  69.6 7.9 %edge.1 = (bf16[1024,128]{1,0:T(8,128)(2,1)S(1)}, f32[624,128]{1,0:T(8,128)S(1)}, bf16[1648,128]{1,0:T(8,128)(2,1)S(1)}) custom-call(s32[1]{0:T(128)} %bitcast.1.z_ref, s32[1]{0:T(128)S(6)} %copy.14.count_ref, bf16[464,1024]{1,0:T(8,128)(2,1)S(1)} %rotate.3.eg0, bf16[464,1024]{1,0:T(8,128)(2,1)S(1)} %rotate.4.eg2, bf16[464,1024]{1,0:T(8,128)(2,1)S(1)} %rotate.5.eg1, ...), custom_call_target="tpu_custom_call" | custom-call | tf_op jit(solution)/shard_map/edge/pallas_call | solution.py:375
  77.6 2.1 %collective-permute-start.11 = (bf16[1648,128]{1,0:T(8,128)(2,1)S(1)}, bf16[1648,128]{1,0:T(8,128)(2,1)S(1)}, u32[]{:S(2)}, u32[]{:S(2)}) collective-permute-start(bf16[1648,128]{1,0:T(8,128)(2,1)S(1)} %get-tuple-element.55), channel_id=1, source_target_pairs={{0,1},{1,0},{2,3},{3,2},{4,5},{5,4},{6,7},{7,6},{8,9},{9,8},{10,11... | collective-permute-start | bytes 1265672 | tf_op jit(solution)/shard_map/ppermute | solution.py:474
  82.1 7.2 %all-to-all-start = ((bf16[16,128,128]{2,1,0:T(8,128)(2,1)}), bf16[16,128,128]{2,1,0:T(8,128)(2,1)S(1)}, u32[]{:S(2)}, u32[]{:S(2)}) async-start(bf16[16,128,128]{2,1,0:T(8,128)(2,1)} %pad_maximum_fusion), calls=%async_computation | async-start | bytes 1048576 | tf_op jit(solution)/shard_map/all_to_all | solution.py:556
  89.4 2.0 %collective-permute-start.12 = (bf16[112,128]{1,0:T(8,128)(2,1)S(1)}, bf16[112,128]{1,0:T(8,128)(2,1)S(1)}, u32[]{:S(2)}, u32[]{:S(2)}) collective-permute-start(bf16[112,128]{1,0:T(8,128)(2,1)S(1)} %get-tuple-element.65), channel_id=1, source_target_pairs={{0,480},{16,48},{32,0},{48,80},{64,32},{80,112},{96,64},{112,144},... | collective-permute-start | bytes 86024 | tf_op jit(solution)/shard_map/ppermute | solution.py:481
  91.5 8.3 %all-to-all-done = bf16[16,128,128]{2,1,0:T(8,128)(2,1)S(1)} async-done(((bf16[16,128,128]{2,1,0:T(8,128)(2,1)}), bf16[16,128,128]{2,1,0:T(8,128)(2,1)S(1)}, u32[]{:S(2)}, u32[]{:S(2)}) %all-to-all-start) | async-done | bytes 524320 | tf_op jit(solution)/shard_map/all_to_all | solution.py:556
  99.9 10.5 %collective-permute-start.13 = (bf16[288,128]{1,0:T(8,128)(2,1)S(1)}, bf16[288,128]{1,0:T(8,128)(2,1)S(1)}, u32[]{:S(2)}, u32[]{:S(2)}) collective-permute-start(bf16[288,128]{1,0:T(8,128)(2,1)S(1)} %pad_maximum_fusion.1), channel_id=1, source_target_pairs={{0,16},{16,0},{32,48},{48,32},{64,80},{80,64},{96,112},{112,96},{1... | collective-permute-start | bytes 221192 | tf_op jit(solution)/shard_map/ppermute | solution.py:477
  110.4 6.0 %collective-permute-done.13.rim_ref.got_ref = bf16[288,128]{1,0:T(8,128)(2,1)S(1)} collective-permute-done((bf16[288,128]{1,0:T(8,128)(2,1)S(1)}, bf16[288,128]{1,0:T(8,128)(2,1)S(1)}, u32[]{:S(2)}, u32[]{:S(2)}) %collective-permute-start.13) | collective-permute-done | bytes 73760 | tf_op jit(solution)/shard_map/ppermute | solution.py:477
  (38 shorter events, 6.3 us)
Async XLA Ops:
  0.6 52.0 %copy-start = (bf16[235,1024]{1,0:T(8,128)(2,1)S(1)}, bf16[235,1024]{1,0:T(8,128)(2,1)}, u32[]{:S(2)}) copy-start(bf16[235,1024]{1,0:T(8,128)(2,1)} %wig_ref.9) | copy-start | bytes 1443844
  2.9 49.7 %copy-start.3 = (bf16[400,128]{1,0:T(8,128)(2,1)S(1)}, bf16[400,128]{1,0:T(8,128)(2,1)}, u32[]{:S(2)}) copy-start(bf16[400,128]{1,0:T(8,128)(2,1)} %get-tuple-element.32.near_ref) | copy-start | bytes 307204
  2.9 33.2 %collective-permute-start = (bf16[400,128]{1,0:T(8,128)(2,1)}, bf16[400,128]{1,0:T(8,128)(2,1)S(1)}, u32[]{:S(2)}, u32[]{:S(2)}) collective-permute-start(bf16[400,128]{1,0:T(8,128)(2,1)} %get-tuple-element.32.near_ref), channel_id=1, source_target_pairs={{0,8},{1,9},{2,10},{3,11},{4,12},{5,13},{6,14},{7,15},{8,0},{9,1},... | collective-permute-start | bytes 307208 | tf_op jit(solution)/shard_map/ppermute | solution.py:474
  12.1 24.0 %collective-permute-start.1 = (bf16[400,128]{1,0:T(8,128)(2,1)}, bf16[400,128]{1,0:T(8,128)(2,1)S(1)}, u32[]{:S(2)}, u32[]{:S(2)}) collective-permute-start(bf16[400,128]{1,0:T(8,128)(2,1)} %get-tuple-element.32.near_ref), channel_id=1, source_target_pairs={{0,4},{1,5},{2,6},{3,7},{4,0},{5,1},{6,2},{7,3},{8,12},{9,13},{10,... | collective-permute-start | bytes 307208 | tf_op jit(solution)/shard_map/ppermute | solution.py:474
  17.3 18.8 %collective-permute-start.2 = (bf16[400,128]{1,0:T(8,128)(2,1)}, bf16[400,128]{1,0:T(8,128)(2,1)S(1)}, u32[]{:S(2)}, u32[]{:S(2)}) collective-permute-start(bf16[400,128]{1,0:T(8,128)(2,1)} %get-tuple-element.32.near_ref), channel_id=1, source_target_pairs={{0,2},{1,3},{2,0},{3,1},{4,6},{5,7},{6,4},{7,5},{8,10},{9,11},{10,... | collective-permute-start | bytes 307208 | tf_op jit(solution)/shard_map/ppermute | solution.py:474
  21.2 15.0 %collective-permute-start.3 = (bf16[224,128]{1,0:T(8,128)(2,1)}, bf16[224,128]{1,0:T(8,128)(2,1)S(1)}, u32[]{:S(2)}, u32[]{:S(2)}) collective-permute-start(bf16[224,128]{1,0:T(8,128)(2,1)} %get-tuple-element.33), channel_id=1, source_target_pairs={{0,16},{16,0},{32,48},{48,32},{64,80},{80,64},{96,112},{112,96},{1... | collective-permute-start | bytes 172040 | tf_op jit(solution)/shard_map/ppermute | solution.py:477
  36.2 22.1 %collective-permute-start.8 = (bf16[1376,128]{1,0:T(8,128)(2,1)}, bf16[1376,128]{1,0:T(8,128)(2,1)S(1)}, u32[]{:S(2)}, u32[]{:S(2)}) collective-permute-start(bf16[1376,128]{1,0:T(8,128)(2,1)} %get-tuple-element.41.own_ref), channel_id=1, source_target_pairs={{0,1},{1,0},{2,3},{3,2},{4,5},{5,4},{6,7},{7,6},{8,9},{9,8},{10,11... | collective-permute-start | bytes 1056776 | tf_op jit(solution)/shard_map/ppermute | solution.py:474
  38.1 20.8 %collective-permute-start.4 = (bf16[400,128]{1,0:T(8,128)(2,1)S(1)}, bf16[400,128]{1,0:T(8,128)(2,1)S(1)}, u32[]{:S(2)}, u32[]{:S(2)}) collective-permute-start(bf16[400,128]{1,0:T(8,128)(2,1)S(1)} %collective-permute-done.far_ref), channel_id=1, source_target_pairs={{0,4},{1,5},{2,6},{3,7},{4,0},{5,1},{6,2},{7,3},{8,12},{9,13},{10,... | collective-permute-start | bytes 307208 | tf_op jit(solution)/shard_map/ppermute | solution.py:474
  40.8 18.1 %collective-permute-start.5 = (bf16[400,128]{1,0:T(8,128)(2,1)S(1)}, bf16[400,128]{1,0:T(8,128)(2,1)S(1)}, u32[]{:S(2)}, u32[]{:S(2)}) collective-permute-start(bf16[400,128]{1,0:T(8,128)(2,1)S(1)} %collective-permute-done.far_ref), channel_id=1, source_target_pairs={{0,2},{1,3},{2,0},{3,1},{4,6},{5,7},{6,4},{7,5},{8,10},{9,11},{10,... | collective-permute-start | bytes 307208 | tf_op jit(solution)/shard_map/ppermute | solution.py:474
  46.6 12.3 %collective-permute-start.6 = (bf16[400,128]{1,0:T(8,128)(2,1)S(1)}, bf16[400,128]{1,0:T(8,128)(2,1)S(1)}, u32[]{:S(2)}, u32[]{:S(2)}) collective-permute-start(bf16[400,128]{1,0:T(8,128)(2,1)S(1)} %collective-permute-done.1.near_ref), channel_id=1, source_target_pairs={{0,2},{1,3},{2,0},{3,1},{4,6},{5,7},{6,4},{7,5},{8,10},{9,11},{10,... | collective-permute-start | bytes 307208 | tf_op jit(solution)/shard_map/ppermute | solution.py:474
  48.5 7.2 %collective-permute-start.7 = (bf16[112,128]{1,0:T(8,128)(2,1)S(1)}, bf16[112,128]{1,0:T(8,128)(2,1)S(1)}, u32[]{:S(2)}, u32[]{:S(2)}) collective-permute-start(bf16[112,128]{1,0:T(8,128)(2,1)S(1)} %constant_dynamic-slice_fusion), channel_id=1, source_target_pairs={{0,32},{16,496},{32,64},{48,16},{64,96},{80,48},{96,128},{112,80},... | collective-permute-start | bytes 86024 | tf_op jit(solution)/shard_map/ppermute | solution.py:481
  52.6 0.7 copy-start.5
  52.6 0.7 copy-start.4
  53.3 2.4 %copy-start.2 = (bf16[400,128]{1,0:T(8,128)(2,1)S(1)}, bf16[400,128]{1,0:T(8,128)(2,1)}, u32[]{:S(2)}) copy-start(bf16[400,128]{1,0:T(8,128)(2,1)} %get-tuple-element.37.node_ref) | copy-start | bytes 307204
  55.7 0.7 copy-start.6
  56.4 1.9 %copy-start.1 = (bf16[1376,128]{1,0:T(8,128)(2,1)S(1)}, bf16[1376,128]{1,0:T(8,128)(2,1)}, u32[]{:S(2)}) copy-start(bf16[1376,128]{1,0:T(8,128)(2,1)} %get-tuple-element.41.own_ref) | copy-start | bytes 1056772
  58.9 10.7 %collective-permute-start.10 = (bf16[256,1024]{1,0:T(8,128)(2,1)S(1)}, bf16[256,1024]{1,0:T(8,128)(2,1)S(1)}, u32[]{:S(2)}, u32[]{:S(2)}) collective-permute-start(bf16[256,1024]{1,0:T(8,128)(2,1)S(1)} %edge_in.1.xo_ref), channel_id=1, source_target_pairs={{0,1},{1,0},{2,3},{3,2},{4,5},{5,4},{6,7},{7,6},{8,9},{9,8},{10,11... | collective-permute-start | bytes 1572872 | tf_op jit(solution)/shard_map/ppermute | solution.py:474
  60.8 8.8 %collective-permute-start.9 = (bf16[400,128]{1,0:T(8,128)(2,1)S(1)}, bf16[400,128]{1,0:T(8,128)(2,1)S(1)}, u32[]{:S(2)}, u32[]{:S(2)}) collective-permute-start(bf16[400,128]{1,0:T(8,128)(2,1)S(1)} %collective-permute-done.4.far_ref), channel_id=1, source_target_pairs={{0,2},{1,3},{2,0},{3,1},{4,6},{5,7},{6,4},{7,5},{8,10},{9,11},{10,... | collective-permute-start | bytes 307208 | tf_op jit(solution)/shard_map/ppermute | solution.py:474
  77.6 3.7 %collective-permute-start.11 = (bf16[1648,128]{1,0:T(8,128)(2,1)S(1)}, bf16[1648,128]{1,0:T(8,128)(2,1)S(1)}, u32[]{:S(2)}, u32[]{:S(2)}) collective-permute-start(bf16[1648,128]{1,0:T(8,128)(2,1)S(1)} %get-tuple-element.55), channel_id=1, source_target_pairs={{0,1},{1,0},{2,3},{3,2},{4,5},{5,4},{6,7},{7,6},{8,9},{9,8},{10,11... | collective-permute-start | bytes 1265672 | tf_op jit(solution)/shard_map/ppermute | solution.py:474
  82.1 17.6 %all-to-all-start = ((bf16[16,128,128]{2,1,0:T(8,128)(2,1)}), bf16[16,128,128]{2,1,0:T(8,128)(2,1)S(1)}, u32[]{:S(2)}, u32[]{:S(2)}) async-start(bf16[16,128,128]{2,1,0:T(8,128)(2,1)} %pad_maximum_fusion), calls=%async_computation | async-start | bytes 1048576 | tf_op jit(solution)/shard_map/all_to_all | solution.py:556
  89.4 10.4 %collective-permute-start.12 = (bf16[112,128]{1,0:T(8,128)(2,1)S(1)}, bf16[112,128]{1,0:T(8,128)(2,1)S(1)}, u32[]{:S(2)}, u32[]{:S(2)}) collective-permute-start(bf16[112,128]{1,0:T(8,128)(2,1)S(1)} %get-tuple-element.65), channel_id=1, source_target_pairs={{0,480},{16,48},{32,0},{48,80},{64,32},{80,112},{96,64},{112,144},... | collective-permute-start | bytes 86024 | tf_op jit(solution)/shard_map/ppermute | solution.py:481
  99.9 16.5 %collective-permute-start.13 = (bf16[288,128]{1,0:T(8,128)(2,1)S(1)}, bf16[288,128]{1,0:T(8,128)(2,1)S(1)}, u32[]{:S(2)}, u32[]{:S(2)}) collective-permute-start(bf16[288,128]{1,0:T(8,128)(2,1)S(1)} %pad_maximum_fusion.1), channel_id=1, source_target_pairs={{0,16},{16,0},{32,48},{48,32},{64,80},{80,64},{96,112},{112,96},{1... | collective-permute-start | bytes 221192 | tf_op jit(solution)/shard_map/ppermute | solution.py:477

commit v8 on v7

--- a/solution.py
+++ b/solution.py
@@ -503,11 +503,11 @@
     b4 = across(b0, 8)
     b2 = across(b0, 4)
     b1 = across(b0, 2)
-    b4, b2, b1, near, w_own = lax.optimization_barrier((b4, b2, b1, near, w_own))
+    far = shift(lax.dynamic_slice_in_dim(near, 112 * high, 112, 0), True)
+    b4, b2, b1, far, w_own = lax.optimization_barrier((b4, b2, b1, far, w_own))
     b6 = across(b4, 4)
     b5 = across(b4, 2)
     b3 = across(b2, 2)
-    far = shift(lax.dynamic_slice_in_dim(near, 112 * high, 112, 0), True)
     eg0 = rotated(b0, b4)
     far, eg0 = lax.optimization_barrier((far, eg0))
 

time: 119 us -> 115 us (0.966)
  starting transfers between devices: 69.8 us -> 66.1 us
    ppermute x10, starting transfers between devices: 38.5 us -> 29.1 us  [across(): return lax.ppermute(x, 'chan', [(i, i ^ mask) for i in range(16)])]
    ppermute x2, starting transfers between devices: 18.7 us -> 24.1 us  [cross(): return lax.ppermute(x, 'brick', [(i, i ^ 1) for i in range(32)])]
    ppermute x2, waiting for transfers between devices: 12.8 us -> 9.01 us  [cross(): return lax.ppermute(x, 'brick', [(i, i ^ 1) for i in range(32)])]
    ppermute x2, waiting for transfers between devices: 0.01 us -> 2.36 us  [shift(): return lax.ppermute(x, 'brick', route)]
  transfers between devices with their start and end apart: 15 -> 15, of which waited for: 4 -> 6; matrix products, arithmetic and copies ran while one was open for 0% -> 0% of each run, Pallas kernels for 8% -> 8%
where the time goes in v8:
time: 115 us; the launch traced here: 114 us
  starting transfers between devices  66.1 us (57%)
  waiting for transfers between devices  22.3 us (19%)
  Pallas kernels  21.7 us (19%)
  between operations  1.65 us (1%)
  local copies, waits for them, and re-layouts  1.36 us (1%)
    ppermute x10, starting transfers between devices, across(): return lax.ppermute(x, 'chan', [(i, i ^ mask) for i in range(16)])  29.1 us
    ppermute x2, starting transfers between devices, cross(): return lax.ppermute(x, 'brick', [(i, i ^ 1) for i in range(32)])  24.1 us
    ppermute x2, waiting for transfers between devices, cross(): return lax.ppermute(x, 'brick', [(i, i ^ 1) for i in range(32)])  9.01 us
    all_to_all x1, waiting for transfers between devices, body(): pieces = lax.all_to_all(send, 'brick', 0, 0, axis_index_groups=groups)  8.25 us
    pallas_call x1, Pallas kernels, edge_call(): pl.pallas_call(edge_kernel, out_shape=(sds((1024, 128), BF), sds((624, 12...  7.92 us
    all_to_all x1, starting transfers between devices, body(): pieces = lax.all_to_all(send, 'brick', 0, 0, axis_index_groups=groups)  7.48 us
    pallas_call x3, Pallas kernels, rotate_call(): pl.pallas_call(rotate_kernel, out_shape=sds((464, slots), BF), grid=(slot...  7.24 us
    ppermute x2, starting transfers between devices, shift(): return lax.ppermute(x, 'brick', route)  5.41 us
  transfers between devices with their start and end apart: 15, of which 6 were waited for; matrix products, arithmetic and copies ran while one was open for 0% of the time, Pallas kernels for 8%

profile of v8, /device:TPU:2, one launch (start us, length us, event | category | flops | bytes accessed | tf_op | source)
XLA Modules:
  0.0 114.1 jit_solution(9122015552929869575)
XLA Ops:
  0.6 2.3 %pack.1 = (bf16[400,128]{1,0:T(8,128)(2,1)}, bf16[400,128]{1,0:T(8,128)(2,1)}, bf16[224,128]{1,0:T(8,128)(2,1)}, bf16[1376,128]{1,0:T(8,128)(2,1)}) custom-call(bf16[49,8,128]{2,1,0:T(8,128)(2,1)} %node_ref.1, bf16[49,8,128]{2,1,0:T(8,128)(2,1)} %cot_ref.1, bf16[49,8,128]{2,1,0:T(8,128)(2,1)} %bitcast.40, bf16[72,8,128]{2,1,0:T(8,128)(2,1)} %bitcast.38, ...), custom_call_target="tpu_custom_call" | custom-call | flops 1 | bytes 1 | tf_op jit(solution)/shard_map/pack/pallas_call | solution.py:488
  2.9 15.8 %collective-permute-start.3 = (bf16[224,128]{1,0:T(8,128)(2,1)}, bf16[224,128]{1,0:T(8,128)(2,1)S(1)}, u32[]{:S(2)}, u32[]{:S(2)}) collective-permute-start(bf16[224,128]{1,0:T(8,128)(2,1)} %get-tuple-element.33), channel_id=1, source_target_pairs={{0,16},{16,0},{32,48},{48,32},{64,80},{80,64},{96,112},{112,96},{1... | collective-permute-start | bytes 172040 | tf_op jit(solution)/shard_map/ppermute | solution.py:477
  18.8 4.3 %collective-permute-start = (bf16[400,128]{1,0:T(8,128)(2,1)}, bf16[400,128]{1,0:T(8,128)(2,1)S(1)}, u32[]{:S(2)}, u32[]{:S(2)}) collective-permute-start(bf16[400,128]{1,0:T(8,128)(2,1)} %get-tuple-element.32.near_ref), channel_id=1, source_target_pairs={{0,8},{1,9},{2,10},{3,11},{4,12},{5,13},{6,14},{7,15},{8,0},{9,1},... | collective-permute-start | bytes 307208 | tf_op jit(solution)/shard_map/ppermute | solution.py:474
  23.1 3.4 %collective-permute-start.1 = (bf16[400,128]{1,0:T(8,128)(2,1)}, bf16[400,128]{1,0:T(8,128)(2,1)S(1)}, u32[]{:S(2)}, u32[]{:S(2)}) collective-permute-start(bf16[400,128]{1,0:T(8,128)(2,1)} %get-tuple-element.32.near_ref), channel_id=1, source_target_pairs={{0,4},{1,5},{2,6},{3,7},{4,0},{5,1},{6,2},{7,3},{8,12},{9,13},{10,... | collective-permute-start | bytes 307208 | tf_op jit(solution)/shard_map/ppermute | solution.py:474
  26.5 2.9 %collective-permute-start.2 = (bf16[400,128]{1,0:T(8,128)(2,1)}, bf16[400,128]{1,0:T(8,128)(2,1)S(1)}, u32[]{:S(2)}, u32[]{:S(2)}) collective-permute-start(bf16[400,128]{1,0:T(8,128)(2,1)} %get-tuple-element.32.near_ref), channel_id=1, source_target_pairs={{0,2},{1,3},{2,0},{3,1},{4,6},{5,7},{6,4},{7,5},{8,10},{9,11},{10,... | collective-permute-start | bytes 307208 | tf_op jit(solution)/shard_map/ppermute | solution.py:474
  29.4 3.4 %collective-permute-start.4 = (bf16[112,128]{1,0:T(8,128)(2,1)S(1)}, bf16[112,128]{1,0:T(8,128)(2,1)S(1)}, u32[]{:S(2)}, u32[]{:S(2)}) collective-permute-start(bf16[112,128]{1,0:T(8,128)(2,1)S(1)} %constant_dynamic-slice_fusion), channel_id=1, source_target_pairs={{0,32},{16,496},{32,64},{48,16},{64,96},{80,48},{96,128},{112,80},... | collective-permute-start | bytes 86024 | tf_op jit(solution)/shard_map/ppermute | solution.py:481
  32.8 2.4 %collective-permute-done.4.far_ref = bf16[112,128]{1,0:T(8,128)(2,1)S(1)} collective-permute-done((bf16[112,128]{1,0:T(8,128)(2,1)S(1)}, bf16[112,128]{1,0:T(8,128)(2,1)S(1)}, u32[]{:S(2)}, u32[]{:S(2)}) %collective-permute-start.4) | collective-permute-done | bytes 28704 | tf_op jit(solution)/shard_map/ppermute | solution.py:481
  35.9 1.9 %collective-permute-start.8 = (bf16[1376,128]{1,0:T(8,128)(2,1)}, bf16[1376,128]{1,0:T(8,128)(2,1)S(1)}, u32[]{:S(2)}, u32[]{:S(2)}) collective-permute-start(bf16[1376,128]{1,0:T(8,128)(2,1)} %get-tuple-element.41.own_ref), channel_id=1, source_target_pairs={{0,1},{1,0},{2,3},{3,2},{4,5},{5,4},{6,7},{7,6},{8,9},{9,8},{10,11... | collective-permute-start | bytes 1056776 | tf_op jit(solution)/shard_map/ppermute | solution.py:474
  37.8 4.8 %collective-permute-start.5 = (bf16[400,128]{1,0:T(8,128)(2,1)S(1)}, bf16[400,128]{1,0:T(8,128)(2,1)S(1)}, u32[]{:S(2)}, u32[]{:S(2)}) collective-permute-start(bf16[400,128]{1,0:T(8,128)(2,1)S(1)} %collective-permute-done.far_ref), channel_id=1, source_target_pairs={{0,4},{1,5},{2,6},{3,7},{4,0},{5,1},{6,2},{7,3},{8,12},{9,13},{10,... | collective-permute-start | bytes 307208 | tf_op jit(solution)/shard_map/ppermute | solution.py:474
  42.6 1.9 %collective-permute-start.6 = (bf16[400,128]{1,0:T(8,128)(2,1)S(1)}, bf16[400,128]{1,0:T(8,128)(2,1)S(1)}, u32[]{:S(2)}, u32[]{:S(2)}) collective-permute-start(bf16[400,128]{1,0:T(8,128)(2,1)S(1)} %collective-permute-done.far_ref), channel_id=1, source_target_pairs={{0,2},{1,3},{2,0},{3,1},{4,6},{5,7},{6,4},{7,5},{8,10},{9,11},{10,... | collective-permute-start | bytes 307208 | tf_op jit(solution)/shard_map/ppermute | solution.py:474
  44.5 3.9 %collective-permute-start.7 = (bf16[400,128]{1,0:T(8,128)(2,1)S(1)}, bf16[400,128]{1,0:T(8,128)(2,1)S(1)}, u32[]{:S(2)}, u32[]{:S(2)}) collective-permute-start(bf16[400,128]{1,0:T(8,128)(2,1)S(1)} %collective-permute-done.1.near_ref), channel_id=1, source_target_pairs={{0,2},{1,3},{2,0},{3,1},{4,6},{5,7},{6,4},{7,5},{8,10},{9,11},{10,... | collective-permute-start | bytes 307208 | tf_op jit(solution)/shard_map/ppermute | solution.py:474
  49.8 2.4 %rotate.3.eg0 = bf16[464,1024]{1,0:T(8,128)(2,1)S(1)} custom-call(s32[1]{0:T(128)} %bitcast.1.z_ref, s32[1]{0:T(128)S(6)} %copy.14.count_ref, bf16[400,128]{1,0:T(8,128)(2,1)S(1)} %copy-done.3, bf16[400,128]{1,0:T(8,128)(2,1)S(1)} %collective-permute-done.far_ref, s32[1,1024]{1,0:T(1,128)S(1)} %bitcast.24, f32[1,1024]{1,0:T(1,128)S(1)} %bitcast.28, ...), custom_call_target="tpu_custom_call" | custom-call | tf_op jit(solution)/shard_map/rotate/pallas_call | solution.py:360
  52.9 1.9 %edge_in.1.xo_ref = bf16[256,1024]{1,0:T(8,128)(2,1)S(1)} custom-call(s32[1]{0:T(128)} %bitcast.h_ref, bf16[400,128]{1,0:T(8,128)(2,1)S(1)} %copy-done.2, bf16[224,128]{1,0:T(8,128)(2,1)S(1)} %collective-permute-done.3.near_ref, bf16[112,128]{1,0:T(8,128)(2,1)S(1)} %collective-permute-done.4.far_ref, s32[1,1024]{1,0:T(1,128)S(1)} %bitcast.32, ...), custom_call_target="tpu_custom_call" | custom-call | flops 1 | bytes 1 | tf_op jit(solution)/shard_map/edge_in/pallas_call | solution.py:527
  55.4 1.9 %collective-permute-start.10 = (bf16[256,1024]{1,0:T(8,128)(2,1)S(1)}, bf16[256,1024]{1,0:T(8,128)(2,1)S(1)}, u32[]{:S(2)}, u32[]{:S(2)}) collective-permute-start(bf16[256,1024]{1,0:T(8,128)(2,1)S(1)} %edge_in.1.xo_ref), channel_id=1, source_target_pairs={{0,1},{1,0},{2,3},{3,2},{4,5},{5,4},{6,7},{7,6},{8,9},{9,8},{10,11... | collective-permute-start | bytes 1572872 | tf_op jit(solution)/shard_map/ppermute | solution.py:474
  57.4 1.9 %collective-permute-start.9 = (bf16[400,128]{1,0:T(8,128)(2,1)S(1)}, bf16[400,128]{1,0:T(8,128)(2,1)S(1)}, u32[]{:S(2)}, u32[]{:S(2)}) collective-permute-start(bf16[400,128]{1,0:T(8,128)(2,1)S(1)} %collective-permute-done.5.far_ref), channel_id=1, source_target_pairs={{0,2},{1,3},{2,0},{3,1},{4,6},{5,7},{6,4},{7,5},{8,10},{9,11},{10,... | collective-permute-start | bytes 307208 | tf_op jit(solution)/shard_map/ppermute | solution.py:474
  59.3 2.4 %rotate.4.eg2 = bf16[464,1024]{1,0:T(8,128)(2,1)S(1)} custom-call(s32[1]{0:T(128)} %bitcast.1.z_ref, s32[1]{0:T(128)S(6)} %copy.14.count_ref, bf16[400,128]{1,0:T(8,128)(2,1)S(1)} %collective-permute-done.1.near_ref, bf16[400,128]{1,0:T(8,128)(2,1)S(1)} %collective-permute-done.5.far_ref, s32[1,1024]{1,0:T(1,128)S(1)} %bitcast.25, f32[1,1024]{1,0:T(1,128)S(1)} %bitcast.29, ...), custom_call_target="tpu_custom_call" | custom-call | tf_op jit(solution)/shard_map/rotate/pallas_call | solution.py:360
  61.7 2.4 %rotate.5.eg1 = bf16[464,1024]{1,0:T(8,128)(2,1)S(1)} custom-call(s32[1]{0:T(128)} %bitcast.1.z_ref, s32[1]{0:T(128)S(6)} %copy.14.count_ref, bf16[400,128]{1,0:T(8,128)(2,1)S(1)} %collective-permute-done.2.near_ref, bf16[400,128]{1,0:T(8,128)(2,1)S(1)} %collective-permute-done.6.far_ref, s32[1,1024]{1,0:T(1,128)S(1)} %bitcast.26, f32[1,1024]{1,0:T(1,128)S(1)} %bitcast.30, ...), custom_call_target="tpu_custom_call" | custom-call | tf_op jit(solution)/shard_map/rotate/pallas_call | solution.py:360
  64.6 7.9 %edge.1 = (bf16[1024,128]{1,0:T(8,128)(2,1)S(1)}, f32[624,128]{1,0:T(8,128)S(1)}, bf16[1648,128]{1,0:T(8,128)(2,1)S(1)}) custom-call(s32[1]{0:T(128)} %bitcast.1.z_ref, s32[1]{0:T(128)S(6)} %copy.14.count_ref, bf16[464,1024]{1,0:T(8,128)(2,1)S(1)} %rotate.3.eg0, bf16[464,1024]{1,0:T(8,128)(2,1)S(1)} %rotate.4.eg2, bf16[464,1024]{1,0:T(8,128)(2,1)S(1)} %rotate.5.eg1, ...), custom_call_target="tpu_custom_call" | custom-call | tf_op jit(solution)/shard_map/edge/pallas_call | solution.py:375
  72.5 2.1 %collective-permute-start.11 = (bf16[1648,128]{1,0:T(8,128)(2,1)S(1)}, bf16[1648,128]{1,0:T(8,128)(2,1)S(1)}, u32[]{:S(2)}, u32[]{:S(2)}) collective-permute-start(bf16[1648,128]{1,0:T(8,128)(2,1)S(1)} %get-tuple-element.55), channel_id=1, source_target_pairs={{0,1},{1,0},{2,3},{3,2},{4,5},{5,4},{6,7},{7,6},{8,9},{9,8},{10,11... | collective-permute-start | bytes 1265672 | tf_op jit(solution)/shard_map/ppermute | solution.py:474
  77.0 7.5 %all-to-all-start = ((bf16[16,128,128]{2,1,0:T(8,128)(2,1)}), bf16[16,128,128]{2,1,0:T(8,128)(2,1)S(1)}, u32[]{:S(2)}, u32[]{:S(2)}) async-start(bf16[16,128,128]{2,1,0:T(8,128)(2,1)} %pad_maximum_fusion), calls=%async_computation | async-start | bytes 1048576 | tf_op jit(solution)/shard_map/all_to_all | solution.py:556
  84.6 2.0 %collective-permute-start.12 = (bf16[112,128]{1,0:T(8,128)(2,1)S(1)}, bf16[112,128]{1,0:T(8,128)(2,1)S(1)}, u32[]{:S(2)}, u32[]{:S(2)}) collective-permute-start(bf16[112,128]{1,0:T(8,128)(2,1)S(1)} %get-tuple-element.65), channel_id=1, source_target_pairs={{0,480},{16,48},{32,0},{48,80},{64,32},{80,112},{96,64},{112,144},... | collective-permute-start | bytes 86024 | tf_op jit(solution)/shard_map/ppermute | solution.py:481
  86.6 8.2 %all-to-all-done = bf16[16,128,128]{2,1,0:T(8,128)(2,1)S(1)} async-done(((bf16[16,128,128]{2,1,0:T(8,128)(2,1)}), bf16[16,128,128]{2,1,0:T(8,128)(2,1)S(1)}, u32[]{:S(2)}, u32[]{:S(2)}) %all-to-all-start) | async-done | bytes 524320 | tf_op jit(solution)/shard_map/all_to_all | solution.py:556
  95.0 8.3 %collective-permute-start.13 = (bf16[288,128]{1,0:T(8,128)(2,1)S(1)}, bf16[288,128]{1,0:T(8,128)(2,1)S(1)}, u32[]{:S(2)}, u32[]{:S(2)}) collective-permute-start(bf16[288,128]{1,0:T(8,128)(2,1)S(1)} %pad_maximum_fusion.1), channel_id=1, source_target_pairs={{0,16},{16,0},{32,48},{48,32},{64,80},{80,64},{96,112},{112,96},{1... | collective-permute-start | bytes 221192 | tf_op jit(solution)/shard_map/ppermute | solution.py:477
  103.3 9.0 %collective-permute-done.13.rim_ref.got_ref = bf16[288,128]{1,0:T(8,128)(2,1)S(1)} collective-permute-done((bf16[288,128]{1,0:T(8,128)(2,1)S(1)}, bf16[288,128]{1,0:T(8,128)(2,1)S(1)}, u32[]{:S(2)}, u32[]{:S(2)}) %collective-permute-start.13) | collective-permute-done | bytes 73760 | tf_op jit(solution)/shard_map/ppermute | solution.py:477
  (38 shorter events, 7.4 us)
Async XLA Ops:
  0.6 48.5 %copy-start = (bf16[235,1024]{1,0:T(8,128)(2,1)S(1)}, bf16[235,1024]{1,0:T(8,128)(2,1)}, u32[]{:S(2)}) copy-start(bf16[235,1024]{1,0:T(8,128)(2,1)} %wig_ref.9) | copy-start | bytes 1443844
  2.9 46.2 %copy-start.3 = (bf16[400,128]{1,0:T(8,128)(2,1)S(1)}, bf16[400,128]{1,0:T(8,128)(2,1)}, u32[]{:S(2)}) copy-start(bf16[400,128]{1,0:T(8,128)(2,1)} %get-tuple-element.32.near_ref) | copy-start | bytes 307204
  2.9 26.5 %collective-permute-start.3 = (bf16[224,128]{1,0:T(8,128)(2,1)}, bf16[224,128]{1,0:T(8,128)(2,1)S(1)}, u32[]{:S(2)}, u32[]{:S(2)}) collective-permute-start(bf16[224,128]{1,0:T(8,128)(2,1)} %get-tuple-element.33), channel_id=1, source_target_pairs={{0,16},{16,0},{32,48},{48,32},{64,80},{80,64},{96,112},{112,96},{1... | collective-permute-start | bytes 172040 | tf_op jit(solution)/shard_map/ppermute | solution.py:477
  18.8 17.1 %collective-permute-start = (bf16[400,128]{1,0:T(8,128)(2,1)}, bf16[400,128]{1,0:T(8,128)(2,1)S(1)}, u32[]{:S(2)}, u32[]{:S(2)}) collective-permute-start(bf16[400,128]{1,0:T(8,128)(2,1)} %get-tuple-element.32.near_ref), channel_id=1, source_target_pairs={{0,8},{1,9},{2,10},{3,11},{4,12},{5,13},{6,14},{7,15},{8,0},{9,1},... | collective-permute-start | bytes 307208 | tf_op jit(solution)/shard_map/ppermute | solution.py:474
  23.1 12.8 %collective-permute-start.1 = (bf16[400,128]{1,0:T(8,128)(2,1)}, bf16[400,128]{1,0:T(8,128)(2,1)S(1)}, u32[]{:S(2)}, u32[]{:S(2)}) collective-permute-start(bf16[400,128]{1,0:T(8,128)(2,1)} %get-tuple-element.32.near_ref), channel_id=1, source_target_pairs={{0,4},{1,5},{2,6},{3,7},{4,0},{5,1},{6,2},{7,3},{8,12},{9,13},{10,... | collective-permute-start | bytes 307208 | tf_op jit(solution)/shard_map/ppermute | solution.py:474
  26.5 9.4 %collective-permute-start.2 = (bf16[400,128]{1,0:T(8,128)(2,1)}, bf16[400,128]{1,0:T(8,128)(2,1)S(1)}, u32[]{:S(2)}, u32[]{:S(2)}) collective-permute-start(bf16[400,128]{1,0:T(8,128)(2,1)} %get-tuple-element.32.near_ref), channel_id=1, source_target_pairs={{0,2},{1,3},{2,0},{3,1},{4,6},{5,7},{6,4},{7,5},{8,10},{9,11},{10,... | collective-permute-start | bytes 307208 | tf_op jit(solution)/shard_map/ppermute | solution.py:474
  29.4 5.8 %collective-permute-start.4 = (bf16[112,128]{1,0:T(8,128)(2,1)S(1)}, bf16[112,128]{1,0:T(8,128)(2,1)S(1)}, u32[]{:S(2)}, u32[]{:S(2)}) collective-permute-start(bf16[112,128]{1,0:T(8,128)(2,1)S(1)} %constant_dynamic-slice_fusion), channel_id=1, source_target_pairs={{0,32},{16,496},{32,64},{48,16},{64,96},{80,48},{96,128},{112,80},... | collective-permute-start | bytes 86024 | tf_op jit(solution)/shard_map/ppermute | solution.py:481
  35.9 19.0 %collective-permute-start.8 = (bf16[1376,128]{1,0:T(8,128)(2,1)}, bf16[1376,128]{1,0:T(8,128)(2,1)S(1)}, u32[]{:S(2)}, u32[]{:S(2)}) collective-permute-start(bf16[1376,128]{1,0:T(8,128)(2,1)} %get-tuple-element.41.own_ref), channel_id=1, source_target_pairs={{0,1},{1,0},{2,3},{3,2},{4,5},{5,4},{6,7},{7,6},{8,9},{9,8},{10,11... | collective-permute-start | bytes 1056776 | tf_op jit(solution)/shard_map/ppermute | solution.py:474
  37.8 17.6 %collective-permute-start.5 = (bf16[400,128]{1,0:T(8,128)(2,1)S(1)}, bf16[400,128]{1,0:T(8,128)(2,1)S(1)}, u32[]{:S(2)}, u32[]{:S(2)}) collective-permute-start(bf16[400,128]{1,0:T(8,128)(2,1)S(1)} %collective-permute-done.far_ref), channel_id=1, source_target_pairs={{0,4},{1,5},{2,6},{3,7},{4,0},{5,1},{6,2},{7,3},{8,12},{9,13},{10,... | collective-permute-start | bytes 307208 | tf_op jit(solution)/shard_map/ppermute | solution.py:474
  42.6 12.8 %collective-permute-start.6 = (bf16[400,128]{1,0:T(8,128)(2,1)S(1)}, bf16[400,128]{1,0:T(8,128)(2,1)S(1)}, u32[]{:S(2)}, u32[]{:S(2)}) collective-permute-start(bf16[400,128]{1,0:T(8,128)(2,1)S(1)} %collective-permute-done.far_ref), channel_id=1, source_target_pairs={{0,2},{1,3},{2,0},{3,1},{4,6},{5,7},{6,4},{7,5},{8,10},{9,11},{10,... | collective-permute-start | bytes 307208 | tf_op jit(solution)/shard_map/ppermute | solution.py:474
  44.5 10.9 %collective-permute-start.7 = (bf16[400,128]{1,0:T(8,128)(2,1)S(1)}, bf16[400,128]{1,0:T(8,128)(2,1)S(1)}, u32[]{:S(2)}, u32[]{:S(2)}) collective-permute-start(bf16[400,128]{1,0:T(8,128)(2,1)S(1)} %collective-permute-done.1.near_ref), channel_id=1, source_target_pairs={{0,2},{1,3},{2,0},{3,1},{4,6},{5,7},{6,4},{7,5},{8,10},{9,11},{10,... | collective-permute-start | bytes 307208 | tf_op jit(solution)/shard_map/ppermute | solution.py:474
  49.1 0.7 copy-start.5
  49.1 0.7 copy-start.4
  49.8 2.4 %copy-start.2 = (bf16[400,128]{1,0:T(8,128)(2,1)S(1)}, bf16[400,128]{1,0:T(8,128)(2,1)}, u32[]{:S(2)}) copy-start(bf16[400,128]{1,0:T(8,128)(2,1)} %get-tuple-element.37.node_ref) | copy-start | bytes 307204
  52.2 0.7 copy-start.6
  52.9 1.9 %copy-start.1 = (bf16[1376,128]{1,0:T(8,128)(2,1)S(1)}, bf16[1376,128]{1,0:T(8,128)(2,1)}, u32[]{:S(2)}) copy-start(bf16[1376,128]{1,0:T(8,128)(2,1)} %get-tuple-element.41.own_ref) | copy-start | bytes 1056772
  55.4 9.1 %collective-permute-start.10 = (bf16[256,1024]{1,0:T(8,128)(2,1)S(1)}, bf16[256,1024]{1,0:T(8,128)(2,1)S(1)}, u32[]{:S(2)}, u32[]{:S(2)}) collective-permute-start(bf16[256,1024]{1,0:T(8,128)(2,1)S(1)} %edge_in.1.xo_ref), channel_id=1, source_target_pairs={{0,1},{1,0},{2,3},{3,2},{4,5},{5,4},{6,7},{7,6},{8,9},{9,8},{10,11... | collective-permute-start | bytes 1572872 | tf_op jit(solution)/shard_map/ppermute | solution.py:474
  57.4 7.2 %collective-permute-start.9 = (bf16[400,128]{1,0:T(8,128)(2,1)S(1)}, bf16[400,128]{1,0:T(8,128)(2,1)S(1)}, u32[]{:S(2)}, u32[]{:S(2)}) collective-permute-start(bf16[400,128]{1,0:T(8,128)(2,1)S(1)} %collective-permute-done.5.far_ref), channel_id=1, source_target_pairs={{0,2},{1,3},{2,0},{3,1},{4,6},{5,7},{6,4},{7,5},{8,10},{9,11},{10,... | collective-permute-start | bytes 307208 | tf_op jit(solution)/shard_map/ppermute | solution.py:474
  72.5 3.7 %collective-permute-start.11 = (bf16[1648,128]{1,0:T(8,128)(2,1)S(1)}, bf16[1648,128]{1,0:T(8,128)(2,1)S(1)}, u32[]{:S(2)}, u32[]{:S(2)}) collective-permute-start(bf16[1648,128]{1,0:T(8,128)(2,1)S(1)} %get-tuple-element.55), channel_id=1, source_target_pairs={{0,1},{1,0},{2,3},{3,2},{4,5},{5,4},{6,7},{7,6},{8,9},{9,8},{10,11... | collective-permute-start | bytes 1265672 | tf_op jit(solution)/shard_map/ppermute | solution.py:474
  77.0 17.8 %all-to-all-start = ((bf16[16,128,128]{2,1,0:T(8,128)(2,1)}), bf16[16,128,128]{2,1,0:T(8,128)(2,1)S(1)}, u32[]{:S(2)}, u32[]{:S(2)}) async-start(bf16[16,128,128]{2,1,0:T(8,128)(2,1)} %pad_maximum_fusion), calls=%async_computation | async-start | bytes 1048576 | tf_op jit(solution)/shard_map/all_to_all | solution.py:556
  84.6 10.4 %collective-permute-start.12 = (bf16[112,128]{1,0:T(8,128)(2,1)S(1)}, bf16[112,128]{1,0:T(8,128)(2,1)S(1)}, u32[]{:S(2)}, u32[]{:S(2)}) collective-permute-start(bf16[112,128]{1,0:T(8,128)(2,1)S(1)} %get-tuple-element.65), channel_id=1, source_target_pairs={{0,480},{16,48},{32,0},{48,80},{64,32},{80,112},{96,64},{112,144},... | collective-permute-start | bytes 86024 | tf_op jit(solution)/shard_map/ppermute | solution.py:481
  95.0 17.3 %collective-permute-start.13 = (bf16[288,128]{1,0:T(8,128)(2,1)S(1)}, bf16[288,128]{1,0:T(8,128)(2,1)S(1)}, u32[]{:S(2)}, u32[]{:S(2)}) collective-permute-start(bf16[288,128]{1,0:T(8,128)(2,1)S(1)} %pad_maximum_fusion.1), channel_id=1, source_target_pairs={{0,16},{16,0},{32,48},{48,32},{64,80},{80,64},{96,112},{112,96},{1... | collective-permute-start | bytes 221192 | tf_op jit(solution)/shard_map/ppermute | solution.py:477

commit v9 on v8

--- a/solution.py
+++ b/solution.py
@@ -150,8 +150,7 @@
 
     def pick(offset):
         spot = lane - offset
-        block = (spot // 8 % 2) * 4 + spot // 16
-        wanted = block * 16 + k * 8 + spot % 8
+        wanted = (spot // 8) * 16 + k * 8 + spot % 8
         return hot((spot >= 0) & (spot < 64) & (chan == wanted))
 
     low, high = pick(0), pick(64)
@@ -193,8 +192,8 @@
 
 
 def rotate_pair(z, near_ref, far_ref, dest, rot, gathered, store):
-    gathered[z // 4] = mm(near_ref[...], dest)
-    gathered[1 - z // 4] = mm(far_ref[...], dest)
+    gathered[z % 2] = mm(near_ref[...], dest)
+    gathered[1 - z % 2] = mm(far_ref[...], dest)
     for half in range(EB // LANES):
         lanes = slice(half * LANES, half * LANES + LANES)
         for degree in range(7):
@@ -221,18 +220,22 @@
     return jnp.where(slot < count_ref[0], 0.25 * scale_ref[...], 0.0)
 
 
-def rotate_kernel(z_ref, count_ref, near_ref, far_ref, dst_ref, scale_ref, wig_ref, eg_ref, gathered, rot):
+def rotate_kernel(pairs, z_ref, count_ref, *refs):
+    blocks, (dst_ref, scale_ref, wig_ref), outs = refs[: 2 * pairs], refs[2 * pairs : 2 * pairs + 3], refs[2 * pairs + 3 : -2]
+    gathered, rot = refs[-2:]
     rot[...] = wig_ref[...].astype(F32) * edge_factor(pl.program_id(0), count_ref, scale_ref)
     dest = hot(iota((LANES, EB), 0) == dst_ref[...])
-
-    def store(place, lanes, tile):
-        eg_ref[place * 16 : place * 16 + 16, lanes] = tile
-
-    rotate_pair(z_ref[0], near_ref, far_ref, dest, rot, gathered, store)
+    for pair, eg_ref in enumerate(outs):
+
+        def store(place, lanes, tile, eg_ref=eg_ref):
+            eg_ref[place * 16 : place * 16 + 16, lanes] = tile
+
+        near_ref, far_ref = blocks[2 * pair : 2 * pair + 2]
+        rotate_pair(z_ref[0], near_ref, far_ref, dest, rot, gathered.at[pair], store)
 
 
 def edge_kernel(
-    z_ref, count_ref, eg0, eg2, eg1, near_ref, far_ref,
+    z_ref, count_ref, eg0, eg1, eg2, near_ref, far_ref,
     dst_ref, src_ref, scale_ref, wig_ref, xo_ref, xs_ref, zero_ref, one_ref, two_ref,
     so_ref, go_ref, sib_ref,
     gathered, rot, plain, eg, acc, back, full, atoms, rims,
@@ -252,13 +255,13 @@
     dest = hot(iota((LANES, EB), 0) == dst_ref[...])
 
     def rows_of(place, n):
-        return pl.ds(pl.multiple_of(place * 64 + ((z % 4) ^ n) * 16, 16), 16)
+        return pl.ds(pl.multiple_of(place * 64 + ((z // 2) ^ n) * 16, 16), 16)
 
     def store(place, lanes, tile):
         eg[rows_of(place, 3), lanes] = tile
 
     rotate_pair(z, near_ref, far_ref, dest, rot, gathered, store)
-    for n, ref in ((0, eg0), (2, eg2), (1, eg1)):
+    for n, ref in ((0, eg0), (1, eg1), (2, eg2)):
         for place in range(29):
             eg[rows_of(place, n), :] = ref[place * 16 : place * 16 + 16]
 
@@ -316,7 +319,7 @@
     def _():
         for zb in range(8):
             tiles = []
-            spot = zb % 4 * 16 + zb // 4 * 8
+            spot = zb * 8
             for t in range(4):
                 tile = acc[t * 64 + spot : t * 64 + spot + 8]
                 if t < 3:
@@ -355,18 +358,19 @@
     return pl.BlockSpec((235, EB), lambda i: (0, i))
 
 
-def rotate_call(z_s, edge_count, pair, dst, scale, wigner):
+def rotate_call(z_s, edge_count, blocks, dst, scale, wigner):
     slots = dst.shape[1]
+    pairs = len(blocks) // 2
     return pl.pallas_call(
-        rotate_kernel,
-        out_shape=sds((464, slots), BF),
+        functools.partial(rotate_kernel, pairs),
+        out_shape=[sds((464, slots), BF)] * pairs,
         grid=(slots // EB,),
-        in_specs=[smem(), smem(), whole((400, 128)), whole((400, 128)), row_spec(), row_spec(), wig_spec()],
-        out_specs=pl.BlockSpec((464, EB), lambda i: (0, i)),
-        scratch_shapes=[pltpu.VMEM((2, 400, EB), F32), pltpu.VMEM((235, EB), F32)],
+        in_specs=[smem(), smem()] + [whole((400, 128))] * len(blocks) + [row_spec(), row_spec(), wig_spec()],
+        out_specs=[pl.BlockSpec((464, EB), lambda i: (0, i))] * pairs,
+        scratch_shapes=[pltpu.VMEM((pairs, 2, 400, EB), F32), pltpu.VMEM((235, EB), F32)],
         compiler_params=params(),
         name="rotate",
-    )(z_s, edge_count, *pair, dst, scale, wigner)
+    )(z_s, edge_count, *blocks, dst, scale, wigner)
 
 
 def edge_call(z_s, edge_count, egs, pair, dst, src, scale, wigner, x_own, x_sib, weights):
@@ -497,31 +501,14 @@
     )(node_x, cotangent, *w_tiles)
     near = cross(rims)
 
-    def rotated(*pair):
-        return rotate_call(z_s, edge_count, pair, dst, scale, wigner)
+    def rotated(*blocks):
+        return rotate_call(z_s, edge_count, blocks, dst, scale, wigner)
 
     b4 = across(b0, 8)
     b2 = across(b0, 4)
     b1 = across(b0, 2)
     far = shift(lax.dynamic_slice_in_dim(near, 112 * high, 112, 0), True)
-    b4, b2, b1, far, w_own = lax.optimization_barrier((b4, b2, b1, far, w_own))
-    b6 = across(b4, 4)
-    b5 = across(b4, 2)
-    b3 = across(b2, 2)
-    eg0 = rotated(b0, b4)
-    far, eg0 = lax.optimization_barrier((far, eg0))
-
-    w_sib = across(w_own, 1)
-    wz, wo, wt = pl.pallas_call(
-        weight_kernel,
-        out_shape=(sds((112, 512), BF), sds((192, 768), BF), sds((160, 640), BF)),
-        grid=(1,),
-        in_specs=[smem(), whole((1376, 128)), whole((1376, 128))],
-        out_specs=(whole((112, 512)), whole((192, 768)), whole((160, 640))),
-        compiler_params=params(),
-        cost_estimate=light(),
-        name="weights",
-    )(k_s, w_own, w_sib)
+    (eg0,) = rotated(b0, b1)
 
     x_spec = pl.BlockSpec((256, EB), lambda i: (0, i))
     x_own = pl.pallas_call(
@@ -535,25 +522,47 @@
         cost_estimate=light(),
         name="edge_in",
     )(h_s, node, near, far, src, wigner)
-    b6, b5, b3, x_own, eg0, wz, wo, wt = lax.optimization_barrier(
-        (b6, b5, b3, x_own, eg0, wz, wo, wt)
-    )
+    b4, b2, w_own, x_own, eg0 = lax.optimization_barrier((b4, b2, w_own, x_own, eg0))
+    b6 = across(b4, 4)
+    b5 = across(b4, 2)
+    b3 = across(b2, 2)
+
+    w_sib = across(w_own, 1)
+    wz, wo, wt = pl.pallas_call(
+        weight_kernel,
+        out_shape=(sds((112, 512), BF), sds((192, 768), BF), sds((160, 640), BF)),
+        grid=(1,),
+        in_specs=[smem(), whole((1376, 128)), whole((1376, 128))],
+        out_specs=(whole((112, 512)), whole((192, 768)), whole((160, 640))),
+        compiler_params=params(),
+        cost_estimate=light(),
+        name="weights",
+    )(k_s, w_own, w_sib)
+
+    b6, b5, b3, x_own, wz, wo, wt = lax.optimization_barrier((b6, b5, b3, x_own, wz, wo, wt))
     b7 = across(b6, 2)
-    eg2 = rotated(b2, b6)
-    eg1 = rotated(b1, b5)
+    eg1, eg2 = rotated(b2, b3, b4, b5)
     x_sib = across(x_own, 1)
 
     s_own, g_own, to_sib = edge_call(
-        z_s, edge_count, (eg0, eg2, eg1), (b3, b7), dst, src, scale, wigner, x_own, x_sib, (wz, wo, wt)
+        z_s, edge_count, (eg0, eg1, eg2), (b6, b7), dst, src, scale, wigner, x_own, x_sib, (wz, wo, wt)
     )
 
     got = across(to_sib, 1)
     s_got = got[:1024].reshape(8, 128, 128)
     s_own = s_own.reshape(8, 128, 128)
-    is_even = core == 0
-    send = jnp.concatenate([jnp.where(is_even, s_own, s_got), jnp.where(is_even, s_got, s_own)], axis=0)
-    groups = [[2 * (2 * zb + p) + h for p in range(2) for zb in range(8)] for h in range(2)]
-    pieces = lax.all_to_all(send, "brick", 0, 0, axis_index_groups=groups)
+    send = jnp.concatenate([s_own, s_got], axis=0)
+    groups = [
+        [
+            (2 * (2 * zb + (k ^ p)) + h) * 16 + 2 * zl + k
+            for p in range(2)
+            for zb in range(8)
+        ]
+        for h in range(2)
+        for zl in range(8)
+        for k in range(2)
+    ]
+    pieces = lax.all_to_all(send, ("brick", "chan"), 0, 0, axis_index_groups=groups)
     summed = pieces.astype(F32).sum(axis=0).reshape(16, 2, 4, 128)
     mine = jnp.where(high == 0, summed[:, 0], summed[:, 1])
     other = jnp.where(high == 0, summed[:, 1], summed[:, 0])

time: 115 us -> 117 us (1.017)
  the two profiles are of different devices: /device:TPU:2 before, /device:TPU:36 now
where the time goes in v9:
time: 117 us; the launch traced here: 116 us
  starting transfers between devices  67 us (57%)
  waiting for transfers between devices  24.3 us (21%)
  Pallas kernels  21.2 us (18%)
  between operations  1.66 us (1%)
    ppermute x10, starting transfers between devices, across(): return lax.ppermute(x, 'chan', [(i, i ^ mask) for i in range(16)])  29.8 us
    ppermute x2, starting transfers between devices, cross(): return lax.ppermute(x, 'brick', [(i, i ^ 1) for i in range(32)])  24.2 us
    ppermute x2, waiting for transfers between devices, cross(): return lax.ppermute(x, 'brick', [(i, i ^ 1) for i in range(32)])  9.67 us
    all_to_all x1, waiting for transfers between devices, body(): lax.all_to_all(send, ('brick', 'chan'), 0, 0, axis_index_groups=groups)  7.96 us
    pallas_call x1, Pallas kernels, edge_call(): pl.pallas_call(edge_kernel, out_shape=(sds((1024, 128), BF), sds((624, 12...  7.89 us
    all_to_all x1, starting transfers between devices, body(): lax.all_to_all(send, ('brick', 'chan'), 0, 0, axis_index_groups=groups)  7.46 us
    pallas_call x2, Pallas kernels, rotate_call(): pl.pallas_call(functools.partial(rotate_kernel, pairs), out_shape=[sds((4...  6.77 us
    ppermute x2, starting transfers between devices, shift(): return lax.ppermute(x, 'brick', route)  5.58 us
  transfers between devices with their start and end apart: 15, of which 6 were waited for; matrix products, arithmetic and copies ran while one was open for 0% of the time, Pallas kernels for 8%

profile of v9, /device:TPU:36, one launch (start us, length us, event | category | flops | bytes accessed | tf_op | source)
XLA Modules:
  0.0 115.9 jit_solution(11605329784350503338)
XLA Ops:
  0.6 2.3 %pack.1 = (bf16[400,128]{1,0:T(8,128)(2,1)}, bf16[400,128]{1,0:T(8,128)(2,1)}, bf16[224,128]{1,0:T(8,128)(2,1)}, bf16[1376,128]{1,0:T(8,128)(2,1)}) custom-call(bf16[49,8,128]{2,1,0:T(8,128)(2,1)} %node_ref.1, bf16[49,8,128]{2,1,0:T(8,128)(2,1)} %cot_ref.1, bf16[49,8,128]{2,1,0:T(8,128)(2,1)} %bitcast.38, bf16[72,8,128]{2,1,0:T(8,128)(2,1)} %bitcast.36, ...), custom_call_target="tpu_custom_call" | custom-call | flops 1 | bytes 1 | tf_op jit(solution)/shard_map/pack/pallas_call | solution.py:492
  2.9 14.9 %collective-permute-start.2 = (bf16[224,128]{1,0:T(8,128)(2,1)}, bf16[224,128]{1,0:T(8,128)(2,1)S(1)}, u32[]{:S(2)}, u32[]{:S(2)}) collective-permute-start(bf16[224,128]{1,0:T(8,128)(2,1)} %get-tuple-element.34), channel_id=1, source_target_pairs={{0,16},{16,0},{32,48},{48,32},{64,80},{80,64},{96,112},{112,96},{1... | collective-permute-start | bytes 172040 | tf_op jit(solution)/shard_map/ppermute | solution.py:481
  17.9 2.9 %collective-permute-start.4 = (bf16[400,128]{1,0:T(8,128)(2,1)}, bf16[400,128]{1,0:T(8,128)(2,1)S(1)}, u32[]{:S(2)}, u32[]{:S(2)}) collective-permute-start(bf16[400,128]{1,0:T(8,128)(2,1)} %get-tuple-element.31.refs_0_), channel_id=1, source_target_pairs={{0,2},{1,3},{2,0},{3,1},{4,6},{5,7},{6,4},{7,5},{8,10},{9,11},{10,... | collective-permute-start | bytes 307208 | tf_op jit(solution)/shard_map/ppermute | solution.py:478
  20.8 4.3 %collective-permute-start = (bf16[400,128]{1,0:T(8,128)(2,1)}, bf16[400,128]{1,0:T(8,128)(2,1)S(1)}, u32[]{:S(2)}, u32[]{:S(2)}) collective-permute-start(bf16[400,128]{1,0:T(8,128)(2,1)} %get-tuple-element.31.refs_0_), channel_id=1, source_target_pairs={{0,8},{1,9},{2,10},{3,11},{4,12},{5,13},{6,14},{7,15},{8,0},{9,1},... | collective-permute-start | bytes 307208 | tf_op jit(solution)/shard_map/ppermute | solution.py:478
  25.1 3.4 %collective-permute-start.1 = (bf16[400,128]{1,0:T(8,128)(2,1)}, bf16[400,128]{1,0:T(8,128)(2,1)S(1)}, u32[]{:S(2)}, u32[]{:S(2)}) collective-permute-start(bf16[400,128]{1,0:T(8,128)(2,1)} %get-tuple-element.31.refs_0_), channel_id=1, source_target_pairs={{0,4},{1,5},{2,6},{3,7},{4,0},{5,1},{6,2},{7,3},{8,12},{9,13},{10,... | collective-permute-start | bytes 307208 | tf_op jit(solution)/shard_map/ppermute | solution.py:478
  28.5 3.1 %collective-permute-start.3 = (bf16[112,128]{1,0:T(8,128)(2,1)S(1)}, bf16[112,128]{1,0:T(8,128)(2,1)S(1)}, u32[]{:S(2)}, u32[]{:S(2)}) collective-permute-start(bf16[112,128]{1,0:T(8,128)(2,1)S(1)} %constant_dynamic-slice_fusion), channel_id=1, source_target_pairs={{0,32},{16,496},{32,64},{48,16},{64,96},{80,48},{96,128},{112,80},... | collective-permute-start | bytes 86024 | tf_op jit(solution)/shard_map/ppermute | solution.py:485
  32.3 2.0 %collective-permute-done.3.far_ref = bf16[112,128]{1,0:T(8,128)(2,1)S(1)} collective-permute-done((bf16[112,128]{1,0:T(8,128)(2,1)S(1)}, bf16[112,128]{1,0:T(8,128)(2,1)S(1)}, u32[]{:S(2)}, u32[]{:S(2)}) %collective-permute-start.3) | collective-permute-done | bytes 28704 | tf_op jit(solution)/shard_map/ppermute | solution.py:485
  34.3 1.9 %edge_in.1.xo_ref = bf16[256,1024]{1,0:T(8,128)(2,1)S(1)} custom-call(s32[1]{0:T(128)} %bitcast.h_ref, bf16[400,128]{1,0:T(8,128)(2,1)S(1)} %copy-done.3, bf16[224,128]{1,0:T(8,128)(2,1)S(1)} %collective-permute-done.2.near_ref, bf16[112,128]{1,0:T(8,128)(2,1)S(1)} %collective-permute-done.3.far_ref, s32[1,1024]{1,0:T(1,128)S(1)} %bitcast.31, ...), custom_call_target="tpu_custom_call" | custom-call | flops 1 | bytes 1 | tf_op jit(solution)/shard_map/edge_in/pallas_call | solution.py:514
  37.0 2.3 %rotate.2.eg0 = bf16[464,1024]{1,0:T(8,128)(2,1)S(1)} custom-call(s32[1]{0:T(128)} %bitcast.1.z_ref, s32[1]{0:T(128)S(6)} %copy.14.count_ref, bf16[400,128]{1,0:T(8,128)(2,1)S(1)} %copy-done.2, bf16[400,128]{1,0:T(8,128)(2,1)S(1)} %collective-permute-done.4.refs_1_, s32[1,1024]{1,0:T(1,128)S(1)} %bitcast.25, f32[1,1024]{1,0:T(1,128)S(1)} %bitcast.28, ...), custom_call_target="tpu_custom_call" | custom-call | tf_op jit(solution)/shard_map/rotate/pallas_call | solution.py:364
  39.3 1.9 %collective-permute-start.8 = (bf16[1376,128]{1,0:T(8,128)(2,1)S(1)}, bf16[1376,128]{1,0:T(8,128)(2,1)S(1)}, u32[]{:S(2)}, u32[]{:S(2)}) collective-permute-start(bf16[1376,128]{1,0:T(8,128)(2,1)S(1)} %copy-done.1), channel_id=1, source_target_pairs={{0,1},{1,0},{2,3},{3,2},{4,5},{5,4},{6,7},{7,6},{8,9},{9,8},{10,11... | collective-permute-start | bytes 1056776 | tf_op jit(solution)/shard_map/ppermute | solution.py:478
  41.3 3.3 %collective-permute-start.5 = (bf16[400,128]{1,0:T(8,128)(2,1)S(1)}, bf16[400,128]{1,0:T(8,128)(2,1)S(1)}, u32[]{:S(2)}, u32[]{:S(2)}) collective-permute-start(bf16[400,128]{1,0:T(8,128)(2,1)S(1)} %collective-permute-done.refs_2_), channel_id=1, source_target_pairs={{0,4},{1,5},{2,6},{3,7},{4,0},{5,1},{6,2},{7,3},{8,12},{9,13},{10,... | collective-permute-start | bytes 307208 | tf_op jit(solution)/shard_map/ppermute | solution.py:478
  44.6 2.9 %collective-permute-start.6 = (bf16[400,128]{1,0:T(8,128)(2,1)S(1)}, bf16[400,128]{1,0:T(8,128)(2,1)S(1)}, u32[]{:S(2)}, u32[]{:S(2)}) collective-permute-start(bf16[400,128]{1,0:T(8,128)(2,1)S(1)} %collective-permute-done.refs_2_), channel_id=1, source_target_pairs={{0,2},{1,3},{2,0},{3,1},{4,6},{5,7},{6,4},{7,5},{8,10},{9,11},{10,... | collective-permute-start | bytes 307208 | tf_op jit(solution)/shard_map/ppermute | solution.py:478
  47.6 2.9 %collective-permute-start.7 = (bf16[400,128]{1,0:T(8,128)(2,1)S(1)}, bf16[400,128]{1,0:T(8,128)(2,1)S(1)}, u32[]{:S(2)}, u32[]{:S(2)}) collective-permute-start(bf16[400,128]{1,0:T(8,128)(2,1)S(1)} %collective-permute-done.1.refs_0_), channel_id=1, source_target_pairs={{0,2},{1,3},{2,0},{3,1},{4,6},{5,7},{6,4},{7,5},{8,10},{9,11},{10,... | collective-permute-start | bytes 307208 | tf_op jit(solution)/shard_map/ppermute | solution.py:478
  52.3 1.9 %collective-permute-done.7.refs_1_ = bf16[400,128]{1,0:T(8,128)(2,1)S(1)} collective-permute-done((bf16[400,128]{1,0:T(8,128)(2,1)S(1)}, bf16[400,128]{1,0:T(8,128)(2,1)S(1)}, u32[]{:S(2)}, u32[]{:S(2)}) %collective-permute-start.7) | collective-permute-done | bytes 102432 | tf_op jit(solution)/shard_map/ppermute | solution.py:478
  54.2 1.9 %collective-permute-start.10 = (bf16[256,1024]{1,0:T(8,128)(2,1)S(1)}, bf16[256,1024]{1,0:T(8,128)(2,1)S(1)}, u32[]{:S(2)}, u32[]{:S(2)}) collective-permute-start(bf16[256,1024]{1,0:T(8,128)(2,1)S(1)} %edge_in.1.xo_ref), channel_id=1, source_target_pairs={{0,1},{1,0},{2,3},{3,2},{4,5},{5,4},{6,7},{7,6},{8,9},{9,8},{10,11... | collective-permute-start | bytes 1572872 | tf_op jit(solution)/shard_map/ppermute | solution.py:478
  56.1 4.1 %collective-permute-start.9 = (bf16[400,128]{1,0:T(8,128)(2,1)S(1)}, bf16[400,128]{1,0:T(8,128)(2,1)S(1)}, u32[]{:S(2)}, u32[]{:S(2)}) collective-permute-start(bf16[400,128]{1,0:T(8,128)(2,1)S(1)} %collective-permute-done.5.near_ref), channel_id=1, source_target_pairs={{0,2},{1,3},{2,0},{3,1},{4,6},{5,7},{6,4},{7,5},{8,10},{9,11},{10,... | collective-permute-start | bytes 307208 | tf_op jit(solution)/shard_map/ppermute | solution.py:478
  60.2 4.4 %rotate.3 = (bf16[464,1024]{1,0:T(8,128)(2,1)S(1)}, bf16[464,1024]{1,0:T(8,128)(2,1)S(1)}) custom-call(s32[1]{0:T(128)} %bitcast.1.z_ref, s32[1]{0:T(128)S(6)} %copy.14.count_ref, bf16[400,128]{1,0:T(8,128)(2,1)S(1)} %collective-permute-done.1.refs_0_, bf16[400,128]{1,0:T(8,128)(2,1)S(1)} %collective-permute-done.7.refs_1_, ...), custom_call_target="tpu_custom_call" | custom-call | tf_op jit(solution)/shard_map/rotate/pallas_call | solution.py:364
  64.7 7.9 %edge.1 = (bf16[1024,128]{1,0:T(8,128)(2,1)S(1)}, f32[624,128]{1,0:T(8,128)S(1)}, bf16[1648,128]{1,0:T(8,128)(2,1)S(1)}) custom-call(s32[1]{0:T(128)} %bitcast.1.z_ref, s32[1]{0:T(128)S(6)} %copy.14.count_ref, bf16[464,1024]{1,0:T(8,128)(2,1)S(1)} %rotate.2.eg0, bf16[464,1024]{1,0:T(8,128)(2,1)S(1)} %get-tuple-element.45.eg1, ...), custom_call_target="tpu_custom_call" | custom-call | tf_op jit(solution)/shard_map/edge/pallas_call | solution.py:379
  72.6 2.1 %collective-permute-start.11 = (bf16[1648,128]{1,0:T(8,128)(2,1)S(1)}, bf16[1648,128]{1,0:T(8,128)(2,1)S(1)}, u32[]{:S(2)}, u32[]{:S(2)}) collective-permute-start(bf16[1648,128]{1,0:T(8,128)(2,1)S(1)} %get-tuple-element.53), channel_id=1, source_target_pairs={{0,1},{1,0},{2,3},{3,2},{4,5},{5,4},{6,7},{7,6},{8,9},{9,8},{10,11... | collective-permute-start | bytes 1265672 | tf_op jit(solution)/shard_map/ppermute | solution.py:478
  77.1 7.5 %all-to-all-start = ((bf16[16,128,128]{2,1,0:T(8,128)(2,1)}), bf16[16,128,128]{2,1,0:T(8,128)(2,1)S(1)}, u32[]{:S(2)}, u32[]{:S(2)}) async-start(bf16[16,128,128]{2,1,0:T(8,128)(2,1)} %pad_maximum_fusion), calls=%async_computation | async-start | bytes 1048576 | tf_op jit(solution)/shard_map/all_to_all | solution.py:565
  84.6 2.5 %collective-permute-start.12 = (bf16[112,128]{1,0:T(8,128)(2,1)S(1)}, bf16[112,128]{1,0:T(8,128)(2,1)S(1)}, u32[]{:S(2)}, u32[]{:S(2)}) collective-permute-start(bf16[112,128]{1,0:T(8,128)(2,1)S(1)} %get-tuple-element.61), channel_id=1, source_target_pairs={{0,480},{16,48},{32,0},{48,80},{64,32},{80,112},{96,64},{112,144},... | collective-permute-start | bytes 86024 | tf_op jit(solution)/shard_map/ppermute | solution.py:485
  87.1 8.0 %all-to-all-done = bf16[16,128,128]{2,1,0:T(8,128)(2,1)S(1)} async-done(((bf16[16,128,128]{2,1,0:T(8,128)(2,1)}), bf16[16,128,128]{2,1,0:T(8,128)(2,1)S(1)}, u32[]{:S(2)}, u32[]{:S(2)}) %all-to-all-start) | async-done | bytes 524320 | tf_op jit(solution)/shard_map/all_to_all | solution.py:565
  95.2 9.2 %collective-permute-start.13 = (bf16[288,128]{1,0:T(8,128)(2,1)S(1)}, bf16[288,128]{1,0:T(8,128)(2,1)S(1)}, u32[]{:S(2)}, u32[]{:S(2)}) collective-permute-start(bf16[288,128]{1,0:T(8,128)(2,1)S(1)} %pad_maximum_fusion.1), channel_id=1, source_target_pairs={{0,16},{16,0},{32,48},{48,32},{64,80},{80,64},{96,112},{112,96},{1... | collective-permute-start | bytes 221192 | tf_op jit(solution)/shard_map/ppermute | solution.py:481
  104.4 9.7 %collective-permute-done.13.rim_ref.got_ref = bf16[288,128]{1,0:T(8,128)(2,1)S(1)} collective-permute-done((bf16[288,128]{1,0:T(8,128)(2,1)S(1)}, bf16[288,128]{1,0:T(8,128)(2,1)S(1)}, u32[]{:S(2)}, u32[]{:S(2)}) %collective-permute-start.13) | collective-permute-done | bytes 73760 | tf_op jit(solution)/shard_map/ppermute | solution.py:481
  (37 shorter events, 6.9 us)
Async XLA Ops:
  0.6 33.7 %copy-start = (bf16[235,1024]{1,0:T(8,128)(2,1)S(1)}, bf16[235,1024]{1,0:T(8,128)(2,1)}, u32[]{:S(2)}) copy-start(bf16[235,1024]{1,0:T(8,128)(2,1)} %wig_ref.3) | copy-start | bytes 1443844
  2.9 31.4 %copy-start.3 = (bf16[400,128]{1,0:T(8,128)(2,1)S(1)}, bf16[400,128]{1,0:T(8,128)(2,1)}, u32[]{:S(2)}) copy-start(bf16[400,128]{1,0:T(8,128)(2,1)} %get-tuple-element.33.node_ref) | copy-start | bytes 307204
  2.9 25.6 %collective-permute-start.2 = (bf16[224,128]{1,0:T(8,128)(2,1)}, bf16[224,128]{1,0:T(8,128)(2,1)S(1)}, u32[]{:S(2)}, u32[]{:S(2)}) collective-permute-start(bf16[224,128]{1,0:T(8,128)(2,1)} %get-tuple-element.34), channel_id=1, source_target_pairs={{0,16},{16,0},{32,48},{48,32},{64,80},{80,64},{96,112},{112,96},{1... | collective-permute-start | bytes 172040 | tf_op jit(solution)/shard_map/ppermute | solution.py:481
  17.9 18.4 %collective-permute-start.4 = (bf16[400,128]{1,0:T(8,128)(2,1)}, bf16[400,128]{1,0:T(8,128)(2,1)S(1)}, u32[]{:S(2)}, u32[]{:S(2)}) collective-permute-start(bf16[400,128]{1,0:T(8,128)(2,1)} %get-tuple-element.31.refs_0_), channel_id=1, source_target_pairs={{0,2},{1,3},{2,0},{3,1},{4,6},{5,7},{6,4},{7,5},{8,10},{9,11},{10,... | collective-permute-start | bytes 307208 | tf_op jit(solution)/shard_map/ppermute | solution.py:478
  20.8 18.5 %collective-permute-start = (bf16[400,128]{1,0:T(8,128)(2,1)}, bf16[400,128]{1,0:T(8,128)(2,1)S(1)}, u32[]{:S(2)}, u32[]{:S(2)}) collective-permute-start(bf16[400,128]{1,0:T(8,128)(2,1)} %get-tuple-element.31.refs_0_), channel_id=1, source_target_pairs={{0,8},{1,9},{2,10},{3,11},{4,12},{5,13},{6,14},{7,15},{8,0},{9,1},... | collective-permute-start | bytes 307208 | tf_op jit(solution)/shard_map/ppermute | solution.py:478
  25.1 14.2 %collective-permute-start.1 = (bf16[400,128]{1,0:T(8,128)(2,1)}, bf16[400,128]{1,0:T(8,128)(2,1)S(1)}, u32[]{:S(2)}, u32[]{:S(2)}) collective-permute-start(bf16[400,128]{1,0:T(8,128)(2,1)} %get-tuple-element.31.refs_0_), channel_id=1, source_target_pairs={{0,4},{1,5},{2,6},{3,7},{4,0},{5,1},{6,2},{7,3},{8,12},{9,13},{10,... | collective-permute-start | bytes 307208 | tf_op jit(solution)/shard_map/ppermute | solution.py:478
  28.5 5.8 %collective-permute-start.3 = (bf16[112,128]{1,0:T(8,128)(2,1)S(1)}, bf16[112,128]{1,0:T(8,128)(2,1)S(1)}, u32[]{:S(2)}, u32[]{:S(2)}) collective-permute-start(bf16[112,128]{1,0:T(8,128)(2,1)S(1)} %constant_dynamic-slice_fusion), channel_id=1, source_target_pairs={{0,32},{16,496},{32,64},{48,16},{64,96},{80,48},{96,128},{112,80},... | collective-permute-start | bytes 86024 | tf_op jit(solution)/shard_map/ppermute | solution.py:485
  32.3 2.0 %copy-start.6 = (s32[1024]{0:T(1024)S(1)}, s32[1024]{0:T(1024)}, u32[]{:S(2)}) copy-start(s32[1024]{0:T(1024)} %param.13) | copy-start | bytes 12292
  34.3 2.0 %copy-start.2 = (bf16[400,128]{1,0:T(8,128)(2,1)S(1)}, bf16[400,128]{1,0:T(8,128)(2,1)}, u32[]{:S(2)}) copy-start(bf16[400,128]{1,0:T(8,128)(2,1)} %get-tuple-element.31.refs_0_) | copy-start | bytes 307204
  34.3 2.0 %copy-start.5 = (f32[1024]{0:T(1024)S(1)}, f32[1024]{0:T(1024)}, u32[]{:S(2)}) copy-start(f32[1024]{0:T(1024)} %param.15) | copy-start | bytes 12292
  36.3 0.7 copy-start.4
  37.0 2.4 %copy-start.1 = (bf16[1376,128]{1,0:T(8,128)(2,1)S(1)}, bf16[1376,128]{1,0:T(8,128)(2,1)}, u32[]{:S(2)}) copy-start(bf16[1376,128]{1,0:T(8,128)(2,1)} %get-tuple-element.39.own_ref) | copy-start | bytes 1056772
  39.3 11.1 %collective-permute-start.8 = (bf16[1376,128]{1,0:T(8,128)(2,1)S(1)}, bf16[1376,128]{1,0:T(8,128)(2,1)S(1)}, u32[]{:S(2)}, u32[]{:S(2)}) collective-permute-start(bf16[1376,128]{1,0:T(8,128)(2,1)S(1)} %copy-done.1), channel_id=1, source_target_pairs={{0,1},{1,0},{2,3},{3,2},{4,5},{5,4},{6,7},{7,6},{8,9},{9,8},{10,11... | collective-permute-start | bytes 1056776 | tf_op jit(solution)/shard_map/ppermute | solution.py:478
  41.3 9.8 %collective-permute-start.5 = (bf16[400,128]{1,0:T(8,128)(2,1)S(1)}, bf16[400,128]{1,0:T(8,128)(2,1)S(1)}, u32[]{:S(2)}, u32[]{:S(2)}) collective-permute-start(bf16[400,128]{1,0:T(8,128)(2,1)S(1)} %collective-permute-done.refs_2_), channel_id=1, source_target_pairs={{0,4},{1,5},{2,6},{3,7},{4,0},{5,1},{6,2},{7,3},{8,12},{9,13},{10,... | collective-permute-start | bytes 307208 | tf_op jit(solution)/shard_map/ppermute | solution.py:478
  44.6 7.7 %collective-permute-start.6 = (bf16[400,128]{1,0:T(8,128)(2,1)S(1)}, bf16[400,128]{1,0:T(8,128)(2,1)S(1)}, u32[]{:S(2)}, u32[]{:S(2)}) collective-permute-start(bf16[400,128]{1,0:T(8,128)(2,1)S(1)} %collective-permute-done.refs_2_), channel_id=1, source_target_pairs={{0,2},{1,3},{2,0},{3,1},{4,6},{5,7},{6,4},{7,5},{8,10},{9,11},{10,... | collective-permute-start | bytes 307208 | tf_op jit(solution)/shard_map/ppermute | solution.py:478
  47.6 6.6 %collective-permute-start.7 = (bf16[400,128]{1,0:T(8,128)(2,1)S(1)}, bf16[400,128]{1,0:T(8,128)(2,1)S(1)}, u32[]{:S(2)}, u32[]{:S(2)}) collective-permute-start(bf16[400,128]{1,0:T(8,128)(2,1)S(1)} %collective-permute-done.1.refs_0_), channel_id=1, source_target_pairs={{0,2},{1,3},{2,0},{3,1},{4,6},{5,7},{6,4},{7,5},{8,10},{9,11},{10,... | collective-permute-start | bytes 307208 | tf_op jit(solution)/shard_map/ppermute | solution.py:478
  54.2 10.5 %collective-permute-start.10 = (bf16[256,1024]{1,0:T(8,128)(2,1)S(1)}, bf16[256,1024]{1,0:T(8,128)(2,1)S(1)}, u32[]{:S(2)}, u32[]{:S(2)}) collective-permute-start(bf16[256,1024]{1,0:T(8,128)(2,1)S(1)} %edge_in.1.xo_ref), channel_id=1, source_target_pairs={{0,1},{1,0},{2,3},{3,2},{4,5},{5,4},{6,7},{7,6},{8,9},{9,8},{10,11... | collective-permute-start | bytes 1572872 | tf_op jit(solution)/shard_map/ppermute | solution.py:478
  56.1 8.5 %collective-permute-start.9 = (bf16[400,128]{1,0:T(8,128)(2,1)S(1)}, bf16[400,128]{1,0:T(8,128)(2,1)S(1)}, u32[]{:S(2)}, u32[]{:S(2)}) collective-permute-start(bf16[400,128]{1,0:T(8,128)(2,1)S(1)} %collective-permute-done.5.near_ref), channel_id=1, source_target_pairs={{0,2},{1,3},{2,0},{3,1},{4,6},{5,7},{6,4},{7,5},{8,10},{9,11},{10,... | collective-permute-start | bytes 307208 | tf_op jit(solution)/shard_map/ppermute | solution.py:478
  72.6 3.7 %collective-permute-start.11 = (bf16[1648,128]{1,0:T(8,128)(2,1)S(1)}, bf16[1648,128]{1,0:T(8,128)(2,1)S(1)}, u32[]{:S(2)}, u32[]{:S(2)}) collective-permute-start(bf16[1648,128]{1,0:T(8,128)(2,1)S(1)} %get-tuple-element.53), channel_id=1, source_target_pairs={{0,1},{1,0},{2,3},{3,2},{4,5},{5,4},{6,7},{7,6},{8,9},{9,8},{10,11... | collective-permute-start | bytes 1265672 | tf_op jit(solution)/shard_map/ppermute | solution.py:478
  77.1 18.0 %all-to-all-start = ((bf16[16,128,128]{2,1,0:T(8,128)(2,1)}), bf16[16,128,128]{2,1,0:T(8,128)(2,1)S(1)}, u32[]{:S(2)}, u32[]{:S(2)}) async-start(bf16[16,128,128]{2,1,0:T(8,128)(2,1)} %pad_maximum_fusion), calls=%async_computation | async-start | bytes 1048576 | tf_op jit(solution)/shard_map/all_to_all | solution.py:565
  84.6 10.6 %collective-permute-start.12 = (bf16[112,128]{1,0:T(8,128)(2,1)S(1)}, bf16[112,128]{1,0:T(8,128)(2,1)S(1)}, u32[]{:S(2)}, u32[]{:S(2)}) collective-permute-start(bf16[112,128]{1,0:T(8,128)(2,1)S(1)} %get-tuple-element.61), channel_id=1, source_target_pairs={{0,480},{16,48},{32,0},{48,80},{64,32},{80,112},{96,64},{112,144},... | collective-permute-start | bytes 86024 | tf_op jit(solution)/shard_map/ppermute | solution.py:485
  95.2 18.9 %collective-permute-start.13 = (bf16[288,128]{1,0:T(8,128)(2,1)S(1)}, bf16[288,128]{1,0:T(8,128)(2,1)S(1)}, u32[]{:S(2)}, u32[]{:S(2)}) collective-permute-start(bf16[288,128]{1,0:T(8,128)(2,1)S(1)} %pad_maximum_fusion.1), channel_id=1, source_target_pairs={{0,16},{16,0},{32,48},{48,32},{64,80},{80,64},{96,112},{112,96},{1... | collective-permute-start | bytes 221192 | tf_op jit(solution)/shard_map/ppermute | solution.py:481

commit v10 on v9

--- a/solution.py
+++ b/solution.py
@@ -13,6 +13,7 @@
 LANES = 128
 VMEM_LIMIT = 28 * 1024 * 1024
 PACK_VMEM = 60 * 1024 * 1024
+X_ROWS = 2048
 ZORD = (0, 2, 4, 6, 1, 3, 5)
 
 NN = (((1,), (0,)), ((), ()))
@@ -106,7 +107,13 @@
     weight_out[...] = jnp.concatenate(parts + [blank], axis=0).astype(BF)
 
 
-def edge_in_kernel(h_ref, node_ref, near_ref, far_ref, src_ref, wig_ref, x_ref, rot, gathered):
+def edge_in_kernel(h_ref, node_ref, near_ref, far_ref, weight_ref, src_ref, wig_ref, x_ref, rot, gathered):
+    step = pl.program_id(0)
+
+    @pl.when(step == 0)
+    def _():
+        x_ref[X_ROWS:] = weight_ref[...]
+
     h = h_ref[0]
     src = src_ref[...]
     own, before, after = source_hots(src)
@@ -141,7 +148,10 @@
         (208, [rows[r] for r in range(24, 29)] + [blank]),
     ]
     for start, members in groups:
-        x_ref[start : start + 8 * len(members), :] = jnp.concatenate(members, axis=0).astype(BF)
+        block = jnp.concatenate(members, axis=0).astype(BF)
+        for half in range(EB // LANES):
+            row = pl.multiple_of(step * (256 * EB // LANES) + 256 * half + start, 16)
+            x_ref[pl.ds(row, 8 * len(members)), :] = block[:, half * LANES : half * LANES + LANES]
 
 
 def weight_kernel(k_ref, own_ref, sib_ref, zero_ref, one_ref, two_ref):
@@ -154,7 +164,7 @@
         return hot((spot >= 0) & (spot < 64) & (chan == wanted))
 
     low, high = pick(0), pick(64)
-    own, sib = own_ref[...], sib_ref[...]
+    own, sib = own_ref[X_ROWS:], sib_ref[X_ROWS:]
     sides = [(mm(own, low), mm(own, high)), (mm(sib, low), mm(sib, high))]
 
     def tile(entries, place):
@@ -271,7 +281,10 @@
     def blank(rows):
         return jnp.zeros((rows, EB), BF)
 
-    xo, xs = xo_ref[...], xs_ref[...]
+    def tiles_of(ref):
+        return jnp.concatenate([ref[256 * n : 256 * n + 256] for n in range(EB // LANES)], axis=1)
+
+    xo, xs = tiles_of(xo_ref), tiles_of(xs_ref)
     acc[0:448] += mm(eg[0:448], stacked(xo[:64], blank(64), xs[:64], blank(64)), NT)
     for start, count, plus, minus in ((448, 6, 64, 112), (1216, 5, 160, 208)):
         ahead = stacked(
@@ -375,7 +388,7 @@
 
 def edge_call(z_s, edge_count, egs, pair, dst, src, scale, wigner, x_own, x_sib, weights):
     slots = dst.shape[1]
-    x_spec = pl.BlockSpec((256, EB), lambda i: (0, i))
+    x_spec = pl.BlockSpec((256 * EB // LANES, LANES), lambda i: (i, 0))
     return pl.pallas_call(
         edge_kernel,
         out_shape=(sds((1024, 128), BF), sds((624, 128), F32), sds((1648, 128), BF)),
@@ -508,41 +521,40 @@
     b2 = across(b0, 4)
     b1 = across(b0, 2)
     far = shift(lax.dynamic_slice_in_dim(near, 112 * high, 112, 0), True)
-    (eg0,) = rotated(b0, b1)
-
-    x_spec = pl.BlockSpec((256, EB), lambda i: (0, i))
+
     x_own = pl.pallas_call(
         edge_in_kernel,
-        out_shape=sds((256, slots), BF),
+        out_shape=sds((X_ROWS + 1376, 128), BF),
         grid=(steps,),
-        in_specs=[smem(), whole((400, 128)), whole((224, 128)), whole((112, 128)), row_spec(), wig_spec()],
-        out_specs=x_spec,
+        in_specs=[smem(), whole((400, 128)), whole((224, 128)), whole((112, 128)), whole((1376, 128))]
+        + [row_spec(), wig_spec()],
+        out_specs=whole((X_ROWS + 1376, 128)),
         scratch_shapes=[pltpu.VMEM((235, EB), F32), pltpu.VMEM((400, EB), F32)],
         compiler_params=params(),
         cost_estimate=light(),
         name="edge_in",
-    )(h_s, node, near, far, src, wigner)
-    b4, b2, w_own, x_own, eg0 = lax.optimization_barrier((b4, b2, w_own, x_own, eg0))
+    )(h_s, node, near, far, w_own, src, wigner)
+    b4, b2, b1, x_own = lax.optimization_barrier((b4, b2, b1, x_own))
     b6 = across(b4, 4)
     b5 = across(b4, 2)
     b3 = across(b2, 2)
-
-    w_sib = across(w_own, 1)
+    (eg0,) = rotated(b0, b1)
+
+    b6, b5, b3, x_own, eg0 = lax.optimization_barrier((b6, b5, b3, x_own, eg0))
+    b7 = across(b6, 2)
+    eg1, eg2 = rotated(b2, b3, b4, b5)
+    x_sib = across(x_own, 1)
+
     wz, wo, wt = pl.pallas_call(
         weight_kernel,
         out_shape=(sds((112, 512), BF), sds((192, 768), BF), sds((160, 640), BF)),
         grid=(1,),
-        in_specs=[smem(), whole((1376, 128)), whole((1376, 128))],
+        in_specs=[smem(), whole((X_ROWS + 1376, 128)), whole((X_ROWS + 1376, 128))],
         out_specs=(whole((112, 512)), whole((192, 768)), whole((160, 640))),
         compiler_params=params(),
         cost_estimate=light(),
         name="weights",
-    )(k_s, w_own, w_sib)
-
-    b6, b5, b3, x_own, wz, wo, wt = lax.optimization_barrier((b6, b5, b3, x_own, wz, wo, wt))
-    b7 = across(b6, 2)
-    eg1, eg2 = rotated(b2, b3, b4, b5)
-    x_sib = across(x_own, 1)
+    )(k_s, x_own, x_sib)
 
     s_own, g_own, to_sib = edge_call(
         z_s, edge_count, (eg0, eg1, eg2), (b6, b7), dst, src, scale, wigner, x_own, x_sib, (wz, wo, wt)

time: 117 us -> 115 us (0.983)
  the two profiles are of different devices: /device:TPU:36 before, /device:TPU:4 now
where the time goes in v10:
time: 115 us; the launch traced here: 114 us
  starting transfers between devices  65.1 us (57%)
  Pallas kernels  21.9 us (19%)
  waiting for transfers between devices  21.2 us (18%)
  local copies, waits for them, and re-layouts  3.22 us (3%)
  between operations  1.66 us (1%)
    ppermute x9, starting transfers between devices, across(): return lax.ppermute(x, 'chan', [(i, i ^ mask) for i in range(16)])  26.8 us
    ppermute x2, starting transfers between devices, cross(): return lax.ppermute(x, 'brick', [(i, i ^ 1) for i in range(32)])  25.4 us
    ppermute x2, waiting for transfers between devices, cross(): return lax.ppermute(x, 'brick', [(i, i ^ 1) for i in range(32)])  9.09 us
    pallas_call x1, Pallas kernels, edge_call(): pl.pallas_call(edge_kernel, out_shape=(sds((1024, 128), BF), sds((624, 12...  8.63 us
    all_to_all x1, waiting for transfers between devices, body(): lax.all_to_all(send, ('brick', 'chan'), 0, 0, axis_index_groups=groups)  7.94 us
    all_to_all x1, starting transfers between devices, body(): lax.all_to_all(send, ('brick', 'chan'), 0, 0, axis_index_groups=groups)  7.43 us
    pallas_call x2, Pallas kernels, rotate_call(): pl.pallas_call(functools.partial(rotate_kernel, pairs), out_shape=[sds((4...  6.74 us
    ppermute x2, starting transfers between devices, shift(): return lax.ppermute(x, 'brick', route)  5.58 us
  transfers between devices with their start and end apart: 14, of which 4 were waited for; matrix products, arithmetic and copies ran while one was open for 0% of the time, Pallas kernels for 8%

profile of v10, /device:TPU:4, one launch (start us, length us, event | category | flops | bytes accessed | tf_op | source)
XLA Modules:
  0.0 114.2 jit_solution(10254100996806414670)
XLA Ops:
  0.6 2.3 %pack.1 = (bf16[400,128]{1,0:T(8,128)(2,1)}, bf16[400,128]{1,0:T(8,128)(2,1)}, bf16[224,128]{1,0:T(8,128)(2,1)}, bf16[1376,128]{1,0:T(8,128)(2,1)}) custom-call(bf16[49,8,128]{2,1,0:T(8,128)(2,1)} %node_ref.1, bf16[49,8,128]{2,1,0:T(8,128)(2,1)} %cot_ref.1, bf16[49,8,128]{2,1,0:T(8,128)(2,1)} %bitcast.38, bf16[72,8,128]{2,1,0:T(8,128)(2,1)} %bitcast.36, ...), custom_call_target="tpu_custom_call" | custom-call | flops 1 | bytes 1 | tf_op jit(solution)/shard_map/pack/pallas_call | solution.py:505
  2.9 15.8 %collective-permute-start.3 = (bf16[224,128]{1,0:T(8,128)(2,1)}, bf16[224,128]{1,0:T(8,128)(2,1)S(1)}, u32[]{:S(2)}, u32[]{:S(2)}) collective-permute-start(bf16[224,128]{1,0:T(8,128)(2,1)} %get-tuple-element.30), channel_id=1, source_target_pairs={{0,16},{16,0},{32,48},{48,32},{64,80},{80,64},{96,112},{112,96},{1... | collective-permute-start | bytes 172040 | tf_op jit(solution)/shard_map/ppermute | solution.py:494
  18.8 4.3 %collective-permute-start = (bf16[400,128]{1,0:T(8,128)(2,1)}, bf16[400,128]{1,0:T(8,128)(2,1)S(1)}, u32[]{:S(2)}, u32[]{:S(2)}) collective-permute-start(bf16[400,128]{1,0:T(8,128)(2,1)} %get-tuple-element.28.refs_0_), channel_id=1, source_target_pairs={{0,8},{1,9},{2,10},{3,11},{4,12},{5,13},{6,14},{7,15},{8,0},{9,1},... | collective-permute-start | bytes 307208 | tf_op jit(solution)/shard_map/ppermute | solution.py:491
  23.1 3.4 %collective-permute-start.1 = (bf16[400,128]{1,0:T(8,128)(2,1)}, bf16[400,128]{1,0:T(8,128)(2,1)S(1)}, u32[]{:S(2)}, u32[]{:S(2)}) collective-permute-start(bf16[400,128]{1,0:T(8,128)(2,1)} %get-tuple-element.28.refs_0_), channel_id=1, source_target_pairs={{0,4},{1,5},{2,6},{3,7},{4,0},{5,1},{6,2},{7,3},{8,12},{9,13},{10,... | collective-permute-start | bytes 307208 | tf_op jit(solution)/shard_map/ppermute | solution.py:491
  26.5 2.9 %collective-permute-start.2 = (bf16[400,128]{1,0:T(8,128)(2,1)}, bf16[400,128]{1,0:T(8,128)(2,1)S(1)}, u32[]{:S(2)}, u32[]{:S(2)}) collective-permute-start(bf16[400,128]{1,0:T(8,128)(2,1)} %get-tuple-element.28.refs_0_), channel_id=1, source_target_pairs={{0,2},{1,3},{2,0},{3,1},{4,6},{5,7},{6,4},{7,5},{8,10},{9,11},{10,... | collective-permute-start | bytes 307208 | tf_op jit(solution)/shard_map/ppermute | solution.py:491
  29.5 3.1 %collective-permute-start.4 = (bf16[112,128]{1,0:T(8,128)(2,1)S(1)}, bf16[112,128]{1,0:T(8,128)(2,1)S(1)}, u32[]{:S(2)}, u32[]{:S(2)}) collective-permute-start(bf16[112,128]{1,0:T(8,128)(2,1)S(1)} %constant_dynamic-slice_fusion), channel_id=1, source_target_pairs={{0,32},{16,496},{32,64},{48,16},{64,96},{80,48},{96,128},{112,80},... | collective-permute-start | bytes 86024 | tf_op jit(solution)/shard_map/ppermute | solution.py:498
  32.6 2.7 %collective-permute-done.4.far_ref = bf16[112,128]{1,0:T(8,128)(2,1)S(1)} collective-permute-done((bf16[112,128]{1,0:T(8,128)(2,1)S(1)}, bf16[112,128]{1,0:T(8,128)(2,1)S(1)}, u32[]{:S(2)}, u32[]{:S(2)}) %collective-permute-start.4) | collective-permute-done | bytes 28704 | tf_op jit(solution)/shard_map/ppermute | solution.py:498
  35.2 1.0 copy-done.1
  36.2 1.9 %edge_in.1.own_ref.xo_ref = bf16[3424,128]{1,0:T(8,128)(2,1)S(1)} custom-call(s32[1]{0:T(128)} %bitcast.h_ref, bf16[400,128]{1,0:T(8,128)(2,1)S(1)} %copy-done.5, bf16[224,128]{1,0:T(8,128)(2,1)S(1)} %collective-permute-done.3.near_ref, bf16[112,128]{1,0:T(8,128)(2,1)S(1)} %collective-permute-done.4.far_ref, bf16[1376,128]{1,0:T(8,128)(2,1)S(1)} %copy-done.1, ...), custom_call_target="tpu_custom_call" | custom-call | flops 1 | bytes 1 | tf_op jit(solution)/shard_map/edge_in/pallas_call | solution.py:525
  38.2 3.4 %collective-permute-start.5 = (bf16[400,128]{1,0:T(8,128)(2,1)S(1)}, bf16[400,128]{1,0:T(8,128)(2,1)}, u32[]{:S(2)}, u32[]{:S(2)}) collective-permute-start(bf16[400,128]{1,0:T(8,128)(2,1)S(1)} %collective-permute-done.refs_2_), channel_id=1, source_target_pairs={{0,4},{1,5},{2,6},{3,7},{4,0},{5,1},{6,2},{7,3},{8,12},{9,13},{10,... | collective-permute-start | bytes 307208 | tf_op jit(solution)/shard_map/ppermute | solution.py:491
  41.5 2.9 %collective-permute-start.6 = (bf16[400,128]{1,0:T(8,128)(2,1)S(1)}, bf16[400,128]{1,0:T(8,128)(2,1)S(1)}, u32[]{:S(2)}, u32[]{:S(2)}) collective-permute-start(bf16[400,128]{1,0:T(8,128)(2,1)S(1)} %collective-permute-done.refs_2_), channel_id=1, source_target_pairs={{0,2},{1,3},{2,0},{3,1},{4,6},{5,7},{6,4},{7,5},{8,10},{9,11},{10,... | collective-permute-start | bytes 307208 | tf_op jit(solution)/shard_map/ppermute | solution.py:491
  44.5 2.9 %collective-permute-start.7 = (bf16[400,128]{1,0:T(8,128)(2,1)S(1)}, bf16[400,128]{1,0:T(8,128)(2,1)S(1)}, u32[]{:S(2)}, u32[]{:S(2)}) collective-permute-start(bf16[400,128]{1,0:T(8,128)(2,1)S(1)} %collective-permute-done.1.refs_0_), channel_id=1, source_target_pairs={{0,2},{1,3},{2,0},{3,1},{4,6},{5,7},{6,4},{7,5},{8,10},{9,11},{10,... | collective-permute-start | bytes 307208 | tf_op jit(solution)/shard_map/ppermute | solution.py:491
  48.8 2.3 %rotate.2.eg0 = bf16[464,1024]{1,0:T(8,128)(2,1)S(1)} custom-call(s32[1]{0:T(128)} %bitcast.1.z_ref, s32[1]{0:T(128)S(6)} %copy.14.count_ref, bf16[400,128]{1,0:T(8,128)(2,1)S(1)} %copy-done.2, bf16[400,128]{1,0:T(8,128)(2,1)S(1)} %collective-permute-done.2.refs_1_, s32[1,1024]{1,0:T(1,128)S(1)} %bitcast.25, f32[1,1024]{1,0:T(1,128)S(1)} %bitcast.28, ...), custom_call_target="tpu_custom_call" | custom-call | tf_op jit(solution)/shard_map/rotate/pallas_call | solution.py:377
  51.8 1.9 %collective-permute-start.9 = (bf16[3424,128]{1,0:T(8,128)(2,1)S(1)}, bf16[3424,128]{1,0:T(8,128)(2,1)S(1)}, u32[]{:S(2)}, u32[]{:S(2)}) collective-permute-start(bf16[3424,128]{1,0:T(8,128)(2,1)S(1)} %edge_in.1.own_ref.xo_ref), channel_id=1, source_target_pairs={{0,1},{1,0},{2,3},{3,2},{4,5},{5,4},{6,7},{7,6},{8,9},{9,8},{10,11... | collective-permute-start | bytes 2629640 | tf_op jit(solution)/shard_map/ppermute | solution.py:491
  53.7 2.9 %collective-permute-start.8 = (bf16[400,128]{1,0:T(8,128)(2,1)}, bf16[400,128]{1,0:T(8,128)(2,1)}, u32[]{:S(2)}, u32[]{:S(2)}) collective-permute-start(bf16[400,128]{1,0:T(8,128)(2,1)} %collective-permute-done.5.near_ref), channel_id=1, source_target_pairs={{0,2},{1,3},{2,0},{3,1},{4,6},{5,7},{6,4},{7,5},{8,10},{9,11},{10,... | collective-permute-start | bytes 307208 | tf_op jit(solution)/shard_map/ppermute | solution.py:491
  57.6 4.4 %rotate.3 = (bf16[464,1024]{1,0:T(8,128)(2,1)S(1)}, bf16[464,1024]{1,0:T(8,128)(2,1)S(1)}) custom-call(s32[1]{0:T(128)} %bitcast.1.z_ref, s32[1]{0:T(128)S(6)} %copy.14.count_ref, bf16[400,128]{1,0:T(8,128)(2,1)S(1)} %collective-permute-done.1.refs_0_, bf16[400,128]{1,0:T(8,128)(2,1)S(1)} %copy-done.4, bf16[400,128]{1,0:T(8,128)(2,1)S(1)} %collective-permute-done.refs_2_, ...), custom_call_target="tpu_custom_call" | custom-call | tf_op jit(solution)/shard_map/rotate/pallas_call | solution.py:377
  62.5 8.6 %edge.1 = (bf16[1024,128]{1,0:T(8,128)(2,1)S(1)}, f32[624,128]{1,0:T(8,128)S(1)}, bf16[1648,128]{1,0:T(8,128)(2,1)S(1)}) custom-call(s32[1]{0:T(128)} %bitcast.1.z_ref, s32[1]{0:T(128)S(6)} %copy.14.count_ref, bf16[464,1024]{1,0:T(8,128)(2,1)S(1)} %rotate.2.eg0, bf16[464,1024]{1,0:T(8,128)(2,1)S(1)} %get-tuple-element.39.eg1, ...), custom_call_target="tpu_custom_call" | custom-call | tf_op jit(solution)/shard_map/edge/pallas_call | solution.py:392
  71.2 2.1 %collective-permute-start.10 = (bf16[1648,128]{1,0:T(8,128)(2,1)S(1)}, bf16[1648,128]{1,0:T(8,128)(2,1)S(1)}, u32[]{:S(2)}, u32[]{:S(2)}) collective-permute-start(bf16[1648,128]{1,0:T(8,128)(2,1)S(1)} %get-tuple-element.47), channel_id=1, source_target_pairs={{0,1},{1,0},{2,3},{3,2},{4,5},{5,4},{6,7},{7,6},{8,9},{9,8},{10,11... | collective-permute-start | bytes 1265672 | tf_op jit(solution)/shard_map/ppermute | solution.py:491
  73.3 1.5 %collective-permute-done.10 = bf16[1648,128]{1,0:T(8,128)(2,1)S(1)} collective-permute-done((bf16[1648,128]{1,0:T(8,128)(2,1)S(1)}, bf16[1648,128]{1,0:T(8,128)(2,1)S(1)}, u32[]{:S(2)}, u32[]{:S(2)}) %collective-permute-start.10) | collective-permute-done | bytes 421920 | tf_op jit(solution)/shard_map/ppermute | solution.py:491
  75.7 7.4 %all-to-all-start = ((bf16[16,128,128]{2,1,0:T(8,128)(2,1)}), bf16[16,128,128]{2,1,0:T(8,128)(2,1)S(1)}, u32[]{:S(2)}, u32[]{:S(2)}) async-start(bf16[16,128,128]{2,1,0:T(8,128)(2,1)} %pad_maximum_fusion), calls=%async_computation | async-start | bytes 1048576 | tf_op jit(solution)/shard_map/all_to_all | solution.py:577
  83.2 2.5 %collective-permute-start.11 = (bf16[112,128]{1,0:T(8,128)(2,1)S(1)}, bf16[112,128]{1,0:T(8,128)(2,1)S(1)}, u32[]{:S(2)}, u32[]{:S(2)}) collective-permute-start(bf16[112,128]{1,0:T(8,128)(2,1)S(1)} %get-tuple-element.55), channel_id=1, source_target_pairs={{0,480},{16,48},{32,0},{48,80},{64,32},{80,112},{96,64},{112,144},... | collective-permute-start | bytes 86024 | tf_op jit(solution)/shard_map/ppermute | solution.py:498
  85.7 7.9 %all-to-all-done = bf16[16,128,128]{2,1,0:T(8,128)(2,1)S(1)} async-done(((bf16[16,128,128]{2,1,0:T(8,128)(2,1)}), bf16[16,128,128]{2,1,0:T(8,128)(2,1)S(1)}, u32[]{:S(2)}, u32[]{:S(2)}) %all-to-all-start) | async-done | bytes 524320 | tf_op jit(solution)/shard_map/all_to_all | solution.py:577
  93.8 9.5 %collective-permute-start.12 = (bf16[288,128]{1,0:T(8,128)(2,1)S(1)}, bf16[288,128]{1,0:T(8,128)(2,1)S(1)}, u32[]{:S(2)}, u32[]{:S(2)}) collective-permute-start(bf16[288,128]{1,0:T(8,128)(2,1)S(1)} %pad_maximum_fusion.1), channel_id=1, source_target_pairs={{0,16},{16,0},{32,48},{48,32},{64,80},{80,64},{96,112},{112,96},{1... | collective-permute-start | bytes 221192 | tf_op jit(solution)/shard_map/ppermute | solution.py:494
  103.3 9.1 %collective-permute-done.12.rim_ref.got_ref = bf16[288,128]{1,0:T(8,128)(2,1)S(1)} collective-permute-done((bf16[288,128]{1,0:T(8,128)(2,1)S(1)}, bf16[288,128]{1,0:T(8,128)(2,1)S(1)}, u32[]{:S(2)}, u32[]{:S(2)}) %collective-permute-start.12) | collective-permute-done | bytes 73760 | tf_op jit(solution)/shard_map/ppermute | solution.py:494
  (39 shorter events, 5.6 us)
Async XLA Ops:
  0.6 34.6 %copy-start = (bf16[235,1024]{1,0:T(8,128)(2,1)S(1)}, bf16[235,1024]{1,0:T(8,128)(2,1)}, u32[]{:S(2)}) copy-start(bf16[235,1024]{1,0:T(8,128)(2,1)} %wig_ref.3) | copy-start | bytes 1443844
  2.9 32.3 %copy-start.5 = (bf16[400,128]{1,0:T(8,128)(2,1)S(1)}, bf16[400,128]{1,0:T(8,128)(2,1)}, u32[]{:S(2)}) copy-start(bf16[400,128]{1,0:T(8,128)(2,1)} %get-tuple-element.29.node_ref) | copy-start | bytes 307204
  2.9 26.5 %collective-permute-start.3 = (bf16[224,128]{1,0:T(8,128)(2,1)}, bf16[224,128]{1,0:T(8,128)(2,1)S(1)}, u32[]{:S(2)}, u32[]{:S(2)}) collective-permute-start(bf16[224,128]{1,0:T(8,128)(2,1)} %get-tuple-element.30), channel_id=1, source_target_pairs={{0,16},{16,0},{32,48},{48,32},{64,80},{80,64},{96,112},{112,96},{1... | collective-permute-start | bytes 172040 | tf_op jit(solution)/shard_map/ppermute | solution.py:494
  18.8 19.4 %collective-permute-start = (bf16[400,128]{1,0:T(8,128)(2,1)}, bf16[400,128]{1,0:T(8,128)(2,1)S(1)}, u32[]{:S(2)}, u32[]{:S(2)}) collective-permute-start(bf16[400,128]{1,0:T(8,128)(2,1)} %get-tuple-element.28.refs_0_), channel_id=1, source_target_pairs={{0,8},{1,9},{2,10},{3,11},{4,12},{5,13},{6,14},{7,15},{8,0},{9,1},... | collective-permute-start | bytes 307208 | tf_op jit(solution)/shard_map/ppermute | solution.py:491
  23.1 15.1 %collective-permute-start.1 = (bf16[400,128]{1,0:T(8,128)(2,1)}, bf16[400,128]{1,0:T(8,128)(2,1)S(1)}, u32[]{:S(2)}, u32[]{:S(2)}) collective-permute-start(bf16[400,128]{1,0:T(8,128)(2,1)} %get-tuple-element.28.refs_0_), channel_id=1, source_target_pairs={{0,4},{1,5},{2,6},{3,7},{4,0},{5,1},{6,2},{7,3},{8,12},{9,13},{10,... | collective-permute-start | bytes 307208 | tf_op jit(solution)/shard_map/ppermute | solution.py:491
  26.5 11.7 %collective-permute-start.2 = (bf16[400,128]{1,0:T(8,128)(2,1)}, bf16[400,128]{1,0:T(8,128)(2,1)S(1)}, u32[]{:S(2)}, u32[]{:S(2)}) collective-permute-start(bf16[400,128]{1,0:T(8,128)(2,1)} %get-tuple-element.28.refs_0_), channel_id=1, source_target_pairs={{0,2},{1,3},{2,0},{3,1},{4,6},{5,7},{6,4},{7,5},{8,10},{9,11},{10,... | collective-permute-start | bytes 307208 | tf_op jit(solution)/shard_map/ppermute | solution.py:491
  29.4 5.8 %copy-start.8 = (s32[1024]{0:T(1024)S(1)}, s32[1024]{0:T(1024)}, u32[]{:S(2)}) copy-start(s32[1024]{0:T(1024)} %param.13) | copy-start | bytes 12292
  29.5 5.8 %collective-permute-start.4 = (bf16[112,128]{1,0:T(8,128)(2,1)S(1)}, bf16[112,128]{1,0:T(8,128)(2,1)S(1)}, u32[]{:S(2)}, u32[]{:S(2)}) collective-permute-start(bf16[112,128]{1,0:T(8,128)(2,1)S(1)} %constant_dynamic-slice_fusion), channel_id=1, source_target_pairs={{0,32},{16,496},{32,64},{48,16},{64,96},{80,48},{96,128},{112,80},... | collective-permute-start | bytes 86024 | tf_op jit(solution)/shard_map/ppermute | solution.py:498
  35.2 1.0 copy-start.1
  36.2 11.9 %copy-start.2 = (bf16[400,128]{1,0:T(8,128)(2,1)S(1)}, bf16[400,128]{1,0:T(8,128)(2,1)}, u32[]{:S(2)}) copy-start(bf16[400,128]{1,0:T(8,128)(2,1)} %get-tuple-element.28.refs_0_) | copy-start | bytes 307204
  38.2 12.9 %collective-permute-start.5 = (bf16[400,128]{1,0:T(8,128)(2,1)S(1)}, bf16[400,128]{1,0:T(8,128)(2,1)}, u32[]{:S(2)}, u32[]{:S(2)}) collective-permute-start(bf16[400,128]{1,0:T(8,128)(2,1)S(1)} %collective-permute-done.refs_2_), channel_id=1, source_target_pairs={{0,4},{1,5},{2,6},{3,7},{4,0},{5,1},{6,2},{7,3},{8,12},{9,13},{10,... | collective-permute-start | bytes 307208 | tf_op jit(solution)/shard_map/ppermute | solution.py:491
  41.5 9.6 %collective-permute-start.6 = (bf16[400,128]{1,0:T(8,128)(2,1)S(1)}, bf16[400,128]{1,0:T(8,128)(2,1)S(1)}, u32[]{:S(2)}, u32[]{:S(2)}) collective-permute-start(bf16[400,128]{1,0:T(8,128)(2,1)S(1)} %collective-permute-done.refs_2_), channel_id=1, source_target_pairs={{0,2},{1,3},{2,0},{3,1},{4,6},{5,7},{6,4},{7,5},{8,10},{9,11},{10,... | collective-permute-start | bytes 307208 | tf_op jit(solution)/shard_map/ppermute | solution.py:491
  44.5 6.7 %collective-permute-start.7 = (bf16[400,128]{1,0:T(8,128)(2,1)S(1)}, bf16[400,128]{1,0:T(8,128)(2,1)S(1)}, u32[]{:S(2)}, u32[]{:S(2)}) collective-permute-start(bf16[400,128]{1,0:T(8,128)(2,1)S(1)} %collective-permute-done.1.refs_0_), channel_id=1, source_target_pairs={{0,2},{1,3},{2,0},{3,1},{4,6},{5,7},{6,4},{7,5},{8,10},{9,11},{10,... | collective-permute-start | bytes 307208 | tf_op jit(solution)/shard_map/ppermute | solution.py:491
  48.1 0.7 copy-start.7
  48.1 0.7 copy-start.6
  51.1 0.6 copy-start.3
  51.8 10.2 %collective-permute-start.9 = (bf16[3424,128]{1,0:T(8,128)(2,1)S(1)}, bf16[3424,128]{1,0:T(8,128)(2,1)S(1)}, u32[]{:S(2)}, u32[]{:S(2)}) collective-permute-start(bf16[3424,128]{1,0:T(8,128)(2,1)S(1)} %edge_in.1.own_ref.xo_ref), channel_id=1, source_target_pairs={{0,1},{1,0},{2,3},{3,2},{4,5},{5,4},{6,7},{7,6},{8,9},{9,8},{10,11... | collective-permute-start | bytes 2629640 | tf_op jit(solution)/shard_map/ppermute | solution.py:491
  53.7 8.8 %collective-permute-start.8 = (bf16[400,128]{1,0:T(8,128)(2,1)}, bf16[400,128]{1,0:T(8,128)(2,1)}, u32[]{:S(2)}, u32[]{:S(2)}) collective-permute-start(bf16[400,128]{1,0:T(8,128)(2,1)} %collective-permute-done.5.near_ref), channel_id=1, source_target_pairs={{0,2},{1,3},{2,0},{3,1},{4,6},{5,7},{6,4},{7,5},{8,10},{9,11},{10,... | collective-permute-start | bytes 307208 | tf_op jit(solution)/shard_map/ppermute | solution.py:491
  56.7 0.9 copy-start.4
  71.2 3.7 %collective-permute-start.10 = (bf16[1648,128]{1,0:T(8,128)(2,1)S(1)}, bf16[1648,128]{1,0:T(8,128)(2,1)S(1)}, u32[]{:S(2)}, u32[]{:S(2)}) collective-permute-start(bf16[1648,128]{1,0:T(8,128)(2,1)S(1)} %get-tuple-element.47), channel_id=1, source_target_pairs={{0,1},{1,0},{2,3},{3,2},{4,5},{5,4},{6,7},{7,6},{8,9},{9,8},{10,11... | collective-permute-start | bytes 1265672 | tf_op jit(solution)/shard_map/ppermute | solution.py:491
  75.7 17.9 %all-to-all-start = ((bf16[16,128,128]{2,1,0:T(8,128)(2,1)}), bf16[16,128,128]{2,1,0:T(8,128)(2,1)S(1)}, u32[]{:S(2)}, u32[]{:S(2)}) async-start(bf16[16,128,128]{2,1,0:T(8,128)(2,1)} %pad_maximum_fusion), calls=%async_computation | async-start | bytes 1048576 | tf_op jit(solution)/shard_map/all_to_all | solution.py:577
  83.2 10.5 %collective-permute-start.11 = (bf16[112,128]{1,0:T(8,128)(2,1)S(1)}, bf16[112,128]{1,0:T(8,128)(2,1)S(1)}, u32[]{:S(2)}, u32[]{:S(2)}) collective-permute-start(bf16[112,128]{1,0:T(8,128)(2,1)S(1)} %get-tuple-element.55), channel_id=1, source_target_pairs={{0,480},{16,48},{32,0},{48,80},{64,32},{80,112},{96,64},{112,144},... | collective-permute-start | bytes 86024 | tf_op jit(solution)/shard_map/ppermute | solution.py:498
  93.8 18.6 %collective-permute-start.12 = (bf16[288,128]{1,0:T(8,128)(2,1)S(1)}, bf16[288,128]{1,0:T(8,128)(2,1)S(1)}, u32[]{:S(2)}, u32[]{:S(2)}) collective-permute-start(bf16[288,128]{1,0:T(8,128)(2,1)S(1)} %pad_maximum_fusion.1), channel_id=1, source_target_pairs={{0,16},{16,0},{32,48},{48,32},{64,80},{80,64},{96,112},{112,96},{1... | collective-permute-start | bytes 221192 | tf_op jit(solution)/shard_map/ppermute | solution.py:494

commit v11 on v10

--- a/solution.py
+++ b/solution.py
@@ -107,13 +107,19 @@
     weight_out[...] = jnp.concatenate(parts + [blank], axis=0).astype(BF)
 
 
-def edge_in_kernel(h_ref, node_ref, near_ref, far_ref, weight_ref, src_ref, wig_ref, x_ref, rot, gathered):
+def edge_in_kernel(
+    h_ref, count_ref, node_ref, near_ref, far_ref, weight_ref, src_ref, dst_ref, scale_ref, wig_ref,
+    x_ref, factor_ref, dest_ref, rot, gathered, sem,
+):
     step = pl.program_id(0)
+    copy = pltpu.make_async_copy(weight_ref, x_ref.at[pl.ds(X_ROWS, 1376)], sem)
 
     @pl.when(step == 0)
     def _():
-        x_ref[X_ROWS:] = weight_ref[...]
-
+        copy.start()
+
+    factor_ref[...] = edge_factor(step, count_ref, scale_ref)
+    dest_ref[...] = dst_ref[...]
     h = h_ref[0]
     src = src_ref[...]
     own, before, after = source_hots(src)
@@ -153,6 +159,10 @@
             row = pl.multiple_of(step * (256 * EB // LANES) + 256 * half + start, 16)
             x_ref[pl.ds(row, 8 * len(members)), :] = block[:, half * LANES : half * LANES + LANES]
 
+    @pl.when(step == pl.num_programs(0) - 1)
+    def _():
+        copy.wait()
+
 
 def weight_kernel(k_ref, own_ref, sib_ref, zero_ref, one_ref, two_ref):
     k = k_ref[0]
@@ -230,10 +240,10 @@
     return jnp.where(slot < count_ref[0], 0.25 * scale_ref[...], 0.0)
 
 
-def rotate_kernel(pairs, z_ref, count_ref, *refs):
-    blocks, (dst_ref, scale_ref, wig_ref), outs = refs[: 2 * pairs], refs[2 * pairs : 2 * pairs + 3], refs[2 * pairs + 3 : -2]
+def rotate_kernel(pairs, z_ref, *refs):
+    blocks, (dst_ref, factor_ref, wig_ref), outs = refs[: 2 * pairs], refs[2 * pairs : 2 * pairs + 3], refs[2 * pairs + 3 : -2]
     gathered, rot = refs[-2:]
-    rot[...] = wig_ref[...].astype(F32) * edge_factor(pl.program_id(0), count_ref, scale_ref)
+    rot[...] = wig_ref[...].astype(F32) * factor_ref[...]
     dest = hot(iota((LANES, EB), 0) == dst_ref[...])
     for pair, eg_ref in enumerate(outs):
 
@@ -245,8 +255,8 @@
 
 
 def edge_kernel(
-    z_ref, count_ref, eg0, eg1, eg2, near_ref, far_ref,
-    dst_ref, src_ref, scale_ref, wig_ref, xo_ref, xs_ref, zero_ref, one_ref, two_ref,
+    z_ref, eg0, eg1, eg2, near_ref, far_ref,
+    dst_ref, src_ref, factor_ref, wig_ref, xo_ref, xs_ref, zero_ref, one_ref, two_ref,
     so_ref, go_ref, sib_ref,
     gathered, rot, plain, eg, acc, back, full, atoms, rims,
 ):
@@ -261,7 +271,7 @@
     z = z_ref[0]
     entries = wig_ref[...].astype(F32)
     plain[...] = entries
-    rot[...] = entries * edge_factor(step, count_ref, scale_ref)
+    rot[...] = entries * factor_ref[...]
     dest = hot(iota((LANES, EB), 0) == dst_ref[...])
 
     def rows_of(place, n):
@@ -371,29 +381,29 @@
     return pl.BlockSpec((235, EB), lambda i: (0, i))
 
 
-def rotate_call(z_s, edge_count, blocks, dst, scale, wigner):
+def rotate_call(z_s, blocks, dst, factor, wigner):
     slots = dst.shape[1]
     pairs = len(blocks) // 2
     return pl.pallas_call(
         functools.partial(rotate_kernel, pairs),
         out_shape=[sds((464, slots), BF)] * pairs,
         grid=(slots // EB,),
-        in_specs=[smem(), smem()] + [whole((400, 128))] * len(blocks) + [row_spec(), row_spec(), wig_spec()],
+        in_specs=[smem()] + [whole((400, 128))] * len(blocks) + [row_spec(), row_spec(), wig_spec()],
         out_specs=[pl.BlockSpec((464, EB), lambda i: (0, i))] * pairs,
         scratch_shapes=[pltpu.VMEM((pairs, 2, 400, EB), F32), pltpu.VMEM((235, EB), F32)],
         compiler_params=params(),
         name="rotate",
-    )(z_s, edge_count, *blocks, dst, scale, wigner)
-
-
-def edge_call(z_s, edge_count, egs, pair, dst, src, scale, wigner, x_own, x_sib, weights):
+    )(z_s, *blocks, dst, factor, wigner)
+
+
+def edge_call(z_s, egs, pair, dst, src, factor, wigner, x_own, x_sib, weights):
     slots = dst.shape[1]
     x_spec = pl.BlockSpec((256 * EB // LANES, LANES), lambda i: (i, 0))
     return pl.pallas_call(
         edge_kernel,
         out_shape=(sds((1024, 128), BF), sds((624, 128), F32), sds((1648, 128), BF)),
         grid=(slots // EB,),
-        in_specs=[smem(), smem()]
+        in_specs=[smem()]
         + [pl.BlockSpec((464, EB), lambda i: (0, i))] * 3
         + [whole((400, 128)), whole((400, 128)), row_spec(), row_spec(), row_spec(), wig_spec(), x_spec, x_spec]
         + [whole((112, 512)), whole((192, 768)), whole((160, 640))],
@@ -411,10 +421,10 @@
         ],
         compiler_params=params(),
         name="edge",
-    )(z_s, edge_count, *egs, *pair, dst, src, scale, wigner, x_own, x_sib, *weights)
-
-
-def finish_kernel(mine_ref, got_ref, zero_ref, one_ref, two_ref):
+    )(z_s, *egs, *pair, dst, src, factor, wigner, x_own, x_sib, *weights)
+
+
+def finish(mine_ref, got_ref, zero_ref, one_ref, two_ref):
     total = mine_ref[...] + got_ref[224:288].astype(F32)
 
     def moved(lane):
@@ -434,7 +444,8 @@
                     ref[w, lp, l] = source[row : row + 4, 0:8]
 
 
-def join_kernel(h_ref, own_ref, rim_ref, out_ref):
+def end_kernel(h_ref, own_ref, mine_ref, rim_ref, out_ref, zero_ref, one_ref, two_ref):
+    finish(mine_ref, rim_ref, zero_ref, one_ref, two_ref)
     h = h_ref[0]
     base_a = jnp.where(h == 0, 96, 0)
     base_b = 96 - base_a
@@ -515,25 +526,25 @@
     near = cross(rims)
 
     def rotated(*blocks):
-        return rotate_call(z_s, edge_count, blocks, dst, scale, wigner)
+        return rotate_call(z_s, blocks, dest, factor, wigner)
 
     b4 = across(b0, 8)
     b2 = across(b0, 4)
     b1 = across(b0, 2)
     far = shift(lax.dynamic_slice_in_dim(near, 112 * high, 112, 0), True)
 
-    x_own = pl.pallas_call(
+    x_own, factor, dest = pl.pallas_call(
         edge_in_kernel,
-        out_shape=sds((X_ROWS + 1376, 128), BF),
+        out_shape=(sds((X_ROWS + 1376, 128), BF), sds((1, slots), F32), sds((1, slots), jnp.int32)),
         grid=(steps,),
-        in_specs=[smem(), whole((400, 128)), whole((224, 128)), whole((112, 128)), whole((1376, 128))]
-        + [row_spec(), wig_spec()],
-        out_specs=whole((X_ROWS + 1376, 128)),
-        scratch_shapes=[pltpu.VMEM((235, EB), F32), pltpu.VMEM((400, EB), F32)],
+        in_specs=[smem(), smem(), whole((400, 128)), whole((224, 128)), whole((112, 128))]
+        + [pl.BlockSpec(memory_space=pltpu.HBM), row_spec(), row_spec(), row_spec(), wig_spec()],
+        out_specs=(whole((X_ROWS + 1376, 128)), row_spec(), row_spec()),
+        scratch_shapes=[pltpu.VMEM((235, EB), F32), pltpu.VMEM((400, EB), F32), pltpu.SemaphoreType.DMA],
         compiler_params=params(),
         cost_estimate=light(),
         name="edge_in",
-    )(h_s, node, near, far, w_own, src, wigner)
+    )(h_s, edge_count, node, near, far, w_own, src, dst, scale, wigner)
     b4, b2, b1, x_own = lax.optimization_barrier((b4, b2, b1, x_own))
     b6 = across(b4, 4)
     b5 = across(b4, 2)
@@ -557,7 +568,7 @@
     )(k_s, x_own, x_sib)
 
     s_own, g_own, to_sib = edge_call(
-        z_s, edge_count, (eg0, eg1, eg2), (b6, b7), dst, src, scale, wigner, x_own, x_sib, (wz, wo, wt)
+        z_s, (eg0, eg1, eg2), (b6, b7), dest, src, factor, wigner, x_own, x_sib, (wz, wo, wt)
     )
 
     got = across(to_sib, 1)
@@ -585,27 +596,25 @@
     far_rim = shift(jnp.where(high == 0, left, right), False)
 
     crossed = cross(jnp.concatenate([near_rim, far_rim, other.astype(BF).reshape(64, 128)], axis=0))
-    grad_x = pl.pallas_call(
-        join_kernel,
-        out_shape=sds((49, 8, 128), F32),
+    grad_x, zero, one, second = pl.pallas_call(
+        end_kernel,
+        out_shape=(
+            sds((49, 8, 128), F32),
+            sds((7, 7, 4, 8), F32),
+            sds((2, 6, 6, 4, 8), F32),
+            sds((2, 5, 5, 4, 8), F32),
+        ),
         grid=(1,),
-        in_specs=[smem(), whole((624, 128)), whole((288, 128))],
-        out_specs=whole((49, 8, 128)),
+        in_specs=[smem(), whole((624, 128)), whole((64, 128)), whole((288, 128))],
+        out_specs=(
+            whole((49, 8, 128)),
+            whole((7, 7, 4, 8)),
+            whole((2, 6, 6, 4, 8)),
+            whole((2, 5, 5, 4, 8)),
+        ),
         compiler_params=params(),
-        cost_estimate=light(),
-        name="join",
-    )(h_s, g_all, crossed)
-
-    zero, one, second = pl.pallas_call(
-        finish_kernel,
-        out_shape=(sds((7, 7, 4, 8), F32), sds((2, 6, 6, 4, 8), F32), sds((2, 5, 5, 4, 8), F32)),
-        grid=(1,),
-        in_specs=[whole((64, 128)), whole((288, 128))],
-        out_specs=(whole((7, 7, 4, 8)), whole((2, 6, 6, 4, 8)), whole((2, 5, 5, 4, 8))),
-        compiler_params=params(),
-        cost_estimate=light(),
-        name="finish",
-    )(mine.reshape(64, 128), crossed)
+        name="end",
+    )(h_s, g_all, mine.reshape(64, 128), crossed)
     grad_zero = zero.transpose(0, 3, 1, 2)
     grad_one = one.transpose(0, 1, 4, 2, 3)
     grad_two = second.transpose(0, 1, 4, 2, 3)

time: 115 us -> 114 us (level)
    ppermute x9, waiting for transfers between devices: 1.55 us -> 2.77 us  [across(): return lax.ppermute(x, 'chan', [(i, i ^ mask) for i in range(16)])]
    pallas_call x3 -> x2, Pallas kernels: 3.72 us -> 3.08 us  [the longest x1 2.09 us: body(): pl.pallas_call(edge_in_kernel, out_shape=(sds((X_ROWS + 1376, 128), BF),...]
  transfers between devices with their start and end apart: 14 -> 14, of which waited for: 4 -> 5; matrix products, arithmetic and copies ran while one was open for 0% -> 0% of each run, Pallas kernels for 8% -> 8%
where the time goes in v11:
time: 114 us; the launch traced here: 113 us
  starting transfers between devices  64.2 us (56%)
  waiting for transfers between devices  21.4 us (19%)
  Pallas kernels  21.3 us (19%)
  local copies, waits for them, and re-layouts  3.24 us (3%)
  between operations  1.63 us (1%)
    ppermute x9, starting transfers between devices, across(): return lax.ppermute(x, 'chan', [(i, i ^ mask) for i in range(16)])  26.7 us
    ppermute x2, starting transfers between devices, cross(): return lax.ppermute(x, 'brick', [(i, i ^ 1) for i in range(32)])  24.5 us
    ppermute x2, waiting for transfers between devices, cross(): return lax.ppermute(x, 'brick', [(i, i ^ 1) for i in range(32)])  8.67 us
    pallas_call x1, Pallas kernels, edge_call(): pl.pallas_call(edge_kernel, out_shape=(sds((1024, 128), BF), sds((624, 12...  8.64 us
    all_to_all x1, waiting for transfers between devices, body(): lax.all_to_all(send, ('brick', 'chan'), 0, 0, axis_index_groups=groups)  7.95 us
    all_to_all x1, starting transfers between devices, body(): lax.all_to_all(send, ('brick', 'chan'), 0, 0, axis_index_groups=groups)  7.45 us
    pallas_call x2, Pallas kernels, rotate_call(): pl.pallas_call(functools.partial(rotate_kernel, pairs), out_shape=[sds((4...  6.76 us
    ppermute x2, starting transfers between devices, shift(): return lax.ppermute(x, 'brick', route)  5.58 us
  transfers between devices with their start and end apart: 14, of which 5 were waited for; matrix products, arithmetic and copies ran while one was open for 0% of the time, Pallas kernels for 8%

profile of v11, /device:TPU:4, one launch (start us, length us, event | category | flops | bytes accessed | tf_op | source)
XLA Modules:
  0.0 112.8 jit_solution(9942384965137728735)
XLA Ops:
  0.7 2.3 %pack.1 = (bf16[400,128]{1,0:T(8,128)(2,1)}, bf16[400,128]{1,0:T(8,128)(2,1)}, bf16[224,128]{1,0:T(8,128)(2,1)}, bf16[1376,128]{1,0:T(8,128)(2,1)}) custom-call(bf16[49,8,128]{2,1,0:T(8,128)(2,1)} %node_ref.1, bf16[49,8,128]{2,1,0:T(8,128)(2,1)} %cot_ref.1, bf16[49,8,128]{2,1,0:T(8,128)(2,1)} %bitcast.34, bf16[72,8,128]{2,1,0:T(8,128)(2,1)} %bitcast.32, ...), custom_call_target="tpu_custom_call" | custom-call | flops 1 | bytes 1 | tf_op jit(solution)/shard_map/pack/pallas_call | solution.py:516
  2.9 15.8 %collective-permute-start.3 = (bf16[224,128]{1,0:T(8,128)(2,1)}, bf16[224,128]{1,0:T(8,128)(2,1)S(1)}, u32[]{:S(2)}, u32[]{:S(2)}) collective-permute-start(bf16[224,128]{1,0:T(8,128)(2,1)} %get-tuple-element.34), channel_id=1, source_target_pairs={{0,16},{16,0},{32,48},{48,32},{64,80},{80,64},{96,112},{112,96},{1... | collective-permute-start | bytes 172040 | tf_op jit(solution)/shard_map/ppermute | solution.py:505
  18.8 4.3 %collective-permute-start = (bf16[400,128]{1,0:T(8,128)(2,1)}, bf16[400,128]{1,0:T(8,128)(2,1)S(1)}, u32[]{:S(2)}, u32[]{:S(2)}) collective-permute-start(bf16[400,128]{1,0:T(8,128)(2,1)} %get-tuple-element.32.refs_0_), channel_id=1, source_target_pairs={{0,8},{1,9},{2,10},{3,11},{4,12},{5,13},{6,14},{7,15},{8,0},{9,1},... | collective-permute-start | bytes 307208 | tf_op jit(solution)/shard_map/ppermute | solution.py:502
  23.1 3.4 %collective-permute-start.1 = (bf16[400,128]{1,0:T(8,128)(2,1)}, bf16[400,128]{1,0:T(8,128)(2,1)S(1)}, u32[]{:S(2)}, u32[]{:S(2)}) collective-permute-start(bf16[400,128]{1,0:T(8,128)(2,1)} %get-tuple-element.32.refs_0_), channel_id=1, source_target_pairs={{0,4},{1,5},{2,6},{3,7},{4,0},{5,1},{6,2},{7,3},{8,12},{9,13},{10,... | collective-permute-start | bytes 307208 | tf_op jit(solution)/shard_map/ppermute | solution.py:502
  26.5 2.9 %collective-permute-start.2 = (bf16[400,128]{1,0:T(8,128)(2,1)}, bf16[400,128]{1,0:T(8,128)(2,1)S(1)}, u32[]{:S(2)}, u32[]{:S(2)}) collective-permute-start(bf16[400,128]{1,0:T(8,128)(2,1)} %get-tuple-element.32.refs_0_), channel_id=1, source_target_pairs={{0,2},{1,3},{2,0},{3,1},{4,6},{5,7},{6,4},{7,5},{8,10},{9,11},{10,... | collective-permute-start | bytes 307208 | tf_op jit(solution)/shard_map/ppermute | solution.py:502
  29.4 3.1 %collective-permute-start.4 = (bf16[112,128]{1,0:T(8,128)(2,1)S(1)}, bf16[112,128]{1,0:T(8,128)(2,1)S(1)}, u32[]{:S(2)}, u32[]{:S(2)}) collective-permute-start(bf16[112,128]{1,0:T(8,128)(2,1)S(1)} %constant_dynamic-slice_fusion), channel_id=1, source_target_pairs={{0,32},{16,496},{32,64},{48,16},{64,96},{80,48},{96,128},{112,80},... | collective-permute-start | bytes 86024 | tf_op jit(solution)/shard_map/ppermute | solution.py:509
  33.2 2.0 %collective-permute-done.4.far_ref = bf16[112,128]{1,0:T(8,128)(2,1)S(1)} collective-permute-done((bf16[112,128]{1,0:T(8,128)(2,1)S(1)}, bf16[112,128]{1,0:T(8,128)(2,1)S(1)}, u32[]{:S(2)}, u32[]{:S(2)}) %collective-permute-start.4) | collective-permute-done | bytes 28704 | tf_op jit(solution)/shard_map/ppermute | solution.py:509
  36.9 2.1 %edge_in.1 = (bf16[3424,128]{1,0:T(8,128)(2,1)S(1)}, f32[1,1024]{1,0:T(1,128)S(1)}, s32[1,1024]{1,0:T(1,128)S(1)}) custom-call(s32[1]{0:T(128)} %bitcast.h_ref, s32[1]{0:T(128)S(6)} %copy.14.count_ref, bf16[400,128]{1,0:T(8,128)(2,1)S(1)} %copy-done.3, bf16[224,128]{1,0:T(8,128)(2,1)S(1)} %collective-permute-done.3.near_ref, ...), custom_call_target="tpu_custom_call" | custom-call | flops 1 | bytes 1 | tf_op jit(solution)/shard_map/edge_in/pallas_call | solution.py:536
  39.0 3.4 %collective-permute-start.5 = (bf16[400,128]{1,0:T(8,128)(2,1)S(1)}, bf16[400,128]{1,0:T(8,128)(2,1)}, u32[]{:S(2)}, u32[]{:S(2)}) collective-permute-start(bf16[400,128]{1,0:T(8,128)(2,1)S(1)} %collective-permute-done.refs_2_), channel_id=1, source_target_pairs={{0,4},{1,5},{2,6},{3,7},{4,0},{5,1},{6,2},{7,3},{8,12},{9,13},{10,... | collective-permute-start | bytes 307208 | tf_op jit(solution)/shard_map/ppermute | solution.py:502
  42.4 2.9 %collective-permute-start.6 = (bf16[400,128]{1,0:T(8,128)(2,1)S(1)}, bf16[400,128]{1,0:T(8,128)(2,1)S(1)}, u32[]{:S(2)}, u32[]{:S(2)}) collective-permute-start(bf16[400,128]{1,0:T(8,128)(2,1)S(1)} %collective-permute-done.refs_2_), channel_id=1, source_target_pairs={{0,2},{1,3},{2,0},{3,1},{4,6},{5,7},{6,4},{7,5},{8,10},{9,11},{10,... | collective-permute-start | bytes 307208 | tf_op jit(solution)/shard_map/ppermute | solution.py:502
  45.3 2.9 %collective-permute-start.7 = (bf16[400,128]{1,0:T(8,128)(2,1)S(1)}, bf16[400,128]{1,0:T(8,128)(2,1)S(1)}, u32[]{:S(2)}, u32[]{:S(2)}) collective-permute-start(bf16[400,128]{1,0:T(8,128)(2,1)S(1)} %collective-permute-done.1.refs_0_), channel_id=1, source_target_pairs={{0,2},{1,3},{2,0},{3,1},{4,6},{5,7},{6,4},{7,5},{8,10},{9,11},{10,... | collective-permute-start | bytes 307208 | tf_op jit(solution)/shard_map/ppermute | solution.py:502
  48.3 2.4 %rotate.2.eg0 = bf16[464,1024]{1,0:T(8,128)(2,1)S(1)} custom-call(s32[1]{0:T(128)} %bitcast.1.z_ref, bf16[400,128]{1,0:T(8,128)(2,1)S(1)} %copy-done.2, bf16[400,128]{1,0:T(8,128)(2,1)S(1)} %collective-permute-done.2.refs_1_, s32[1,1024]{1,0:T(1,128)S(1)} %get-tuple-element.41.refs_2_.refs_4_.dst_ref, ...), custom_call_target="tpu_custom_call" | custom-call | tf_op jit(solution)/shard_map/rotate/pallas_call | solution.py:387
  50.7 1.2 %collective-permute-done.7.refs_1_ = bf16[400,128]{1,0:T(8,128)(2,1)S(1)} collective-permute-done((bf16[400,128]{1,0:T(8,128)(2,1)S(1)}, bf16[400,128]{1,0:T(8,128)(2,1)S(1)}, u32[]{:S(2)}, u32[]{:S(2)}) %collective-permute-start.7) | collective-permute-done | bytes 102432 | tf_op jit(solution)/shard_map/ppermute | solution.py:502
  52.5 1.9 %collective-permute-start.9 = (bf16[3424,128]{1,0:T(8,128)(2,1)S(1)}, bf16[3424,128]{1,0:T(8,128)(2,1)S(1)}, u32[]{:S(2)}, u32[]{:S(2)}) collective-permute-start(bf16[3424,128]{1,0:T(8,128)(2,1)S(1)} %get-tuple-element.49.own_ref.xo_ref), channel_id=1, source_target_pairs={{0,1},{1,0},{2,3},{3,2},{4,5},{5,4},{6,7},{7,6},{8,9},{9,8},{10,11... | collective-permute-start | bytes 2629640 | tf_op jit(solution)/shard_map/ppermute | solution.py:502
  54.4 2.9 %collective-permute-start.8 = (bf16[400,128]{1,0:T(8,128)(2,1)}, bf16[400,128]{1,0:T(8,128)(2,1)}, u32[]{:S(2)}, u32[]{:S(2)}) collective-permute-start(bf16[400,128]{1,0:T(8,128)(2,1)} %collective-permute-done.5.near_ref), channel_id=1, source_target_pairs={{0,2},{1,3},{2,0},{3,1},{4,6},{5,7},{6,4},{7,5},{8,10},{9,11},{10,... | collective-permute-start | bytes 307208 | tf_op jit(solution)/shard_map/ppermute | solution.py:502
  58.3 4.4 %rotate.3 = (bf16[464,1024]{1,0:T(8,128)(2,1)S(1)}, bf16[464,1024]{1,0:T(8,128)(2,1)S(1)}) custom-call(s32[1]{0:T(128)} %bitcast.1.z_ref, bf16[400,128]{1,0:T(8,128)(2,1)S(1)} %collective-permute-done.1.refs_0_, bf16[400,128]{1,0:T(8,128)(2,1)S(1)} %copy-done.5, bf16[400,128]{1,0:T(8,128)(2,1)S(1)} %collective-permute-done.refs_2_, ...), custom_call_target="tpu_custom_call" | custom-call | tf_op jit(solution)/shard_map/rotate/pallas_call | solution.py:387
  63.2 8.6 %edge.1 = (bf16[1024,128]{1,0:T(8,128)(2,1)S(1)}, f32[624,128]{1,0:T(8,128)S(1)}, bf16[1648,128]{1,0:T(8,128)(2,1)S(1)}) custom-call(s32[1]{0:T(128)} %bitcast.1.z_ref, bf16[464,1024]{1,0:T(8,128)(2,1)S(1)} %rotate.2.eg0, bf16[464,1024]{1,0:T(8,128)(2,1)S(1)} %get-tuple-element.46.eg1, bf16[464,1024]{1,0:T(8,128)(2,1)S(1)} %get-tuple-element.47.eg2, ...), custom_call_target="tpu_custom_call" | custom-call | tf_op jit(solution)/shard_map/edge/pallas_call | solution.py:402
  71.9 2.1 %collective-permute-start.10 = (bf16[1648,128]{1,0:T(8,128)(2,1)S(1)}, bf16[1648,128]{1,0:T(8,128)(2,1)S(1)}, u32[]{:S(2)}, u32[]{:S(2)}) collective-permute-start(bf16[1648,128]{1,0:T(8,128)(2,1)S(1)} %get-tuple-element.54), channel_id=1, source_target_pairs={{0,1},{1,0},{2,3},{3,2},{4,5},{5,4},{6,7},{7,6},{8,9},{9,8},{10,11... | collective-permute-start | bytes 1265672 | tf_op jit(solution)/shard_map/ppermute | solution.py:502
  74.0 1.5 %collective-permute-done.10 = bf16[1648,128]{1,0:T(8,128)(2,1)S(1)} collective-permute-done((bf16[1648,128]{1,0:T(8,128)(2,1)S(1)}, bf16[1648,128]{1,0:T(8,128)(2,1)S(1)}, u32[]{:S(2)}, u32[]{:S(2)}) %collective-permute-start.10) | collective-permute-done | bytes 421920 | tf_op jit(solution)/shard_map/ppermute | solution.py:502
  76.4 7.5 %all-to-all-start = ((bf16[16,128,128]{2,1,0:T(8,128)(2,1)}), bf16[16,128,128]{2,1,0:T(8,128)(2,1)S(1)}, u32[]{:S(2)}, u32[]{:S(2)}) async-start(bf16[16,128,128]{2,1,0:T(8,128)(2,1)} %pad_maximum_fusion), calls=%async_computation | async-start | bytes 1048576 | tf_op jit(solution)/shard_map/all_to_all | solution.py:588
  83.9 2.5 %collective-permute-start.11 = (bf16[112,128]{1,0:T(8,128)(2,1)S(1)}, bf16[112,128]{1,0:T(8,128)(2,1)S(1)}, u32[]{:S(2)}, u32[]{:S(2)}) collective-permute-start(bf16[112,128]{1,0:T(8,128)(2,1)S(1)} %get-tuple-element.63), channel_id=1, source_target_pairs={{0,480},{16,48},{32,0},{48,80},{64,32},{80,112},{96,64},{112,144},... | collective-permute-start | bytes 86024 | tf_op jit(solution)/shard_map/ppermute | solution.py:509
  86.4 8.0 %all-to-all-done = bf16[16,128,128]{2,1,0:T(8,128)(2,1)S(1)} async-done(((bf16[16,128,128]{2,1,0:T(8,128)(2,1)}), bf16[16,128,128]{2,1,0:T(8,128)(2,1)S(1)}, u32[]{:S(2)}, u32[]{:S(2)}) %all-to-all-start) | async-done | bytes 524320 | tf_op jit(solution)/shard_map/all_to_all | solution.py:588
  94.5 8.6 %collective-permute-start.12 = (bf16[288,128]{1,0:T(8,128)(2,1)S(1)}, bf16[288,128]{1,0:T(8,128)(2,1)S(1)}, u32[]{:S(2)}, u32[]{:S(2)}) collective-permute-start(bf16[288,128]{1,0:T(8,128)(2,1)S(1)} %pad_maximum_fusion.1), channel_id=1, source_target_pairs={{0,16},{16,0},{32,48},{48,32},{64,80},{80,64},{96,112},{112,96},{1... | collective-permute-start | bytes 221192 | tf_op jit(solution)/shard_map/ppermute | solution.py:505
  103.2 8.7 %collective-permute-done.12.rim_ref = bf16[288,128]{1,0:T(8,128)(2,1)S(1)} collective-permute-done((bf16[288,128]{1,0:T(8,128)(2,1)S(1)}, bf16[288,128]{1,0:T(8,128)(2,1)S(1)}, u32[]{:S(2)}, u32[]{:S(2)}) %collective-permute-start.12) | collective-permute-done | bytes 73760 | tf_op jit(solution)/shard_map/ppermute | solution.py:505
  (38 shorter events, 5.8 us)
Async XLA Ops:
  0.6 34.6 %copy-start = (bf16[235,1024]{1,0:T(8,128)(2,1)S(1)}, bf16[235,1024]{1,0:T(8,128)(2,1)}, u32[]{:S(2)}) copy-start(bf16[235,1024]{1,0:T(8,128)(2,1)} %wig_ref.3) | copy-start | bytes 1443844
  0.6 34.6 %copy-start.8 = (f32[1024]{0:T(1024)S(1)}, f32[1024]{0:T(1024)}, u32[]{:S(2)}) copy-start(f32[1024]{0:T(1024)} %param.15) | copy-start | bytes 12292
  2.9 32.3 %copy-start.3 = (bf16[400,128]{1,0:T(8,128)(2,1)S(1)}, bf16[400,128]{1,0:T(8,128)(2,1)}, u32[]{:S(2)}) copy-start(bf16[400,128]{1,0:T(8,128)(2,1)} %get-tuple-element.33.node_ref) | copy-start | bytes 307204
  2.9 26.5 %collective-permute-start.3 = (bf16[224,128]{1,0:T(8,128)(2,1)}, bf16[224,128]{1,0:T(8,128)(2,1)S(1)}, u32[]{:S(2)}, u32[]{:S(2)}) collective-permute-start(bf16[224,128]{1,0:T(8,128)(2,1)} %get-tuple-element.34), channel_id=1, source_target_pairs={{0,16},{16,0},{32,48},{48,32},{64,80},{80,64},{96,112},{112,96},{1... | collective-permute-start | bytes 172040 | tf_op jit(solution)/shard_map/ppermute | solution.py:505
  18.8 20.2 %collective-permute-start = (bf16[400,128]{1,0:T(8,128)(2,1)}, bf16[400,128]{1,0:T(8,128)(2,1)S(1)}, u32[]{:S(2)}, u32[]{:S(2)}) collective-permute-start(bf16[400,128]{1,0:T(8,128)(2,1)} %get-tuple-element.32.refs_0_), channel_id=1, source_target_pairs={{0,8},{1,9},{2,10},{3,11},{4,12},{5,13},{6,14},{7,15},{8,0},{9,1},... | collective-permute-start | bytes 307208 | tf_op jit(solution)/shard_map/ppermute | solution.py:502
  23.1 15.9 %collective-permute-start.1 = (bf16[400,128]{1,0:T(8,128)(2,1)}, bf16[400,128]{1,0:T(8,128)(2,1)S(1)}, u32[]{:S(2)}, u32[]{:S(2)}) collective-permute-start(bf16[400,128]{1,0:T(8,128)(2,1)} %get-tuple-element.32.refs_0_), channel_id=1, source_target_pairs={{0,4},{1,5},{2,6},{3,7},{4,0},{5,1},{6,2},{7,3},{8,12},{9,13},{10,... | collective-permute-start | bytes 307208 | tf_op jit(solution)/shard_map/ppermute | solution.py:502
  26.5 12.6 %collective-permute-start.2 = (bf16[400,128]{1,0:T(8,128)(2,1)}, bf16[400,128]{1,0:T(8,128)(2,1)S(1)}, u32[]{:S(2)}, u32[]{:S(2)}) collective-permute-start(bf16[400,128]{1,0:T(8,128)(2,1)} %get-tuple-element.32.refs_0_), channel_id=1, source_target_pairs={{0,2},{1,3},{2,0},{3,1},{4,6},{5,7},{6,4},{7,5},{8,10},{9,11},{10,... | collective-permute-start | bytes 307208 | tf_op jit(solution)/shard_map/ppermute | solution.py:502
  29.4 5.8 %collective-permute-start.4 = (bf16[112,128]{1,0:T(8,128)(2,1)S(1)}, bf16[112,128]{1,0:T(8,128)(2,1)S(1)}, u32[]{:S(2)}, u32[]{:S(2)}) collective-permute-start(bf16[112,128]{1,0:T(8,128)(2,1)S(1)} %constant_dynamic-slice_fusion), channel_id=1, source_target_pairs={{0,32},{16,496},{32,64},{48,16},{64,96},{80,48},{96,128},{112,80},... | collective-permute-start | bytes 86024 | tf_op jit(solution)/shard_map/ppermute | solution.py:509
  35.2 0.7 copy-start.7
  35.2 0.7 copy-start.6
  35.9 1.0 copy-start.1
  36.9 11.4 %copy-start.2 = (bf16[400,128]{1,0:T(8,128)(2,1)S(1)}, bf16[400,128]{1,0:T(8,128)(2,1)}, u32[]{:S(2)}) copy-start(bf16[400,128]{1,0:T(8,128)(2,1)} %get-tuple-element.32.refs_0_) | copy-start | bytes 307204
  39.0 11.6 %collective-permute-start.5 = (bf16[400,128]{1,0:T(8,128)(2,1)S(1)}, bf16[400,128]{1,0:T(8,128)(2,1)}, u32[]{:S(2)}, u32[]{:S(2)}) collective-permute-start(bf16[400,128]{1,0:T(8,128)(2,1)S(1)} %collective-permute-done.refs_2_), channel_id=1, source_target_pairs={{0,4},{1,5},{2,6},{3,7},{4,0},{5,1},{6,2},{7,3},{8,12},{9,13},{10,... | collective-permute-start | bytes 307208 | tf_op jit(solution)/shard_map/ppermute | solution.py:502
  42.4 8.3 %collective-permute-start.6 = (bf16[400,128]{1,0:T(8,128)(2,1)S(1)}, bf16[400,128]{1,0:T(8,128)(2,1)S(1)}, u32[]{:S(2)}, u32[]{:S(2)}) collective-permute-start(bf16[400,128]{1,0:T(8,128)(2,1)S(1)} %collective-permute-done.refs_2_), channel_id=1, source_target_pairs={{0,2},{1,3},{2,0},{3,1},{4,6},{5,7},{6,4},{7,5},{8,10},{9,11},{10,... | collective-permute-start | bytes 307208 | tf_op jit(solution)/shard_map/ppermute | solution.py:502
  45.3 6.6 %collective-permute-start.7 = (bf16[400,128]{1,0:T(8,128)(2,1)S(1)}, bf16[400,128]{1,0:T(8,128)(2,1)S(1)}, u32[]{:S(2)}, u32[]{:S(2)}) collective-permute-start(bf16[400,128]{1,0:T(8,128)(2,1)S(1)} %collective-permute-done.1.refs_0_), channel_id=1, source_target_pairs={{0,2},{1,3},{2,0},{3,1},{4,6},{5,7},{6,4},{7,5},{8,10},{9,11},{10,... | collective-permute-start | bytes 307208 | tf_op jit(solution)/shard_map/ppermute | solution.py:502
  51.9 0.6 copy-start.4
  52.5 10.2 %collective-permute-start.9 = (bf16[3424,128]{1,0:T(8,128)(2,1)S(1)}, bf16[3424,128]{1,0:T(8,128)(2,1)S(1)}, u32[]{:S(2)}, u32[]{:S(2)}) collective-permute-start(bf16[3424,128]{1,0:T(8,128)(2,1)S(1)} %get-tuple-element.49.own_ref.xo_ref), channel_id=1, source_target_pairs={{0,1},{1,0},{2,3},{3,2},{4,5},{5,4},{6,7},{7,6},{8,9},{9,8},{10,11... | collective-permute-start | bytes 2629640 | tf_op jit(solution)/shard_map/ppermute | solution.py:502
  54.4 8.8 %collective-permute-start.8 = (bf16[400,128]{1,0:T(8,128)(2,1)}, bf16[400,128]{1,0:T(8,128)(2,1)}, u32[]{:S(2)}, u32[]{:S(2)}) collective-permute-start(bf16[400,128]{1,0:T(8,128)(2,1)} %collective-permute-done.5.near_ref), channel_id=1, source_target_pairs={{0,2},{1,3},{2,0},{3,1},{4,6},{5,7},{6,4},{7,5},{8,10},{9,11},{10,... | collective-permute-start | bytes 307208 | tf_op jit(solution)/shard_map/ppermute | solution.py:502
  57.4 0.9 copy-start.5
  71.9 3.7 %collective-permute-start.10 = (bf16[1648,128]{1,0:T(8,128)(2,1)S(1)}, bf16[1648,128]{1,0:T(8,128)(2,1)S(1)}, u32[]{:S(2)}, u32[]{:S(2)}) collective-permute-start(bf16[1648,128]{1,0:T(8,128)(2,1)S(1)} %get-tuple-element.54), channel_id=1, source_target_pairs={{0,1},{1,0},{2,3},{3,2},{4,5},{5,4},{6,7},{7,6},{8,9},{9,8},{10,11... | collective-permute-start | bytes 1265672 | tf_op jit(solution)/shard_map/ppermute | solution.py:502
  76.4 18.0 %all-to-all-start = ((bf16[16,128,128]{2,1,0:T(8,128)(2,1)}), bf16[16,128,128]{2,1,0:T(8,128)(2,1)S(1)}, u32[]{:S(2)}, u32[]{:S(2)}) async-start(bf16[16,128,128]{2,1,0:T(8,128)(2,1)} %pad_maximum_fusion), calls=%async_computation | async-start | bytes 1048576 | tf_op jit(solution)/shard_map/all_to_all | solution.py:588
  83.9 10.5 %collective-permute-start.11 = (bf16[112,128]{1,0:T(8,128)(2,1)S(1)}, bf16[112,128]{1,0:T(8,128)(2,1)S(1)}, u32[]{:S(2)}, u32[]{:S(2)}) collective-permute-start(bf16[112,128]{1,0:T(8,128)(2,1)S(1)} %get-tuple-element.63), channel_id=1, source_target_pairs={{0,480},{16,48},{32,0},{48,80},{64,32},{80,112},{96,64},{112,144},... | collective-permute-start | bytes 86024 | tf_op jit(solution)/shard_map/ppermute | solution.py:509
  94.5 17.3 %collective-permute-start.12 = (bf16[288,128]{1,0:T(8,128)(2,1)S(1)}, bf16[288,128]{1,0:T(8,128)(2,1)S(1)}, u32[]{:S(2)}, u32[]{:S(2)}) collective-permute-start(bf16[288,128]{1,0:T(8,128)(2,1)S(1)} %pad_maximum_fusion.1), channel_id=1, source_target_pairs={{0,16},{16,0},{32,48},{48,32},{64,80},{80,64},{96,112},{112,96},{1... | collective-permute-start | bytes 221192 | tf_op jit(solution)/shard_map/ppermute | solution.py:505

commit v12 on v11

--- a/solution.py
+++ b/solution.py
@@ -553,7 +553,8 @@
 
     b6, b5, b3, x_own, eg0 = lax.optimization_barrier((b6, b5, b3, x_own, eg0))
     b7 = across(b6, 2)
-    eg1, eg2 = rotated(b2, b3, b4, b5)
+    (eg1,) = rotated(b2, b3)
+    (eg2,) = rotated(b4, b5)
     x_sib = across(x_own, 1)
 
     wz, wo, wt = pl.pallas_call(

time: 114 us -> 114 us (level)
  the two profiles are of different devices: /device:TPU:4 before, /device:TPU:56 now
where the time goes in v12:
time: 114 us; the launch traced here: 113 us
  starting transfers between devices  65.1 us (57%)
  Pallas kernels  21.6 us (19%)
  waiting for transfers between devices  21.5 us (19%)
  local copies, waits for them, and re-layouts  2.36 us (2%)
  between operations  1.65 us (1%)
    ppermute x9, starting transfers between devices, across(): return lax.ppermute(x, 'chan', [(i, i ^ mask) for i in range(16)])  26.7 us
    ppermute x2, starting transfers between devices, cross(): return lax.ppermute(x, 'brick', [(i, i ^ 1) for i in range(32)])  25 us
    ppermute x2, waiting for transfers between devices, cross(): return lax.ppermute(x, 'brick', [(i, i ^ 1) for i in range(32)])  9.4 us
    pallas_call x1, Pallas kernels, edge_call(): pl.pallas_call(edge_kernel, out_shape=(sds((1024, 128), BF), sds((624, 12...  8.62 us
    ppermute x2, starting transfers between devices, shift(): return lax.ppermute(x, 'brick', route)  8.28 us
    pallas_call x3, Pallas kernels, rotate_call(): pl.pallas_call(functools.partial(rotate_kernel, pairs), out_shape=[sds((4...  7.04 us
    all_to_all x1, waiting for transfers between devices, body(): lax.all_to_all(send, ('brick', 'chan'), 0, 0, axis_index_groups=groups)  5.51 us
    all_to_all x1, starting transfers between devices, body(): lax.all_to_all(send, ('brick', 'chan'), 0, 0, axis_index_groups=groups)  5.05 us
  transfers between devices with their start and end apart: 14, of which 5 were waited for; matrix products, arithmetic and copies ran while one was open for 0% of the time, Pallas kernels for 9%

profile of v12, /device:TPU:56, one launch (start us, length us, event | category | flops | bytes accessed | tf_op | source)
XLA Modules:
  0.0 113.2 jit_solution(13480812140361464949)
XLA Ops:
  0.7 2.3 %pack.1 = (bf16[400,128]{1,0:T(8,128)(2,1)}, bf16[400,128]{1,0:T(8,128)(2,1)}, bf16[224,128]{1,0:T(8,128)(2,1)}, bf16[1376,128]{1,0:T(8,128)(2,1)}) custom-call(bf16[49,8,128]{2,1,0:T(8,128)(2,1)} %node_ref.1, bf16[49,8,128]{2,1,0:T(8,128)(2,1)} %cot_ref.1, bf16[49,8,128]{2,1,0:T(8,128)(2,1)} %bitcast.34, bf16[72,8,128]{2,1,0:T(8,128)(2,1)} %bitcast.32, ...), custom_call_target="tpu_custom_call" | custom-call | flops 1 | bytes 1 | tf_op jit(solution)/shard_map/pack/pallas_call | solution.py:516
  2.9 14.9 %collective-permute-start.3 = (bf16[224,128]{1,0:T(8,128)(2,1)}, bf16[224,128]{1,0:T(8,128)(2,1)S(1)}, u32[]{:S(2)}, u32[]{:S(2)}) collective-permute-start(bf16[224,128]{1,0:T(8,128)(2,1)} %get-tuple-element.32), channel_id=1, source_target_pairs={{0,16},{16,0},{32,48},{48,32},{64,80},{80,64},{96,112},{112,96},{1... | collective-permute-start | bytes 172040 | tf_op jit(solution)/shard_map/ppermute | solution.py:505
  17.9 4.3 %collective-permute-start = (bf16[400,128]{1,0:T(8,128)(2,1)}, bf16[400,128]{1,0:T(8,128)(2,1)S(1)}, u32[]{:S(2)}, u32[]{:S(2)}) collective-permute-start(bf16[400,128]{1,0:T(8,128)(2,1)} %get-tuple-element.30.refs_0_), channel_id=1, source_target_pairs={{0,8},{1,9},{2,10},{3,11},{4,12},{5,13},{6,14},{7,15},{8,0},{9,1},... | collective-permute-start | bytes 307208 | tf_op jit(solution)/shard_map/ppermute | solution.py:502
  22.2 3.4 %collective-permute-start.1 = (bf16[400,128]{1,0:T(8,128)(2,1)}, bf16[400,128]{1,0:T(8,128)(2,1)S(1)}, u32[]{:S(2)}, u32[]{:S(2)}) collective-permute-start(bf16[400,128]{1,0:T(8,128)(2,1)} %get-tuple-element.30.refs_0_), channel_id=1, source_target_pairs={{0,4},{1,5},{2,6},{3,7},{4,0},{5,1},{6,2},{7,3},{8,12},{9,13},{10,... | collective-permute-start | bytes 307208 | tf_op jit(solution)/shard_map/ppermute | solution.py:502
  25.6 2.9 %collective-permute-start.2 = (bf16[400,128]{1,0:T(8,128)(2,1)}, bf16[400,128]{1,0:T(8,128)(2,1)S(1)}, u32[]{:S(2)}, u32[]{:S(2)}) collective-permute-start(bf16[400,128]{1,0:T(8,128)(2,1)} %get-tuple-element.30.refs_0_), channel_id=1, source_target_pairs={{0,2},{1,3},{2,0},{3,1},{4,6},{5,7},{6,4},{7,5},{8,10},{9,11},{10,... | collective-permute-start | bytes 307208 | tf_op jit(solution)/shard_map/ppermute | solution.py:502
  28.5 3.4 %collective-permute-start.4 = (bf16[112,128]{1,0:T(8,128)(2,1)S(1)}, bf16[112,128]{1,0:T(8,128)(2,1)S(1)}, u32[]{:S(2)}, u32[]{:S(2)}) collective-permute-start(bf16[112,128]{1,0:T(8,128)(2,1)S(1)} %constant_dynamic-slice_fusion), channel_id=1, source_target_pairs={{0,32},{16,496},{32,64},{48,16},{64,96},{80,48},{96,128},{112,80},... | collective-permute-start | bytes 86024 | tf_op jit(solution)/shard_map/ppermute | solution.py:509
  32.6 3.8 %collective-permute-done.4.far_ref = bf16[112,128]{1,0:T(8,128)(2,1)S(1)} collective-permute-done((bf16[112,128]{1,0:T(8,128)(2,1)S(1)}, bf16[112,128]{1,0:T(8,128)(2,1)S(1)}, u32[]{:S(2)}, u32[]{:S(2)}) %collective-permute-start.4) | collective-permute-done | bytes 28704 | tf_op jit(solution)/shard_map/ppermute | solution.py:509
  38.1 2.1 %edge_in.1 = (bf16[3424,128]{1,0:T(8,128)(2,1)S(1)}, f32[1,1024]{1,0:T(1,128)S(1)}, s32[1,1024]{1,0:T(1,128)S(1)}) custom-call(s32[1]{0:T(128)} %bitcast.h_ref, s32[1]{0:T(128)S(6)} %copy.14.count_ref, bf16[400,128]{1,0:T(8,128)(2,1)S(1)} %copy-done.3, bf16[224,128]{1,0:T(8,128)(2,1)S(1)} %collective-permute-done.3.near_ref, ...), custom_call_target="tpu_custom_call" | custom-call | flops 1 | bytes 1 | tf_op jit(solution)/shard_map/edge_in/pallas_call | solution.py:536
  40.2 3.4 %collective-permute-start.5 = (bf16[400,128]{1,0:T(8,128)(2,1)S(1)}, bf16[400,128]{1,0:T(8,128)(2,1)}, u32[]{:S(2)}, u32[]{:S(2)}) collective-permute-start(bf16[400,128]{1,0:T(8,128)(2,1)S(1)} %collective-permute-done.refs_0_), channel_id=1, source_target_pairs={{0,4},{1,5},{2,6},{3,7},{4,0},{5,1},{6,2},{7,3},{8,12},{9,13},{10,... | collective-permute-start | bytes 307208 | tf_op jit(solution)/shard_map/ppermute | solution.py:502
  43.6 2.9 %collective-permute-start.6 = (bf16[400,128]{1,0:T(8,128)(2,1)S(1)}, bf16[400,128]{1,0:T(8,128)(2,1)S(1)}, u32[]{:S(2)}, u32[]{:S(2)}) collective-permute-start(bf16[400,128]{1,0:T(8,128)(2,1)S(1)} %collective-permute-done.refs_0_), channel_id=1, source_target_pairs={{0,2},{1,3},{2,0},{3,1},{4,6},{5,7},{6,4},{7,5},{8,10},{9,11},{10,... | collective-permute-start | bytes 307208 | tf_op jit(solution)/shard_map/ppermute | solution.py:502
  46.5 2.9 %collective-permute-start.7 = (bf16[400,128]{1,0:T(8,128)(2,1)S(1)}, bf16[400,128]{1,0:T(8,128)(2,1)S(1)}, u32[]{:S(2)}, u32[]{:S(2)}) collective-permute-start(bf16[400,128]{1,0:T(8,128)(2,1)S(1)} %collective-permute-done.1.refs_0_), channel_id=1, source_target_pairs={{0,2},{1,3},{2,0},{3,1},{4,6},{5,7},{6,4},{7,5},{8,10},{9,11},{10,... | collective-permute-start | bytes 307208 | tf_op jit(solution)/shard_map/ppermute | solution.py:502
  49.5 2.4 %rotate.3.eg0 = bf16[464,1024]{1,0:T(8,128)(2,1)S(1)} custom-call(s32[1]{0:T(128)} %bitcast.1.z_ref, bf16[400,128]{1,0:T(8,128)(2,1)S(1)} %copy-done.2, bf16[400,128]{1,0:T(8,128)(2,1)S(1)} %collective-permute-done.2.refs_1_, s32[1,1024]{1,0:T(1,128)S(1)} %get-tuple-element.39.refs_2_.dst_ref, f32[1,1024]{1,0:T(1,128)S(1)} %get-tuple-element.40.refs_3_.factor_ref, ...), custom_call_target="tpu_custom_call" | custom-call | tf_op jit(solution)/shard_map/rotate/pallas_call | solution.py:387
  53.7 1.9 %collective-permute-start.9 = (bf16[3424,128]{1,0:T(8,128)(2,1)S(1)}, bf16[3424,128]{1,0:T(8,128)(2,1)S(1)}, u32[]{:S(2)}, u32[]{:S(2)}) collective-permute-start(bf16[3424,128]{1,0:T(8,128)(2,1)S(1)} %get-tuple-element.45.own_ref.xo_ref), channel_id=1, source_target_pairs={{0,1},{1,0},{2,3},{3,2},{4,5},{5,4},{6,7},{7,6},{8,9},{9,8},{10,11... | collective-permute-start | bytes 2629640 | tf_op jit(solution)/shard_map/ppermute | solution.py:502
  55.6 2.9 %collective-permute-start.8 = (bf16[400,128]{1,0:T(8,128)(2,1)}, bf16[400,128]{1,0:T(8,128)(2,1)}, u32[]{:S(2)}, u32[]{:S(2)}) collective-permute-start(bf16[400,128]{1,0:T(8,128)(2,1)} %collective-permute-done.5.near_ref), channel_id=1, source_target_pairs={{0,2},{1,3},{2,0},{3,1},{4,6},{5,7},{6,4},{7,5},{8,10},{9,11},{10,... | collective-permute-start | bytes 307208 | tf_op jit(solution)/shard_map/ppermute | solution.py:502
  58.6 2.4 %rotate.5.eg2 = bf16[464,1024]{1,0:T(8,128)(2,1)S(1)} custom-call(s32[1]{0:T(128)} %bitcast.1.z_ref, bf16[400,128]{1,0:T(8,128)(2,1)S(1)} %collective-permute-done.refs_0_, bf16[400,128]{1,0:T(8,128)(2,1)S(1)} %collective-permute-done.6.refs_1_, s32[1,1024]{1,0:T(1,128)S(1)} %get-tuple-element.39.refs_2_.dst_ref, ...), custom_call_target="tpu_custom_call" | custom-call | tf_op jit(solution)/shard_map/rotate/pallas_call | solution.py:387
  61.0 2.3 %rotate.4.eg1 = bf16[464,1024]{1,0:T(8,128)(2,1)S(1)} custom-call(s32[1]{0:T(128)} %bitcast.1.z_ref, bf16[400,128]{1,0:T(8,128)(2,1)S(1)} %collective-permute-done.1.refs_0_, bf16[400,128]{1,0:T(8,128)(2,1)S(1)} %copy-done.5, s32[1,1024]{1,0:T(1,128)S(1)} %get-tuple-element.39.refs_2_.dst_ref, f32[1,1024]{1,0:T(1,128)S(1)} %get-tuple-element.40.refs_3_.factor_ref, ...), custom_call_target="tpu_custom_call" | custom-call | tf_op jit(solution)/shard_map/rotate/pallas_call | solution.py:387
  63.9 8.6 %edge.1 = (bf16[1024,128]{1,0:T(8,128)(2,1)S(1)}, f32[624,128]{1,0:T(8,128)S(1)}, bf16[1648,128]{1,0:T(8,128)(2,1)S(1)}) custom-call(s32[1]{0:T(128)} %bitcast.1.z_ref, bf16[464,1024]{1,0:T(8,128)(2,1)S(1)} %rotate.3.eg0, bf16[464,1024]{1,0:T(8,128)(2,1)S(1)} %rotate.4.eg1, bf16[464,1024]{1,0:T(8,128)(2,1)S(1)} %rotate.5.eg2, ...), custom_call_target="tpu_custom_call" | custom-call | tf_op jit(solution)/shard_map/edge/pallas_call | solution.py:402
  72.5 2.1 %collective-permute-start.10 = (bf16[1648,128]{1,0:T(8,128)(2,1)S(1)}, bf16[1648,128]{1,0:T(8,128)(2,1)S(1)}, u32[]{:S(2)}, u32[]{:S(2)}) collective-permute-start(bf16[1648,128]{1,0:T(8,128)(2,1)S(1)} %get-tuple-element.50), channel_id=1, source_target_pairs={{0,1},{1,0},{2,3},{3,2},{4,5},{5,4},{6,7},{7,6},{8,9},{9,8},{10,11... | collective-permute-start | bytes 1265672 | tf_op jit(solution)/shard_map/ppermute | solution.py:502
  74.6 1.5 %collective-permute-done.10 = bf16[1648,128]{1,0:T(8,128)(2,1)S(1)} collective-permute-done((bf16[1648,128]{1,0:T(8,128)(2,1)S(1)}, bf16[1648,128]{1,0:T(8,128)(2,1)S(1)}, u32[]{:S(2)}, u32[]{:S(2)}) %collective-permute-start.10) | collective-permute-done | bytes 421920 | tf_op jit(solution)/shard_map/ppermute | solution.py:502
  77.0 5.0 %all-to-all-start = ((bf16[16,128,128]{2,1,0:T(8,128)(2,1)}), bf16[16,128,128]{2,1,0:T(8,128)(2,1)S(1)}, u32[]{:S(2)}, u32[]{:S(2)}) async-start(bf16[16,128,128]{2,1,0:T(8,128)(2,1)} %pad_maximum_fusion), calls=%async_computation | async-start | bytes 1048576 | tf_op jit(solution)/shard_map/all_to_all | solution.py:589
  82.2 4.9 %collective-permute-start.11 = (bf16[112,128]{1,0:T(8,128)(2,1)S(1)}, bf16[112,128]{1,0:T(8,128)(2,1)S(1)}, u32[]{:S(2)}, u32[]{:S(2)}) collective-permute-start(bf16[112,128]{1,0:T(8,128)(2,1)S(1)} %get-tuple-element.59), channel_id=1, source_target_pairs={{0,480},{16,48},{32,0},{48,80},{64,32},{80,112},{96,64},{112,144},... | collective-permute-start | bytes 86024 | tf_op jit(solution)/shard_map/ppermute | solution.py:509
  87.1 5.5 %all-to-all-done = bf16[16,128,128]{2,1,0:T(8,128)(2,1)S(1)} async-done(((bf16[16,128,128]{2,1,0:T(8,128)(2,1)}), bf16[16,128,128]{2,1,0:T(8,128)(2,1)S(1)}, u32[]{:S(2)}, u32[]{:S(2)}) %all-to-all-start) | async-done | bytes 524320 | tf_op jit(solution)/shard_map/all_to_all | solution.py:589
  92.7 10.1 %collective-permute-start.12 = (bf16[288,128]{1,0:T(8,128)(2,1)S(1)}, bf16[288,128]{1,0:T(8,128)(2,1)S(1)}, u32[]{:S(2)}, u32[]{:S(2)}) collective-permute-start(bf16[288,128]{1,0:T(8,128)(2,1)S(1)} %pad_maximum_fusion.1), channel_id=1, source_target_pairs={{0,16},{16,0},{32,48},{48,32},{64,80},{80,64},{96,112},{112,96},{1... | collective-permute-start | bytes 221192 | tf_op jit(solution)/shard_map/ppermute | solution.py:505
  102.8 9.4 %collective-permute-done.12.rim_ref = bf16[288,128]{1,0:T(8,128)(2,1)S(1)} collective-permute-done((bf16[288,128]{1,0:T(8,128)(2,1)S(1)}, bf16[288,128]{1,0:T(8,128)(2,1)S(1)}, u32[]{:S(2)}, u32[]{:S(2)}) %collective-permute-start.12) | collective-permute-done | bytes 73760 | tf_op jit(solution)/shard_map/ppermute | solution.py:505
  (39 shorter events, 6.1 us)
Async XLA Ops:
  0.6 35.8 %copy-start = (bf16[235,1024]{1,0:T(8,128)(2,1)S(1)}, bf16[235,1024]{1,0:T(8,128)(2,1)}, u32[]{:S(2)}) copy-start(bf16[235,1024]{1,0:T(8,128)(2,1)} %wig_ref.3) | copy-start | bytes 1443844
  0.6 35.8 %copy-start.8 = (f32[1024]{0:T(1024)S(1)}, f32[1024]{0:T(1024)}, u32[]{:S(2)}) copy-start(f32[1024]{0:T(1024)} %param.15) | copy-start | bytes 12292
  2.9 33.5 %copy-start.3 = (bf16[400,128]{1,0:T(8,128)(2,1)S(1)}, bf16[400,128]{1,0:T(8,128)(2,1)}, u32[]{:S(2)}) copy-start(bf16[400,128]{1,0:T(8,128)(2,1)} %get-tuple-element.31.node_ref) | copy-start | bytes 307204
  2.9 25.6 %collective-permute-start.3 = (bf16[224,128]{1,0:T(8,128)(2,1)}, bf16[224,128]{1,0:T(8,128)(2,1)S(1)}, u32[]{:S(2)}, u32[]{:S(2)}) collective-permute-start(bf16[224,128]{1,0:T(8,128)(2,1)} %get-tuple-element.32), channel_id=1, source_target_pairs={{0,16},{16,0},{32,48},{48,32},{64,80},{80,64},{96,112},{112,96},{1... | collective-permute-start | bytes 172040 | tf_op jit(solution)/shard_map/ppermute | solution.py:505
  17.9 22.3 %collective-permute-start = (bf16[400,128]{1,0:T(8,128)(2,1)}, bf16[400,128]{1,0:T(8,128)(2,1)S(1)}, u32[]{:S(2)}, u32[]{:S(2)}) collective-permute-start(bf16[400,128]{1,0:T(8,128)(2,1)} %get-tuple-element.30.refs_0_), channel_id=1, source_target_pairs={{0,8},{1,9},{2,10},{3,11},{4,12},{5,13},{6,14},{7,15},{8,0},{9,1},... | collective-permute-start | bytes 307208 | tf_op jit(solution)/shard_map/ppermute | solution.py:502
  22.2 18.0 %collective-permute-start.1 = (bf16[400,128]{1,0:T(8,128)(2,1)}, bf16[400,128]{1,0:T(8,128)(2,1)S(1)}, u32[]{:S(2)}, u32[]{:S(2)}) collective-permute-start(bf16[400,128]{1,0:T(8,128)(2,1)} %get-tuple-element.30.refs_0_), channel_id=1, source_target_pairs={{0,4},{1,5},{2,6},{3,7},{4,0},{5,1},{6,2},{7,3},{8,12},{9,13},{10,... | collective-permute-start | bytes 307208 | tf_op jit(solution)/shard_map/ppermute | solution.py:502
  25.6 14.7 %collective-permute-start.2 = (bf16[400,128]{1,0:T(8,128)(2,1)}, bf16[400,128]{1,0:T(8,128)(2,1)S(1)}, u32[]{:S(2)}, u32[]{:S(2)}) collective-permute-start(bf16[400,128]{1,0:T(8,128)(2,1)} %get-tuple-element.30.refs_0_), channel_id=1, source_target_pairs={{0,2},{1,3},{2,0},{3,1},{4,6},{5,7},{6,4},{7,5},{8,10},{9,11},{10,... | collective-permute-start | bytes 307208 | tf_op jit(solution)/shard_map/ppermute | solution.py:502
  28.5 7.9 %collective-permute-start.4 = (bf16[112,128]{1,0:T(8,128)(2,1)S(1)}, bf16[112,128]{1,0:T(8,128)(2,1)S(1)}, u32[]{:S(2)}, u32[]{:S(2)}) collective-permute-start(bf16[112,128]{1,0:T(8,128)(2,1)S(1)} %constant_dynamic-slice_fusion), channel_id=1, source_target_pairs={{0,32},{16,496},{32,64},{48,16},{64,96},{80,48},{96,128},{112,80},... | collective-permute-start | bytes 86024 | tf_op jit(solution)/shard_map/ppermute | solution.py:509
  36.4 0.7 copy-start.7
  36.4 0.7 copy-start.6
  37.1 1.0 copy-start.1
  38.1 11.4 %copy-start.2 = (bf16[400,128]{1,0:T(8,128)(2,1)S(1)}, bf16[400,128]{1,0:T(8,128)(2,1)}, u32[]{:S(2)}) copy-start(bf16[400,128]{1,0:T(8,128)(2,1)} %get-tuple-element.30.refs_0_) | copy-start | bytes 307204
  40.2 11.6 %collective-permute-start.5 = (bf16[400,128]{1,0:T(8,128)(2,1)S(1)}, bf16[400,128]{1,0:T(8,128)(2,1)}, u32[]{:S(2)}, u32[]{:S(2)}) collective-permute-start(bf16[400,128]{1,0:T(8,128)(2,1)S(1)} %collective-permute-done.refs_0_), channel_id=1, source_target_pairs={{0,4},{1,5},{2,6},{3,7},{4,0},{5,1},{6,2},{7,3},{8,12},{9,13},{10,... | collective-permute-start | bytes 307208 | tf_op jit(solution)/shard_map/ppermute | solution.py:502
  43.6 8.3 %collective-permute-start.6 = (bf16[400,128]{1,0:T(8,128)(2,1)S(1)}, bf16[400,128]{1,0:T(8,128)(2,1)S(1)}, u32[]{:S(2)}, u32[]{:S(2)}) collective-permute-start(bf16[400,128]{1,0:T(8,128)(2,1)S(1)} %collective-permute-done.refs_0_), channel_id=1, source_target_pairs={{0,2},{1,3},{2,0},{3,1},{4,6},{5,7},{6,4},{7,5},{8,10},{9,11},{10,... | collective-permute-start | bytes 307208 | tf_op jit(solution)/shard_map/ppermute | solution.py:502
  46.5 6.6 %collective-permute-start.7 = (bf16[400,128]{1,0:T(8,128)(2,1)S(1)}, bf16[400,128]{1,0:T(8,128)(2,1)S(1)}, u32[]{:S(2)}, u32[]{:S(2)}) collective-permute-start(bf16[400,128]{1,0:T(8,128)(2,1)S(1)} %collective-permute-done.1.refs_0_), channel_id=1, source_target_pairs={{0,2},{1,3},{2,0},{3,1},{4,6},{5,7},{6,4},{7,5},{8,10},{9,11},{10,... | collective-permute-start | bytes 307208 | tf_op jit(solution)/shard_map/ppermute | solution.py:502
  53.1 0.6 copy-start.4
  53.7 9.6 %collective-permute-start.9 = (bf16[3424,128]{1,0:T(8,128)(2,1)S(1)}, bf16[3424,128]{1,0:T(8,128)(2,1)S(1)}, u32[]{:S(2)}, u32[]{:S(2)}) collective-permute-start(bf16[3424,128]{1,0:T(8,128)(2,1)S(1)} %get-tuple-element.45.own_ref.xo_ref), channel_id=1, source_target_pairs={{0,1},{1,0},{2,3},{3,2},{4,5},{5,4},{6,7},{7,6},{8,9},{9,8},{10,11... | collective-permute-start | bytes 2629640 | tf_op jit(solution)/shard_map/ppermute | solution.py:502
  55.6 8.2 %collective-permute-start.8 = (bf16[400,128]{1,0:T(8,128)(2,1)}, bf16[400,128]{1,0:T(8,128)(2,1)}, u32[]{:S(2)}, u32[]{:S(2)}) collective-permute-start(bf16[400,128]{1,0:T(8,128)(2,1)} %collective-permute-done.5.near_ref), channel_id=1, source_target_pairs={{0,2},{1,3},{2,0},{3,1},{4,6},{5,7},{6,4},{7,5},{8,10},{9,11},{10,... | collective-permute-start | bytes 307208 | tf_op jit(solution)/shard_map/ppermute | solution.py:502
  58.6 2.4 %copy-start.5 = (bf16[400,128]{1,0:T(8,128)(2,1)S(1)}, bf16[400,128]{1,0:T(8,128)(2,1)}, u32[]{:S(2)}) copy-start(bf16[400,128]{1,0:T(8,128)(2,1)} %copy-done.4) | copy-start | bytes 307204
  72.5 3.7 %collective-permute-start.10 = (bf16[1648,128]{1,0:T(8,128)(2,1)S(1)}, bf16[1648,128]{1,0:T(8,128)(2,1)S(1)}, u32[]{:S(2)}, u32[]{:S(2)}) collective-permute-start(bf16[1648,128]{1,0:T(8,128)(2,1)S(1)} %get-tuple-element.50), channel_id=1, source_target_pairs={{0,1},{1,0},{2,3},{3,2},{4,5},{5,4},{6,7},{7,6},{8,9},{9,8},{10,11... | collective-permute-start | bytes 1265672 | tf_op jit(solution)/shard_map/ppermute | solution.py:502
  77.0 15.5 %all-to-all-start = ((bf16[16,128,128]{2,1,0:T(8,128)(2,1)}), bf16[16,128,128]{2,1,0:T(8,128)(2,1)S(1)}, u32[]{:S(2)}, u32[]{:S(2)}) async-start(bf16[16,128,128]{2,1,0:T(8,128)(2,1)} %pad_maximum_fusion), calls=%async_computation | async-start | bytes 1048576 | tf_op jit(solution)/shard_map/all_to_all | solution.py:589
  82.2 10.5 %collective-permute-start.11 = (bf16[112,128]{1,0:T(8,128)(2,1)S(1)}, bf16[112,128]{1,0:T(8,128)(2,1)S(1)}, u32[]{:S(2)}, u32[]{:S(2)}) collective-permute-start(bf16[112,128]{1,0:T(8,128)(2,1)S(1)} %get-tuple-element.59), channel_id=1, source_target_pairs={{0,480},{16,48},{32,0},{48,80},{64,32},{80,112},{96,64},{112,144},... | collective-permute-start | bytes 86024 | tf_op jit(solution)/shard_map/ppermute | solution.py:509
  92.7 19.5 %collective-permute-start.12 = (bf16[288,128]{1,0:T(8,128)(2,1)S(1)}, bf16[288,128]{1,0:T(8,128)(2,1)S(1)}, u32[]{:S(2)}, u32[]{:S(2)}) collective-permute-start(bf16[288,128]{1,0:T(8,128)(2,1)S(1)} %pad_maximum_fusion.1), channel_id=1, source_target_pairs={{0,16},{16,0},{32,48},{48,32},{64,80},{80,64},{96,112},{112,96},{1... | collective-permute-start | bytes 221192 | tf_op jit(solution)/shard_map/ppermute | solution.py:505
